TPU v7x, 32 devices: a whole 2x2x4 slice. The times are simulated.
32 devices in a mesh: prow: 4 (over z), pcol: 4 (over y, core), pl: 2 (over x).
Axes of the slice: x: 2, y: 2, z: 4, core: 2. Of those that a mesh axis runs over, the one named last changes fastest.
Arguments:
- factor_cols: bfloat16 [32768, 512], P(('prow', 'pcol'), 'pl'), may hold values from -0.25 to 0.25
- modal_at_loads: bfloat16 [2048, 32768], P(None, ('prow', 'pcol')), may hold values from -0.03125 to 0.03125
- mode_shapes: bfloat16 [8192, 2048], P(('prow', 'pl')), may hold values from -0.125 to 0.125
- natural_freq: float32 [2048], replicated, may hold values from 0.5 to 2
- damping: float32 [2048], replicated, may hold values from 0.05 to 0.2
Outputs:
- cospectrum: float32 [8192, 8192], P(('prow', 'pl'), 'pcol')
All inputs are finite; a program needn't handle non-finite values.
Results may differ from a plain program's by a relative error of at most 0.022.
Values may be sent and summed in bfloat16 or wider, within the bound.
No kernel may reach another device: no remote copies, remote signals or barrier semaphores. Data moves between devices by JAX's collectives and lax.ppermute only.
A program may use at most 128 MiB of HBM per device.

v0:
```python
import jax
import jax.numpy as jnp
from jax import lax
from jax.sharding import PartitionSpec as P


def from_root(array, axis, root):
    mine = lax.axis_index(axis) == root
    return lax.psum(jnp.where(mine, array, jnp.zeros_like(array)), axis)


def transfer_pair(natural_freq, damping):
    detuning = natural_freq * natural_freq - 1.0
    damper = 2.0 * damping * natural_freq
    modulus = detuning * detuning + damper * damper
    return (detuning / modulus, -damper / modulus)


def outer_rows(left_rows, right_rows):
    return lax.dot_general(
        left_rows, right_rows, (((1,), (1,)), ((), ())), preferred_element_type=jnp.float32
    )


def body(factor_cols, modal_at_loads, mode_shapes, natural_freq, damping):
    in_phase, quadrature = transfer_pair(natural_freq, damping)
    own_rows = lax.psum_scatter(
        jnp.dot(modal_at_loads, factor_cols, preferred_element_type=jnp.float32),
        ("prow", "pcol"),
        scatter_dimension=0,
        tiled=True,
    )
    modal_load = lax.all_gather(own_rows.astype(jnp.bfloat16), ("prow", "pcol"), axis=0, tiled=True)
    modal_wide = modal_load.astype(jnp.float32)
    pseudo = jnp.concatenate(
        [
            (in_phase[:, None] * modal_wide).astype(jnp.bfloat16),
            (quadrature[:, None] * modal_wide).astype(jnp.bfloat16),
        ],
        axis=1,
    )
    block = pseudo.shape[0] // lax.axis_size(("prow", "pcol"))
    first_row = lax.axis_index(("prow", "pcol")) * block
    own_pseudo = lax.dynamic_slice_in_dim(pseudo, first_row, block, 0)
    partial_gram = outer_rows(own_pseudo, pseudo)
    gram_block = lax.psum(partial_gram.astype(jnp.bfloat16), "pl")
    modal_gram = lax.all_gather(gram_block, ("prow", "pcol"), axis=0, tiled=True)
    weighted = jnp.dot(mode_shapes, modal_gram, preferred_element_type=jnp.float32).astype(
        jnp.bfloat16
    )
    panel_piece = from_root(mode_shapes, "prow", lax.axis_index("pcol"))
    return outer_rows(weighted, lax.all_gather(panel_piece, "pl", axis=0, tiled=True))


def solution(mesh):
    in_specs = (
        P(("prow", "pcol"), "pl"),
        P(None, ("prow", "pcol")),
        P(("prow", "pl"), None),
        P(),
        P(),
    )
    out_specs = P(("prow", "pl"), "pcol")
    return jax.shard_map(body, mesh=mesh, in_specs=in_specs, out_specs=out_specs, check_vma=False)
```

profile of v0, /device:TPU:4, one launch (start us, length us, event | category | flops | bytes accessed | tf_op | source)
XLA Modules:
  0.0 485.0 jit_solution(5799082119248472755)
XLA Ops:
  7.4 0.0 copy-start
  7.4 0.0 reduce-scatter.2.cloned.1.call-start
  7.4 1.2 copy-done
  8.6 7.1 %fusion.11 = f32[2048,256]{1,0:T(8,128)} fusion(bf16[2048,2048]{1,0:T(8,128)(2,1)} %param.6, bf16[2048,256]{1,0:T(8,128)(2,1)S(1)} %copy-done), kind=kOutput, calls=%fused_computation.20 | convolution fusion | flops 2147483648 | bytes 11534336 | tf_op jit(solution)/shard_map/dot_general | solution.py:28
  15.6 0.0 reduce-scatter.2.cloned.1.call-update
  15.7 0.0 all-gather.4.cloned.1.call-start
  15.7 62.5 %reduce-scatter.2.cloned.1.call-done = f32[128,256]{1,0:T(8,128)} async-done(((f32[2048,256]{1,0:T(8,128)}), f32[128,256]{1,0:T(8,128)}) %reduce-scatter.2.cloned.1.call-update) | async-done | bytes 131088 | tf_op jit(solution)/shard_map/reduce_scatter | solution.py:27
  78.3 1.5 convert_element_type.19
  79.8 0.0 all-gather.4.cloned.1.call-update
  79.8 0.0 all-reduce.5.cloned.1.call-start
  79.9 2.3 broadcast_select_fusion
  82.2 0.0 copy-start.1
  82.2 0.0 copy-start.2
  82.2 0.0 all-reduce.5.cloned.1.call-update
  82.2 0.0 all-reduce.3.cloned.1.call-start
  82.3 0.6 copy-done.1
  82.9 0.0 copy-done.2
  82.9 88.3 %all-gather.4.cloned.1.call-done = bf16[2048,256]{1,0:T(8,128)(2,1)} async-done(((bf16[128,256]{1,0:T(8,128)(2,1)}), bf16[2048,256]{1,0:T(8,128)(2,1)}) %all-gather.4.cloned.1.call-update) | async-done | bytes 1048592 | tf_op jit(solution)/shard_map/all_gather | solution.py:33
  171.2 1.8 fusion.4
  173.0 1.6 convolution_convert_fusion
  174.6 0.0 all-reduce.3.cloned.1.call-update
  174.6 0.0 all-gather.8.cloned.1.call-start
  174.7 65.5 %all-reduce.5.cloned.1.call-done = bf16[1024,2048]{1,0:T(8,128)(2,1)} async-done(((bf16[1024,2048]{1,0:T(8,128)(2,1)}), bf16[1024,2048]{1,0:T(8,128)(2,1)}) %all-reduce.5.cloned.1.call-update) | async-done | bytes 4194320 | tf_op jit(solution)/shard_map/psum | solution.py:9
  240.2 0.0 all-gather.8.cloned.1.call-update
  240.3 0.2 all-gather.6.cloned.1.call-start
  240.5 29.3 %all-reduce.3.cloned.1.call-done = bf16[128,2048]{1,0:T(8,128)(2,1)} async-done(((bf16[128,2048]{1,0:T(8,128)(2,1)}), bf16[128,2048]{1,0:T(8,128)(2,1)}) %all-reduce.3.cloned.1.call-update) | async-done | bytes 524304 | tf_op jit(solution)/shard_map/psum | solution.py:46
  269.8 0.0 all-gather.6.cloned.1.call-update
  269.8 105.3 %all-gather.8.cloned.1.call-done = bf16[2048,2048]{1,0:T(8,128)(2,1)} async-done(((bf16[1024,2048]{1,0:T(8,128)(2,1)}), bf16[2048,2048]{1,0:T(8,128)(2,1)}) %all-gather.8.cloned.1.call-update) | async-done | bytes 8388624 | tf_op jit(solution)/shard_map/all_gather | solution.py:52
  375.1 76.0 %all-gather.6.cloned.1.call-done = bf16[2048,2048]{1,0:T(8,128)(2,1)} async-done(((bf16[128,2048]{1,0:T(8,128)(2,1)}), bf16[2048,2048]{1,0:T(8,128)(2,1)}) %all-gather.6.cloned.1.call-update) | async-done | bytes 8388624 | tf_op jit(solution)/shard_map/all_gather | solution.py:47
  451.1 26.3 %fusion = f32[1024,2048]{1,0:T(8,128)} fusion(bf16[2048,2048]{1,0:T(8,128)(2,1)} %all-gather.8.cloned.1.call-done, bf16[2048,2048]{1,0:T(8,128)(2,1)} %all-gather.6.cloned.1.call-done, bf16[1024,2048]{1,0:T(8,128)(2,1)} %param.7), kind=kOutput, calls=%fused_computation | convolution fusion | flops 17181966336 | bytes 29360128 | tf_op jit(solution)/shard_map/dot_general | solution.py:20
  (1 shorter events, 0.0 us)
Async XLA Ops:
  7.4 1.2 copy-start
  7.4 70.9 %reduce-scatter.2.cloned.1.call-start = ((), (), s32[]{:S(2)}) async-start(), calls=%async_computation.1 | async-start | bytes 2228224 | tf_op jit(solution)/shard_map/reduce_scatter | solution.py:27
  15.7 155.5 %all-gather.4.cloned.1.call-start = ((), (), s32[]{:S(2)}) async-start(), calls=%async_computation.2 | async-start | bytes 1114112 | tf_op jit(solution)/shard_map/all_gather | solution.py:33
  79.8 160.4 %all-reduce.5.cloned.1.call-start = ((), (), s32[]{:S(2)}) async-start(), calls=%async_computation.5 | async-start | bytes 8388608 | tf_op jit(solution)/shard_map/psum | solution.py:9
  82.2 0.7 copy-start.1
  82.2 0.7 copy-start.2
  82.2 187.6 %all-reduce.3.cloned.1.call-start = ((), (), s32[]{:S(2)}) async-start(), calls=%async_computation.3 | async-start | bytes 1048576 | tf_op jit(solution)/shard_map/psum | solution.py:46
  174.6 200.5 %all-gather.8.cloned.1.call-start = ((), (), s32[]{:S(2)}) async-start(), calls=%async_computation.6 | async-start | bytes 12582912 | tf_op jit(solution)/shard_map/all_gather | solution.py:52
  240.3 210.9 %all-gather.6.cloned.1.call-start = ((), (), s32[]{:S(2)}) async-start(), calls=%async_computation.4 | async-start | bytes 8912896 | tf_op jit(solution)/shard_map/all_gather | solution.py:47
Sparse Core Ops, SparseCore 0:
  15.8 62.4 reduce-scatter.1
  80.4 90.7 all-gather.3
Sparse Core Ops, SparseCore 1:
  82.7 157.5 all-reduce.4
  242.4 27.3 all-reduce.2
  271.3 103.8 all-gather.7
  377.5 73.5 all-gather.5
where the time goes:
time: 488 us; the launch traced here: 485 us
  waiting for transfers between devices  427 us (88%)
  matrix products  35 us (7%)
  between operations  15.1 us (3%)
  other arithmetic  5.6 us (1%)
    all_gather x1, waiting for transfers between devices, body(): lax.all_gather(panel_piece, 'pl', axis=0, tiled=True)  105 us
    all_gather x1, waiting for transfers between devices, body(): lax.all_gather(own_rows.astype(jnp.bfloat16), ('prow', 'pcol'), axis=0, t...  88.3 us
    all_gather x1, waiting for transfers between devices, body(): lax.all_gather(gram_block, ('prow', 'pcol'), axis=0, tiled=True)  76 us
    psum x1, waiting for transfers between devices, from_root(): return lax.psum(jnp.where(mine, array, jnp.zeros_like(array)), axis)  65.5 us
    reduce_scatter x1, waiting for transfers between devices, body(): lax.psum_scatter(jnp.dot(modal_at_loads, factor_cols, preferred_element_t...  62.5 us
    psum x1, waiting for transfers between devices, body(): gram_block = lax.psum(partial_gram.astype(jnp.bfloat16), 'pl')  29.3 us
    dot_general x2, matrix products, outer_rows(): lax.dot_general(left_rows, right_rows, (((1,), (1,)), ((), ())), preferre...  27.9 us
  transfers between devices with their start and end apart: 6, of which 6 were waited for; matrix products, arithmetic and copies ran while one was open for 1% of the time, Pallas kernels for 0%

commit v1 on v0

v1 whole, which is shorter than its diff:
```python
import functools

import jax
import jax.numpy as jnp
from jax import lax
from jax.experimental import pallas as pl
from jax.experimental.pallas import tpu as pltpu
from jax.sharding import PartitionSpec as P

AXES = ("prow", "pcol", "pl")
CORES = 2
CHUNKS = 4
LATE = 0
WIDE = 512
VMEM_BYTES = 48 * 1024 * 1024


def transfer_pair(natural_freq, damping):
    detuning = natural_freq * natural_freq - 1.0
    damper = 2.0 * damping * natural_freq
    modulus = detuning * detuning + damper * damper
    return detuning / modulus, -damper / modulus


def moves(sizes, source_of):
    rows, cols, groups = sizes
    pairs = []
    for i in range(rows):
        for j in range(cols):
            for k in range(groups):
                a, b, c = source_of(i, j, k)
                pairs.append(((a * cols + b) * groups + c, (i * cols + j) * groups + k))
    return pairs


def swap(array, sizes, di, dj, dk):
    return lax.ppermute(array, AXES, moves(sizes, lambda i, j, k: (i ^ di, j ^ dj, k ^ dk)))


def across(array, sizes, flip):
    return lax.ppermute(array, AXES, moves(sizes, lambda i, j, k: (j, i ^ flip, k)))


def outer_rows(left_rows, right_rows):
    return lax.dot_general(
        left_rows, right_rows, (((1,), (1,)), ((), ())), preferred_element_type=jnp.float32
    )


def load_kernel(rows, spots, scale, *refs):
    out = refs[-1]
    blocks = refs[: spots.shape[0] - 1]
    for at, block in enumerate(blocks):
        for part in range(block.shape[0] // rows):
            first = pl.multiple_of(spots[1 + at] + (spots[0] ^ part) * rows, rows)
            load = block[part * rows : (part + 1) * rows, :].astype(jnp.float32)
            out[pl.ds(first, rows), :] = (scale[0, pl.ds(first, rows), :] * load).astype(out.dtype)


def place_loads(blocks, firsts, own_row, rows, group, groups, scale, loads):
    modes, wide = scale.shape[1], blocks[0].shape[1]
    spots = jnp.stack([own_row, *firsts]).astype(jnp.int32)
    column = jnp.reshape(group, (1,)).astype(jnp.int32)
    given = [] if loads is None else [loads]
    return pl.pallas_call(
        lambda spots, column, *refs: load_kernel(rows, spots, *refs),
        grid_spec=pltpu.PrefetchScalarGridSpec(
            num_scalar_prefetch=2,
            grid=(2,),
            in_specs=[pl.BlockSpec((1, modes, 1), lambda g, spots, column: (g, 0, 0))]
            + [pl.BlockSpec(b.shape, lambda g, spots, column: (0, 0)) for b in blocks]
            + [pl.BlockSpec(memory_space=pl.ANY) for _ in given],
            out_specs=pl.BlockSpec((modes, wide), lambda g, spots, column: (0, g * groups + column[0])),
        ),
        out_shape=jax.ShapeDtypeStruct((modes, 2 * groups * wide), jnp.bfloat16),
        input_output_aliases={3 + len(blocks): 0} if given else {},
        compiler_params=pltpu.CompilerParams(vmem_limit_bytes=VMEM_BYTES),
    )(spots, column, scale, *blocks, *given)


def shape_kernel(place, shapes, loads, left, *refs):
    out = refs[-1]
    right = jnp.dot(shapes[...], loads[...], preferred_element_type=jnp.float32).astype(jnp.bfloat16)
    part = outer_rows(left[...], right)

    @pl.when(pl.program_id(0) == 0)
    def _():
        out[...] = part

    @pl.when(pl.program_id(0) != 0)
    def _():
        out[...] += part


def place_panel(shapes, loads, left, place, columns, panel):
    modes, wide = loads.shape
    rows, chunk = left.shape[0], shapes.shape[0]
    step = min(WIDE, wide)
    given = [] if panel is None else [panel]
    return pl.pallas_call(
        shape_kernel,
        grid_spec=pltpu.PrefetchScalarGridSpec(
            num_scalar_prefetch=1,
            grid=(wide // step,),
            in_specs=[
                pl.BlockSpec((chunk, modes), lambda g, place: (0, 0)),
                pl.BlockSpec((modes, step), lambda g, place: (0, g)),
                pl.BlockSpec((rows, step), lambda g, place: (0, g)),
            ]
            + [pl.BlockSpec(memory_space=pl.ANY) for _ in given],
            out_specs=pl.BlockSpec((rows, chunk), lambda g, place: (0, place[0])),
        ),
        out_shape=jax.ShapeDtypeStruct((rows, columns), jnp.float32),
        input_output_aliases={4: 0} if given else {},
        compiler_params=pltpu.CompilerParams(vmem_limit_bytes=VMEM_BYTES),
        cost_estimate=pl.CostEstimate(
            flops=2 * chunk * wide * (modes + rows),
            bytes_accessed=2 * wide * (modes + rows) + 2 * chunk * modes + 4 * rows * chunk,
            transcendentals=0,
        ),
    )(jnp.reshape(place, (1,)).astype(jnp.int32), shapes, loads, left, *given)


def body(sizes, factor_cols, modal_at_loads, mode_shapes, natural_freq, damping):
    n_rows, n_cols, n_groups = sizes
    n_high = n_cols // CORES
    row, col, group = (lax.axis_index(axis) for axis in AXES)
    high, core = col // CORES, col % CORES
    scale = jnp.stack(transfer_pair(natural_freq, damping))[:, :, None]

    own_rows = mode_shapes.shape[0]
    chunk = max(own_rows // CHUNKS, min(own_rows, 128))
    chunks = own_rows // chunk
    same = [
        across(mode_shapes[q * chunk : (q + 1) * chunk], sizes, CORES * (q % 2)) for q in range(chunks)
    ]
    other = [[swap(piece, sizes, 0, 0, d) for d in range(1, n_groups)] for piece in same]

    modes = modal_at_loads.shape[0]
    half, block = modes // CORES, modes // (n_rows * n_cols)
    away = lax.dynamic_slice_in_dim(modal_at_loads, (1 - core) * half, half, 0)
    here = lax.dynamic_slice_in_dim(modal_at_loads, core * half, half, 0)
    sent = jnp.dot(away, factor_cols, preferred_element_type=jnp.float32).astype(jnp.bfloat16)
    came = swap(sent, sizes, 0, 1, 0)
    partial = jnp.dot(here, factor_cols, preferred_element_type=jnp.float32) + came.astype(jnp.float32)
    partial = partial.astype(jnp.bfloat16)
    total = None
    for dh in range(n_high):
        for dr in range(n_rows):
            first = ((high ^ dh) * n_rows + (row ^ dr)) * block
            part = lax.dynamic_slice_in_dim(partial, first, block, 0)
            if dh or dr:
                part = swap(part, sizes, dr, dh * CORES, 0)
            part = part.astype(jnp.float32)
            total = part if total is None else total + part
    own = total.astype(jnp.bfloat16)
    line = jnp.concatenate([own] + [swap(own, sizes, d, 0, 0) for d in range(1, n_rows)], axis=0)
    loads = None
    for dk in range(n_groups):
        mine = [
            swap(line, sizes, 0, dh * CORES, dk) if dh or dk else line for dh in range(n_high)
        ]
        theirs = [swap(piece, sizes, 0, 1, 0) for piece in mine]
        firsts = [
            (which * n_high + (high ^ dh)) * n_rows * block
            for which in (core, 1 - core)
            for dh in range(n_high)
        ]
        loads = place_loads(
            mine + theirs, firsts, row, block, group ^ dk, n_groups, scale, loads
        )

    left = jnp.dot(mode_shapes, loads, preferred_element_type=jnp.float32).astype(jnp.bfloat16)
    panel = None
    columns = own_rows * n_groups
    for q in range(chunks):
        for dk in range(n_groups):
            piece = other[q][dk - 1] if dk else same[q]
            place = (group ^ dk) * chunks + q
            panel = place_panel(piece, loads, left, place, columns, panel)
    return panel


def solution(mesh):
    sizes = tuple(mesh.shape[axis] for axis in AXES)
    in_specs = (
        P(("prow", "pcol"), "pl"),
        P(None, ("prow", "pcol")),
        P(("prow", "pl"), None),
        P(),
        P(),
    )
    out_specs = P(("prow", "pl"), "pcol")
    return jax.shard_map(
        functools.partial(body, sizes), mesh=mesh, in_specs=in_specs, out_specs=out_specs, check_vma=False
    )
```

time: 488 us -> 247 us (0.51)
  the two profiles are of different devices: /device:TPU:4 before, /device:TPU:20 now
where the time goes in v1:
time: 247 us; the launch traced here: 246 us
  waiting for transfers between devices  138 us (56%)
  Pallas kernels  46.8 us (19%)
  starting transfers between devices  38 us (15%)
  matrix products  13.7 us (6%)
  local copies, waits for them, and re-layouts  8.82 us (4%)
    ppermute x22, waiting for transfers between devices, swap(): lax.ppermute(array, AXES, moves(sizes, lambda i, j, k: (i ^ di, j ^ dj, k...  92.2 us
    ppermute x4, waiting for transfers between devices, across(): lax.ppermute(array, AXES, moves(sizes, lambda i, j, k: (j, i ^ flip, k)))  45.8 us
    pallas_call x8, Pallas kernels, place_panel(): pl.pallas_call(shape_kernel, grid_spec=pltpu.PrefetchScalarGridSpec(num_s...  40.7 us
    ppermute x22, starting transfers between devices, swap(): lax.ppermute(array, AXES, moves(sizes, lambda i, j, k: (i ^ di, j ^ dj, k...  24.8 us
    ppermute x4, starting transfers between devices, across(): lax.ppermute(array, AXES, moves(sizes, lambda i, j, k: (j, i ^ flip, k)))  13.2 us
    dot_general x1, matrix products, body(): jnp.dot(mode_shapes, loads, preferred_element_type=jnp.float32)  6.87 us
    unnamed x22, local copies, waits for them, and re-layouts  6.18 us
    pallas_call x2, Pallas kernels, place_loads(): pl.pallas_call(lambda spots, column, *refs: load_kernel(rows, spots, *ref...  6.07 us
  transfers between devices with their start and end apart: 26, of which 13 were waited for; matrix products, arithmetic and copies ran while one was open for 4% of the time, Pallas kernels for 17%

profile of v1, /device:TPU:20, one launch (start us, length us, event | category | flops | bytes accessed | tf_op | source)
XLA Modules:
  0.0 245.7 jit_solution(8724255794803112099)
XLA Ops:
  0.0 1.2 copy-done
  1.2 3.4 %fusion.4 = bf16[1024,256]{1,0:T(8,128)(2,1)S(1)} fusion(bf16[2048,256]{1,0:T(8,128)(2,1)S(1)} %copy-done, bf16[2048,2048]{1,0:T(8,128)(2,1)} %param.6, s32[]{:T(128)S(6)} %select_n.44), kind=kOutput, calls=%fused_computation.5 | convolution fusion | flops 1074003968 | bytes 5767172 | tf_op jit(solution)/shard_map/dot_general | solution.py:143
  4.7 0.1 collective-permute-start.2
  4.8 0.0 copy-start.7
  4.8 1.8 collective-permute-done.2
  6.6 3.4 %add_convert_fusion = bf16[1024,256]{1,0:T(8,128)(2,1)S(1)} fusion(bf16[1024,256]{1,0:T(8,128)(2,1)S(1)} %collective-permute-done.2, bf16[2048,256]{1,0:T(8,128)(2,1)S(1)} %copy-done, bf16[2048,2048]{1,0:T(8,128)(2,1)} %param.6, s32[]{:T(128)S(6)} %select_n.43), kind=kOutput, calls=%fused_computation.6 | convolution fusion | flops 1074528256 | bytes 6291460 | tf_op jit(solution)/shard_map/dot_general | solution.py:145
  10.1 0.1 constant_dynamic-slice_fusion.6
  10.1 1.6 collective-permute-start.3
  11.8 0.3 collective-permute-start.4
  12.1 1.6 collective-permute-start.5
  13.7 0.5 collective-permute-start.6
  14.2 3.4 %collective-permute-start.7 = (bf16[128,256]{1,0:T(8,128)(2,1)S(1)}, bf16[128,256]{1,0:T(8,128)(2,1)S(1)}, u32[]{:S(2)}, u32[]{:S(2)}) collective-permute-start(bf16[128,256]{1,0:T(8,128)(2,1)S(1)} %get-tuple-element.12), channel_id=1, source_target_pairs={{12,0},{13,1},{14,2},{15,3},{8,4},{9,5},{10,6},{11,7},{4,8},{5,9},... | collective-permute-start | bytes 196616 | tf_op jit(solution)/shard_map/ppermute | solution.py:37
  17.6 0.0 collective-permute-done.3
  17.6 0.0 collective-permute-done.4
  17.7 1.9 collective-permute-start.9
  19.6 1.9 fusion.12
  21.4 0.7 collective-permute-done.5
  22.1 1.7 collective-permute-start.24
  23.9 0.7 collective-permute-done.9
  24.6 0.1 add_convert_fusion.1
  24.7 3.2 %collective-permute-start.10 = (bf16[128,256]{1,0:T(8,128)(2,1)S(1)}, bf16[128,256]{1,0:T(8,128)(2,1)S(1)}, u32[]{:S(2)}, u32[]{:S(2)}) collective-permute-start(bf16[128,256]{1,0:T(8,128)(2,1)S(1)} %add_convert_fusion.1), channel_id=1, source_target_pairs={{8,0},{9,1},{10,2},{11,3},{12,4},{13,5},{14,6},{15,7},{0,8},{1,9},... | collective-permute-start | bytes 196616 | tf_op jit(solution)/shard_map/ppermute | solution.py:37
  27.9 1.5 collective-permute-start.12
  29.4 12.9 %collective-permute-done.10 = bf16[128,256]{1,0:T(8,128)(2,1)S(1)} collective-permute-done((bf16[128,256]{1,0:T(8,128)(2,1)S(1)}, bf16[128,256]{1,0:T(8,128)(2,1)S(1)}, u32[]{:S(2)}, u32[]{:S(2)}) %collective-permute-start.10) | collective-permute-done | bytes 65568 | tf_op jit(solution)/shard_map/ppermute | solution.py:37
  42.3 9.5 %collective-permute-done.11 = bf16[128,256]{1,0:T(8,128)(2,1)S(1)} collective-permute-done((bf16[128,256]{1,0:T(8,128)(2,1)S(1)}, bf16[128,256]{1,0:T(8,128)(2,1)S(1)}, u32[]{:S(2)}, u32[]{:S(2)}) %collective-permute-start.11) | collective-permute-done | bytes 65568 | tf_op jit(solution)/shard_map/ppermute | solution.py:37
  51.8 22.6 %collective-permute-done.12 = bf16[128,256]{1,0:T(8,128)(2,1)S(1)} collective-permute-done((bf16[128,256]{1,0:T(8,128)(2,1)S(1)}, bf16[128,256]{1,0:T(8,128)(2,1)S(1)}, u32[]{:S(2)}, u32[]{:S(2)}) %collective-permute-start.12) | collective-permute-done | bytes 65568 | tf_op jit(solution)/shard_map/ppermute | solution.py:37
  74.5 1.4 collective-permute-start.17
  75.9 0.1 collective-permute-start.18
  75.9 1.5 collective-permute-start.13
  77.4 2.0 collective-permute-start.22
  79.4 15.3 %collective-permute-done.17.refs_2_ = bf16[512,256]{1,0:T(8,128)(2,1)S(1)} collective-permute-done((bf16[512,256]{1,0:T(8,128)(2,1)S(1)}, bf16[512,256]{1,0:T(8,128)(2,1)S(1)}, u32[]{:S(2)}, u32[]{:S(2)}) %collective-permute-start.17) | collective-permute-done | bytes 262176 | tf_op jit(solution)/shard_map/ppermute | solution.py:37
  94.7 9.4 %collective-permute-start.20 = (bf16[256,2048]{1,0:T(8,128)(2,1)}, bf16[256,2048]{1,0:T(8,128)(2,1)}, u32[]{:S(2)}, u32[]{:S(2)}) collective-permute-start(bf16[256,2048]{1,0:T(8,128)(2,1)} %get-tuple-element.6), channel_id=1, source_target_pairs={{0,0},{1,1},{8,2},{9,3},{16,4},{17,5},{24,6},{25,7},{2,8},{3,9},{1... | collective-permute-start | bytes 3145736 | tf_op jit(solution)/shard_map/ppermute | solution.py:41
  104.1 0.7 copy-done.3
  104.8 0.0 collective-permute-start
  104.8 2.9 %collective-permute-start.14 = (bf16[512,256]{1,0:T(8,128)(2,1)S(1)}, bf16[512,256]{1,0:T(8,128)(2,1)}, u32[]{:S(2)}, u32[]{:S(2)}) collective-permute-start(bf16[512,256]{1,0:T(8,128)(2,1)S(1)} %pad_maximum_fusion.refs_1_), channel_id=1, source_target_pairs={{5,0},{4,1},{7,2},{6,3},{1,4},{0,5},{3,6},{2,7},{13,8},{12,9},{15,... | collective-permute-start | bytes 786440 | tf_op jit(solution)/shard_map/ppermute | solution.py:37
  107.8 6.6 %collective-permute-done.14.refs_2_ = bf16[512,256]{1,0:T(8,128)(2,1)} collective-permute-done((bf16[512,256]{1,0:T(8,128)(2,1)S(1)}, bf16[512,256]{1,0:T(8,128)(2,1)}, u32[]{:S(2)}, u32[]{:S(2)}) %collective-permute-start.14) | collective-permute-done | bytes 262176 | tf_op jit(solution)/shard_map/ppermute | solution.py:37
  114.3 0.7 copy-done.1
  115.0 0.5 collective-permute-start.15
  115.6 0.3 collective-permute-done.19.refs_4_
  115.9 0.7 copy-done.5
  116.6 0.1 collective-permute-start.16
  116.8 0.6 copy.16.refs_0_
  117.4 0.1 stack.38.spots
  117.5 1.0 copy-done.2
  118.5 0.9 copy-done.4
  119.4 0.9 copy-done.6
  120.4 2.3 shard_map.55.refs_5_
  122.7 25.6 %collective-permute-done.22.shapes = bf16[256,2048]{1,0:T(8,128)(2,1)} collective-permute-done((bf16[256,2048]{1,0:T(8,128)(2,1)}, bf16[256,2048]{1,0:T(8,128)(2,1)}, u32[]{:S(2)}, u32[]{:S(2)}) %collective-permute-start.22) | collective-permute-done | bytes 1048608 | tf_op jit(solution)/shard_map/ppermute | solution.py:41
  148.2 0.5 collective-permute-start.25
  148.8 1.5 collective-permute-start.23
  150.3 20.3 %collective-permute-done.shapes = bf16[256,2048]{1,0:T(8,128)(2,1)} collective-permute-done((bf16[256,2048]{1,0:T(8,128)(2,1)}, bf16[256,2048]{1,0:T(8,128)(2,1)}, u32[]{:S(2)}, u32[]{:S(2)}) %collective-permute-start) | collective-permute-done | bytes 1048608 | tf_op jit(solution)/shard_map/ppermute | solution.py:41
  170.5 0.5 collective-permute-start.21
  171.1 1.5 collective-permute-start.1
  172.6 3.8 %shard_map.56.loads = bf16[2048,1024]{1,0:T(8,128)(2,1)} custom-call(s32[5]{0:T(128)S(1)} %stack.38.spots, s32[1]{0:T(128)} %bitcast.6.column, f32[2,2048,1]{2,1,0:T(8,128)S(1)} %copy.16.refs_0_, bf16[512,256]{1,0:T(8,128)(2,1)} %collective-permute-done.13.refs_1_, bf16[512,256]{1,0:T(8,128)(2,1)} %collective-permute-done.14.refs_2_, ...), custom_call_target="tpu_custom_call", output_to_operand_aliasing={{}: (7, {})} | custom-call | tf_op jit(solution)/shard_map/pallas_call | solution.py:65
  176.3 6.9 %convert_bitcast_fusion.left = bf16[1024,1024]{1,0:T(8,128)(2,1)S(1)} fusion(bf16[1024,2048]{1,0:T(8,128)(2,1)S(1)} %copy-done.8, bf16[2048,1024]{1,0:T(8,128)(2,1)} %shard_map.56.loads), kind=kOutput, calls=%fused_computation.4 | convolution fusion | flops 4296015872 | bytes 10485760 | tf_op jit(solution)/shard_map/dot_general | solution.py:173
  183.2 5.2 %shard_map.57.refs_0_ = f32[1024,2048]{1,0:T(8,128)} custom-call(s32[1]{0:T(128)} %bitcast.18.place, bf16[256,2048]{1,0:T(8,128)(2,1)} %collective-permute-done.24.shapes, bf16[2048,1024]{1,0:T(8,128)(2,1)} %shard_map.56.loads, bf16[1024,1024]{1,0:T(8,128)(2,1)S(1)} %convert_bitcast_fusion.left), custom_call_target="tpu_custom_call" | custom-call | flops 1610612736 | bytes 8388608 | tf_op jit(solution)/shard_map/pallas_call | solution.py:100
  188.5 5.0 %shard_map.58.refs_0_ = f32[1024,2048]{1,0:T(8,128)} custom-call(s32[1]{0:T(128)} %bitcast.17.place, bf16[256,2048]{1,0:T(8,128)(2,1)S(1)} %collective-permute-done.25.shapes, bf16[2048,1024]{1,0:T(8,128)(2,1)} %shard_map.56.loads, bf16[1024,1024]{1,0:T(8,128)(2,1)S(1)} %convert_bitcast_fusion.left, ...), custom_call_target="tpu_custom_call", output_to_operand_aliasing={{}: (4, {})} | custom-call | flops 1610612736 | bytes 8388608 | tf_op jit(solution)/shard_map/pallas_call | solution.py:100
  193.4 5.2 %shard_map.59.refs_0_ = f32[1024,2048]{1,0:T(8,128)} custom-call(s32[1]{0:T(128)} %bitcast.16.place, bf16[256,2048]{1,0:T(8,128)(2,1)} %collective-permute-done.22.shapes, bf16[2048,1024]{1,0:T(8,128)(2,1)} %shard_map.56.loads, bf16[1024,1024]{1,0:T(8,128)(2,1)S(1)} %convert_bitcast_fusion.left, ...), custom_call_target="tpu_custom_call", output_to_operand_aliasing={{}: (4, {})} | custom-call | flops 1610612736 | bytes 8388608 | tf_op jit(solution)/shard_map/pallas_call | solution.py:100
  198.6 4.9 %shard_map.60.refs_0_ = f32[1024,2048]{1,0:T(8,128)} custom-call(s32[1]{0:T(128)} %bitcast.15.place, bf16[256,2048]{1,0:T(8,128)(2,1)S(1)} %collective-permute-done.23.shapes, bf16[2048,1024]{1,0:T(8,128)(2,1)} %shard_map.56.loads, bf16[1024,1024]{1,0:T(8,128)(2,1)S(1)} %convert_bitcast_fusion.left, ...), custom_call_target="tpu_custom_call", output_to_operand_aliasing={{}: (4, {})} | custom-call | flops 1610612736 | bytes 8388608 | tf_op jit(solution)/shard_map/pallas_call | solution.py:100
  203.6 5.2 %shard_map.61.refs_0_ = f32[1024,2048]{1,0:T(8,128)} custom-call(s32[1]{0:T(128)} %bitcast.14.place, bf16[256,2048]{1,0:T(8,128)(2,1)} %collective-permute-done.20.shapes, bf16[2048,1024]{1,0:T(8,128)(2,1)} %shard_map.56.loads, bf16[1024,1024]{1,0:T(8,128)(2,1)S(1)} %convert_bitcast_fusion.left, ...), custom_call_target="tpu_custom_call", output_to_operand_aliasing={{}: (4, {})} | custom-call | flops 1610612736 | bytes 8388608 | tf_op jit(solution)/shard_map/pallas_call | solution.py:100
  208.8 10.6 %collective-permute-done.21.shapes = bf16[256,2048]{1,0:T(8,128)(2,1)S(1)} collective-permute-done((bf16[256,2048]{1,0:T(8,128)(2,1)}, bf16[256,2048]{1,0:T(8,128)(2,1)S(1)}, u32[]{:S(2)}, u32[]{:S(2)}) %collective-permute-start.21) | collective-permute-done | bytes 1048608 | tf_op jit(solution)/shard_map/ppermute | solution.py:37
  219.4 5.0 %shard_map.62.refs_0_ = f32[1024,2048]{1,0:T(8,128)} custom-call(s32[1]{0:T(128)} %bitcast.13.place, bf16[256,2048]{1,0:T(8,128)(2,1)S(1)} %collective-permute-done.21.shapes, bf16[2048,1024]{1,0:T(8,128)(2,1)} %shard_map.56.loads, bf16[1024,1024]{1,0:T(8,128)(2,1)S(1)} %convert_bitcast_fusion.left, ...), custom_call_target="tpu_custom_call", output_to_operand_aliasing={{}: (4, {})} | custom-call | flops 1610612736 | bytes 8388608 | tf_op jit(solution)/shard_map/pallas_call | solution.py:100
  224.4 5.2 %shard_map.63.refs_0_ = f32[1024,2048]{1,0:T(8,128)} custom-call(s32[1]{0:T(128)} %bitcast.12.place, bf16[256,2048]{1,0:T(8,128)(2,1)} %collective-permute-done.shapes, bf16[2048,1024]{1,0:T(8,128)(2,1)} %shard_map.56.loads, bf16[1024,1024]{1,0:T(8,128)(2,1)S(1)} %convert_bitcast_fusion.left, ...), custom_call_target="tpu_custom_call", output_to_operand_aliasing={{}: (4, {})} | custom-call | flops 1610612736 | bytes 8388608 | tf_op jit(solution)/shard_map/pallas_call | solution.py:100
  229.6 11.1 %collective-permute-done.1.shapes = bf16[256,2048]{1,0:T(8,128)(2,1)S(1)} collective-permute-done((bf16[256,2048]{1,0:T(8,128)(2,1)}, bf16[256,2048]{1,0:T(8,128)(2,1)S(1)}, u32[]{:S(2)}, u32[]{:S(2)}) %collective-permute-start.1) | collective-permute-done | bytes 1048608 | tf_op jit(solution)/shard_map/ppermute | solution.py:37
  240.7 5.0 %shard_map.64 = f32[1024,2048]{1,0:T(8,128)} custom-call(s32[1]{0:T(128)} %bitcast.place, bf16[256,2048]{1,0:T(8,128)(2,1)S(1)} %collective-permute-done.1.shapes, bf16[2048,1024]{1,0:T(8,128)(2,1)} %shard_map.56.loads, bf16[1024,1024]{1,0:T(8,128)(2,1)S(1)} %convert_bitcast_fusion.left, f32[1024,2048]{1,0:T(8,128)} %shard_map.63.refs_0_), custom_call_target="tpu_custom_call", output_to_operand_aliasing={{}: (4, {})} | custom-call | flops 1610612736 | bytes 8388608 | tf_op jit(solution)/shard_map/pallas_call | solution.py:100
  (31 shorter events, 0.1 us)
Async XLA Ops:
  0.0 1.2 copy-start
  4.7 2.0 collective-permute-start.2
  4.8 14.7 %copy-start.7 = (bf16[1024,2048]{1,0:T(8,128)(2,1)S(1)}, bf16[1024,2048]{1,0:T(8,128)(2,1)}, u32[]{:S(2)}) copy-start(bf16[1024,2048]{1,0:T(8,128)(2,1)} %param.7) | copy-start | bytes 12582916
  10.1 7.5 %collective-permute-start.3 = (bf16[128,256]{1,0:T(8,128)(2,1)S(1)}, bf16[128,256]{1,0:T(8,128)(2,1)S(1)}, u32[]{:S(2)}, u32[]{:S(2)}) collective-permute-start(bf16[128,256]{1,0:T(8,128)(2,1)S(1)} %get-tuple-element.9), channel_id=1, source_target_pairs={{8,0},{9,1},{10,2},{11,3},{12,4},{13,5},{14,6},{15,7},{0,8},{1,9},... | collective-permute-start | bytes 196616 | tf_op jit(solution)/shard_map/ppermute | solution.py:37
  11.8 5.9 %collective-permute-start.4 = (bf16[128,256]{1,0:T(8,128)(2,1)S(1)}, bf16[128,256]{1,0:T(8,128)(2,1)S(1)}, u32[]{:S(2)}, u32[]{:S(2)}) collective-permute-start(bf16[128,256]{1,0:T(8,128)(2,1)S(1)} %get-tuple-element.15), channel_id=1, source_target_pairs={{16,0},{17,1},{18,2},{19,3},{20,4},{21,5},{22,6},{23,7},{24,8},{25... | collective-permute-start | bytes 196616 | tf_op jit(solution)/shard_map/ppermute | solution.py:37
  12.1 10.0 %collective-permute-start.5 = (bf16[128,256]{1,0:T(8,128)(2,1)S(1)}, bf16[128,256]{1,0:T(8,128)(2,1)S(1)}, u32[]{:S(2)}, u32[]{:S(2)}) collective-permute-start(bf16[128,256]{1,0:T(8,128)(2,1)S(1)} %get-tuple-element.14), channel_id=1, source_target_pairs={{24,0},{25,1},{26,2},{27,3},{28,4},{29,5},{30,6},{31,7},{16,8},{17... | collective-permute-start | bytes 196616 | tf_op jit(solution)/shard_map/ppermute | solution.py:37
  13.7 10.2 %collective-permute-start.6 = (bf16[128,256]{1,0:T(8,128)(2,1)S(1)}, bf16[128,256]{1,0:T(8,128)(2,1)S(1)}, u32[]{:S(2)}, u32[]{:S(2)}) collective-permute-start(bf16[128,256]{1,0:T(8,128)(2,1)S(1)} %get-tuple-element.13), channel_id=1, source_target_pairs={{4,0},{5,1},{6,2},{7,3},{0,4},{1,5},{2,6},{3,7},{12,8},{13,9},{14,... | collective-permute-start | bytes 196616 | tf_op jit(solution)/shard_map/ppermute | solution.py:37
  14.2 9.7 %collective-permute-start.7 = (bf16[128,256]{1,0:T(8,128)(2,1)S(1)}, bf16[128,256]{1,0:T(8,128)(2,1)S(1)}, u32[]{:S(2)}, u32[]{:S(2)}) collective-permute-start(bf16[128,256]{1,0:T(8,128)(2,1)S(1)} %get-tuple-element.12), channel_id=1, source_target_pairs={{12,0},{13,1},{14,2},{15,3},{8,4},{9,5},{10,6},{11,7},{4,8},{5,9},... | collective-permute-start | bytes 196616 | tf_op jit(solution)/shard_map/ppermute | solution.py:37
  17.6 6.2 %collective-permute-start.8 = (bf16[128,256]{1,0:T(8,128)(2,1)S(1)}, bf16[128,256]{1,0:T(8,128)(2,1)S(1)}, u32[]{:S(2)}, u32[]{:S(2)}) collective-permute-start(bf16[128,256]{1,0:T(8,128)(2,1)S(1)} %get-tuple-element.11), channel_id=1, source_target_pairs={{20,0},{21,1},{22,2},{23,3},{16,4},{17,5},{18,6},{19,7},{28,8},{29... | collective-permute-start | bytes 196616 | tf_op jit(solution)/shard_map/ppermute | solution.py:37
  17.7 99.1 %copy-start.9 = (f32[2048]{0:T(1024)S(1)}, f32[2048]{0:T(1024)}, u32[]{:S(2)}) copy-start(f32[2048]{0:T(1024)} %param.8) | copy-start | bytes 24580
  17.7 99.1 %copy-start.10 = (f32[2048]{0:T(1024)S(1)}, f32[2048]{0:T(1024)}, u32[]{:S(2)}) copy-start(f32[2048]{0:T(1024)} %param.9) | copy-start | bytes 24580
  17.7 6.9 %collective-permute-start.9 = (bf16[128,256]{1,0:T(8,128)(2,1)S(1)}, bf16[128,256]{1,0:T(8,128)(2,1)S(1)}, u32[]{:S(2)}, u32[]{:S(2)}) collective-permute-start(bf16[128,256]{1,0:T(8,128)(2,1)S(1)} %get-tuple-element.10), channel_id=1, source_target_pairs={{28,0},{29,1},{30,2},{31,3},{24,4},{25,5},{26,6},{27,7},{20,8},{21... | collective-permute-start | bytes 196616 | tf_op jit(solution)/shard_map/ppermute | solution.py:37
  22.1 92.9 %collective-permute-start.24 = (bf16[256,2048]{1,0:T(8,128)(2,1)S(1)}, bf16[256,2048]{1,0:T(8,128)(2,1)}, u32[]{:S(2)}, u32[]{:S(2)}) collective-permute-start(bf16[256,2048]{1,0:T(8,128)(2,1)S(1)} %get-tuple-element.5), channel_id=1, source_target_pairs={{0,0},{1,1},{8,2},{9,3},{16,4},{17,5},{24,6},{25,7},{2,8},{3,9},{1... | collective-permute-start | bytes 3145736 | tf_op jit(solution)/shard_map/ppermute | solution.py:41
  24.7 17.6 %collective-permute-start.10 = (bf16[128,256]{1,0:T(8,128)(2,1)S(1)}, bf16[128,256]{1,0:T(8,128)(2,1)S(1)}, u32[]{:S(2)}, u32[]{:S(2)}) collective-permute-start(bf16[128,256]{1,0:T(8,128)(2,1)S(1)} %add_convert_fusion.1), channel_id=1, source_target_pairs={{8,0},{9,1},{10,2},{11,3},{12,4},{13,5},{14,6},{15,7},{0,8},{1,9},... | collective-permute-start | bytes 196616 | tf_op jit(solution)/shard_map/ppermute | solution.py:37
  27.9 23.9 %collective-permute-start.11 = (bf16[128,256]{1,0:T(8,128)(2,1)S(1)}, bf16[128,256]{1,0:T(8,128)(2,1)S(1)}, u32[]{:S(2)}, u32[]{:S(2)}) collective-permute-start(bf16[128,256]{1,0:T(8,128)(2,1)S(1)} %add_convert_fusion.1), channel_id=1, source_target_pairs={{16,0},{17,1},{18,2},{19,3},{20,4},{21,5},{22,6},{23,7},{24,8},{25... | collective-permute-start | bytes 196616 | tf_op jit(solution)/shard_map/ppermute | solution.py:37
  27.9 46.6 %collective-permute-start.12 = (bf16[128,256]{1,0:T(8,128)(2,1)S(1)}, bf16[128,256]{1,0:T(8,128)(2,1)S(1)}, u32[]{:S(2)}, u32[]{:S(2)}) collective-permute-start(bf16[128,256]{1,0:T(8,128)(2,1)S(1)} %add_convert_fusion.1), channel_id=1, source_target_pairs={{24,0},{25,1},{26,2},{27,3},{28,4},{29,5},{30,6},{31,7},{16,8},{17... | collective-permute-start | bytes 196616 | tf_op jit(solution)/shard_map/ppermute | solution.py:37
  74.5 20.2 %collective-permute-start.17 = (bf16[512,256]{1,0:T(8,128)(2,1)S(1)}, bf16[512,256]{1,0:T(8,128)(2,1)S(1)}, u32[]{:S(2)}, u32[]{:S(2)}) collective-permute-start(bf16[512,256]{1,0:T(8,128)(2,1)S(1)} %pad_maximum_fusion.refs_1_), channel_id=1, source_target_pairs={{4,0},{5,1},{6,2},{7,3},{0,4},{1,5},{2,6},{3,7},{12,8},{13,9},{14,... | collective-permute-start | bytes 786440 | tf_op jit(solution)/shard_map/ppermute | solution.py:37
  75.9 28.3 %collective-permute-start.18 = (bf16[512,256]{1,0:T(8,128)(2,1)S(1)}, bf16[512,256]{1,0:T(8,128)(2,1)S(1)}, u32[]{:S(2)}, u32[]{:S(2)}) collective-permute-start(bf16[512,256]{1,0:T(8,128)(2,1)S(1)} %pad_maximum_fusion.refs_1_), channel_id=1, source_target_pairs={{2,0},{3,1},{0,2},{1,3},{6,4},{7,5},{4,6},{5,7},{10,8},{11,9},{8,1... | collective-permute-start | bytes 786440 | tf_op jit(solution)/shard_map/ppermute | solution.py:37
  75.9 28.9 %collective-permute-start.13 = (bf16[512,256]{1,0:T(8,128)(2,1)S(1)}, bf16[512,256]{1,0:T(8,128)(2,1)}, u32[]{:S(2)}, u32[]{:S(2)}) collective-permute-start(bf16[512,256]{1,0:T(8,128)(2,1)S(1)} %pad_maximum_fusion.refs_1_), channel_id=1, source_target_pairs={{1,0},{0,1},{3,2},{2,3},{5,4},{4,5},{7,6},{6,7},{9,8},{8,9},{11,10... | collective-permute-start | bytes 786440 | tf_op jit(solution)/shard_map/ppermute | solution.py:37
  77.4 70.8 %collective-permute-start.22 = (bf16[256,2048]{1,0:T(8,128)(2,1)}, bf16[256,2048]{1,0:T(8,128)(2,1)}, u32[]{:S(2)}, u32[]{:S(2)}) collective-permute-start(bf16[256,2048]{1,0:T(8,128)(2,1)} %get-tuple-element.8), channel_id=1, source_target_pairs={{4,0},{5,1},{12,2},{13,3},{20,4},{21,5},{28,6},{29,7},{6,8},{7,9},... | collective-permute-start | bytes 3145736 | tf_op jit(solution)/shard_map/ppermute | solution.py:41
  94.7 54.1 %collective-permute-start.20 = (bf16[256,2048]{1,0:T(8,128)(2,1)}, bf16[256,2048]{1,0:T(8,128)(2,1)}, u32[]{:S(2)}, u32[]{:S(2)}) collective-permute-start(bf16[256,2048]{1,0:T(8,128)(2,1)} %get-tuple-element.6), channel_id=1, source_target_pairs={{0,0},{1,1},{8,2},{9,3},{16,4},{17,5},{24,6},{25,7},{2,8},{3,9},{1... | collective-permute-start | bytes 3145736 | tf_op jit(solution)/shard_map/ppermute | solution.py:41
  104.1 0.7 copy-start.3
  104.8 65.7 %collective-permute-start = (bf16[256,2048]{1,0:T(8,128)(2,1)}, bf16[256,2048]{1,0:T(8,128)(2,1)}, u32[]{:S(2)}, u32[]{:S(2)}) collective-permute-start(bf16[256,2048]{1,0:T(8,128)(2,1)} %get-tuple-element.7), channel_id=1, source_target_pairs={{4,0},{5,1},{12,2},{13,3},{20,4},{21,5},{28,6},{29,7},{6,8},{7,9},... | collective-permute-start | bytes 3145736 | tf_op jit(solution)/shard_map/ppermute | solution.py:41
  104.8 9.5 %collective-permute-start.14 = (bf16[512,256]{1,0:T(8,128)(2,1)S(1)}, bf16[512,256]{1,0:T(8,128)(2,1)}, u32[]{:S(2)}, u32[]{:S(2)}) collective-permute-start(bf16[512,256]{1,0:T(8,128)(2,1)S(1)} %pad_maximum_fusion.refs_1_), channel_id=1, source_target_pairs={{5,0},{4,1},{7,2},{6,3},{1,4},{0,5},{3,6},{2,7},{13,8},{12,9},{15,... | collective-permute-start | bytes 786440 | tf_op jit(solution)/shard_map/ppermute | solution.py:37
  114.3 1.5 collective-permute-start.19
  114.3 0.7 copy-start.1
  115.0 56.0 %collective-permute-start.15 = (bf16[512,256]{1,0:T(8,128)(2,1)}, bf16[512,256]{1,0:T(8,128)(2,1)}, u32[]{:S(2)}, u32[]{:S(2)}) collective-permute-start(bf16[512,256]{1,0:T(8,128)(2,1)} %collective-permute-done.13.refs_1_), channel_id=1, source_target_pairs={{2,0},{3,1},{0,2},{1,3},{6,4},{7,5},{4,6},{5,7},{10,8},{11,9},{8,1... | collective-permute-start | bytes 786440 | tf_op jit(solution)/shard_map/ppermute | solution.py:37
  115.9 0.7 copy-start.5
  116.6 56.0 %collective-permute-start.16 = (bf16[512,256]{1,0:T(8,128)(2,1)}, bf16[512,256]{1,0:T(8,128)(2,1)}, u32[]{:S(2)}, u32[]{:S(2)}) collective-permute-start(bf16[512,256]{1,0:T(8,128)(2,1)} %collective-permute-done.14.refs_2_), channel_id=1, source_target_pairs={{2,0},{3,1},{0,2},{1,3},{6,4},{7,5},{4,6},{5,7},{10,8},{11,9},{8,1... | collective-permute-start | bytes 786440 | tf_op jit(solution)/shard_map/ppermute | solution.py:37
  117.5 1.0 copy-start.2
  118.5 0.9 copy-start.4
  119.4 0.9 copy-start.6
  148.2 40.2 %collective-permute-start.25 = (bf16[256,2048]{1,0:T(8,128)(2,1)}, bf16[256,2048]{1,0:T(8,128)(2,1)S(1)}, u32[]{:S(2)}, u32[]{:S(2)}) collective-permute-start(bf16[256,2048]{1,0:T(8,128)(2,1)} %collective-permute-done.24.shapes), channel_id=1, source_target_pairs={{1,0},{0,1},{3,2},{2,3},{5,4},{4,5},{7,6},{6,7},{9,8},{8,9},{11,10... | collective-permute-start | bytes 3145736 | tf_op jit(solution)/shard_map/ppermute | solution.py:37
  148.8 49.9 %collective-permute-start.23 = (bf16[256,2048]{1,0:T(8,128)(2,1)}, bf16[256,2048]{1,0:T(8,128)(2,1)S(1)}, u32[]{:S(2)}, u32[]{:S(2)}) collective-permute-start(bf16[256,2048]{1,0:T(8,128)(2,1)} %collective-permute-done.22.shapes), channel_id=1, source_target_pairs={{1,0},{0,1},{3,2},{2,3},{5,4},{4,5},{7,6},{6,7},{9,8},{8,9},{11,10... | collective-permute-start | bytes 3145736 | tf_op jit(solution)/shard_map/ppermute | solution.py:37
  170.5 48.9 %collective-permute-start.21 = (bf16[256,2048]{1,0:T(8,128)(2,1)}, bf16[256,2048]{1,0:T(8,128)(2,1)S(1)}, u32[]{:S(2)}, u32[]{:S(2)}) collective-permute-start(bf16[256,2048]{1,0:T(8,128)(2,1)} %collective-permute-done.20.shapes), channel_id=1, source_target_pairs={{1,0},{0,1},{3,2},{2,3},{5,4},{4,5},{7,6},{6,7},{9,8},{8,9},{11,10... | collective-permute-start | bytes 3145736 | tf_op jit(solution)/shard_map/ppermute | solution.py:37
  171.1 69.6 %collective-permute-start.1 = (bf16[256,2048]{1,0:T(8,128)(2,1)}, bf16[256,2048]{1,0:T(8,128)(2,1)S(1)}, u32[]{:S(2)}, u32[]{:S(2)}) collective-permute-start(bf16[256,2048]{1,0:T(8,128)(2,1)} %collective-permute-done.shapes), channel_id=1, source_target_pairs={{1,0},{0,1},{3,2},{2,3},{5,4},{4,5},{7,6},{6,7},{9,8},{8,9},{11,10... | collective-permute-start | bytes 3145736 | tf_op jit(solution)/shard_map/ppermute | solution.py:37
  172.6 3.8 %copy-start.8 = (bf16[1024,2048]{1,0:T(8,128)(2,1)S(1)}, bf16[1024,2048]{1,0:T(8,128)(2,1)}, u32[]{:S(2)}) copy-start(bf16[1024,2048]{1,0:T(8,128)(2,1)} %param.7) | copy-start | bytes 12582916

commit v2 on v1

v2 whole, which is shorter than its diff:
```python
import functools

import jax
import jax.numpy as jnp
from jax import lax
from jax.experimental import pallas as pl
from jax.experimental.pallas import tpu as pltpu
from jax.sharding import PartitionSpec as P

AXES = ("prow", "pcol", "pl")
CORES = 2
CHUNKS = (1, 1, 2, 2, 2)
AHEAD = 2
MIB = 1024 * 1024


def transfer_pair(natural_freq, damping):
    detuning = natural_freq * natural_freq - 1.0
    damper = 2.0 * damping * natural_freq
    modulus = detuning * detuning + damper * damper
    return detuning / modulus, -damper / modulus


def moves(sizes, source_of):
    rows, cols, groups = sizes
    pairs = []
    for i in range(rows):
        for j in range(cols):
            for k in range(groups):
                a, b, c = source_of(i, j, k)
                pairs.append(((a * cols + b) * groups + c, (i * cols + j) * groups + k))
    return pairs


def swap(array, sizes, di, dj, dk):
    return lax.ppermute(array, AXES, moves(sizes, lambda i, j, k: (i ^ di, j ^ dj, k ^ dk)))


def across(array, sizes, flip):
    return lax.ppermute(array, AXES, moves(sizes, lambda i, j, k: (j, i ^ flip, k)))


def cheap():
    return pl.CostEstimate(flops=1, bytes_accessed=1, transcendentals=0)


def after(array, *earlier):
    return pl.pallas_call(
        lambda *refs: None,
        in_specs=[pl.BlockSpec(memory_space=pl.ANY)] * (1 + len(earlier)),
        out_specs=pl.BlockSpec(memory_space=pl.ANY),
        out_shape=jax.ShapeDtypeStruct(array.shape, array.dtype),
        input_output_aliases={0: 0},
        cost_estimate=cheap(),
    )(array, *earlier)


def outer_rows(left_rows, right_rows):
    return lax.dot_general(
        left_rows, right_rows, (((1,), (1,)), ((), ())), preferred_element_type=jnp.float32
    )


def product_kernel(order, a, b, out):
    out[...] = jnp.dot(a[...], b[...], preferred_element_type=jnp.float32).astype(out.dtype)


def row_product(a, b, order, tile, dtype, limit):
    depth, wide = b.shape
    return pl.pallas_call(
        product_kernel,
        grid_spec=pltpu.PrefetchScalarGridSpec(
            num_scalar_prefetch=1,
            grid=(order.shape[0],),
            in_specs=[
                pl.BlockSpec((tile, depth), lambda g, order: (order[g], 0)),
                pl.BlockSpec((depth, wide), lambda g, order: (0, 0)),
            ],
            out_specs=pl.BlockSpec((tile, wide), lambda g, order: (g, 0)),
        ),
        out_shape=jax.ShapeDtypeStruct((order.shape[0] * tile, wide), dtype),
        compiler_params=pltpu.CompilerParams(vmem_limit_bytes=limit),
        cost_estimate=cheap(),
    )(order.astype(jnp.int32), a, b)


def load_kernel(rows, spots, scale, *refs):
    out = refs[-1]
    blocks = refs[: spots.shape[0] - 1]
    for at, block in enumerate(blocks):
        for part in range(block.shape[0] // rows):
            first = pl.multiple_of(spots[1 + at] + (spots[0] ^ part) * rows, rows)
            load = block[part * rows : (part + 1) * rows, :].astype(jnp.float32)
            out[pl.ds(first, rows), :] = (scale[0, pl.ds(first, rows), :] * load).astype(out.dtype)


def place_loads(blocks, firsts, own_row, rows, group, groups, scale, loads):
    modes, wide = scale.shape[1], blocks[0].shape[1]
    spots = jnp.stack([own_row, *firsts]).astype(jnp.int32)
    column = jnp.reshape(group, (1,)).astype(jnp.int32)
    given = [] if loads is None else [loads]
    return pl.pallas_call(
        lambda spots, column, *refs: load_kernel(rows, spots, *refs),
        grid_spec=pltpu.PrefetchScalarGridSpec(
            num_scalar_prefetch=2,
            grid=(2,),
            in_specs=[pl.BlockSpec((1, modes, 1), lambda g, spots, column: (g, 0, 0))]
            + [pl.BlockSpec(b.shape, lambda g, spots, column: (0, 0)) for b in blocks]
            + [pl.BlockSpec(memory_space=pl.ANY) for _ in given],
            out_specs=pl.BlockSpec((modes, wide), lambda g, spots, column: (0, g * groups + column[0])),
        ),
        out_shape=jax.ShapeDtypeStruct((modes, 2 * groups * wide), jnp.bfloat16),
        input_output_aliases={3 + len(blocks): 0} if given else {},
        compiler_params=pltpu.CompilerParams(vmem_limit_bytes=12 * MIB),
        cost_estimate=cheap(),
    )(spots, column, scale, *blocks, *given)


def panel_kernel(count, spots, *refs):
    lefts, rights, out = refs[:count], refs[count : 2 * count], refs[-1]
    depth = lefts[0].shape[1]

    def total(first):
        terms = [outer_rows(lefts[d ^ first][...], rights[d][...]) for d in range(count)]
        return functools.reduce(lambda a, b: a + b, terms)

    for first in range(count):
        @pl.when(spots[1] == first)
        def _():
            out[...] = total(first)


def place_panel(lefts, rights, first, place, columns, panel):
    rows, depth = lefts[0].shape
    chunk, count = rights[0].shape[0], len(lefts)
    given = [] if panel is None else [panel]
    tile = min(rows, 256)
    step = min(depth, 512)
    spots = jnp.stack([place, first]).astype(jnp.int32)
    return pl.pallas_call(
        functools.partial(panel_kernel, count),
        grid_spec=pltpu.PrefetchScalarGridSpec(
            num_scalar_prefetch=1,
            grid=(rows // tile,),
            in_specs=[pl.BlockSpec((tile, depth), lambda g, spots: (g, 0)) for _ in lefts]
            + [pl.BlockSpec((chunk, depth), lambda g, spots: (0, 0)) for _ in rights]
            + [pl.BlockSpec(memory_space=pl.ANY) for _ in given],
            out_specs=pl.BlockSpec((tile, chunk), lambda g, spots: (g, spots[0])),
        ),
        out_shape=jax.ShapeDtypeStruct((rows, columns), jnp.float32),
        input_output_aliases={1 + 2 * count: 0} if given else {},
        compiler_params=pltpu.CompilerParams(vmem_limit_bytes=24 * MIB),
        cost_estimate=pl.CostEstimate(
            flops=2 * rows * chunk * depth * count,
            bytes_accessed=2 * (rows + chunk) * depth * count + 4 * rows * chunk,
            transcendentals=0,
        ),
    )(spots, *lefts, *rights, *given)


def body(sizes, factor_cols, modal_at_loads, mode_shapes, natural_freq, damping):
    n_rows, n_cols, n_groups = sizes
    n_high = n_cols // CORES
    row, col, group = (lax.axis_index(axis) for axis in AXES)
    high, core = col // CORES, col % CORES
    scale = jnp.stack(transfer_pair(natural_freq, damping))[:, :, None]
    own_rows, modes = mode_shapes.shape

    part = factor_cols.shape[1] // n_high
    block = modes // CORES // n_rows
    order = row ^ jnp.arange(n_rows)
    sent = row_product(modal_at_loads, factor_cols, (1 - core) * n_rows + order, block, jnp.bfloat16, 56 * MIB)
    came = swap(sent, sizes, 0, 1, 0)
    here = row_product(modal_at_loads, factor_cols, core * n_rows + order, block, jnp.float32, 56 * MIB)
    total = here + came.astype(jnp.float32)
    own = None
    for dh in range(n_high):
        columns = lax.dynamic_slice_in_dim(total, (high ^ dh) * part, part, 1)
        for dr in range(n_rows):
            piece = columns[dr * block : (dr + 1) * block]
            if dh or dr:
                piece = swap(piece.astype(jnp.bfloat16), sizes, dr, dh * CORES, 0).astype(jnp.float32)
            own = piece if own is None else own + piece
    own = own.astype(jnp.bfloat16)
    loads = None
    for dk in range(n_groups):
        mine = [swap(own, sizes, dr, 0, dk) if dr or dk else own for dr in range(n_rows)]
        mine = jnp.concatenate(mine, axis=0)
        theirs = swap(mine, sizes, 0, 1, 0)
        firsts = [which * n_rows * block for which in (core, 1 - core)]
        loads = place_loads([mine, theirs], firsts, row, block, group ^ dk, n_groups, scale, loads)

    tile = min(own_rows, 256)
    left = row_product(mode_shapes, loads, jnp.arange(own_rows // tile), tile, jnp.bfloat16, 56 * MIB)
    half = own_rows // CORES
    lefts = [left]
    for dh in range(1, n_high):
        sent = lax.dynamic_slice_in_dim(left, core * half, half, 0)
        came = swap(sent, sizes, 0, dh * CORES, 0)
        rest = swap(came, sizes, 0, 1, 0)
        lefts.append(
            jnp.where(core == 0, jnp.concatenate([came, rest], 0), jnp.concatenate([rest, came], 0))
        )

    unit = max(own_rows // sum(CHUNKS), min(own_rows, 128))
    spans, first = [], 0
    while first < own_rows:
        size = min(CHUNKS[min(len(spans), len(CHUNKS) - 1)] * unit, own_rows - first)
        spans.append((first, size))
        first += size

    landed, others = [], []
    for at, (first, size) in enumerate(spans):
        piece = left[first : first + size]
        if at >= AHEAD:
            piece = after(piece, *landed[at - AHEAD])
        landed.append([across(piece, sizes, dh * CORES) for dh in range(n_high)])
        others.append([[swap(p, sizes, 0, 0, dk) for p in landed[at]] for dk in range(1, n_groups)])

    panel, columns = None, own_rows * n_groups
    turn = (row // CORES) ^ high
    for at, (first, size) in enumerate(spans):
        for dk in range(n_groups):
            rights = others[at][dk - 1] if dk else landed[at]
            place = (group ^ dk) * (own_rows // size) + first // size
            panel = place_panel(lefts, rights, turn, place, columns, panel)
    return panel


def solution(mesh):
    sizes = tuple(mesh.shape[axis] for axis in AXES)
    in_specs = (
        P(("prow", "pcol"), "pl"),
        P(None, ("prow", "pcol")),
        P(("prow", "pl"), None),
        P(),
        P(),
    )
    out_specs = P(("prow", "pl"), "pcol")
    return jax.shard_map(
        functools.partial(body, sizes), mesh=mesh, in_specs=in_specs, out_specs=out_specs, check_vma=False
    )
```

time: 247 us -> 154 us (0.62)
  the two profiles are of different devices: /device:TPU:20 before, /device:TPU:4 now
where the time goes in v2:
time: 154 us; the launch traced here: 151 us
  starting transfers between devices  62.1 us (40%)
  Pallas kernels  50.6 us (33%)
  waiting for transfers between devices  23.3 us (15%)
  local copies, waits for them, and re-layouts  9.79 us (6%)
  other arithmetic  5.06 us (3%)
    ppermute x29, starting transfers between devices, swap(): lax.ppermute(array, AXES, moves(sizes, lambda i, j, k: (i ^ di, j ^ dj, k...  44.5 us
    pallas_call x10, Pallas kernels, place_panel(): pl.pallas_call(functools.partial(panel_kernel, count), grid_spec=pltpu.Pr...  29.3 us
    pallas_call x3, Pallas kernels, row_product(): pl.pallas_call(product_kernel, grid_spec=pltpu.PrefetchScalarGridSpec(num...  18.4 us
    ppermute x10, starting transfers between devices, across(): lax.ppermute(array, AXES, moves(sizes, lambda i, j, k: (j, i ^ flip, k)))  17.6 us
    ppermute x29, waiting for transfers between devices, swap(): lax.ppermute(array, AXES, moves(sizes, lambda i, j, k: (i ^ di, j ^ dj, k...  15.5 us
    ppermute x10, waiting for transfers between devices, across(): lax.ppermute(array, AXES, moves(sizes, lambda i, j, k: (j, i ^ flip, k)))  7.77 us
    unnamed x35, local copies, waits for them, and re-layouts  4.32 us
    slice x2, local copies, waits for them, and re-layouts, body(): piece = left[first:first + size]  3.12 us
  transfers between devices with their start and end apart: 39, of which 10 were waited for; matrix products, arithmetic and copies ran while one was open for 4% of the time, Pallas kernels for 22%

profile of v2, /device:TPU:4, one launch (start us, length us, event | category | flops | bytes accessed | tf_op | source)
XLA Modules:
  0.0 151.2 jit_solution(17793941878242578440)
XLA Ops:
  0.0 0.5 fusion.8.order
  0.5 5.7 %shard_map.56 = bf16[1024,256]{1,0:T(8,128)(2,1)} custom-call(s32[4]{0:T(128)} %fusion.8.order, bf16[2048,2048]{1,0:T(8,128)(2,1)} %a.4, bf16[2048,256]{1,0:T(8,128)(2,1)} %b.3), custom_call_target="tpu_custom_call" | custom-call | flops 1 | bytes 1 | tf_op jit(solution)/shard_map/pallas_call | solution.py:70
  6.2 0.5 fusion.9.order
  6.8 5.8 %shard_map.55 = f32[1024,256]{1,0:T(8,128)} custom-call(s32[4]{0:T(128)} %fusion.9.order, bf16[2048,2048]{1,0:T(8,128)(2,1)} %a.4, bf16[2048,256]{1,0:T(8,128)(2,1)} %b.3), custom_call_target="tpu_custom_call" | custom-call | flops 1 | bytes 1 | tf_op jit(solution)/shard_map/pallas_call | solution.py:70
  12.6 1.3 convert_add_fusion
  14.1 3.0 %collective-permute-start.5 = (bf16[256,128]{1,0:T(8,128)(2,1)S(1)}, bf16[256,128]{1,0:T(8,128)(2,1)S(1)}, u32[]{:S(2)}, u32[]{:S(2)}) collective-permute-start(bf16[256,128]{1,0:T(8,128)(2,1)S(1)} %get-tuple-element.18), channel_id=1, source_target_pairs={{12,0},{13,1},{14,2},{15,3},{8,4},{9,5},{10,6},{11,7},{4,8},{5,9},... | collective-permute-start | bytes 196616 | tf_op jit(solution)/shard_map/ppermute | solution.py:36
  17.1 2.5 %collective-permute-start.6 = (bf16[256,128]{1,0:T(8,128)(2,1)S(1)}, bf16[256,128]{1,0:T(8,128)(2,1)S(1)}, u32[]{:S(2)}, u32[]{:S(2)}) collective-permute-start(bf16[256,128]{1,0:T(8,128)(2,1)S(1)} %get-tuple-element.17), channel_id=1, source_target_pairs={{20,0},{21,1},{22,2},{23,3},{16,4},{17,5},{18,6},{19,7},{28,8},{29... | collective-permute-start | bytes 196616 | tf_op jit(solution)/shard_map/ppermute | solution.py:36
  19.7 1.2 collective-permute-start.7
  20.9 0.7 collective-permute-start.1
  21.6 3.5 %collective-permute-start.2 = (bf16[256,128]{1,0:T(8,128)(2,1)S(1)}, bf16[256,128]{1,0:T(8,128)(2,1)S(1)}, u32[]{:S(2)}, u32[]{:S(2)}) collective-permute-start(bf16[256,128]{1,0:T(8,128)(2,1)S(1)} %get-tuple-element.14), channel_id=1, source_target_pairs={{16,0},{17,1},{18,2},{19,3},{20,4},{21,5},{22,6},{23,7},{24,8},{25... | collective-permute-start | bytes 196616 | tf_op jit(solution)/shard_map/ppermute | solution.py:36
  25.1 0.2 collective-permute-start.3
  25.3 2.1 %collective-permute-done.7 = bf16[256,128]{1,0:T(8,128)(2,1)S(1)} collective-permute-done((bf16[256,128]{1,0:T(8,128)(2,1)S(1)}, bf16[256,128]{1,0:T(8,128)(2,1)S(1)}, u32[]{:S(2)}, u32[]{:S(2)}) %collective-permute-start.7) | collective-permute-done | bytes 65568 | tf_op jit(solution)/shard_map/ppermute | solution.py:36
  27.5 3.0 %collective-permute-done.2 = bf16[256,128]{1,0:T(8,128)(2,1)S(1)} collective-permute-done((bf16[256,128]{1,0:T(8,128)(2,1)S(1)}, bf16[256,128]{1,0:T(8,128)(2,1)S(1)}, u32[]{:S(2)}, u32[]{:S(2)}) %collective-permute-start.2) | collective-permute-done | bytes 65568 | tf_op jit(solution)/shard_map/ppermute | solution.py:36
  30.4 0.8 collective-permute-done.3
  31.3 1.2 collective-permute-start.13
  32.5 2.0 %collective-permute-start.14 = (bf16[256,128]{1,0:T(8,128)(2,1)S(1)}, bf16[256,128]{1,0:T(8,128)(2,1)S(1)}, u32[]{:S(2)}, u32[]{:S(2)}) collective-permute-start(bf16[256,128]{1,0:T(8,128)(2,1)S(1)} %fusion.6), channel_id=1, source_target_pairs={{16,0},{17,1},{18,2},{19,3},{20,4},{21,5},{22,6},{23,7},{24,8},{25... | collective-permute-start | bytes 196616 | tf_op jit(solution)/shard_map/ppermute | solution.py:36
  34.5 1.3 collective-permute-start.15
  35.8 1.6 %collective-permute-start.8 = (bf16[256,128]{1,0:T(8,128)(2,1)S(1)}, bf16[256,128]{1,0:T(8,128)(2,1)S(1)}, u32[]{:S(2)}, u32[]{:S(2)}) collective-permute-start(bf16[256,128]{1,0:T(8,128)(2,1)S(1)} %fusion.6), channel_id=1, source_target_pairs={{1,0},{0,1},{3,2},{2,3},{5,4},{4,5},{7,6},{6,7},{9,8},{8,9},{11,10... | collective-permute-start | bytes 196616 | tf_op jit(solution)/shard_map/ppermute | solution.py:36
  37.6 3.8 %collective-permute-start.10 = (bf16[256,128]{1,0:T(8,128)(2,1)S(1)}, bf16[256,128]{1,0:T(8,128)(2,1)S(1)}, u32[]{:S(2)}, u32[]{:S(2)}) collective-permute-start(bf16[256,128]{1,0:T(8,128)(2,1)S(1)} %fusion.6), channel_id=1, source_target_pairs={{17,0},{16,1},{19,2},{18,3},{21,4},{20,5},{23,6},{22,7},{25,8},{24... | collective-permute-start | bytes 196616 | tf_op jit(solution)/shard_map/ppermute | solution.py:36
  41.4 2.7 %collective-permute-start.11 = (bf16[256,128]{1,0:T(8,128)(2,1)S(1)}, bf16[256,128]{1,0:T(8,128)(2,1)S(1)}, u32[]{:S(2)}, u32[]{:S(2)}) collective-permute-start(bf16[256,128]{1,0:T(8,128)(2,1)S(1)} %fusion.6), channel_id=1, source_target_pairs={{25,0},{24,1},{27,2},{26,3},{29,4},{28,5},{31,6},{30,7},{17,8},{16... | collective-permute-start | bytes 196616 | tf_op jit(solution)/shard_map/ppermute | solution.py:36
  44.3 1.5 collective-permute-done.10
  45.7 2.6 %collective-permute-done.11 = bf16[256,128]{1,0:T(8,128)(2,1)S(1)} collective-permute-done((bf16[256,128]{1,0:T(8,128)(2,1)S(1)}, bf16[256,128]{1,0:T(8,128)(2,1)S(1)}, u32[]{:S(2)}, u32[]{:S(2)}) %collective-permute-start.11) | collective-permute-done | bytes 65568 | tf_op jit(solution)/shard_map/ppermute | solution.py:36
  48.5 0.6 copy.20.refs_0_
  49.3 1.5 shard_map.57.refs_3_
  50.8 1.5 shard_map.58.b
  52.3 1.3 copy-done.1
  53.6 0.5 iota.6.order
  54.1 6.9 %shard_map.59.refs_0_ = bf16[1024,512]{1,0:T(8,128)(2,1)} custom-call(s32[4]{0:T(128)} %iota.6.order, bf16[1024,2048]{1,0:T(8,128)(2,1)} %a.5, bf16[2048,512]{1,0:T(8,128)(2,1)} %copy-done.1), custom_call_target="tpu_custom_call" | custom-call | flops 1 | bytes 1 | tf_op jit(solution)/shard_map/pallas_call | solution.py:70
  61.0 1.1 fusion.10
  62.1 1.1 constant_dynamic-slice_fusion
  63.1 1.3 collective-permute-start.17
  64.4 1.9 %collective-permute-start.19 = (bf16[128,512]{1,0:T(8,128)(2,1)S(1)}, bf16[128,512]{1,0:T(8,128)(2,1)S(1)}, u32[]{:S(2)}, u32[]{:S(2)}) collective-permute-start(bf16[128,512]{1,0:T(8,128)(2,1)S(1)} %get-tuple-element.6), channel_id=1, source_target_pairs={{0,0},{1,1},{8,2},{9,3},{16,4},{17,5},{24,6},{25,7},{2,8},{3,9},{1... | collective-permute-start | bytes 393224 | tf_op jit(solution)/shard_map/ppermute | solution.py:40
  66.5 5.7 %collective-permute-start.27 = (bf16[128,512]{1,0:T(8,128)(2,1)S(1)}, bf16[128,512]{1,0:T(8,128)(2,1)S(1)}, u32[]{:S(2)}, u32[]{:S(2)}) collective-permute-start(bf16[128,512]{1,0:T(8,128)(2,1)S(1)} %get-tuple-element.5), channel_id=1, source_target_pairs={{0,0},{1,1},{8,2},{9,3},{16,4},{17,5},{24,6},{25,7},{2,8},{3,9},{1... | collective-permute-start | bytes 393224 | tf_op jit(solution)/shard_map/ppermute | solution.py:40
  72.3 3.4 %collective-permute-done.19.refs_1_.refs_2_ = bf16[128,512]{1,0:T(8,128)(2,1)S(1)} collective-permute-done((bf16[128,512]{1,0:T(8,128)(2,1)S(1)}, bf16[128,512]{1,0:T(8,128)(2,1)S(1)}, u32[]{:S(2)}, u32[]{:S(2)}) %collective-permute-start.19) | collective-permute-done | bytes 131104 | tf_op jit(solution)/shard_map/ppermute | solution.py:40
  75.8 2.0 %fusion.11 = (bf16[256,512]{1,0:T(8,128)(2,1)}, bf16[256,512]{1,0:T(8,128)(2,1)}, bf16[256,512]{1,0:T(8,128)(2,1)}) fusion(bf16[1024,512]{1,0:T(8,128)(2,1)} %shard_map.59.refs_0_), kind=kLoop, calls=%fused_computation.39 | loop fusion | bytes 1572864 | tf_op jit(solution)/shard_map/slice | solution.py:214
  77.8 2.7 %collective-permute-done.20.refs_2_.refs_3_ = bf16[128,512]{1,0:T(8,128)(2,1)S(1)} collective-permute-done((bf16[128,512]{1,0:T(8,128)(2,1)S(1)}, bf16[128,512]{1,0:T(8,128)(2,1)S(1)}, u32[]{:S(2)}, u32[]{:S(2)}) %collective-permute-start.20) | collective-permute-done | bytes 131104 | tf_op jit(solution)/shard_map/ppermute | solution.py:40
  80.5 0.7 copy-done.10
  81.2 1.9 %collective-permute-start.21 = (bf16[256,512]{1,0:T(8,128)(2,1)}, bf16[256,512]{1,0:T(8,128)(2,1)S(1)}, u32[]{:S(2)}, u32[]{:S(2)}) collective-permute-start(bf16[256,512]{1,0:T(8,128)(2,1)} %shard_map.60), channel_id=1, source_target_pairs={{0,0},{1,1},{8,2},{9,3},{16,4},{17,5},{24,6},{25,7},{2,8},{3,9},{1... | collective-permute-start | bytes 786440 | tf_op jit(solution)/shard_map/ppermute | solution.py:40
  83.1 2.1 %collective-permute-start.22 = (bf16[256,512]{1,0:T(8,128)(2,1)}, bf16[256,512]{1,0:T(8,128)(2,1)S(1)}, u32[]{:S(2)}, u32[]{:S(2)}) collective-permute-start(bf16[256,512]{1,0:T(8,128)(2,1)} %shard_map.60), channel_id=1, source_target_pairs={{4,0},{5,1},{12,2},{13,3},{20,4},{21,5},{28,6},{29,7},{6,8},{7,9},... | collective-permute-start | bytes 786440 | tf_op jit(solution)/shard_map/ppermute | solution.py:40
  85.2 0.5 collective-permute-start.38
  85.8 1.5 collective-permute-start.35
  87.4 3.0 %collective-permute-done.38.refs_3_ = bf16[128,512]{1,0:T(8,128)(2,1)S(1)} collective-permute-done((bf16[128,512]{1,0:T(8,128)(2,1)}, bf16[128,512]{1,0:T(8,128)(2,1)S(1)}, u32[]{:S(2)}, u32[]{:S(2)}) %collective-permute-start.38) | collective-permute-done | bytes 131104 | tf_op jit(solution)/shard_map/ppermute | solution.py:36
  90.4 3.7 %collective-permute-start.29 = (bf16[256,512]{1,0:T(8,128)(2,1)}, bf16[256,512]{1,0:T(8,128)(2,1)S(1)}, u32[]{:S(2)}, u32[]{:S(2)}) collective-permute-start(bf16[256,512]{1,0:T(8,128)(2,1)} %shard_map.62), channel_id=1, source_target_pairs={{0,0},{1,1},{8,2},{9,3},{16,4},{17,5},{24,6},{25,7},{2,8},{3,9},{1... | collective-permute-start | bytes 786440 | tf_op jit(solution)/shard_map/ppermute | solution.py:40
  94.4 1.6 %collective-permute-done.21.refs_1_.refs_2_ = bf16[256,512]{1,0:T(8,128)(2,1)S(1)} collective-permute-done((bf16[256,512]{1,0:T(8,128)(2,1)}, bf16[256,512]{1,0:T(8,128)(2,1)S(1)}, u32[]{:S(2)}, u32[]{:S(2)}) %collective-permute-start.21) | collective-permute-done | bytes 262176 | tf_op jit(solution)/shard_map/ppermute | solution.py:40
  96.0 7.6 %collective-permute-start.36 = (bf16[128,512]{1,0:T(8,128)(2,1)}, bf16[128,512]{1,0:T(8,128)(2,1)S(1)}, u32[]{:S(2)}, u32[]{:S(2)}) collective-permute-start(bf16[128,512]{1,0:T(8,128)(2,1)} %copy-done.12), channel_id=1, source_target_pairs={{1,0},{0,1},{3,2},{2,3},{5,4},{4,5},{7,6},{6,7},{9,8},{8,9},{11,10... | collective-permute-start | bytes 393224 | tf_op jit(solution)/shard_map/ppermute | solution.py:36
  103.8 0.5 copy-done.4
  104.3 2.4 %collective-permute-done.36.refs_3_ = bf16[128,512]{1,0:T(8,128)(2,1)S(1)} collective-permute-done((bf16[128,512]{1,0:T(8,128)(2,1)}, bf16[128,512]{1,0:T(8,128)(2,1)S(1)}, u32[]{:S(2)}, u32[]{:S(2)}) %collective-permute-start.36) | collective-permute-done | bytes 131104 | tf_op jit(solution)/shard_map/ppermute | solution.py:36
  106.7 1.9 %collective-permute-start.23 = (bf16[256,512]{1,0:T(8,128)(2,1)}, bf16[256,512]{1,0:T(8,128)(2,1)S(1)}, u32[]{:S(2)}, u32[]{:S(2)}) collective-permute-start(bf16[256,512]{1,0:T(8,128)(2,1)} %shard_map.61), channel_id=1, source_target_pairs={{0,0},{1,1},{8,2},{9,3},{16,4},{17,5},{24,6},{25,7},{2,8},{3,9},{1... | collective-permute-start | bytes 786440 | tf_op jit(solution)/shard_map/ppermute | solution.py:40
  108.8 5.3 %collective-permute-start.34 = (bf16[256,512]{1,0:T(8,128)(2,1)}, bf16[256,512]{1,0:T(8,128)(2,1)S(1)}, u32[]{:S(2)}, u32[]{:S(2)}) collective-permute-start(bf16[256,512]{1,0:T(8,128)(2,1)} %copy-done.4), channel_id=1, source_target_pairs={{1,0},{0,1},{3,2},{2,3},{5,4},{4,5},{7,6},{6,7},{9,8},{8,9},{11,10... | collective-permute-start | bytes 786440 | tf_op jit(solution)/shard_map/ppermute | solution.py:36
  114.2 1.9 %collective-permute-start.32 = (bf16[256,512]{1,0:T(8,128)(2,1)S(1)}, bf16[256,512]{1,0:T(8,128)(2,1)S(1)}, u32[]{:S(2)}, u32[]{:S(2)}) collective-permute-start(bf16[256,512]{1,0:T(8,128)(2,1)S(1)} %collective-permute-done.31.refs_3_), channel_id=1, source_target_pairs={{1,0},{0,1},{3,2},{2,3},{5,4},{4,5},{7,6},{6,7},{9,8},{8,9},{11,10... | collective-permute-start | bytes 786440 | tf_op jit(solution)/shard_map/ppermute | solution.py:36
  116.1 1.8 %maximum_select_fusion.refs_1_ = bf16[1024,512]{1,0:T(8,128)(2,1)S(1)} fusion(bf16[512,512]{1,0:T(8,128)(2,1)} %collective-permute-done.18, bf16[512,512]{1,0:T(8,128)(2,1)} %collective-permute-done.17, pred[]{:T(512)S(6)} %eq.5), kind=kLoop, calls=%fused_computation | loop fusion | flops 4718592 | bytes 2097153 | tf_op jit(solution)/shard_map/jit(_where)/select_n | solution.py:202
  117.9 0.9 copy-done.7
  118.8 0.9 copy-done.11
  119.7 2.8 %shard_map.63.refs_4_ = f32[1024,2048]{1,0:T(8,128)} custom-call(s32[2]{0:T(128)S(1)} %pad_add_fusion.10.spots, bf16[1024,512]{1,0:T(8,128)(2,1)S(1)} %copy-done, bf16[1024,512]{1,0:T(8,128)(2,1)S(1)} %maximum_select_fusion.refs_1_, bf16[128,512]{1,0:T(8,128)(2,1)S(1)} %copy-done.7, bf16[128,512]{1,0:T(8,128)(2,1)S(1)} %copy-done.11), custom_call_target="tpu_custom_call" | custom-call | flops 268435456 | bytes 2883584 | tf_op jit(solution)/shard_map/pallas_call | solution.py:140
  122.5 2.8 %shard_map.64.refs_4_ = f32[1024,2048]{1,0:T(8,128)} custom-call(s32[2]{0:T(128)S(1)} %pad_add_fusion.9.spots, bf16[1024,512]{1,0:T(8,128)(2,1)S(1)} %copy-done, bf16[1024,512]{1,0:T(8,128)(2,1)S(1)} %maximum_select_fusion.refs_1_, bf16[128,512]{1,0:T(8,128)(2,1)S(1)} %collective-permute-done.37.refs_2_, ...), custom_call_target="tpu_custom_call", output_to_operand_aliasing={{}: (5, {})} | custom-call | flops 268435456 | bytes 2883584 | tf_op jit(solution)/shard_map/pallas_call | solution.py:140
  125.4 2.8 %shard_map.65.refs_4_ = f32[1024,2048]{1,0:T(8,128)} custom-call(s32[2]{0:T(128)S(1)} %pad_add_fusion.8.spots, bf16[1024,512]{1,0:T(8,128)(2,1)S(1)} %copy-done, bf16[1024,512]{1,0:T(8,128)(2,1)S(1)} %maximum_select_fusion.refs_1_, bf16[128,512]{1,0:T(8,128)(2,1)S(1)} %copy-done.9, bf16[128,512]{1,0:T(8,128)(2,1)S(1)} %copy-done.13, ...), custom_call_target="tpu_custom_call", output_to_operand_aliasing={{}: (5, {})} | custom-call | flops 268435456 | bytes 2883584 | tf_op jit(solution)/shard_map/pallas_call | solution.py:140
  128.3 1.9 %collective-permute-start.26 = (bf16[256,512]{1,0:T(8,128)(2,1)S(1)}, bf16[256,512]{1,0:T(8,128)(2,1)S(1)}, u32[]{:S(2)}, u32[]{:S(2)}) collective-permute-start(bf16[256,512]{1,0:T(8,128)(2,1)S(1)} %collective-permute-done.25.refs_3_), channel_id=1, source_target_pairs={{1,0},{0,1},{3,2},{2,3},{5,4},{4,5},{7,6},{6,7},{9,8},{8,9},{11,10... | collective-permute-start | bytes 786440 | tf_op jit(solution)/shard_map/ppermute | solution.py:36
  130.3 2.8 %shard_map.66.refs_4_ = f32[1024,2048]{1,0:T(8,128)} custom-call(s32[2]{0:T(128)S(1)} %pad_add_fusion.7.spots, bf16[1024,512]{1,0:T(8,128)(2,1)S(1)} %copy-done, bf16[1024,512]{1,0:T(8,128)(2,1)S(1)} %maximum_select_fusion.refs_1_, bf16[128,512]{1,0:T(8,128)(2,1)S(1)} %collective-permute-done.35.refs_2_, ...), custom_call_target="tpu_custom_call", output_to_operand_aliasing={{}: (5, {})} | custom-call | flops 268435456 | bytes 2883584 | tf_op jit(solution)/shard_map/pallas_call | solution.py:140
  133.1 3.0 %shard_map.67.refs_4_ = f32[1024,2048]{1,0:T(8,128)} custom-call(s32[2]{0:T(128)S(1)} %pad_add_fusion.6.spots, bf16[1024,512]{1,0:T(8,128)(2,1)S(1)} %copy-done, bf16[1024,512]{1,0:T(8,128)(2,1)S(1)} %maximum_select_fusion.refs_1_, bf16[256,512]{1,0:T(8,128)(2,1)S(1)} %copy-done.3, bf16[256,512]{1,0:T(8,128)(2,1)S(1)} %copy-done.5, ...), custom_call_target="tpu_custom_call", output_to_operand_aliasing={{}: (5, {})} | custom-call | flops 536870912 | bytes 3670016 | tf_op jit(solution)/shard_map/pallas_call | solution.py:140
  136.1 3.0 %shard_map.68.refs_4_ = f32[1024,2048]{1,0:T(8,128)} custom-call(s32[2]{0:T(128)S(1)} %pad_add_fusion.5.spots, bf16[1024,512]{1,0:T(8,128)(2,1)S(1)} %copy-done, bf16[1024,512]{1,0:T(8,128)(2,1)S(1)} %maximum_select_fusion.refs_1_, bf16[256,512]{1,0:T(8,128)(2,1)S(1)} %collective-permute-done.33.refs_2_, ...), custom_call_target="tpu_custom_call", output_to_operand_aliasing={{}: (5, {})} | custom-call | flops 536870912 | bytes 3670016 | tf_op jit(solution)/shard_map/pallas_call | solution.py:140
  139.1 3.0 %shard_map.69.refs_4_ = f32[1024,2048]{1,0:T(8,128)} custom-call(s32[2]{0:T(128)S(1)} %pad_add_fusion.4.spots, bf16[1024,512]{1,0:T(8,128)(2,1)S(1)} %copy-done, bf16[1024,512]{1,0:T(8,128)(2,1)S(1)} %maximum_select_fusion.refs_1_, bf16[256,512]{1,0:T(8,128)(2,1)S(1)} %collective-permute-done.29.refs_2_, ...), custom_call_target="tpu_custom_call", output_to_operand_aliasing={{}: (5, {})} | custom-call | flops 536870912 | bytes 3670016 | tf_op jit(solution)/shard_map/pallas_call | solution.py:140
  142.1 3.0 %shard_map.70.refs_4_ = f32[1024,2048]{1,0:T(8,128)} custom-call(s32[2]{0:T(128)S(1)} %pad_add_fusion.3.spots, bf16[1024,512]{1,0:T(8,128)(2,1)S(1)} %copy-done, bf16[1024,512]{1,0:T(8,128)(2,1)S(1)} %maximum_select_fusion.refs_1_, bf16[256,512]{1,0:T(8,128)(2,1)S(1)} %collective-permute-done.30.refs_2_, ...), custom_call_target="tpu_custom_call", output_to_operand_aliasing={{}: (5, {})} | custom-call | flops 536870912 | bytes 3670016 | tf_op jit(solution)/shard_map/pallas_call | solution.py:140
  145.1 3.0 %shard_map.71.refs_4_ = f32[1024,2048]{1,0:T(8,128)} custom-call(s32[2]{0:T(128)S(1)} %get-tuple-element.22.spots, bf16[1024,512]{1,0:T(8,128)(2,1)S(1)} %copy-done, bf16[1024,512]{1,0:T(8,128)(2,1)S(1)} %maximum_select_fusion.refs_1_, bf16[256,512]{1,0:T(8,128)(2,1)S(1)} %collective-permute-done.23.refs_2_, ...), custom_call_target="tpu_custom_call", output_to_operand_aliasing={{}: (5, {})} | custom-call | flops 536870912 | bytes 3670016 | tf_op jit(solution)/shard_map/pallas_call | solution.py:140
  148.2 3.0 %shard_map.72 = f32[1024,2048]{1,0:T(8,128)} custom-call(s32[2]{0:T(128)S(1)} %get-tuple-element.21.spots, bf16[1024,512]{1,0:T(8,128)(2,1)S(1)} %copy-done, bf16[1024,512]{1,0:T(8,128)(2,1)S(1)} %maximum_select_fusion.refs_1_, bf16[256,512]{1,0:T(8,128)(2,1)S(1)} %collective-permute-done.24.refs_2_, ...), custom_call_target="tpu_custom_call", output_to_operand_aliasing={{}: (5, {})} | custom-call | flops 536870912 | bytes 3670016 | tf_op jit(solution)/shard_map/pallas_call | solution.py:140
  (94 shorter events, 2.2 us)
Async XLA Ops:
  6.2 29.6 %copy-start.14 = (f32[2048]{0:T(1024)S(1)}, f32[2048]{0:T(1024)}, u32[]{:S(2)}) copy-start(f32[2048]{0:T(1024)} %param.8) | copy-start | bytes 24580
  6.2 29.6 %copy-start.15 = (f32[2048]{0:T(1024)S(1)}, f32[2048]{0:T(1024)}, u32[]{:S(2)}) copy-start(f32[2048]{0:T(1024)} %param.9) | copy-start | bytes 24580
  6.2 6.3 %collective-permute-start = (bf16[1024,256]{1,0:T(8,128)(2,1)}, bf16[1024,256]{1,0:T(8,128)(2,1)S(1)}, u32[]{:S(2)}, u32[]{:S(2)}) collective-permute-start(bf16[1024,256]{1,0:T(8,128)(2,1)} %shard_map.56), channel_id=1, source_target_pairs={{2,0},{3,1},{0,2},{1,3},{6,4},{7,5},{4,6},{5,7},{10,8},{11,9},{8,1... | collective-permute-start | bytes 1572872 | tf_op jit(solution)/shard_map/ppermute | solution.py:36
  14.0 7.6 %collective-permute-start.4 = (bf16[256,128]{1,0:T(8,128)(2,1)S(1)}, bf16[256,128]{1,0:T(8,128)(2,1)S(1)}, u32[]{:S(2)}, u32[]{:S(2)}) collective-permute-start(bf16[256,128]{1,0:T(8,128)(2,1)S(1)} %get-tuple-element.15), channel_id=1, source_target_pairs={{4,0},{5,1},{6,2},{7,3},{0,4},{1,5},{2,6},{3,7},{12,8},{13,9},{14,... | collective-permute-start | bytes 196616 | tf_op jit(solution)/shard_map/ppermute | solution.py:36
  14.1 11.0 %collective-permute-start.5 = (bf16[256,128]{1,0:T(8,128)(2,1)S(1)}, bf16[256,128]{1,0:T(8,128)(2,1)S(1)}, u32[]{:S(2)}, u32[]{:S(2)}) collective-permute-start(bf16[256,128]{1,0:T(8,128)(2,1)S(1)} %get-tuple-element.18), channel_id=1, source_target_pairs={{12,0},{13,1},{14,2},{15,3},{8,4},{9,5},{10,6},{11,7},{4,8},{5,9},... | collective-permute-start | bytes 196616 | tf_op jit(solution)/shard_map/ppermute | solution.py:36
  17.1 8.2 %collective-permute-start.6 = (bf16[256,128]{1,0:T(8,128)(2,1)S(1)}, bf16[256,128]{1,0:T(8,128)(2,1)S(1)}, u32[]{:S(2)}, u32[]{:S(2)}) collective-permute-start(bf16[256,128]{1,0:T(8,128)(2,1)S(1)} %get-tuple-element.17), channel_id=1, source_target_pairs={{20,0},{21,1},{22,2},{23,3},{16,4},{17,5},{18,6},{19,7},{28,8},{29... | collective-permute-start | bytes 196616 | tf_op jit(solution)/shard_map/ppermute | solution.py:36
  19.7 7.8 %collective-permute-start.7 = (bf16[256,128]{1,0:T(8,128)(2,1)S(1)}, bf16[256,128]{1,0:T(8,128)(2,1)S(1)}, u32[]{:S(2)}, u32[]{:S(2)}) collective-permute-start(bf16[256,128]{1,0:T(8,128)(2,1)S(1)} %get-tuple-element.16), channel_id=1, source_target_pairs={{28,0},{29,1},{30,2},{31,3},{24,4},{25,5},{26,6},{27,7},{20,8},{21... | collective-permute-start | bytes 196616 | tf_op jit(solution)/shard_map/ppermute | solution.py:36
  20.9 6.6 %collective-permute-start.1 = (bf16[256,128]{1,0:T(8,128)(2,1)S(1)}, bf16[256,128]{1,0:T(8,128)(2,1)S(1)}, u32[]{:S(2)}, u32[]{:S(2)}) collective-permute-start(bf16[256,128]{1,0:T(8,128)(2,1)S(1)} %get-tuple-element.12), channel_id=1, source_target_pairs={{8,0},{9,1},{10,2},{11,3},{12,4},{13,5},{14,6},{15,7},{0,8},{1,9},... | collective-permute-start | bytes 196616 | tf_op jit(solution)/shard_map/ppermute | solution.py:36
  21.6 8.8 %collective-permute-start.2 = (bf16[256,128]{1,0:T(8,128)(2,1)S(1)}, bf16[256,128]{1,0:T(8,128)(2,1)S(1)}, u32[]{:S(2)}, u32[]{:S(2)}) collective-permute-start(bf16[256,128]{1,0:T(8,128)(2,1)S(1)} %get-tuple-element.14), channel_id=1, source_target_pairs={{16,0},{17,1},{18,2},{19,3},{20,4},{21,5},{22,6},{23,7},{24,8},{25... | collective-permute-start | bytes 196616 | tf_op jit(solution)/shard_map/ppermute | solution.py:36
  25.1 6.2 %collective-permute-start.3 = (bf16[256,128]{1,0:T(8,128)(2,1)S(1)}, bf16[256,128]{1,0:T(8,128)(2,1)S(1)}, u32[]{:S(2)}, u32[]{:S(2)}) collective-permute-start(bf16[256,128]{1,0:T(8,128)(2,1)S(1)} %get-tuple-element.13), channel_id=1, source_target_pairs={{24,0},{25,1},{26,2},{27,3},{28,4},{29,5},{30,6},{31,7},{16,8},{17... | collective-permute-start | bytes 196616 | tf_op jit(solution)/shard_map/ppermute | solution.py:36
  31.3 6.2 %collective-permute-start.13 = (bf16[256,128]{1,0:T(8,128)(2,1)S(1)}, bf16[256,128]{1,0:T(8,128)(2,1)S(1)}, u32[]{:S(2)}, u32[]{:S(2)}) collective-permute-start(bf16[256,128]{1,0:T(8,128)(2,1)S(1)} %fusion.6), channel_id=1, source_target_pairs={{8,0},{9,1},{10,2},{11,3},{12,4},{13,5},{14,6},{15,7},{0,8},{1,9},... | collective-permute-start | bytes 196616 | tf_op jit(solution)/shard_map/ppermute | solution.py:36
  32.5 8.9 %collective-permute-start.14 = (bf16[256,128]{1,0:T(8,128)(2,1)S(1)}, bf16[256,128]{1,0:T(8,128)(2,1)S(1)}, u32[]{:S(2)}, u32[]{:S(2)}) collective-permute-start(bf16[256,128]{1,0:T(8,128)(2,1)S(1)} %fusion.6), channel_id=1, source_target_pairs={{16,0},{17,1},{18,2},{19,3},{20,4},{21,5},{22,6},{23,7},{24,8},{25... | collective-permute-start | bytes 196616 | tf_op jit(solution)/shard_map/ppermute | solution.py:36
  34.5 9.6 %collective-permute-start.15 = (bf16[256,128]{1,0:T(8,128)(2,1)S(1)}, bf16[256,128]{1,0:T(8,128)(2,1)S(1)}, u32[]{:S(2)}, u32[]{:S(2)}) collective-permute-start(bf16[256,128]{1,0:T(8,128)(2,1)S(1)} %fusion.6), channel_id=1, source_target_pairs={{24,0},{25,1},{26,2},{27,3},{28,4},{29,5},{30,6},{31,7},{16,8},{17... | collective-permute-start | bytes 196616 | tf_op jit(solution)/shard_map/ppermute | solution.py:36
  35.8 8.4 %collective-permute-start.8 = (bf16[256,128]{1,0:T(8,128)(2,1)S(1)}, bf16[256,128]{1,0:T(8,128)(2,1)S(1)}, u32[]{:S(2)}, u32[]{:S(2)}) collective-permute-start(bf16[256,128]{1,0:T(8,128)(2,1)S(1)} %fusion.6), channel_id=1, source_target_pairs={{1,0},{0,1},{3,2},{2,3},{5,4},{4,5},{7,6},{6,7},{9,8},{8,9},{11,10... | collective-permute-start | bytes 196616 | tf_op jit(solution)/shard_map/ppermute | solution.py:36
  37.4 6.9 %collective-permute-start.9 = (bf16[256,128]{1,0:T(8,128)(2,1)S(1)}, bf16[256,128]{1,0:T(8,128)(2,1)S(1)}, u32[]{:S(2)}, u32[]{:S(2)}) collective-permute-start(bf16[256,128]{1,0:T(8,128)(2,1)S(1)} %fusion.6), channel_id=1, source_target_pairs={{9,0},{8,1},{11,2},{10,3},{13,4},{12,5},{15,6},{14,7},{1,8},{0,9},... | collective-permute-start | bytes 196616 | tf_op jit(solution)/shard_map/ppermute | solution.py:36
  37.6 8.2 %collective-permute-start.10 = (bf16[256,128]{1,0:T(8,128)(2,1)S(1)}, bf16[256,128]{1,0:T(8,128)(2,1)S(1)}, u32[]{:S(2)}, u32[]{:S(2)}) collective-permute-start(bf16[256,128]{1,0:T(8,128)(2,1)S(1)} %fusion.6), channel_id=1, source_target_pairs={{17,0},{16,1},{19,2},{18,3},{21,4},{20,5},{23,6},{22,7},{25,8},{24... | collective-permute-start | bytes 196616 | tf_op jit(solution)/shard_map/ppermute | solution.py:36
  41.4 7.0 %collective-permute-start.11 = (bf16[256,128]{1,0:T(8,128)(2,1)S(1)}, bf16[256,128]{1,0:T(8,128)(2,1)S(1)}, u32[]{:S(2)}, u32[]{:S(2)}) collective-permute-start(bf16[256,128]{1,0:T(8,128)(2,1)S(1)} %fusion.6), channel_id=1, source_target_pairs={{25,0},{24,1},{27,2},{26,3},{29,4},{28,5},{31,6},{30,7},{17,8},{16... | collective-permute-start | bytes 196616 | tf_op jit(solution)/shard_map/ppermute | solution.py:36
  44.1 5.2 %collective-permute-start.16 = (bf16[1024,128]{1,0:T(8,128)(2,1)S(1)}, bf16[1024,128]{1,0:T(8,128)(2,1)S(1)}, u32[]{:S(2)}, u32[]{:S(2)}) collective-permute-start(bf16[1024,128]{1,0:T(8,128)(2,1)S(1)} %pad_maximum_fusion.refs_1_), channel_id=1, source_target_pairs={{2,0},{3,1},{0,2},{1,3},{6,4},{7,5},{4,6},{5,7},{10,8},{11,9},{8,1... | collective-permute-start | bytes 786440 | tf_op jit(solution)/shard_map/ppermute | solution.py:36
  48.4 2.4 %collective-permute-start.12 = (bf16[1024,128]{1,0:T(8,128)(2,1)S(1)}, bf16[1024,128]{1,0:T(8,128)(2,1)S(1)}, u32[]{:S(2)}, u32[]{:S(2)}) collective-permute-start(bf16[1024,128]{1,0:T(8,128)(2,1)S(1)} %constant_dynamic-update-slice_fusion.refs_1_), channel_id=1, source_target_pairs={{2,0},{3,1},{0,2},{1,3},{6,4},{7,5},{4,6},{5,7},{10,8},{11,9},{8,1... | collective-permute-start | bytes 786440 | tf_op jit(solution)/shard_map/ppermute | solution.py:36
  52.3 1.3 copy-start.1
  61.0 56.9 %copy-start = (bf16[1024,512]{1,0:T(8,128)(2,1)S(1)}, bf16[1024,512]{1,0:T(8,128)(2,1)}, u32[]{:S(2)}) copy-start(bf16[1024,512]{1,0:T(8,128)(2,1)} %shard_map.59.refs_0_) | copy-start | bytes 3145732
  63.1 24.2 %collective-permute-start.17 = (bf16[512,512]{1,0:T(8,128)(2,1)S(1)}, bf16[512,512]{1,0:T(8,128)(2,1)}, u32[]{:S(2)}, u32[]{:S(2)}) collective-permute-start(bf16[512,512]{1,0:T(8,128)(2,1)S(1)} %constant_dynamic-slice_fusion), channel_id=1, source_target_pairs={{4,0},{5,1},{6,2},{7,3},{0,4},{1,5},{2,6},{3,7},{12,8},{13,9},{14,... | collective-permute-start | bytes 1572872 | tf_op jit(solution)/shard_map/ppermute | solution.py:36
  64.4 11.3 %collective-permute-start.19 = (bf16[128,512]{1,0:T(8,128)(2,1)S(1)}, bf16[128,512]{1,0:T(8,128)(2,1)S(1)}, u32[]{:S(2)}, u32[]{:S(2)}) collective-permute-start(bf16[128,512]{1,0:T(8,128)(2,1)S(1)} %get-tuple-element.6), channel_id=1, source_target_pairs={{0,0},{1,1},{8,2},{9,3},{16,4},{17,5},{24,6},{25,7},{2,8},{3,9},{1... | collective-permute-start | bytes 393224 | tf_op jit(solution)/shard_map/ppermute | solution.py:40
  66.5 14.0 %collective-permute-start.20 = (bf16[128,512]{1,0:T(8,128)(2,1)S(1)}, bf16[128,512]{1,0:T(8,128)(2,1)S(1)}, u32[]{:S(2)}, u32[]{:S(2)}) collective-permute-start(bf16[128,512]{1,0:T(8,128)(2,1)S(1)} %get-tuple-element.6), channel_id=1, source_target_pairs={{4,0},{5,1},{12,2},{13,3},{20,4},{21,5},{28,6},{29,7},{6,8},{7,9},... | collective-permute-start | bytes 393224 | tf_op jit(solution)/shard_map/ppermute | solution.py:40
  66.5 16.6 %collective-permute-start.27 = (bf16[128,512]{1,0:T(8,128)(2,1)S(1)}, bf16[128,512]{1,0:T(8,128)(2,1)S(1)}, u32[]{:S(2)}, u32[]{:S(2)}) collective-permute-start(bf16[128,512]{1,0:T(8,128)(2,1)S(1)} %get-tuple-element.5), channel_id=1, source_target_pairs={{0,0},{1,1},{8,2},{9,3},{16,4},{17,5},{24,6},{25,7},{2,8},{3,9},{1... | collective-permute-start | bytes 393224 | tf_op jit(solution)/shard_map/ppermute | solution.py:40
  72.2 13.0 %collective-permute-start.28 = (bf16[128,512]{1,0:T(8,128)(2,1)S(1)}, bf16[128,512]{1,0:T(8,128)(2,1)S(1)}, u32[]{:S(2)}, u32[]{:S(2)}) collective-permute-start(bf16[128,512]{1,0:T(8,128)(2,1)S(1)} %get-tuple-element.5), channel_id=1, source_target_pairs={{4,0},{5,1},{12,2},{13,3},{20,4},{21,5},{28,6},{29,7},{6,8},{7,9},... | collective-permute-start | bytes 393224 | tf_op jit(solution)/shard_map/ppermute | solution.py:40
  75.7 4.8 %copy-start.6 = (bf16[128,512]{1,0:T(8,128)(2,1)}, bf16[128,512]{1,0:T(8,128)(2,1)S(1)}, u32[]{:S(2)}) copy-start(bf16[128,512]{1,0:T(8,128)(2,1)S(1)} %collective-permute-done.19.refs_1_.refs_2_) | copy-start | bytes 393220
  75.7 10.1 %collective-permute-start.37 = (bf16[128,512]{1,0:T(8,128)(2,1)S(1)}, bf16[128,512]{1,0:T(8,128)(2,1)S(1)}, u32[]{:S(2)}, u32[]{:S(2)}) collective-permute-start(bf16[128,512]{1,0:T(8,128)(2,1)S(1)} %collective-permute-done.19.refs_1_.refs_2_), channel_id=1, source_target_pairs={{1,0},{0,1},{3,2},{2,3},{5,4},{4,5},{7,6},{6,7},{9,8},{8,9},{11,10... | collective-permute-start | bytes 393224 | tf_op jit(solution)/shard_map/ppermute | solution.py:36
  80.5 0.7 copy-start.10
  81.2 14.8 %collective-permute-start.21 = (bf16[256,512]{1,0:T(8,128)(2,1)}, bf16[256,512]{1,0:T(8,128)(2,1)S(1)}, u32[]{:S(2)}, u32[]{:S(2)}) collective-permute-start(bf16[256,512]{1,0:T(8,128)(2,1)} %shard_map.60), channel_id=1, source_target_pairs={{0,0},{1,1},{8,2},{9,3},{16,4},{17,5},{24,6},{25,7},{2,8},{3,9},{1... | collective-permute-start | bytes 786440 | tf_op jit(solution)/shard_map/ppermute | solution.py:40
  83.1 4.3 %copy-start.8 = (bf16[128,512]{1,0:T(8,128)(2,1)}, bf16[128,512]{1,0:T(8,128)(2,1)S(1)}, u32[]{:S(2)}) copy-start(bf16[128,512]{1,0:T(8,128)(2,1)S(1)} %collective-permute-done.27.refs_1_.refs_2_) | copy-start | bytes 393220
  83.1 20.5 %collective-permute-start.22 = (bf16[256,512]{1,0:T(8,128)(2,1)}, bf16[256,512]{1,0:T(8,128)(2,1)S(1)}, u32[]{:S(2)}, u32[]{:S(2)}) collective-permute-start(bf16[256,512]{1,0:T(8,128)(2,1)} %shard_map.60), channel_id=1, source_target_pairs={{4,0},{5,1},{12,2},{13,3},{20,4},{21,5},{28,6},{29,7},{6,8},{7,9},... | collective-permute-start | bytes 786440 | tf_op jit(solution)/shard_map/ppermute | solution.py:40
  85.2 2.2 %copy-start.12 = (bf16[128,512]{1,0:T(8,128)(2,1)}, bf16[128,512]{1,0:T(8,128)(2,1)S(1)}, u32[]{:S(2)}) copy-start(bf16[128,512]{1,0:T(8,128)(2,1)S(1)} %collective-permute-done.28.refs_2_.refs_3_) | copy-start | bytes 393220
  85.2 5.2 %collective-permute-start.38 = (bf16[128,512]{1,0:T(8,128)(2,1)}, bf16[128,512]{1,0:T(8,128)(2,1)S(1)}, u32[]{:S(2)}, u32[]{:S(2)}) collective-permute-start(bf16[128,512]{1,0:T(8,128)(2,1)} %copy-done.10), channel_id=1, source_target_pairs={{1,0},{0,1},{3,2},{2,3},{5,4},{4,5},{7,6},{6,7},{9,8},{8,9},{11,10... | collective-permute-start | bytes 393224 | tf_op jit(solution)/shard_map/ppermute | solution.py:36
  85.8 8.4 %collective-permute-start.35 = (bf16[128,512]{1,0:T(8,128)(2,1)S(1)}, bf16[128,512]{1,0:T(8,128)(2,1)S(1)}, u32[]{:S(2)}, u32[]{:S(2)}) collective-permute-start(bf16[128,512]{1,0:T(8,128)(2,1)S(1)} %collective-permute-done.27.refs_1_.refs_2_), channel_id=1, source_target_pairs={{1,0},{0,1},{3,2},{2,3},{5,4},{4,5},{7,6},{6,7},{9,8},{8,9},{11,10... | collective-permute-start | bytes 393224 | tf_op jit(solution)/shard_map/ppermute | solution.py:36
  87.3 26.8 %collective-permute-start.18 = (bf16[512,512]{1,0:T(8,128)(2,1)}, bf16[512,512]{1,0:T(8,128)(2,1)}, u32[]{:S(2)}, u32[]{:S(2)}) collective-permute-start(bf16[512,512]{1,0:T(8,128)(2,1)} %collective-permute-done.17), channel_id=1, source_target_pairs={{2,0},{3,1},{0,2},{1,3},{6,4},{7,5},{4,6},{5,7},{10,8},{11,9},{8,1... | collective-permute-start | bytes 1572872 | tf_op jit(solution)/shard_map/ppermute | solution.py:36
  90.4 18.2 %collective-permute-start.29 = (bf16[256,512]{1,0:T(8,128)(2,1)}, bf16[256,512]{1,0:T(8,128)(2,1)S(1)}, u32[]{:S(2)}, u32[]{:S(2)}) collective-permute-start(bf16[256,512]{1,0:T(8,128)(2,1)} %shard_map.62), channel_id=1, source_target_pairs={{0,0},{1,1},{8,2},{9,3},{16,4},{17,5},{24,6},{25,7},{2,8},{3,9},{1... | collective-permute-start | bytes 786440 | tf_op jit(solution)/shard_map/ppermute | solution.py:40
  94.2 14.6 %collective-permute-start.31 = (bf16[256,512]{1,0:T(8,128)(2,1)}, bf16[256,512]{1,0:T(8,128)(2,1)S(1)}, u32[]{:S(2)}, u32[]{:S(2)}) collective-permute-start(bf16[256,512]{1,0:T(8,128)(2,1)} %shard_map.62), channel_id=1, source_target_pairs={{4,0},{5,1},{12,2},{13,3},{20,4},{21,5},{28,6},{29,7},{6,8},{7,9},... | collective-permute-start | bytes 786440 | tf_op jit(solution)/shard_map/ppermute | solution.py:40
  96.0 7.8 %copy-start.2 = (bf16[256,512]{1,0:T(8,128)(2,1)}, bf16[256,512]{1,0:T(8,128)(2,1)S(1)}, u32[]{:S(2)}) copy-start(bf16[256,512]{1,0:T(8,128)(2,1)S(1)} %collective-permute-done.21.refs_1_.refs_2_) | copy-start | bytes 786436
  96.0 10.7 %collective-permute-start.36 = (bf16[128,512]{1,0:T(8,128)(2,1)}, bf16[128,512]{1,0:T(8,128)(2,1)S(1)}, u32[]{:S(2)}, u32[]{:S(2)}) collective-permute-start(bf16[128,512]{1,0:T(8,128)(2,1)} %copy-done.12), channel_id=1, source_target_pairs={{1,0},{0,1},{3,2},{2,3},{5,4},{4,5},{7,6},{6,7},{9,8},{8,9},{11,10... | collective-permute-start | bytes 393224 | tf_op jit(solution)/shard_map/ppermute | solution.py:36
  103.6 0.7 copy-start.4
  103.6 10.5 %collective-permute-start.33 = (bf16[256,512]{1,0:T(8,128)(2,1)S(1)}, bf16[256,512]{1,0:T(8,128)(2,1)S(1)}, u32[]{:S(2)}, u32[]{:S(2)}) collective-permute-start(bf16[256,512]{1,0:T(8,128)(2,1)S(1)} %collective-permute-done.21.refs_1_.refs_2_), channel_id=1, source_target_pairs={{1,0},{0,1},{3,2},{2,3},{5,4},{4,5},{7,6},{6,7},{9,8},{8,9},{11,10... | collective-permute-start | bytes 786440 | tf_op jit(solution)/shard_map/ppermute | solution.py:36
  106.7 21.5 %collective-permute-start.23 = (bf16[256,512]{1,0:T(8,128)(2,1)}, bf16[256,512]{1,0:T(8,128)(2,1)S(1)}, u32[]{:S(2)}, u32[]{:S(2)}) collective-permute-start(bf16[256,512]{1,0:T(8,128)(2,1)} %shard_map.61), channel_id=1, source_target_pairs={{0,0},{1,1},{8,2},{9,3},{16,4},{17,5},{24,6},{25,7},{2,8},{3,9},{1... | collective-permute-start | bytes 786440 | tf_op jit(solution)/shard_map/ppermute | solution.py:40
  108.7 19.7 %collective-permute-start.25 = (bf16[256,512]{1,0:T(8,128)(2,1)}, bf16[256,512]{1,0:T(8,128)(2,1)S(1)}, u32[]{:S(2)}, u32[]{:S(2)}) collective-permute-start(bf16[256,512]{1,0:T(8,128)(2,1)} %shard_map.61), channel_id=1, source_target_pairs={{4,0},{5,1},{12,2},{13,3},{20,4},{21,5},{28,6},{29,7},{6,8},{7,9},... | collective-permute-start | bytes 786440 | tf_op jit(solution)/shard_map/ppermute | solution.py:40
  108.8 27.3 %collective-permute-start.34 = (bf16[256,512]{1,0:T(8,128)(2,1)}, bf16[256,512]{1,0:T(8,128)(2,1)S(1)}, u32[]{:S(2)}, u32[]{:S(2)}) collective-permute-start(bf16[256,512]{1,0:T(8,128)(2,1)} %copy-done.4), channel_id=1, source_target_pairs={{1,0},{0,1},{3,2},{2,3},{5,4},{4,5},{7,6},{6,7},{9,8},{8,9},{11,10... | collective-permute-start | bytes 786440 | tf_op jit(solution)/shard_map/ppermute | solution.py:36
  114.1 28.1 %collective-permute-start.30 = (bf16[256,512]{1,0:T(8,128)(2,1)S(1)}, bf16[256,512]{1,0:T(8,128)(2,1)S(1)}, u32[]{:S(2)}, u32[]{:S(2)}) collective-permute-start(bf16[256,512]{1,0:T(8,128)(2,1)S(1)} %collective-permute-done.29.refs_2_), channel_id=1, source_target_pairs={{1,0},{0,1},{3,2},{2,3},{5,4},{4,5},{7,6},{6,7},{9,8},{8,9},{11,10... | collective-permute-start | bytes 786440 | tf_op jit(solution)/shard_map/ppermute | solution.py:36
  114.2 28.0 %collective-permute-start.32 = (bf16[256,512]{1,0:T(8,128)(2,1)S(1)}, bf16[256,512]{1,0:T(8,128)(2,1)S(1)}, u32[]{:S(2)}, u32[]{:S(2)}) collective-permute-start(bf16[256,512]{1,0:T(8,128)(2,1)S(1)} %collective-permute-done.31.refs_3_), channel_id=1, source_target_pairs={{1,0},{0,1},{3,2},{2,3},{5,4},{4,5},{7,6},{6,7},{9,8},{8,9},{11,10... | collective-permute-start | bytes 786440 | tf_op jit(solution)/shard_map/ppermute | solution.py:36
  117.9 0.9 copy-start.7
  118.8 0.9 copy-start.11
  122.5 2.8 %copy-start.9 = (bf16[128,512]{1,0:T(8,128)(2,1)S(1)}, bf16[128,512]{1,0:T(8,128)(2,1)}, u32[]{:S(2)}) copy-start(bf16[128,512]{1,0:T(8,128)(2,1)} %copy-done.8) | copy-start | bytes 393220
  122.5 2.8 %copy-start.13 = (bf16[128,512]{1,0:T(8,128)(2,1)S(1)}, bf16[128,512]{1,0:T(8,128)(2,1)}, u32[]{:S(2)}) copy-start(bf16[128,512]{1,0:T(8,128)(2,1)} %copy-done.12) | copy-start | bytes 393220
  128.2 4.9 %copy-start.3 = (bf16[256,512]{1,0:T(8,128)(2,1)S(1)}, bf16[256,512]{1,0:T(8,128)(2,1)}, u32[]{:S(2)}) copy-start(bf16[256,512]{1,0:T(8,128)(2,1)} %copy-done.2) | copy-start | bytes 786436
  128.2 4.9 %copy-start.5 = (bf16[256,512]{1,0:T(8,128)(2,1)S(1)}, bf16[256,512]{1,0:T(8,128)(2,1)}, u32[]{:S(2)}) copy-start(bf16[256,512]{1,0:T(8,128)(2,1)} %copy-done.4) | copy-start | bytes 786436
  128.2 20.0 %collective-permute-start.24 = (bf16[256,512]{1,0:T(8,128)(2,1)S(1)}, bf16[256,512]{1,0:T(8,128)(2,1)S(1)}, u32[]{:S(2)}, u32[]{:S(2)}) collective-permute-start(bf16[256,512]{1,0:T(8,128)(2,1)S(1)} %collective-permute-done.23.refs_2_), channel_id=1, source_target_pairs={{1,0},{0,1},{3,2},{2,3},{5,4},{4,5},{7,6},{6,7},{9,8},{8,9},{11,10... | collective-permute-start | bytes 786440 | tf_op jit(solution)/shard_map/ppermute | solution.py:36
  128.3 19.8 %collective-permute-start.26 = (bf16[256,512]{1,0:T(8,128)(2,1)S(1)}, bf16[256,512]{1,0:T(8,128)(2,1)S(1)}, u32[]{:S(2)}, u32[]{:S(2)}) collective-permute-start(bf16[256,512]{1,0:T(8,128)(2,1)S(1)} %collective-permute-done.25.refs_3_), channel_id=1, source_target_pairs={{1,0},{0,1},{3,2},{2,3},{5,4},{4,5},{7,6},{6,7},{9,8},{8,9},{11,10... | collective-permute-start | bytes 786440 | tf_op jit(solution)/shard_map/ppermute | solution.py:36

commit v3 on v2

v3 whole, which is shorter than its diff:
```python
import functools

import jax
import jax.numpy as jnp
from jax import lax
from jax.experimental import pallas as pl
from jax.experimental.pallas import tpu as pltpu
from jax.sharding import PartitionSpec as P

AXES = ("prow", "pcol", "pl")
CORES = 2
CHUNKS = (4,4)
UNIT = 4
AHEAD = 1
LEFT = 0
MIB = 1024 * 1024


def transfer_pair(natural_freq, damping):
    detuning = natural_freq * natural_freq - 1.0
    damper = 2.0 * damping * natural_freq
    modulus = detuning * detuning + damper * damper
    return detuning / modulus, -damper / modulus


def moves(sizes, source_of):
    rows, cols, groups = sizes
    pairs = []
    for i in range(rows):
        for j in range(cols):
            for k in range(groups):
                a, b, c = source_of(i, j, k)
                pairs.append(((a * cols + b) * groups + c, (i * cols + j) * groups + k))
    return pairs


def swap(array, sizes, di, dj, dk):
    return lax.ppermute(array, AXES, moves(sizes, lambda i, j, k: (i ^ di, j ^ dj, k ^ dk)))


def across(array, sizes, flip):
    return lax.ppermute(array, AXES, moves(sizes, lambda i, j, k: (j, i ^ flip, k)))


def cheap():
    return pl.CostEstimate(flops=1, bytes_accessed=1, transcendentals=0)


def after(array, *earlier):
    return pl.pallas_call(
        lambda *refs: None,
        in_specs=[pl.BlockSpec(memory_space=pl.ANY)] * (1 + len(earlier)),
        out_specs=pl.BlockSpec(memory_space=pl.ANY),
        out_shape=jax.ShapeDtypeStruct(array.shape, array.dtype),
        input_output_aliases={0: 0},
        cost_estimate=cheap(),
    )(array, *earlier)


def outer_rows(left_rows, right_rows):
    return lax.dot_general(
        left_rows, right_rows, (((1,), (1,)), ((), ())), preferred_element_type=jnp.float32
    )


def product_kernel(a, b, out):
    out[...] = jnp.dot(a[...], b[...], preferred_element_type=jnp.float32).astype(out.dtype)


def row_product(a, b, tile, limit):
    rows, depth = a.shape
    wide = b.shape[1]
    return pl.pallas_call(
        product_kernel,
        grid=(rows // tile,),
        in_specs=[
            pl.BlockSpec((tile, depth), lambda g: (g, 0)),
            pl.BlockSpec((depth, wide), lambda g: (0, 0)),
        ],
        out_specs=pl.BlockSpec((tile, wide), lambda g: (g, 0)),
        out_shape=jax.ShapeDtypeStruct((rows, wide), jnp.bfloat16),
        compiler_params=pltpu.CompilerParams(vmem_limit_bytes=limit),
        cost_estimate=cheap(),
    )(a, b)


def load_kernel(rows, spots, scale, *refs):
    out = refs[-1]
    blocks = refs[: spots.shape[0] - 1]
    for at, block in enumerate(blocks):
        for part in range(block.shape[0] // rows):
            first = pl.multiple_of(spots[1 + at] + (spots[0] ^ part) * rows, rows)
            load = block[part * rows : (part + 1) * rows, :].astype(jnp.float32)
            out[pl.ds(first, rows), :] = (scale[0, pl.ds(first, rows), :] * load).astype(out.dtype)


def place_loads(blocks, firsts, own_row, rows, group, groups, scale, loads):
    modes, wide = scale.shape[1], blocks[0].shape[1]
    spots = jnp.stack([own_row, *firsts]).astype(jnp.int32)
    column = jnp.reshape(group, (1,)).astype(jnp.int32)
    given = [] if loads is None else [loads]
    return pl.pallas_call(
        lambda spots, column, *refs: load_kernel(rows, spots, *refs),
        grid_spec=pltpu.PrefetchScalarGridSpec(
            num_scalar_prefetch=2,
            grid=(2,),
            in_specs=[pl.BlockSpec((1, modes, 1), lambda g, spots, column: (g, 0, 0))]
            + [pl.BlockSpec(b.shape, lambda g, spots, column: (0, 0)) for b in blocks]
            + [pl.BlockSpec(memory_space=pl.ANY) for _ in given],
            out_specs=pl.BlockSpec((modes, wide), lambda g, spots, column: (0, g * groups + column[0])),
        ),
        out_shape=jax.ShapeDtypeStruct((modes, 2 * groups * wide), jnp.bfloat16),
        input_output_aliases={3 + len(blocks): 0} if given else {},
        compiler_params=pltpu.CompilerParams(vmem_limit_bytes=12 * MIB),
        cost_estimate=cheap(),
    )(spots, column, scale, *blocks, *given)


def panel_kernel(count, shape, spots, left, *refs):
    out = refs[-2]
    for unit, pieces in enumerate(shape):
        spans, refs = refs[: pieces * count], refs[pieces * count :]

        def fill(spans=spans, pieces=pieces):
            rights = [
                jnp.concatenate([spans[p * count + d][...] for d in range(count)], axis=1)
                for p in range(pieces)
            ]
            out[...] = outer_rows(left[...], jnp.concatenate(rights, axis=0))

        if len(shape) == 1:
            fill()
        else:
            pl.when(pl.program_id(0) == unit)(fill)


def place_panel(left, units, places, columns, panel, *earlier):
    rows, count = left.shape[0], len(units[0][0])
    chunk = sum(piece[0].shape[0] for piece in units[0])
    shape = tuple(len(unit) for unit in units)
    rights = [array for unit in units for piece in unit for array in piece]
    given = ([] if panel is None else [panel]) + list(earlier)
    whole = pl.BlockSpec(memory_space=pltpu.VMEM)
    return pl.pallas_call(
        functools.partial(panel_kernel, count, shape),
        grid_spec=pltpu.PrefetchScalarGridSpec(
            num_scalar_prefetch=1,
            grid=(len(units),),
            in_specs=[whole] * (1 + len(rights)) + [pl.BlockSpec(memory_space=pl.ANY) for _ in given],
            out_specs=[
                pl.BlockSpec((rows, chunk), lambda g, spots: (0, spots[g])),
                pl.BlockSpec(memory_space=pl.ANY),
            ],
        ),
        out_shape=[
            jax.ShapeDtypeStruct((rows, columns), jnp.float32),
            jax.ShapeDtypeStruct((8, 128), jnp.float32),
        ],
        input_output_aliases={} if panel is None else {2 + len(rights): 0},
        compiler_params=pltpu.CompilerParams(vmem_limit_bytes=12 * MIB),
        cost_estimate=cheap(),
    )(jnp.stack(places).astype(jnp.int32), left, *rights, *given)


def body(sizes, factor_cols, modal_at_loads, mode_shapes, natural_freq, damping):
    n_rows, n_cols, n_groups = sizes
    n_high = n_cols // CORES
    row, col, group = (lax.axis_index(axis) for axis in AXES)
    high, core = col // CORES, col % CORES
    scale = jnp.stack(transfer_pair(natural_freq, damping))[:, :, None]
    own_rows, modes = mode_shapes.shape

    part = factor_cols.shape[1] // n_high
    block = modes // CORES // n_rows
    half = block * n_rows
    away = lax.dynamic_slice_in_dim(modal_at_loads, (1 - core) * half, half, 0)
    here = lax.dynamic_slice_in_dim(modal_at_loads, core * half, half, 0)
    sent = jnp.dot(away, factor_cols, preferred_element_type=jnp.float32).astype(jnp.bfloat16)
    came = swap(sent, sizes, 0, 1, 0)
    total = jnp.dot(here, factor_cols, preferred_element_type=jnp.float32) + came.astype(jnp.float32)
    total = total.astype(jnp.bfloat16)
    own = None
    for dh in range(n_high):
        for dr in range(n_rows):
            piece = lax.dynamic_slice(total, ((row ^ dr) * block, (high ^ dh) * part), (block, part))
            if dh or dr:
                piece = swap(piece, sizes, dr, dh * CORES, 0)
            piece = piece.astype(jnp.float32)
            own = piece if own is None else own + piece
    own = own.astype(jnp.bfloat16)
    loads = None
    for dk in range(n_groups):
        mine = [swap(own, sizes, dr, 0, dk) if dr or dk else own for dr in range(n_rows)]
        mine = jnp.concatenate(mine, axis=0)
        theirs = swap(mine, sizes, 0, 1, 0)
        firsts = [which * n_rows * block for which in (core, 1 - core)]
        loads = place_loads([mine, theirs], firsts, row, block, group ^ dk, n_groups, scale, loads)

    tile, width = min(own_rows, 256), loads.shape[1]
    left = row_product(mode_shapes, loads, tile, 12 * MIB if width <= modes else 56 * MIB)
    lefts = []

    unit = max(own_rows // sum(CHUNKS), min(own_rows, 128))
    spans, first = [], 0
    while first < own_rows:
        size = min(CHUNKS[min(len(spans), len(CHUNKS) - 1)] * unit, own_rows - first)
        spans.append((first, size))
        first += size

    size = min(UNIT * unit, own_rows)
    members = [
        [at for at, (first, _) in enumerate(spans) if first // size == which]
        for which in range(own_rows // size)
    ]
    n, m = len(spans), len(members)
    landed, others = [[] for _ in spans], [None] * n
    panel, columns = None, own_rows * n_groups
    turn = (row // CORES) ^ high

    def launch(at):
        first, count = spans[at]
        for dh in range(n_high):
            piece = left[first : first + count]
            if at >= AHEAD:
                piece = after(piece, landed[at - AHEAD][dh])
            landed[at].append(across(piece, sizes, dh * CORES))

    def widen(*earlier):
        half = own_rows // CORES
        whole = [left]
        for dh in range(1, n_high):
            sent = lax.dynamic_slice_in_dim(left, core * half, half, 0)
            came = swap(after(sent, *earlier), sizes, 0, dh * CORES, 0)
            rest = swap(came, sizes, 0, 1, 0)
            whole.append(
                jnp.where(core == 0, jnp.concatenate([came, rest], 0), jnp.concatenate([rest, came], 0))
            )
        joined = [
            jnp.concatenate([whole[d ^ first] for d in range(n_high)], axis=1) for first in range(n_high)
        ]
        wide = joined[-1]
        for first in range(n_high - 1):
            wide = jnp.where(turn == first, joined[first], wide)
        lefts.append(wide)

    def relay(at):
        if at:
            landed[at] = [
                after(piece, *[pieces[dh] for pieces in others[at - 1]])
                for dh, piece in enumerate(landed[at])
            ]
        others[at] = [[swap(p, sizes, 0, 0, dk) for p in landed[at]] for dk in range(1, n_groups)]

    def fill(wanted, *earlier):
        nonlocal panel
        units = [
            [others[at][dk - 1] if dk else landed[at] for at in members[which]] for which, dk in wanted
        ]
        places = [(group ^ dk) * len(members) + which for which, dk in wanted]
        panel, token = place_panel(lefts[0], units, places, columns, panel, *earlier)
        return token

    for at in range(n):
        launch(at)
        relay(at)
        if at == min(LEFT, n - 1):
            widen(*landed[at])
    pairs = [(which, dk) for dk in range(n_groups) for which in range(m)]
    last = [pair for pair in pairs if pair[1] and members[pair[0]][-1] == n - 1]
    first = [pair for pair in pairs if pair not in last]
    if first:
        fill(first)
    if last:
        fill(last)
    return panel


def solution(mesh):
    sizes = tuple(mesh.shape[axis] for axis in AXES)
    in_specs = (
        P(("prow", "pcol"), "pl"),
        P(None, ("prow", "pcol")),
        P(("prow", "pl"), None),
        P(),
        P(),
    )
    out_specs = P(("prow", "pl"), "pcol")
    return jax.shard_map(
        functools.partial(body, sizes), mesh=mesh, in_specs=in_specs, out_specs=out_specs, check_vma=False
    )
```

time: 154 us -> 146 us (0.948); the launches traced: 151 us -> 146 us
  waiting for transfers between devices: 23.3 us -> 65 us
  Pallas kernels: 50.6 us -> 18.7 us
  starting transfers between devices: 62.1 us -> 34.7 us
  matrix products: 0 us -> 6.86 us
  local copies, waits for them, and re-layouts: 9.79 us -> 15.7 us
    ppermute x10 -> x4, waiting for transfers between devices: 7.77 us -> 42.1 us  [across(): lax.ppermute(array, AXES, moves(sizes, lambda i, j, k: (j, i ^ flip, k)))]
    pallas_call x13 -> x3, Pallas kernels: 47.7 us -> 13.5 us  [the longest x2 10.6 us: place_panel(): pl.pallas_call(functools.partial(panel_kernel, count, shape), grid_spec=p...]
    ppermute x29 -> x23, starting transfers between devices: 44.5 us -> 26.9 us  [swap(): lax.ppermute(array, AXES, moves(sizes, lambda i, j, k: (i ^ di, j ^ dj, k...]
    ppermute x10 -> x4, starting transfers between devices: 17.6 us -> 7.86 us  [across(): lax.ppermute(array, AXES, moves(sizes, lambda i, j, k: (j, i ^ flip, k)))]
    unnamed x35 -> x38, local copies, waits for them, and re-layouts: 4.32 us -> 13.4 us
    ppermute x29 -> x23, waiting for transfers between devices: 15.5 us -> 22.9 us  [swap(): lax.ppermute(array, AXES, moves(sizes, lambda i, j, k: (i ^ di, j ^ dj, k...]
    dot_general x0 -> x2, matrix products: none -> 6.86 us  [the longest x1 3.43 us: body(): jnp.dot(here, factor_cols, preferred_element_type=jnp.float32)]
    add x3 -> x0, other arithmetic: 2.36 us -> none  [the longest x1 1.33 us: body(): total = here + came.astype(jnp.float32)]
  transfers between devices with their start and end apart: 39 -> 27, of which waited for: 10 -> 12; matrix products, arithmetic and copies ran while one was open for 4% -> 6% of each run, Pallas kernels for 22% -> 6%
where the time goes in v3:
time: 146 us
  waiting for transfers between devices  65 us (45%)
  starting transfers between devices  34.7 us (24%)
  Pallas kernels  18.7 us (13%)
  local copies, waits for them, and re-layouts  15.7 us (11%)
  matrix products  6.86 us (5%)
  other arithmetic  4.41 us (3%)
    ppermute x4, waiting for transfers between devices, across(): lax.ppermute(array, AXES, moves(sizes, lambda i, j, k: (j, i ^ flip, k)))  42.1 us
    ppermute x23, starting transfers between devices, swap(): lax.ppermute(array, AXES, moves(sizes, lambda i, j, k: (i ^ di, j ^ dj, k...  26.9 us
    ppermute x23, waiting for transfers between devices, swap(): lax.ppermute(array, AXES, moves(sizes, lambda i, j, k: (i ^ di, j ^ dj, k...  22.9 us
    unnamed x38, local copies, waits for them, and re-layouts  13.4 us
    pallas_call x2, Pallas kernels, place_panel(): pl.pallas_call(functools.partial(panel_kernel, count, shape), grid_spec=p...  10.6 us
    ppermute x4, starting transfers between devices, across(): lax.ppermute(array, AXES, moves(sizes, lambda i, j, k: (j, i ^ flip, k)))  7.86 us
    pallas_call x2, Pallas kernels, place_loads(): pl.pallas_call(lambda spots, column, *refs: load_kernel(rows, spots, *ref...  5.2 us
    dot_general x1, matrix products, body(): jnp.dot(here, factor_cols, preferred_element_type=jnp.float32)  3.43 us
  transfers between devices with their start and end apart: 27, of which 12 were waited for; matrix products, arithmetic and copies ran while one was open for 6% of the time, Pallas kernels for 6%

profile of v3, /device:TPU:4, one launch (start us, length us, event | category | flops | bytes accessed | tf_op | source)
XLA Modules:
  0.0 145.6 jit_solution(7487303244362477962)
XLA Ops:
  0.0 1.2 copy-done
  1.2 3.4 %fusion.4 = bf16[1024,256]{1,0:T(8,128)(2,1)S(1)} fusion(bf16[2048,256]{1,0:T(8,128)(2,1)S(1)} %copy-done, bf16[2048,2048]{1,0:T(8,128)(2,1)} %param.6, s32[]{:T(128)S(6)} %select_n.72), kind=kOutput, calls=%fused_computation.5 | convolution fusion | flops 1074003968 | bytes 5767172 | tf_op jit(solution)/shard_map/dot_general | solution.py:178
  4.8 1.8 %collective-permute-done = bf16[1024,256]{1,0:T(8,128)(2,1)S(1)} collective-permute-done((bf16[1024,256]{1,0:T(8,128)(2,1)S(1)}, bf16[1024,256]{1,0:T(8,128)(2,1)S(1)}, u32[]{:S(2)}, u32[]{:S(2)}) %collective-permute-start) | collective-permute-done | bytes 524320 | tf_op jit(solution)/shard_map/ppermute | solution.py:38
  6.6 3.4 %add_convert_fusion = bf16[1024,256]{1,0:T(8,128)(2,1)S(1)} fusion(bf16[1024,256]{1,0:T(8,128)(2,1)S(1)} %collective-permute-done, bf16[2048,256]{1,0:T(8,128)(2,1)S(1)} %copy-done, bf16[2048,2048]{1,0:T(8,128)(2,1)} %param.6, s32[]{:T(128)S(6)} %select_n.71), kind=kOutput, calls=%fused_computation.7 | convolution fusion | flops 1074528256 | bytes 6291460 | tf_op jit(solution)/shard_map/dot_general | solution.py:180
  10.1 0.1 fusion.13
  10.2 1.6 %collective-permute-start.1 = (bf16[256,128]{1,0:T(8,128)(2,1)S(1)}, bf16[256,128]{1,0:T(8,128)(2,1)S(1)}, u32[]{:S(2)}, u32[]{:S(2)}) collective-permute-start(bf16[256,128]{1,0:T(8,128)(2,1)S(1)} %get-tuple-element.12), channel_id=1, source_target_pairs={{8,0},{9,1},{10,2},{11,3},{12,4},{13,5},{14,6},{15,7},{0,8},{1,9},... | collective-permute-start | bytes 196616 | tf_op jit(solution)/shard_map/ppermute | solution.py:38
  11.8 2.4 %collective-permute-start.7 = (bf16[256,128]{1,0:T(8,128)(2,1)S(1)}, bf16[256,128]{1,0:T(8,128)(2,1)S(1)}, u32[]{:S(2)}, u32[]{:S(2)}) collective-permute-start(bf16[256,128]{1,0:T(8,128)(2,1)S(1)} %get-tuple-element.13), channel_id=1, source_target_pairs={{28,0},{29,1},{30,2},{31,3},{24,4},{25,5},{26,6},{27,7},{20,8},{21... | collective-permute-start | bytes 196616 | tf_op jit(solution)/shard_map/ppermute | solution.py:38
  14.2 0.4 collective-permute-start.6
  14.6 2.4 %collective-permute-start.5 = (bf16[256,128]{1,0:T(8,128)(2,1)S(1)}, bf16[256,128]{1,0:T(8,128)(2,1)S(1)}, u32[]{:S(2)}, u32[]{:S(2)}) collective-permute-start(bf16[256,128]{1,0:T(8,128)(2,1)S(1)} %get-tuple-element.15), channel_id=1, source_target_pairs={{12,0},{13,1},{14,2},{15,3},{8,4},{9,5},{10,6},{11,7},{4,8},{5,9},... | collective-permute-start | bytes 196616 | tf_op jit(solution)/shard_map/ppermute | solution.py:38
  17.1 1.5 %collective-permute-start.4 = (bf16[256,128]{1,0:T(8,128)(2,1)S(1)}, bf16[256,128]{1,0:T(8,128)(2,1)S(1)}, u32[]{:S(2)}, u32[]{:S(2)}) collective-permute-start(bf16[256,128]{1,0:T(8,128)(2,1)S(1)} %get-tuple-element.16), channel_id=1, source_target_pairs={{4,0},{5,1},{6,2},{7,3},{0,4},{1,5},{2,6},{3,7},{12,8},{13,9},{14,... | collective-permute-start | bytes 196616 | tf_op jit(solution)/shard_map/ppermute | solution.py:38
  18.6 2.5 %collective-permute-start.3 = (bf16[256,128]{1,0:T(8,128)(2,1)S(1)}, bf16[256,128]{1,0:T(8,128)(2,1)S(1)}, u32[]{:S(2)}, u32[]{:S(2)}) collective-permute-start(bf16[256,128]{1,0:T(8,128)(2,1)S(1)} %get-tuple-element.17), channel_id=1, source_target_pairs={{24,0},{25,1},{26,2},{27,3},{28,4},{29,5},{30,6},{31,7},{16,8},{17... | collective-permute-start | bytes 196616 | tf_op jit(solution)/shard_map/ppermute | solution.py:38
  21.1 2.0 %collective-permute-start.2 = (bf16[256,128]{1,0:T(8,128)(2,1)S(1)}, bf16[256,128]{1,0:T(8,128)(2,1)S(1)}, u32[]{:S(2)}, u32[]{:S(2)}) collective-permute-start(bf16[256,128]{1,0:T(8,128)(2,1)S(1)} %get-tuple-element.18), channel_id=1, source_target_pairs={{16,0},{17,1},{18,2},{19,3},{20,4},{21,5},{22,6},{23,7},{24,8},{25... | collective-permute-start | bytes 196616 | tf_op jit(solution)/shard_map/ppermute | solution.py:38
  23.1 1.7 %collective-permute-done.3 = bf16[256,128]{1,0:T(8,128)(2,1)S(1)} collective-permute-done((bf16[256,128]{1,0:T(8,128)(2,1)S(1)}, bf16[256,128]{1,0:T(8,128)(2,1)S(1)}, u32[]{:S(2)}, u32[]{:S(2)}) %collective-permute-start.3) | collective-permute-done | bytes 65568 | tf_op jit(solution)/shard_map/ppermute | solution.py:38
  24.8 2.0 %collective-permute-done.2 = bf16[256,128]{1,0:T(8,128)(2,1)S(1)} collective-permute-done((bf16[256,128]{1,0:T(8,128)(2,1)S(1)}, bf16[256,128]{1,0:T(8,128)(2,1)S(1)}, u32[]{:S(2)}, u32[]{:S(2)}) %collective-permute-start.2) | collective-permute-done | bytes 65568 | tf_op jit(solution)/shard_map/ppermute | solution.py:38
  26.7 0.1 add_convert_fusion.1
  26.8 1.6 %collective-permute-start.8 = (bf16[256,128]{1,0:T(8,128)(2,1)S(1)}, bf16[256,128]{1,0:T(8,128)(2,1)S(1)}, u32[]{:S(2)}, u32[]{:S(2)}) collective-permute-start(bf16[256,128]{1,0:T(8,128)(2,1)S(1)} %add_convert_fusion.1), channel_id=1, source_target_pairs={{1,0},{0,1},{3,2},{2,3},{5,4},{4,5},{7,6},{6,7},{9,8},{8,9},{11,10... | collective-permute-start | bytes 196616 | tf_op jit(solution)/shard_map/ppermute | solution.py:38
  28.4 1.8 %collective-permute-start.15 = (bf16[256,128]{1,0:T(8,128)(2,1)S(1)}, bf16[256,128]{1,0:T(8,128)(2,1)S(1)}, u32[]{:S(2)}, u32[]{:S(2)}) collective-permute-start(bf16[256,128]{1,0:T(8,128)(2,1)S(1)} %add_convert_fusion.1), channel_id=1, source_target_pairs={{24,0},{25,1},{26,2},{27,3},{28,4},{29,5},{30,6},{31,7},{16,8},{17... | collective-permute-start | bytes 196616 | tf_op jit(solution)/shard_map/ppermute | solution.py:38
  30.1 2.7 %collective-permute-start.13 = (bf16[256,128]{1,0:T(8,128)(2,1)S(1)}, bf16[256,128]{1,0:T(8,128)(2,1)S(1)}, u32[]{:S(2)}, u32[]{:S(2)}) collective-permute-start(bf16[256,128]{1,0:T(8,128)(2,1)S(1)} %add_convert_fusion.1), channel_id=1, source_target_pairs={{8,0},{9,1},{10,2},{11,3},{12,4},{13,5},{14,6},{15,7},{0,8},{1,9},... | collective-permute-start | bytes 196616 | tf_op jit(solution)/shard_map/ppermute | solution.py:38
  32.8 1.7 %collective-permute-start.11 = (bf16[256,128]{1,0:T(8,128)(2,1)S(1)}, bf16[256,128]{1,0:T(8,128)(2,1)S(1)}, u32[]{:S(2)}, u32[]{:S(2)}) collective-permute-start(bf16[256,128]{1,0:T(8,128)(2,1)S(1)} %add_convert_fusion.1), channel_id=1, source_target_pairs={{25,0},{24,1},{27,2},{26,3},{29,4},{28,5},{31,6},{30,7},{17,8},{16... | collective-permute-start | bytes 196616 | tf_op jit(solution)/shard_map/ppermute | solution.py:38
  34.5 0.4 collective-permute-start.9
  34.9 0.6 constant_dynamic-update-slice_fusion.3
  35.6 4.8 %collective-permute-done.9 = bf16[256,128]{1,0:T(8,128)(2,1)S(1)} collective-permute-done((bf16[256,128]{1,0:T(8,128)(2,1)S(1)}, bf16[256,128]{1,0:T(8,128)(2,1)S(1)}, u32[]{:S(2)}, u32[]{:S(2)}) %collective-permute-start.9) | collective-permute-done | bytes 65568 | tf_op jit(solution)/shard_map/ppermute | solution.py:38
  40.4 1.0 collective-permute-start.10
  41.4 0.6 constant_dynamic-update-slice_fusion.2
  42.0 4.6 %collective-permute-done.10 = bf16[256,128]{1,0:T(8,128)(2,1)S(1)} collective-permute-done((bf16[256,128]{1,0:T(8,128)(2,1)S(1)}, bf16[256,128]{1,0:T(8,128)(2,1)S(1)}, u32[]{:S(2)}, u32[]{:S(2)}) %collective-permute-start.10) | collective-permute-done | bytes 65568 | tf_op jit(solution)/shard_map/ppermute | solution.py:38
  46.6 0.6 constant_dynamic-update-slice_fusion.1
  47.2 0.6 constant_dynamic-update-slice_fusion.refs_1_
  47.9 0.6 collective-permute-start.16
  48.5 0.6 copy.14.refs_0_
  49.2 0.1 pad_add_fusion.spots
  49.2 0.7 collective-permute-done.16.refs_2_
  49.9 2.4 %shard_map.55.refs_3_ = bf16[2048,512]{1,0:T(8,128)(2,1)S(1)} custom-call(s32[3]{0:T(128)S(1)} %pad_add_fusion.spots, s32[1]{0:T(128)} %bitcast.8.column, f32[2,2048,1]{2,1,0:T(8,128)S(1)} %copy.14.refs_0_, bf16[1024,128]{1,0:T(8,128)(2,1)S(1)} %pad_maximum_fusion.refs_1_, bf16[1024,128]{1,0:T(8,128)(2,1)} %collective-permute-done.16.refs_2_), custom_call_target="tpu_custom_call" | custom-call | flops 1 | bytes 1 | tf_op jit(solution)/shard_map/pallas_call | solution.py:102
  52.4 2.8 %shard_map.56.b = bf16[2048,512]{1,0:T(8,128)(2,1)S(1)} custom-call(s32[3]{0:T(128)S(1)} %pad_add_fusion.spots, s32[1]{0:T(128)} %bitcast.4.column, f32[2,2048,1]{2,1,0:T(8,128)S(1)} %copy.14.refs_0_, bf16[1024,128]{1,0:T(8,128)(2,1)} %constant_dynamic-update-slice_fusion.refs_1_, ...), custom_call_target="tpu_custom_call", output_to_operand_aliasing={{}: (5, {})} | custom-call | flops 1 | bytes 1 | tf_op jit(solution)/shard_map/pallas_call | solution.py:102
  55.2 2.9 %shard_map.57 = bf16[1024,512]{1,0:T(8,128)(2,1)S(1)} custom-call(bf16[1024,2048]{1,0:T(8,128)(2,1)S(1)} %copy-done.7, bf16[2048,512]{1,0:T(8,128)(2,1)S(1)} %shard_map.56.b), custom_call_target="tpu_custom_call" | custom-call | flops 1 | bytes 1 | tf_op jit(solution)/shard_map/pallas_call | solution.py:73
  58.0 1.0 copy-done.1
  59.0 0.9 fusion.12
  59.9 2.0 %collective-permute-start.18 = (bf16[512,512]{1,0:T(8,128)(2,1)S(1)}, bf16[512,512]{1,0:T(8,128)(2,1)S(1)}, u32[]{:S(2)}, u32[]{:S(2)}) collective-permute-start(bf16[512,512]{1,0:T(8,128)(2,1)S(1)} %get-tuple-element.10), channel_id=1, source_target_pairs={{4,0},{5,1},{12,2},{13,3},{20,4},{21,5},{28,6},{29,7},{6,8},{7,9},... | collective-permute-start | bytes 1572872 | tf_op jit(solution)/shard_map/ppermute | solution.py:42
  61.9 1.9 %collective-permute-start.17 = (bf16[512,512]{1,0:T(8,128)(2,1)S(1)}, bf16[512,512]{1,0:T(8,128)(2,1)S(1)}, u32[]{:S(2)}, u32[]{:S(2)}) collective-permute-start(bf16[512,512]{1,0:T(8,128)(2,1)S(1)} %get-tuple-element.10), channel_id=1, source_target_pairs={{0,0},{1,1},{8,2},{9,3},{16,4},{17,5},{24,6},{25,7},{2,8},{3,9},{1... | collective-permute-start | bytes 1572872 | tf_op jit(solution)/shard_map/ppermute | solution.py:42
  63.9 20.8 %collective-permute-done.18.refs_2_.refs_1_ = bf16[512,512]{1,0:T(8,128)(2,1)S(1)} collective-permute-done((bf16[512,512]{1,0:T(8,128)(2,1)S(1)}, bf16[512,512]{1,0:T(8,128)(2,1)S(1)}, u32[]{:S(2)}, u32[]{:S(2)}) %collective-permute-start.18) | collective-permute-done | bytes 524320 | tf_op jit(solution)/shard_map/ppermute | solution.py:42
  84.7 6.0 %collective-permute-done.17.refs_1_.refs_0_ = bf16[512,512]{1,0:T(8,128)(2,1)S(1)} collective-permute-done((bf16[512,512]{1,0:T(8,128)(2,1)S(1)}, bf16[512,512]{1,0:T(8,128)(2,1)S(1)}, u32[]{:S(2)}, u32[]{:S(2)}) %collective-permute-start.17) | collective-permute-done | bytes 524320 | tf_op jit(solution)/shard_map/ppermute | solution.py:42
  90.7 0.8 copy-done.4
  91.5 0.8 copy.22.refs_0_
  92.3 2.0 %collective-permute-start.24 = (bf16[512,512]{1,0:T(8,128)(2,1)}, bf16[512,512]{1,0:T(8,128)(2,1)}, u32[]{:S(2)}, u32[]{:S(2)}) collective-permute-start(bf16[512,512]{1,0:T(8,128)(2,1)} %shard_map.61), channel_id=1, source_target_pairs={{4,0},{5,1},{12,2},{13,3},{20,4},{21,5},{28,6},{29,7},{6,8},{7,9},... | collective-permute-start | bytes 1572872 | tf_op jit(solution)/shard_map/ppermute | solution.py:42
  94.3 0.7 collective-permute-start.25
  95.1 1.9 %collective-permute-start.21 = (bf16[512,512]{1,0:T(8,128)(2,1)}, bf16[512,512]{1,0:T(8,128)(2,1)S(1)}, u32[]{:S(2)}, u32[]{:S(2)}) collective-permute-start(bf16[512,512]{1,0:T(8,128)(2,1)} %shard_map.59), channel_id=1, source_target_pairs={{0,0},{1,1},{8,2},{9,3},{16,4},{17,5},{24,6},{25,7},{2,8},{3,9},{1... | collective-permute-start | bytes 1572872 | tf_op jit(solution)/shard_map/ppermute | solution.py:42
  97.0 1.3 collective-permute-start.22
  98.3 5.8 %collective-permute-done.19 = bf16[512,512]{1,0:T(8,128)(2,1)} collective-permute-done((bf16[512,512]{1,0:T(8,128)(2,1)}, bf16[512,512]{1,0:T(8,128)(2,1)}, u32[]{:S(2)}, u32[]{:S(2)}) %collective-permute-start.19) | collective-permute-done | bytes 524320 | tf_op jit(solution)/shard_map/ppermute | solution.py:38
  104.1 7.7 %collective-permute-done.24.refs_0_ = bf16[512,512]{1,0:T(8,128)(2,1)} collective-permute-done((bf16[512,512]{1,0:T(8,128)(2,1)}, bf16[512,512]{1,0:T(8,128)(2,1)}, u32[]{:S(2)}, u32[]{:S(2)}) %collective-permute-start.24) | collective-permute-done | bytes 524320 | tf_op jit(solution)/shard_map/ppermute | solution.py:42
  111.8 0.8 copy-done.8
  112.6 0.9 collective-permute-start.26
  113.5 7.6 %collective-permute-done.21.refs_0_ = bf16[512,512]{1,0:T(8,128)(2,1)S(1)} collective-permute-done((bf16[512,512]{1,0:T(8,128)(2,1)}, bf16[512,512]{1,0:T(8,128)(2,1)S(1)}, u32[]{:S(2)}, u32[]{:S(2)}) %collective-permute-start.21) | collective-permute-done | bytes 524320 | tf_op jit(solution)/shard_map/ppermute | solution.py:42
  121.1 0.8 copy-done.12
  121.9 0.8 copy-done.10
  122.7 1.2 collective-permute-start.23
  124.0 1.8 %maximum_select_fusion.1 = bf16[1024,512]{1,0:T(8,128)(2,1)S(1)} fusion(bf16[512,512]{1,0:T(8,128)(2,1)} %collective-permute-done.20, bf16[512,512]{1,0:T(8,128)(2,1)} %collective-permute-done.19, pred[]{:T(512)S(6)} %eq.9), kind=kLoop, calls=%fused_computation.6 | loop fusion | flops 4718592 | bytes 2097153 | tf_op jit(solution)/shard_map/jit(_where)/select_n | solution.py:236
  125.9 2.3 %maximum_select_fusion.left = bf16[1024,1024]{1,0:T(8,128)(2,1)S(1)} fusion(bf16[1024,512]{1,0:T(8,128)(2,1)S(1)} %maximum_select_fusion.1, bf16[1024,512]{1,0:T(8,128)(2,1)} %copy-done.1, pred[]{:T(512)S(6)} %eq.8), kind=kLoop, calls=%fused_computation.4 | loop fusion | flops 9437184 | bytes 4194305 | tf_op jit(solution)/shard_map/jit(_where)/select_n | solution.py:243
  128.2 1.0 copy-done.3
  129.2 1.0 copy-done.6
  130.3 1.0 copy-done.9
  131.3 1.0 copy-done.11
  132.3 1.0 copy-done.13
  133.4 6.8 %shard_map.63 = (f32[1024,2048]{1,0:T(8,128)}, f32[8,128]{1,0:T(8,128)}) custom-call(s32[3]{0:T(128)S(1)} %pad_add_fusion.1.spots, bf16[1024,1024]{1,0:T(8,128)(2,1)S(1)} %maximum_select_fusion.left, bf16[512,512]{1,0:T(8,128)(2,1)S(1)} %copy-done.6, bf16[512,512]{1,0:T(8,128)(2,1)S(1)} %copy-done.3, bf16[512,512]{1,0:T(8,128)(2,1)S(1)} %copy-done.13, ...), custom_call_target="tpu_custom_call" | custom-call | flops 1 | bytes 1 | tf_op jit(solution)/shard_map/pallas_call | solution.py:144
  140.2 1.6 %collective-permute-done.23.refs_0_ = bf16[512,512]{1,0:T(8,128)(2,1)} collective-permute-done((bf16[512,512]{1,0:T(8,128)(2,1)}, bf16[512,512]{1,0:T(8,128)(2,1)}, u32[]{:S(2)}, u32[]{:S(2)}) %collective-permute-start.23) | collective-permute-done | bytes 524320 | tf_op jit(solution)/shard_map/ppermute | solution.py:38
  141.8 3.8 %shard_map.64 = (f32[1024,2048]{1,0:T(8,128)}, f32[8,128]{1,0:T(8,128)}) custom-call(s32[1]{0:T(128)} %bitcast.spots, bf16[1024,1024]{1,0:T(8,128)(2,1)S(1)} %maximum_select_fusion.left, bf16[512,512]{1,0:T(8,128)(2,1)} %collective-permute-done.23.refs_0_, bf16[512,512]{1,0:T(8,128)(2,1)} %collective-permute-done.26.refs_1_, ...), custom_call_target="tpu_custom_call", output_to_operand_aliasing={{0}: (4, {})} | custom-call | flops 1 | bytes 1 | tf_op jit(solution)/shard_map/pallas_call | solution.py:144
  (52 shorter events, 0.3 us)
Async XLA Ops:
  0.0 1.2 copy-start
  4.7 2.0 %collective-permute-start = (bf16[1024,256]{1,0:T(8,128)(2,1)S(1)}, bf16[1024,256]{1,0:T(8,128)(2,1)S(1)}, u32[]{:S(2)}, u32[]{:S(2)}) collective-permute-start(bf16[1024,256]{1,0:T(8,128)(2,1)S(1)} %fusion.4), channel_id=1, source_target_pairs={{2,0},{3,1},{0,2},{1,3},{6,4},{7,5},{4,6},{5,7},{10,8},{11,9},{8,1... | collective-permute-start | bytes 1572872 | tf_op jit(solution)/shard_map/ppermute | solution.py:38
  4.8 23.5 %copy-start.15 = (f32[2048]{0:T(1024)S(1)}, f32[2048]{0:T(1024)}, u32[]{:S(2)}) copy-start(f32[2048]{0:T(1024)} %param.8) | copy-start | bytes 24580
  4.8 23.5 %copy-start.16 = (f32[2048]{0:T(1024)S(1)}, f32[2048]{0:T(1024)}, u32[]{:S(2)}) copy-start(f32[2048]{0:T(1024)} %param.9) | copy-start | bytes 24580
  10.2 8.4 %collective-permute-start.1 = (bf16[256,128]{1,0:T(8,128)(2,1)S(1)}, bf16[256,128]{1,0:T(8,128)(2,1)S(1)}, u32[]{:S(2)}, u32[]{:S(2)}) collective-permute-start(bf16[256,128]{1,0:T(8,128)(2,1)S(1)} %get-tuple-element.12), channel_id=1, source_target_pairs={{8,0},{9,1},{10,2},{11,3},{12,4},{13,5},{14,6},{15,7},{0,8},{1,9},... | collective-permute-start | bytes 196616 | tf_op jit(solution)/shard_map/ppermute | solution.py:38
  11.8 9.2 %collective-permute-start.7 = (bf16[256,128]{1,0:T(8,128)(2,1)S(1)}, bf16[256,128]{1,0:T(8,128)(2,1)S(1)}, u32[]{:S(2)}, u32[]{:S(2)}) collective-permute-start(bf16[256,128]{1,0:T(8,128)(2,1)S(1)} %get-tuple-element.13), channel_id=1, source_target_pairs={{28,0},{29,1},{30,2},{31,3},{24,4},{25,5},{26,6},{27,7},{20,8},{21... | collective-permute-start | bytes 196616 | tf_op jit(solution)/shard_map/ppermute | solution.py:38
  14.2 8.8 %collective-permute-start.6 = (bf16[256,128]{1,0:T(8,128)(2,1)S(1)}, bf16[256,128]{1,0:T(8,128)(2,1)S(1)}, u32[]{:S(2)}, u32[]{:S(2)}) collective-permute-start(bf16[256,128]{1,0:T(8,128)(2,1)S(1)} %get-tuple-element.14), channel_id=1, source_target_pairs={{20,0},{21,1},{22,2},{23,3},{16,4},{17,5},{18,6},{19,7},{28,8},{29... | collective-permute-start | bytes 196616 | tf_op jit(solution)/shard_map/ppermute | solution.py:38
  14.6 8.4 %collective-permute-start.5 = (bf16[256,128]{1,0:T(8,128)(2,1)S(1)}, bf16[256,128]{1,0:T(8,128)(2,1)S(1)}, u32[]{:S(2)}, u32[]{:S(2)}) collective-permute-start(bf16[256,128]{1,0:T(8,128)(2,1)S(1)} %get-tuple-element.15), channel_id=1, source_target_pairs={{12,0},{13,1},{14,2},{15,3},{8,4},{9,5},{10,6},{11,7},{4,8},{5,9},... | collective-permute-start | bytes 196616 | tf_op jit(solution)/shard_map/ppermute | solution.py:38
  17.1 6.0 %collective-permute-start.4 = (bf16[256,128]{1,0:T(8,128)(2,1)S(1)}, bf16[256,128]{1,0:T(8,128)(2,1)S(1)}, u32[]{:S(2)}, u32[]{:S(2)}) collective-permute-start(bf16[256,128]{1,0:T(8,128)(2,1)S(1)} %get-tuple-element.16), channel_id=1, source_target_pairs={{4,0},{5,1},{6,2},{7,3},{0,4},{1,5},{2,6},{3,7},{12,8},{13,9},{14,... | collective-permute-start | bytes 196616 | tf_op jit(solution)/shard_map/ppermute | solution.py:38
  18.6 6.2 %collective-permute-start.3 = (bf16[256,128]{1,0:T(8,128)(2,1)S(1)}, bf16[256,128]{1,0:T(8,128)(2,1)S(1)}, u32[]{:S(2)}, u32[]{:S(2)}) collective-permute-start(bf16[256,128]{1,0:T(8,128)(2,1)S(1)} %get-tuple-element.17), channel_id=1, source_target_pairs={{24,0},{25,1},{26,2},{27,3},{28,4},{29,5},{30,6},{31,7},{16,8},{17... | collective-permute-start | bytes 196616 | tf_op jit(solution)/shard_map/ppermute | solution.py:38
  21.1 5.6 %collective-permute-start.2 = (bf16[256,128]{1,0:T(8,128)(2,1)S(1)}, bf16[256,128]{1,0:T(8,128)(2,1)S(1)}, u32[]{:S(2)}, u32[]{:S(2)}) collective-permute-start(bf16[256,128]{1,0:T(8,128)(2,1)S(1)} %get-tuple-element.18), channel_id=1, source_target_pairs={{16,0},{17,1},{18,2},{19,3},{20,4},{21,5},{22,6},{23,7},{24,8},{25... | collective-permute-start | bytes 196616 | tf_op jit(solution)/shard_map/ppermute | solution.py:38
  26.8 7.7 %collective-permute-start.8 = (bf16[256,128]{1,0:T(8,128)(2,1)S(1)}, bf16[256,128]{1,0:T(8,128)(2,1)S(1)}, u32[]{:S(2)}, u32[]{:S(2)}) collective-permute-start(bf16[256,128]{1,0:T(8,128)(2,1)S(1)} %add_convert_fusion.1), channel_id=1, source_target_pairs={{1,0},{0,1},{3,2},{2,3},{5,4},{4,5},{7,6},{6,7},{9,8},{8,9},{11,10... | collective-permute-start | bytes 196616 | tf_op jit(solution)/shard_map/ppermute | solution.py:38
  28.4 19.5 %collective-permute-start.15 = (bf16[256,128]{1,0:T(8,128)(2,1)S(1)}, bf16[256,128]{1,0:T(8,128)(2,1)S(1)}, u32[]{:S(2)}, u32[]{:S(2)}) collective-permute-start(bf16[256,128]{1,0:T(8,128)(2,1)S(1)} %add_convert_fusion.1), channel_id=1, source_target_pairs={{24,0},{25,1},{26,2},{27,3},{28,4},{29,5},{30,6},{31,7},{16,8},{17... | collective-permute-start | bytes 196616 | tf_op jit(solution)/shard_map/ppermute | solution.py:38
  30.1 17.7 %collective-permute-start.14 = (bf16[256,128]{1,0:T(8,128)(2,1)S(1)}, bf16[256,128]{1,0:T(8,128)(2,1)S(1)}, u32[]{:S(2)}, u32[]{:S(2)}) collective-permute-start(bf16[256,128]{1,0:T(8,128)(2,1)S(1)} %add_convert_fusion.1), channel_id=1, source_target_pairs={{16,0},{17,1},{18,2},{19,3},{20,4},{21,5},{22,6},{23,7},{24,8},{25... | collective-permute-start | bytes 196616 | tf_op jit(solution)/shard_map/ppermute | solution.py:38
  30.1 17.7 %collective-permute-start.13 = (bf16[256,128]{1,0:T(8,128)(2,1)S(1)}, bf16[256,128]{1,0:T(8,128)(2,1)S(1)}, u32[]{:S(2)}, u32[]{:S(2)}) collective-permute-start(bf16[256,128]{1,0:T(8,128)(2,1)S(1)} %add_convert_fusion.1), channel_id=1, source_target_pairs={{8,0},{9,1},{10,2},{11,3},{12,4},{13,5},{14,6},{15,7},{0,8},{1,9},... | collective-permute-start | bytes 196616 | tf_op jit(solution)/shard_map/ppermute | solution.py:38
  32.8 14.4 %collective-permute-start.11 = (bf16[256,128]{1,0:T(8,128)(2,1)S(1)}, bf16[256,128]{1,0:T(8,128)(2,1)S(1)}, u32[]{:S(2)}, u32[]{:S(2)}) collective-permute-start(bf16[256,128]{1,0:T(8,128)(2,1)S(1)} %add_convert_fusion.1), channel_id=1, source_target_pairs={{25,0},{24,1},{27,2},{26,3},{29,4},{28,5},{31,6},{30,7},{17,8},{16... | collective-permute-start | bytes 196616 | tf_op jit(solution)/shard_map/ppermute | solution.py:38
  34.5 5.9 %collective-permute-start.9 = (bf16[256,128]{1,0:T(8,128)(2,1)S(1)}, bf16[256,128]{1,0:T(8,128)(2,1)S(1)}, u32[]{:S(2)}, u32[]{:S(2)}) collective-permute-start(bf16[256,128]{1,0:T(8,128)(2,1)S(1)} %add_convert_fusion.1), channel_id=1, source_target_pairs={{9,0},{8,1},{11,2},{10,3},{13,4},{12,5},{15,6},{14,7},{1,8},{0,9},... | collective-permute-start | bytes 196616 | tf_op jit(solution)/shard_map/ppermute | solution.py:38
  40.4 6.2 %collective-permute-start.10 = (bf16[256,128]{1,0:T(8,128)(2,1)S(1)}, bf16[256,128]{1,0:T(8,128)(2,1)S(1)}, u32[]{:S(2)}, u32[]{:S(2)}) collective-permute-start(bf16[256,128]{1,0:T(8,128)(2,1)S(1)} %add_convert_fusion.1), channel_id=1, source_target_pairs={{17,0},{16,1},{19,2},{18,3},{21,4},{20,5},{23,6},{22,7},{25,8},{24... | collective-permute-start | bytes 196616 | tf_op jit(solution)/shard_map/ppermute | solution.py:38
  47.9 4.5 %collective-permute-start.12 = (bf16[1024,128]{1,0:T(8,128)(2,1)}, bf16[1024,128]{1,0:T(8,128)(2,1)}, u32[]{:S(2)}, u32[]{:S(2)}) collective-permute-start(bf16[1024,128]{1,0:T(8,128)(2,1)} %constant_dynamic-update-slice_fusion.refs_1_), channel_id=1, source_target_pairs={{2,0},{3,1},{0,2},{1,3},{6,4},{7,5},{4,6},{5,7},{10,8},{11,9},{8,1... | collective-permute-start | bytes 786440 | tf_op jit(solution)/shard_map/ppermute | solution.py:38
  47.9 2.0 %collective-permute-start.16 = (bf16[1024,128]{1,0:T(8,128)(2,1)S(1)}, bf16[1024,128]{1,0:T(8,128)(2,1)}, u32[]{:S(2)}, u32[]{:S(2)}) collective-permute-start(bf16[1024,128]{1,0:T(8,128)(2,1)S(1)} %pad_maximum_fusion.refs_1_), channel_id=1, source_target_pairs={{2,0},{3,1},{0,2},{1,3},{6,4},{7,5},{4,6},{5,7},{10,8},{11,9},{8,1... | collective-permute-start | bytes 786440 | tf_op jit(solution)/shard_map/ppermute | solution.py:38
  52.3 2.8 %copy-start.7 = (bf16[1024,2048]{1,0:T(8,128)(2,1)S(1)}, bf16[1024,2048]{1,0:T(8,128)(2,1)}, u32[]{:S(2)}) copy-start(bf16[1024,2048]{1,0:T(8,128)(2,1)} %a.1) | copy-start | bytes 12582916
  58.0 1.0 copy-start.1
  59.9 35.1 %copy-start.14 = (bf16[512,512]{1,0:T(8,128)(2,1)}, bf16[512,512]{1,0:T(8,128)(2,1)S(1)}, u32[]{:S(2)}) copy-start(bf16[512,512]{1,0:T(8,128)(2,1)S(1)} %get-tuple-element.9.refs_0_) | copy-start | bytes 1572868
  59.9 24.8 %collective-permute-start.18 = (bf16[512,512]{1,0:T(8,128)(2,1)S(1)}, bf16[512,512]{1,0:T(8,128)(2,1)S(1)}, u32[]{:S(2)}, u32[]{:S(2)}) collective-permute-start(bf16[512,512]{1,0:T(8,128)(2,1)S(1)} %get-tuple-element.10), channel_id=1, source_target_pairs={{4,0},{5,1},{12,2},{13,3},{20,4},{21,5},{28,6},{29,7},{6,8},{7,9},... | collective-permute-start | bytes 1572872 | tf_op jit(solution)/shard_map/ppermute | solution.py:42
  61.9 28.8 %collective-permute-start.17 = (bf16[512,512]{1,0:T(8,128)(2,1)S(1)}, bf16[512,512]{1,0:T(8,128)(2,1)S(1)}, u32[]{:S(2)}, u32[]{:S(2)}) collective-permute-start(bf16[512,512]{1,0:T(8,128)(2,1)S(1)} %get-tuple-element.10), channel_id=1, source_target_pairs={{0,0},{1,1},{8,2},{9,3},{16,4},{17,5},{24,6},{25,7},{2,8},{3,9},{1... | collective-permute-start | bytes 1572872 | tf_op jit(solution)/shard_map/ppermute | solution.py:42
  84.7 6.0 %copy-start.2 = (bf16[512,512]{1,0:T(8,128)(2,1)}, bf16[512,512]{1,0:T(8,128)(2,1)S(1)}, u32[]{:S(2)}) copy-start(bf16[512,512]{1,0:T(8,128)(2,1)S(1)} %collective-permute-done.18.refs_2_.refs_1_) | copy-start | bytes 1572868
  90.7 0.8 copy-start.4
  91.5 5.5 %copy-start.5 = (bf16[512,512]{1,0:T(8,128)(2,1)S(1)}, bf16[512,512]{1,0:T(8,128)(2,1)}, u32[]{:S(2)}) copy-start(bf16[512,512]{1,0:T(8,128)(2,1)} %copy-done.4) | copy-start | bytes 1572868
  91.5 12.6 %collective-permute-start.19 = (bf16[512,512]{1,0:T(8,128)(2,1)}, bf16[512,512]{1,0:T(8,128)(2,1)}, u32[]{:S(2)}, u32[]{:S(2)}) collective-permute-start(bf16[512,512]{1,0:T(8,128)(2,1)} %shard_map.58), channel_id=1, source_target_pairs={{4,0},{5,1},{6,2},{7,3},{0,4},{1,5},{2,6},{3,7},{12,8},{13,9},{14,... | collective-permute-start | bytes 1572872 | tf_op jit(solution)/shard_map/ppermute | solution.py:38
  92.3 19.5 %collective-permute-start.24 = (bf16[512,512]{1,0:T(8,128)(2,1)}, bf16[512,512]{1,0:T(8,128)(2,1)}, u32[]{:S(2)}, u32[]{:S(2)}) collective-permute-start(bf16[512,512]{1,0:T(8,128)(2,1)} %shard_map.61), channel_id=1, source_target_pairs={{4,0},{5,1},{12,2},{13,3},{20,4},{21,5},{28,6},{29,7},{6,8},{7,9},... | collective-permute-start | bytes 1572872 | tf_op jit(solution)/shard_map/ppermute | solution.py:42
  94.3 17.5 %collective-permute-start.25 = (bf16[512,512]{1,0:T(8,128)(2,1)}, bf16[512,512]{1,0:T(8,128)(2,1)S(1)}, u32[]{:S(2)}, u32[]{:S(2)}) collective-permute-start(bf16[512,512]{1,0:T(8,128)(2,1)} %copy-done.2), channel_id=1, source_target_pairs={{1,0},{0,1},{3,2},{2,3},{5,4},{4,5},{7,6},{6,7},{9,8},{8,9},{11,10... | collective-permute-start | bytes 1572872 | tf_op jit(solution)/shard_map/ppermute | solution.py:38
  95.1 26.0 %collective-permute-start.21 = (bf16[512,512]{1,0:T(8,128)(2,1)}, bf16[512,512]{1,0:T(8,128)(2,1)S(1)}, u32[]{:S(2)}, u32[]{:S(2)}) collective-permute-start(bf16[512,512]{1,0:T(8,128)(2,1)} %shard_map.59), channel_id=1, source_target_pairs={{0,0},{1,1},{8,2},{9,3},{16,4},{17,5},{24,6},{25,7},{2,8},{3,9},{1... | collective-permute-start | bytes 1572872 | tf_op jit(solution)/shard_map/ppermute | solution.py:42
  97.0 24.1 %collective-permute-start.22 = (bf16[512,512]{1,0:T(8,128)(2,1)S(1)}, bf16[512,512]{1,0:T(8,128)(2,1)S(1)}, u32[]{:S(2)}, u32[]{:S(2)}) collective-permute-start(bf16[512,512]{1,0:T(8,128)(2,1)S(1)} %copy-done.5), channel_id=1, source_target_pairs={{1,0},{0,1},{3,2},{2,3},{5,4},{4,5},{7,6},{6,7},{9,8},{8,9},{11,10... | collective-permute-start | bytes 1572872 | tf_op jit(solution)/shard_map/ppermute | solution.py:38
  104.1 19.9 %collective-permute-start.20 = (bf16[512,512]{1,0:T(8,128)(2,1)}, bf16[512,512]{1,0:T(8,128)(2,1)}, u32[]{:S(2)}, u32[]{:S(2)}) collective-permute-start(bf16[512,512]{1,0:T(8,128)(2,1)} %collective-permute-done.19), channel_id=1, source_target_pairs={{2,0},{3,1},{0,2},{1,3},{6,4},{7,5},{4,6},{5,7},{10,8},{11,9},{8,1... | collective-permute-start | bytes 1572872 | tf_op jit(solution)/shard_map/ppermute | solution.py:38
  111.8 0.8 copy-start.8
  112.6 27.6 %collective-permute-start.26 = (bf16[512,512]{1,0:T(8,128)(2,1)}, bf16[512,512]{1,0:T(8,128)(2,1)}, u32[]{:S(2)}, u32[]{:S(2)}) collective-permute-start(bf16[512,512]{1,0:T(8,128)(2,1)} %shard_map.62.refs_3_), channel_id=1, source_target_pairs={{1,0},{0,1},{3,2},{2,3},{5,4},{4,5},{7,6},{6,7},{9,8},{8,9},{11,10... | collective-permute-start | bytes 1572872 | tf_op jit(solution)/shard_map/ppermute | solution.py:38
  121.1 0.8 copy-start.12
  121.9 0.8 copy-start.10
  122.7 19.1 %collective-permute-start.23 = (bf16[512,512]{1,0:T(8,128)(2,1)}, bf16[512,512]{1,0:T(8,128)(2,1)}, u32[]{:S(2)}, u32[]{:S(2)}) collective-permute-start(bf16[512,512]{1,0:T(8,128)(2,1)} %shard_map.60.refs_2_), channel_id=1, source_target_pairs={{1,0},{0,1},{3,2},{2,3},{5,4},{4,5},{7,6},{6,7},{9,8},{8,9},{11,10... | collective-permute-start | bytes 1572872 | tf_op jit(solution)/shard_map/ppermute | solution.py:38
  128.2 1.0 copy-start.3
  129.2 1.0 copy-start.6
  130.3 1.0 copy-start.9
  131.3 1.0 copy-start.11
  132.3 1.0 copy-start.13

commit v4 on v0

v4 whole, which is shorter than its diff:
```python
import functools

import jax
import jax.numpy as jnp
from jax import lax
from jax.experimental import pallas as pl
from jax.experimental.pallas import tpu as pltpu
from jax.sharding import PartitionSpec as P

AXES = ("prow", "pcol", "pl")
CORES = 2
UNITS = 4
LAST = 1
PROJECT = 48
MIB = 1024 * 1024


def transfer_pair(natural_freq, damping):
    detuning = natural_freq * natural_freq - 1.0
    damper = 2.0 * damping * natural_freq
    modulus = detuning * detuning + damper * damper
    return detuning / modulus, -damper / modulus


def moves(sizes, source_of):
    rows, cols, groups = sizes
    pairs = []
    for i in range(rows):
        for j in range(cols):
            for k in range(groups):
                a, b, c = source_of(i, j, k)
                pairs.append(((a * cols + b) * groups + c, (i * cols + j) * groups + k))
    return pairs


def swap(array, sizes, di, dj, dk):
    return lax.ppermute(array, AXES, moves(sizes, lambda i, j, k: (i ^ di, j ^ dj, k ^ dk)))


def across(array, sizes, flip):
    return lax.ppermute(array, AXES, moves(sizes, lambda i, j, k: (j, i ^ flip, k)))


def cheap():
    return pl.CostEstimate(flops=1, bytes_accessed=1, transcendentals=0)


def after(array, *earlier):
    return pl.pallas_call(
        lambda *refs: None,
        in_specs=[pl.BlockSpec(memory_space=pl.ANY)] * (1 + len(earlier)),
        out_specs=pl.BlockSpec(memory_space=pl.ANY),
        out_shape=jax.ShapeDtypeStruct(array.shape, array.dtype),
        input_output_aliases={0: 0},
        cost_estimate=cheap(),
    )(array, *earlier)


def outer_rows(left_rows, right_rows):
    return lax.dot_general(
        left_rows, right_rows, (((1,), (1,)), ((), ())), preferred_element_type=jnp.float32
    )


def gather_kernel(rows, wide, spots, *refs):
    out = refs[-1]
    count = len(refs) - 1
    parts = out.shape[0] // rows
    for at in range(count):
        dk, dr = divmod(at, parts)
        first = pl.multiple_of((spots[0] ^ dr) * rows, rows)
        left = pl.multiple_of((spots[1] ^ dk) * wide, wide)
        out[pl.ds(first, rows), pl.ds(left, wide)] = refs[at][...]


def gather_loads(blocks, row, group, parts):
    rows, wide = blocks[0].shape
    whole = pl.BlockSpec(memory_space=pltpu.VMEM)
    shape = (rows * parts, wide * (len(blocks) // parts))
    return pl.pallas_call(
        functools.partial(gather_kernel, rows, wide),
        in_specs=[pl.BlockSpec(memory_space=pltpu.SMEM)] + [whole] * len(blocks),
        out_specs=whole,
        out_shape=jax.ShapeDtypeStruct(shape, jnp.bfloat16),
        compiler_params=pltpu.CompilerParams(vmem_limit_bytes=12 * MIB),
        cost_estimate=cheap(),
    )(jnp.stack([row, group]).astype(jnp.int32), *blocks)


def project_kernel(spots, mine, theirs, scale, shapes, out, loads):
    half, wide = mine.shape

    @pl.when(pl.program_id(0) == 0)
    def _():
        strip = min(wide, 256)
        for block, core in ((mine, spots[0]), (theirs, 1 - spots[0])):
            first = pl.multiple_of(core * half, half)

            @pl.loop(0, wide // strip)
            def _(at, block=block, first=first):
                left = pl.multiple_of(at * strip, strip)
                load = block[:, pl.ds(left, strip)].astype(jnp.float32)
                for part in range(2):
                    scaled = scale[part, pl.ds(first, half), :] * load
                    place = pl.multiple_of(part * wide + at * strip, strip)
                    loads[pl.ds(first, half), pl.ds(place, strip)] = scaled.astype(loads.dtype)

    out[...] = jnp.dot(shapes[...], loads[...], preferred_element_type=jnp.float32).astype(out.dtype)


def project(mode_shapes, mine, theirs, scale, core, first, last, tile):
    modes, wide = mode_shapes.shape[1], 2 * mine.shape[1]
    whole = pl.BlockSpec(memory_space=pltpu.VMEM)
    return pl.pallas_call(
        project_kernel,
        grid_spec=pltpu.PrefetchScalarGridSpec(
            num_scalar_prefetch=1,
            grid=(last - first,),
            in_specs=[whole] * 3 + [pl.BlockSpec((tile, modes), lambda g, spots: (first + g, 0))],
            out_specs=pl.BlockSpec((tile, wide), lambda g, spots: (g, 0)),
            scratch_shapes=[pltpu.VMEM((modes, wide), jnp.bfloat16)],
        ),
        out_shape=jax.ShapeDtypeStruct((tile * (last - first), wide), jnp.bfloat16),
        compiler_params=pltpu.CompilerParams(vmem_limit_bytes=PROJECT * MIB),
        cost_estimate=cheap(),
    )(jnp.reshape(core, (1,)).astype(jnp.int32), mine, theirs, scale, mode_shapes)


def widen_kernel(sets, spots, *refs):
    out, own, refs = refs[-1], refs[: len(sets)], refs[len(sets) : -1]
    deep = own[0].shape[1]

    def lay(array, spans, place):
        left, low = pl.multiple_of(place * deep, deep), 0
        for first, count in spans:
            out[first : first + count, pl.ds(left, deep)] = array[low : low + count, :]
            low += count

    for at, spans in enumerate(sets):
        lay(own[at], spans, spots[1])
    for core in range(len(sets)):

        @pl.when(spots[0] == core)
        def _(core=core):
            for at in range(0, len(refs), len(sets)):
                place = spots[1] ^ (at // len(sets) + 1)
                for d in range(len(sets)):
                    lay(refs[at + d], sets[core ^ d], place)


def widen_left(sets, own, others, core, turn, rows):
    whole = pl.BlockSpec(memory_space=pltpu.VMEM)
    deep = own[0].shape[1]
    wide = deep * (1 + len(others) // len(sets))
    return pl.pallas_call(
        functools.partial(widen_kernel, sets),
        in_specs=[pl.BlockSpec(memory_space=pltpu.SMEM)] + [whole] * (len(own) + len(others)),
        out_specs=whole,
        out_shape=jax.ShapeDtypeStruct((rows, wide), jnp.bfloat16),
        compiler_params=pltpu.CompilerParams(vmem_limit_bytes=12 * MIB),
        cost_estimate=cheap(),
    )(jnp.stack([core, turn]).astype(jnp.int32), *own, *others)


def panel_kernel(chunk, count, spots, left, *refs):
    first = pl.multiple_of(pl.program_id(0) * chunk, chunk)
    right = jnp.concatenate([piece[pl.ds(first, chunk), :] for piece in refs[:count]], axis=1)
    refs[-1][...] = outer_rows(left[...], right)


def place_panel(left, pieces, chunk, places, columns, panel):
    rows = left.shape[0]
    given = [] if panel is None else [panel]
    whole = pl.BlockSpec(memory_space=pltpu.VMEM)
    return pl.pallas_call(
        functools.partial(panel_kernel, chunk, len(pieces)),
        grid_spec=pltpu.PrefetchScalarGridSpec(
            num_scalar_prefetch=1,
            grid=(len(places),),
            in_specs=[whole] * (1 + len(pieces)) + [pl.BlockSpec(memory_space=pl.ANY) for _ in given],
            out_specs=pl.BlockSpec((rows, chunk), lambda g, spots: (0, spots[g])),
        ),
        out_shape=jax.ShapeDtypeStruct((rows, columns), jnp.float32),
        input_output_aliases={2 + len(pieces): 0} if given else {},
        compiler_params=pltpu.CompilerParams(vmem_limit_bytes=12 * MIB),
        cost_estimate=cheap(),
    )(jnp.stack(places).astype(jnp.int32), left, *pieces, *given)


def body(sizes, factor_cols, modal_at_loads, mode_shapes, natural_freq, damping):
    n_rows, n_cols, n_groups = sizes
    n_high = n_cols // CORES
    row, col, group = (lax.axis_index(axis) for axis in AXES)
    high, core = col // CORES, col % CORES
    scale = jnp.stack(transfer_pair(natural_freq, damping))[:, :, None]
    own_rows, modes = mode_shapes.shape

    part = factor_cols.shape[1] // n_high
    block = modes // CORES // n_rows
    half = block * n_rows
    away = lax.dynamic_slice_in_dim(modal_at_loads, (1 - core) * half, half, 0)
    here = lax.dynamic_slice_in_dim(modal_at_loads, core * half, half, 0)
    sent = jnp.dot(away, factor_cols, preferred_element_type=jnp.float32).astype(jnp.bfloat16)
    came = swap(sent, sizes, 0, 1, 0)
    total = jnp.dot(here, factor_cols, preferred_element_type=jnp.float32) + came.astype(jnp.float32)
    total = total.astype(jnp.bfloat16)
    own = None
    for dh in range(n_high):
        for dr in range(n_rows):
            piece = lax.dynamic_slice(total, ((row ^ dr) * block, (high ^ dh) * part), (block, part))
            if dh or dr:
                piece = swap(piece, sizes, dr, dh * CORES, 0)
            piece = piece.astype(jnp.float32)
            own = piece if own is None else own + piece
    own = own.astype(jnp.bfloat16)
    blocks = [
        swap(own, sizes, dr, 0, dk) if dr or dk else own for dk in range(n_groups) for dr in range(n_rows)
    ]
    mine = gather_loads(blocks, row, group, n_rows)
    theirs = swap(mine, sizes, 0, 1, 0)

    unit = max(own_rows // UNITS, min(own_rows, 128))
    units = own_rows // unit
    bounds = (0, 1, units - 1, units) if units > 2 else tuple(range(units + 1))
    lots = [
        project(mode_shapes, mine, theirs, scale, core, first, last, unit)
        for first, last in zip(bounds[:-1], bounds[1:])
    ]
    size = own_rows // CORES
    if units == 4:
        sets = (((0, unit), (3 * unit, unit)), ((unit, 2 * unit),))
        halves = [jnp.concatenate([lots[0], lots[2]], axis=0), lots[1]]
    else:
        sets = tuple(((first, size),) for first in range(0, own_rows, size))
        left = jnp.concatenate(lots, axis=0) if len(lots) > 1 else lots[0]
        halves = [left[first : first + size] for first in range(0, own_rows, size)]

    def cross(rows, earlier):
        pair = []
        for dh in range(n_high):
            held = after(rows, *earlier[dh]) if earlier else rows
            pair.append(across(held, sizes, dh * CORES))
        return pair

    def relay(pair, earlier):
        if earlier:
            pair = [after(rows, *[sent[dh] for sent in earlier]) for dh, rows in enumerate(pair)]
        return pair, [[swap(rows, sizes, 0, 0, dk) for rows in pair] for dk in range(1, n_groups)]

    landed = cross(lots[0], [])
    both = []
    if units > 2:
        both = [lots[2]] + [swap(lots[2], sizes, 0, 0, dk) for dk in range(1, n_groups)]
    landed, others = relay(landed, [])
    pieces = [(landed, others, 0)]

    away = jnp.where(core == 0, halves[0], halves[1])
    widened = [swap(after(away, *landed), sizes, 0, dh * CORES, 0) for dh in range(1, n_high)]
    done = list(widened) + [rows for sent in others for rows in sent]

    crossed = landed
    if units > 1:
        crossed = cross(lots[1], [[rows] for rows in crossed])
        done += crossed
        landed, others = relay(crossed, others)
        pieces.append((landed, others, 1))
    if units > 2:
        landed = cross(jnp.concatenate(both, axis=0), [done] * n_high)
        pieces.append((landed, None, units - 1))

    rests = []
    for came in widened:
        came = after(came, *crossed)
        rests += [came, swap(came, sizes, 0, 1, 0)]
    turn = (row // CORES) ^ high
    wide = widen_left(sets, halves, rests, core, turn, own_rows)

    panel, columns = None, own_rows * n_groups

    def fill(pair, first, shifts):
        nonlocal panel
        count = pair[0].shape[0] // unit // len(shifts)
        places = [(group ^ dk) * units + first + at for dk in shifts for at in range(count)]
        panel = place_panel(wide, pair, unit, places, columns, panel)

    for pair, sent, first in pieces:
        if sent is not None:
            fill(pair, first, [0])
    for pair, sent, first in pieces[:1]:
        for dk in range(1, n_groups):
            fill(sent[dk - 1], first, [dk])
    for pair, sent, first in pieces[LAST:] + pieces[1:LAST]:
        if sent is None:
            fill(pair, first, list(range(n_groups)))
        else:
            for dk in range(1, n_groups):
                fill(sent[dk - 1], first, [dk])
    return panel


def solution(mesh):
    sizes = tuple(mesh.shape[axis] for axis in AXES)
    in_specs = (
        P(("prow", "pcol"), "pl"),
        P(None, ("prow", "pcol")),
        P(("prow", "pl"), None),
        P(),
        P(),
    )
    out_specs = P(("prow", "pl"), "pcol")
    return jax.shard_map(
        functools.partial(body, sizes), mesh=mesh, in_specs=in_specs, out_specs=out_specs, check_vma=False
    )
```

time: 488 us -> 135 us (0.28)
  waiting for transfers between devices: 427 us -> 46.8 us
  starting transfers between devices: 0.4 us -> 40 us
  Pallas kernels: 0 us -> 29.1 us
  matrix products: 35 us -> 6.87 us
  between operations: 15.1 us -> 0.31 us
  local copies, waits for them, and re-layouts: 1.85 us -> 7.36 us
    all_gather x3 -> x0, waiting for transfers between devices: 270 us -> none  [the longest x1 105 us: body(): lax.all_gather(panel_piece, 'pl', axis=0, tiled=True)]
    psum x2 -> x0, waiting for transfers between devices: 94.8 us -> none  [the longest x1 65.5 us: from_root(): return lax.psum(jnp.where(mine, array, jnp.zeros_like(array)), axis)]
    reduce_scatter x1 -> x0, waiting for transfers between devices: 62.5 us -> none  [body(): lax.psum_scatter(jnp.dot(modal_at_loads, factor_cols, preferred_element_t...]
    ppermute x0 -> x29, waiting for transfers between devices: none -> 46.8 us  [the longest x23 37.8 us: swap(): lax.ppermute(array, AXES, moves(sizes, lambda i, j, k: (i ^ di, j ^ dj, k...]
    ppermute x0 -> x29, starting transfers between devices: none -> 40 us  [the longest x23 29.3 us: swap(): lax.ppermute(array, AXES, moves(sizes, lambda i, j, k: (i ^ di, j ^ dj, k...]
    pallas_call x0 -> x17, Pallas kernels: none -> 29.1 us  [the longest x5 15.7 us: place_panel(): pl.pallas_call(functools.partial(panel_kernel, chunk, len(pieces)), grid_...]
    dot_general x3 -> x2, matrix products: 35 us -> 6.87 us  [the longest x1 3.43 us: body(): jnp.dot(here, factor_cols, preferred_element_type=jnp.float32)]
  transfers between devices with their start and end apart: 6 -> 29, of which waited for: 6 -> 15; matrix products, arithmetic and copies ran while one was open for 1% -> 4% of each run, Pallas kernels for 0% -> 15%
where the time goes in v4:
time: 135 us; the launch traced here: 133 us
  waiting for transfers between devices  46.8 us (35%)
  starting transfers between devices  40 us (30%)
  Pallas kernels  29.1 us (22%)
  local copies, waits for them, and re-layouts  7.36 us (5%)
  matrix products  6.87 us (5%)
  other arithmetic  3 us (2%)
    ppermute x23, waiting for transfers between devices, swap(): lax.ppermute(array, AXES, moves(sizes, lambda i, j, k: (i ^ di, j ^ dj, k...  37.8 us
    ppermute x23, starting transfers between devices, swap(): lax.ppermute(array, AXES, moves(sizes, lambda i, j, k: (i ^ di, j ^ dj, k...  29.3 us
    pallas_call x5, Pallas kernels, place_panel(): pl.pallas_call(functools.partial(panel_kernel, chunk, len(pieces)), grid_...  15.7 us
    ppermute x6, starting transfers between devices, across(): lax.ppermute(array, AXES, moves(sizes, lambda i, j, k: (j, i ^ flip, k)))  10.7 us
    pallas_call x3, Pallas kernels, project(): pl.pallas_call(project_kernel, grid_spec=pltpu.PrefetchScalarGridSpec(num...  10.7 us
    ppermute x6, waiting for transfers between devices, across(): lax.ppermute(array, AXES, moves(sizes, lambda i, j, k: (j, i ^ flip, k)))  9.03 us
    unnamed x38, local copies, waits for them, and re-layouts  6.63 us
    dot_general x1, matrix products, body(): jnp.dot(here, factor_cols, preferred_element_type=jnp.float32)  3.43 us
  transfers between devices with their start and end apart: 29, of which 15 were waited for; matrix products, arithmetic and copies ran while one was open for 4% of the time, Pallas kernels for 15%

profile of v4, /device:TPU:4, one launch (start us, length us, event | category | flops | bytes accessed | tf_op | source)
XLA Modules:
  0.0 133.4 jit_solution(12131569642269124696)
XLA Ops:
  0.0 1.2 copy-done
  1.2 3.4 %fusion.4 = bf16[1024,256]{1,0:T(8,128)(2,1)S(1)} fusion(bf16[2048,256]{1,0:T(8,128)(2,1)S(1)} %copy-done, bf16[2048,2048]{1,0:T(8,128)(2,1)} %param.6, s32[]{:T(128)S(6)} %select_n.60), kind=kOutput, calls=%fused_computation.4 | convolution fusion | flops 1074003968 | bytes 5767172 | tf_op jit(solution)/shard_map/dot_general | solution.py:203
  4.8 1.8 %collective-permute-done = bf16[1024,256]{1,0:T(8,128)(2,1)S(1)} collective-permute-done((bf16[1024,256]{1,0:T(8,128)(2,1)S(1)}, bf16[1024,256]{1,0:T(8,128)(2,1)S(1)}, u32[]{:S(2)}, u32[]{:S(2)}) %collective-permute-start) | collective-permute-done | bytes 524320 | tf_op jit(solution)/shard_map/ppermute | solution.py:37
  6.7 3.4 %add_convert_fusion = bf16[1024,256]{1,0:T(8,128)(2,1)S(1)} fusion(bf16[1024,256]{1,0:T(8,128)(2,1)S(1)} %collective-permute-done, bf16[2048,256]{1,0:T(8,128)(2,1)S(1)} %copy-done, bf16[2048,2048]{1,0:T(8,128)(2,1)} %param.6, s32[]{:T(128)S(6)} %select_n.59), kind=kOutput, calls=%fused_computation.5 | convolution fusion | flops 1074528256 | bytes 6291460 | tf_op jit(solution)/shard_map/dot_general | solution.py:205
  10.1 0.1 fusion.12
  10.2 1.6 %collective-permute-start.1 = (bf16[256,128]{1,0:T(8,128)(2,1)S(1)}, bf16[256,128]{1,0:T(8,128)(2,1)S(1)}, u32[]{:S(2)}, u32[]{:S(2)}) collective-permute-start(bf16[256,128]{1,0:T(8,128)(2,1)S(1)} %get-tuple-element.7), channel_id=1, source_target_pairs={{8,0},{9,1},{10,2},{11,3},{12,4},{13,5},{14,6},{15,7},{0,8},{1,9},... | collective-permute-start | bytes 196616 | tf_op jit(solution)/shard_map/ppermute | solution.py:37
  11.9 2.6 %collective-permute-start.2 = (bf16[256,128]{1,0:T(8,128)(2,1)S(1)}, bf16[256,128]{1,0:T(8,128)(2,1)S(1)}, u32[]{:S(2)}, u32[]{:S(2)}) collective-permute-start(bf16[256,128]{1,0:T(8,128)(2,1)S(1)} %get-tuple-element.13), channel_id=1, source_target_pairs={{16,0},{17,1},{18,2},{19,3},{20,4},{21,5},{22,6},{23,7},{24,8},{25... | collective-permute-start | bytes 196616 | tf_op jit(solution)/shard_map/ppermute | solution.py:37
  14.4 0.2 collective-permute-start.3
  14.7 0.3 collective-permute-start.4
  15.0 1.9 %collective-permute-start.5 = (bf16[256,128]{1,0:T(8,128)(2,1)S(1)}, bf16[256,128]{1,0:T(8,128)(2,1)S(1)}, u32[]{:S(2)}, u32[]{:S(2)}) collective-permute-start(bf16[256,128]{1,0:T(8,128)(2,1)S(1)} %get-tuple-element.10), channel_id=1, source_target_pairs={{12,0},{13,1},{14,2},{15,3},{8,4},{9,5},{10,6},{11,7},{4,8},{5,9},... | collective-permute-start | bytes 196616 | tf_op jit(solution)/shard_map/ppermute | solution.py:37
  16.8 3.4 %collective-permute-start.6 = (bf16[256,128]{1,0:T(8,128)(2,1)S(1)}, bf16[256,128]{1,0:T(8,128)(2,1)S(1)}, u32[]{:S(2)}, u32[]{:S(2)}) collective-permute-start(bf16[256,128]{1,0:T(8,128)(2,1)S(1)} %get-tuple-element.9), channel_id=1, source_target_pairs={{20,0},{21,1},{22,2},{23,3},{16,4},{17,5},{18,6},{19,7},{28,8},{29... | collective-permute-start | bytes 196616 | tf_op jit(solution)/shard_map/ppermute | solution.py:37
  20.2 2.3 %collective-permute-start.7 = (bf16[256,128]{1,0:T(8,128)(2,1)S(1)}, bf16[256,128]{1,0:T(8,128)(2,1)S(1)}, u32[]{:S(2)}, u32[]{:S(2)}) collective-permute-start(bf16[256,128]{1,0:T(8,128)(2,1)S(1)} %get-tuple-element.8), channel_id=1, source_target_pairs={{28,0},{29,1},{30,2},{31,3},{24,4},{25,5},{26,6},{27,7},{20,8},{21... | collective-permute-start | bytes 196616 | tf_op jit(solution)/shard_map/ppermute | solution.py:37
  22.6 2.4 %collective-permute-done.6 = bf16[256,128]{1,0:T(8,128)(2,1)S(1)} collective-permute-done((bf16[256,128]{1,0:T(8,128)(2,1)S(1)}, bf16[256,128]{1,0:T(8,128)(2,1)S(1)}, u32[]{:S(2)}, u32[]{:S(2)}) %collective-permute-start.6) | collective-permute-done | bytes 65568 | tf_op jit(solution)/shard_map/ppermute | solution.py:37
  25.0 2.2 %collective-permute-done.7 = bf16[256,128]{1,0:T(8,128)(2,1)S(1)} collective-permute-done((bf16[256,128]{1,0:T(8,128)(2,1)S(1)}, bf16[256,128]{1,0:T(8,128)(2,1)S(1)}, u32[]{:S(2)}, u32[]{:S(2)}) %collective-permute-start.7) | collective-permute-done | bytes 65568 | tf_op jit(solution)/shard_map/ppermute | solution.py:37
  27.2 0.1 add_convert_fusion.1.refs_0_
  27.3 2.7 %collective-permute-start.10 = (bf16[256,128]{1,0:T(8,128)(2,1)S(1)}, bf16[256,128]{1,0:T(8,128)(2,1)S(1)}, u32[]{:S(2)}, u32[]{:S(2)}) collective-permute-start(bf16[256,128]{1,0:T(8,128)(2,1)S(1)} %add_convert_fusion.1.refs_0_), channel_id=1, source_target_pairs={{24,0},{25,1},{26,2},{27,3},{28,4},{29,5},{30,6},{31,7},{16,8},{17... | collective-permute-start | bytes 196616 | tf_op jit(solution)/shard_map/ppermute | solution.py:37
  30.0 1.5 %collective-permute-start.11 = (bf16[256,128]{1,0:T(8,128)(2,1)S(1)}, bf16[256,128]{1,0:T(8,128)(2,1)S(1)}, u32[]{:S(2)}, u32[]{:S(2)}) collective-permute-start(bf16[256,128]{1,0:T(8,128)(2,1)S(1)} %add_convert_fusion.1.refs_0_), channel_id=1, source_target_pairs={{1,0},{0,1},{3,2},{2,3},{5,4},{4,5},{7,6},{6,7},{9,8},{8,9},{11,10... | collective-permute-start | bytes 196616 | tf_op jit(solution)/shard_map/ppermute | solution.py:37
  31.5 2.7 %collective-permute-start.13 = (bf16[256,128]{1,0:T(8,128)(2,1)S(1)}, bf16[256,128]{1,0:T(8,128)(2,1)S(1)}, u32[]{:S(2)}, u32[]{:S(2)}) collective-permute-start(bf16[256,128]{1,0:T(8,128)(2,1)S(1)} %add_convert_fusion.1.refs_0_), channel_id=1, source_target_pairs={{17,0},{16,1},{19,2},{18,3},{21,4},{20,5},{23,6},{22,7},{25,8},{24... | collective-permute-start | bytes 196616 | tf_op jit(solution)/shard_map/ppermute | solution.py:37
  34.1 2.6 %collective-permute-start.14 = (bf16[256,128]{1,0:T(8,128)(2,1)S(1)}, bf16[256,128]{1,0:T(8,128)(2,1)S(1)}, u32[]{:S(2)}, u32[]{:S(2)}) collective-permute-start(bf16[256,128]{1,0:T(8,128)(2,1)S(1)} %add_convert_fusion.1.refs_0_), channel_id=1, source_target_pairs={{25,0},{24,1},{27,2},{26,3},{29,4},{28,5},{31,6},{30,7},{17,8},{16... | collective-permute-start | bytes 196616 | tf_op jit(solution)/shard_map/ppermute | solution.py:37
  36.7 1.8 %collective-permute-start.9 = (bf16[256,128]{1,0:T(8,128)(2,1)S(1)}, bf16[256,128]{1,0:T(8,128)(2,1)S(1)}, u32[]{:S(2)}, u32[]{:S(2)}) collective-permute-start(bf16[256,128]{1,0:T(8,128)(2,1)S(1)} %add_convert_fusion.1.refs_0_), channel_id=1, source_target_pairs={{16,0},{17,1},{18,2},{19,3},{20,4},{21,5},{22,6},{23,7},{24,8},{25... | collective-permute-start | bytes 196616 | tf_op jit(solution)/shard_map/ppermute | solution.py:37
  38.5 0.1 pad_add_fusion.2.spots
  38.6 0.5 collective-permute-done.13.refs_6_
  39.1 2.0 %collective-permute-done.14.refs_7_ = bf16[256,128]{1,0:T(8,128)(2,1)S(1)} collective-permute-done((bf16[256,128]{1,0:T(8,128)(2,1)S(1)}, bf16[256,128]{1,0:T(8,128)(2,1)S(1)}, u32[]{:S(2)}, u32[]{:S(2)}) %collective-permute-start.14) | collective-permute-done | bytes 65568 | tf_op jit(solution)/shard_map/ppermute | solution.py:37
  41.1 0.9 collective-permute-done.9.refs_2_
  42.0 1.4 %shard_map.55.mine = bf16[1024,256]{1,0:T(8,128)(2,1)} custom-call(s32[2]{0:T(128)S(1)} %pad_add_fusion.2.spots, bf16[256,128]{1,0:T(8,128)(2,1)S(1)} %add_convert_fusion.1.refs_0_, bf16[256,128]{1,0:T(8,128)(2,1)S(1)} %collective-permute-done.8.refs_1_, bf16[256,128]{1,0:T(8,128)(2,1)S(1)} %collective-permute-done.9.refs_2_, ...), custom_call_target="tpu_custom_call" | custom-call | flops 1 | bytes 1 | tf_op jit(solution)/shard_map/pallas_call | solution.py:80
  43.5 0.6 copy.17.scale
  44.1 1.6 %collective-permute-done.15.theirs = bf16[1024,256]{1,0:T(8,128)(2,1)} collective-permute-done((bf16[1024,256]{1,0:T(8,128)(2,1)}, bf16[1024,256]{1,0:T(8,128)(2,1)}, u32[]{:S(2)}, u32[]{:S(2)}) %collective-permute-start.15) | collective-permute-done | bytes 524320 | tf_op jit(solution)/shard_map/ppermute | solution.py:37
  45.7 3.6 %shard_map.56 = bf16[256,512]{1,0:T(8,128)(2,1)} custom-call(s32[1]{0:T(128)} %bitcast.2.spots, bf16[1024,256]{1,0:T(8,128)(2,1)} %shard_map.55.mine, bf16[1024,256]{1,0:T(8,128)(2,1)} %collective-permute-done.15.theirs, f32[2,2048,1]{2,1,0:T(8,128)S(1)} %copy.17.scale, bf16[1024,2048]{1,0:T(8,128)(2,1)} %shapes.5), custom_call_target="tpu_custom_call" | custom-call | flops 1 | bytes 1 | tf_op jit(solution)/shard_map/pallas_call | solution.py:114
  49.2 0.8 collective-permute-start.17
  50.1 4.2 %collective-permute-start.16 = (bf16[256,512]{1,0:T(8,128)(2,1)}, bf16[256,512]{1,0:T(8,128)(2,1)}, u32[]{:S(2)}, u32[]{:S(2)}) collective-permute-start(bf16[256,512]{1,0:T(8,128)(2,1)} %shard_map.56), channel_id=1, source_target_pairs={{0,0},{1,1},{8,2},{9,3},{16,4},{17,5},{24,6},{25,7},{2,8},{3,9},{1... | collective-permute-start | bytes 786440 | tf_op jit(solution)/shard_map/ppermute | solution.py:41
  54.3 3.6 %shard_map.57 = bf16[256,512]{1,0:T(8,128)(2,1)} custom-call(s32[1]{0:T(128)} %bitcast.2.spots, bf16[1024,256]{1,0:T(8,128)(2,1)} %shard_map.55.mine, bf16[1024,256]{1,0:T(8,128)(2,1)} %collective-permute-done.15.theirs, f32[2,2048,1]{2,1,0:T(8,128)S(1)} %copy.17.scale, bf16[1024,2048]{1,0:T(8,128)(2,1)} %shapes.5), custom_call_target="tpu_custom_call" | custom-call | flops 1 | bytes 1 | tf_op jit(solution)/shard_map/pallas_call | solution.py:114
  57.9 1.5 %collective-permute-start.22 = (bf16[256,512]{1,0:T(8,128)(2,1)}, bf16[256,512]{1,0:T(8,128)(2,1)}, u32[]{:S(2)}, u32[]{:S(2)}) collective-permute-start(bf16[256,512]{1,0:T(8,128)(2,1)} %shard_map.57), channel_id=1, source_target_pairs={{1,0},{0,1},{3,2},{2,3},{5,4},{4,5},{7,6},{6,7},{9,8},{8,9},{11,10... | collective-permute-start | bytes 786440 | tf_op jit(solution)/shard_map/ppermute | solution.py:37
  59.4 3.6 %shard_map.58.refs_1_ = bf16[512,512]{1,0:T(8,128)(2,1)S(1)} custom-call(s32[1]{0:T(128)} %bitcast.2.spots, bf16[1024,256]{1,0:T(8,128)(2,1)} %shard_map.55.mine, bf16[1024,256]{1,0:T(8,128)(2,1)} %collective-permute-done.15.theirs, f32[2,2048,1]{2,1,0:T(8,128)S(1)} %copy.17.scale, bf16[1024,2048]{1,0:T(8,128)(2,1)} %shapes.5), custom_call_target="tpu_custom_call" | custom-call | flops 1 | bytes 1 | tf_op jit(solution)/shard_map/pallas_call | solution.py:114
  63.0 0.8 copy.22.refs_0_
  63.8 0.1 copy-done.1
  63.9 0.8 copy.21.refs_0_
  64.7 0.3 collective-permute-done.17.refs_2_.refs_1_
  65.1 0.7 copy-done.13
  65.8 1.4 %collective-permute-start.20 = (bf16[512,512]{1,0:T(8,128)(2,1)}, bf16[512,512]{1,0:T(8,128)(2,1)S(1)}, u32[]{:S(2)}, u32[]{:S(2)}) collective-permute-start(bf16[512,512]{1,0:T(8,128)(2,1)} %shard_map.61), channel_id=1, source_target_pairs={{4,0},{5,1},{12,2},{13,3},{20,4},{21,5},{28,6},{29,7},{6,8},{7,9},... | collective-permute-start | bytes 1572872 | tf_op jit(solution)/shard_map/ppermute | solution.py:41
  67.2 0.8 collective-permute-done.16.refs_1_.refs_0_
  68.0 2.2 %collective-permute-start.19 = (bf16[512,512]{1,0:T(8,128)(2,1)}, bf16[512,512]{1,0:T(8,128)(2,1)S(1)}, u32[]{:S(2)}, u32[]{:S(2)}) collective-permute-start(bf16[512,512]{1,0:T(8,128)(2,1)} %shard_map.60), channel_id=1, source_target_pairs={{0,0},{1,1},{8,2},{9,3},{16,4},{17,5},{24,6},{25,7},{2,8},{3,9},{1... | collective-permute-start | bytes 1572872 | tf_op jit(solution)/shard_map/ppermute | solution.py:41
  70.3 2.5 %broadcast_select_fusion = (bf16[512,512]{1,0:T(8,128)(2,1)}, bf16[512,512]{1,0:T(8,128)(2,1)}, bf16[512,512]{1,0:T(8,128)(2,1)}) fusion(bf16[512,512]{1,0:T(8,128)(2,1)} %copy-done.1, pred[]{:T(512)S(6)} %eq.5, bf16[256,512]{1,0:T(8,128)(2,1)} %shard_map.57, bf16[256,512]{1,0:T(8,128)(2,1)} %shard_map.56, bf16[256,512]{1,0:T(8,128)(2,1)} %collective-permute-done.22), kind=kLoop, calls=%fused_computation.8 | loop fusion | flops 2359296 | bytes 2883585 | tf_op jit(solution)/shard_map/jit(_where)/select_n | solution.py:257
  72.8 1.2 collective-permute-start.23
  74.0 0.9 collective-permute-start.24
  74.8 7.4 %collective-permute-done.23.refs_2_.refs_1_.refs_0_ = bf16[256,512]{1,0:T(8,128)(2,1)S(1)} collective-permute-done((bf16[256,512]{1,0:T(8,128)(2,1)}, bf16[256,512]{1,0:T(8,128)(2,1)S(1)}, u32[]{:S(2)}, u32[]{:S(2)}) %collective-permute-start.23) | collective-permute-done | bytes 262176 | tf_op jit(solution)/shard_map/ppermute | solution.py:37
  82.2 5.4 %collective-permute-done.24.refs_3_.refs_1_ = bf16[256,512]{1,0:T(8,128)(2,1)S(1)} collective-permute-done((bf16[256,512]{1,0:T(8,128)(2,1)}, bf16[256,512]{1,0:T(8,128)(2,1)S(1)}, u32[]{:S(2)}, u32[]{:S(2)}) %collective-permute-start.24) | collective-permute-done | bytes 262176 | tf_op jit(solution)/shard_map/ppermute | solution.py:37
  87.6 3.8 %collective-permute-done.20.refs_2_.refs_5_.refs_0_ = bf16[512,512]{1,0:T(8,128)(2,1)S(1)} collective-permute-done((bf16[512,512]{1,0:T(8,128)(2,1)}, bf16[512,512]{1,0:T(8,128)(2,1)S(1)}, u32[]{:S(2)}, u32[]{:S(2)}) %collective-permute-start.20) | collective-permute-done | bytes 524320 | tf_op jit(solution)/shard_map/ppermute | solution.py:41
  91.4 4.1 %collective-permute-done.19.refs_1_.refs_4_.refs_0_ = bf16[512,512]{1,0:T(8,128)(2,1)S(1)} collective-permute-done((bf16[512,512]{1,0:T(8,128)(2,1)}, bf16[512,512]{1,0:T(8,128)(2,1)S(1)}, u32[]{:S(2)}, u32[]{:S(2)}) %collective-permute-start.19) | collective-permute-done | bytes 524320 | tf_op jit(solution)/shard_map/ppermute | solution.py:41
  95.4 3.0 %collective-permute-done.18.refs_0_.refs_1_ = bf16[512,512]{1,0:T(8,128)(2,1)S(1)} collective-permute-done((bf16[512,512]{1,0:T(8,128)(2,1)}, bf16[512,512]{1,0:T(8,128)(2,1)S(1)}, u32[]{:S(2)}, u32[]{:S(2)}) %collective-permute-start.18) | collective-permute-done | bytes 524320 | tf_op jit(solution)/shard_map/ppermute | solution.py:37
  98.4 0.8 copy-done.7
  99.2 0.7 collective-permute-start.28
  100.0 1.4 %collective-permute-start.27 = (bf16[512,512]{1,0:T(8,128)(2,1)}, bf16[512,512]{1,0:T(8,128)(2,1)}, u32[]{:S(2)}, u32[]{:S(2)}) collective-permute-start(bf16[512,512]{1,0:T(8,128)(2,1)} %shard_map.65.refs_0_), channel_id=1, source_target_pairs={{1,0},{0,1},{3,2},{2,3},{5,4},{4,5},{7,6},{6,7},{9,8},{8,9},{11,10... | collective-permute-start | bytes 1572872 | tf_op jit(solution)/shard_map/ppermute | solution.py:37
  101.3 2.0 %collective-permute-start.25 = (bf16[512,512]{1,0:T(8,128)(2,1)}, bf16[512,512]{1,0:T(8,128)(2,1)S(1)}, u32[]{:S(2)}, u32[]{:S(2)}) collective-permute-start(bf16[512,512]{1,0:T(8,128)(2,1)} %shard_map.64), channel_id=1, source_target_pairs={{0,0},{1,1},{8,2},{9,3},{16,4},{17,5},{24,6},{25,7},{2,8},{3,9},{1... | collective-permute-start | bytes 1572872 | tf_op jit(solution)/shard_map/ppermute | solution.py:41
  103.4 0.1 pad_add_fusion.1.spots
  103.5 0.1 pad_add_fusion.4.spots
  103.6 1.0 copy-done.8
  104.7 1.0 copy-done.15
  105.7 1.2 shard_map.63.left
  107.0 2.7 %shard_map.67.refs_2_ = f32[1024,2048]{1,0:T(8,128)} custom-call(s32[1]{0:T(128)} %bitcast.14.spots, bf16[1024,1024]{1,0:T(8,128)(2,1)S(1)} %shard_map.63.left, bf16[256,512]{1,0:T(8,128)(2,1)} %collective-permute-done.16.refs_1_.refs_0_, bf16[256,512]{1,0:T(8,128)(2,1)S(1)} %copy-done.14), custom_call_target="tpu_custom_call" | custom-call | flops 1 | bytes 1 | tf_op jit(solution)/shard_map/pallas_call | solution.py:175
  109.7 3.0 %shard_map.68.refs_2_ = f32[1024,2048]{1,0:T(8,128)} custom-call(s32[2]{0:T(128)S(1)} %pad_add_fusion.4.spots, bf16[1024,1024]{1,0:T(8,128)(2,1)S(1)} %shard_map.63.left, bf16[512,512]{1,0:T(8,128)(2,1)S(1)} %copy-done.6, bf16[512,512]{1,0:T(8,128)(2,1)S(1)} %copy-done.4, f32[1024,2048]{1,0:T(8,128)} %shard_map.67.refs_2_), custom_call_target="tpu_custom_call", output_to_operand_aliasing={{}: (4, {})} | custom-call | flops 1 | bytes 1 | tf_op jit(solution)/shard_map/pallas_call | solution.py:175
  112.8 1.7 %shard_map.69.refs_2_ = f32[1024,2048]{1,0:T(8,128)} custom-call(s32[1]{0:T(128)} %bitcast.11.spots, bf16[1024,1024]{1,0:T(8,128)(2,1)S(1)} %shard_map.63.left, bf16[256,512]{1,0:T(8,128)(2,1)S(1)} %copy-done.10, bf16[256,512]{1,0:T(8,128)(2,1)S(1)} %copy-done.12, f32[1024,2048]{1,0:T(8,128)} %shard_map.68.refs_2_), custom_call_target="tpu_custom_call", output_to_operand_aliasing={{}: (4, {})} | custom-call | flops 1 | bytes 1 | tf_op jit(solution)/shard_map/pallas_call | solution.py:175
  114.5 10.7 %collective-permute-done.27.refs_0_ = bf16[512,512]{1,0:T(8,128)(2,1)} collective-permute-done((bf16[512,512]{1,0:T(8,128)(2,1)}, bf16[512,512]{1,0:T(8,128)(2,1)}, u32[]{:S(2)}, u32[]{:S(2)}) %collective-permute-start.27) | collective-permute-done | bytes 524320 | tf_op jit(solution)/shard_map/ppermute | solution.py:37
  125.1 4.2 %shard_map.70.refs_2_ = f32[1024,2048]{1,0:T(8,128)} custom-call(s32[2]{0:T(128)S(1)} %pad_add_fusion.3.spots, bf16[1024,1024]{1,0:T(8,128)(2,1)S(1)} %shard_map.63.left, bf16[512,512]{1,0:T(8,128)(2,1)} %collective-permute-done.27.refs_0_, bf16[512,512]{1,0:T(8,128)(2,1)} %collective-permute-done.28.refs_1_, ...), custom_call_target="tpu_custom_call", output_to_operand_aliasing={{}: (4, {})} | custom-call | flops 1 | bytes 1 | tf_op jit(solution)/shard_map/pallas_call | solution.py:175
  129.4 4.1 %shard_map.71 = f32[1024,2048]{1,0:T(8,128)} custom-call(s32[2]{0:T(128)S(1)} %pad_add_fusion.spots, bf16[1024,1024]{1,0:T(8,128)(2,1)S(1)} %shard_map.63.left, bf16[512,512]{1,0:T(8,128)(2,1)S(1)} %collective-permute-done.25.refs_0_, bf16[512,512]{1,0:T(8,128)(2,1)} %collective-permute-done.26.refs_1_, ...), custom_call_target="tpu_custom_call", output_to_operand_aliasing={{}: (4, {})} | custom-call | flops 1 | bytes 1 | tf_op jit(solution)/shard_map/pallas_call | solution.py:175
  (62 shorter events, 0.4 us)
Async XLA Ops:
  0.0 1.2 copy-start
  4.7 38.8 %copy-start.16 = (f32[2048]{0:T(1024)S(1)}, f32[2048]{0:T(1024)}, u32[]{:S(2)}) copy-start(f32[2048]{0:T(1024)} %param.8) | copy-start | bytes 24580
  4.7 38.7 %copy-start.17 = (f32[2048]{0:T(1024)S(1)}, f32[2048]{0:T(1024)}, u32[]{:S(2)}) copy-start(f32[2048]{0:T(1024)} %param.9) | copy-start | bytes 24580
  4.7 2.0 %collective-permute-start = (bf16[1024,256]{1,0:T(8,128)(2,1)S(1)}, bf16[1024,256]{1,0:T(8,128)(2,1)S(1)}, u32[]{:S(2)}, u32[]{:S(2)}) collective-permute-start(bf16[1024,256]{1,0:T(8,128)(2,1)S(1)} %fusion.4), channel_id=1, source_target_pairs={{2,0},{3,1},{0,2},{1,3},{6,4},{7,5},{4,6},{5,7},{10,8},{11,9},{8,1... | collective-permute-start | bytes 1572872 | tf_op jit(solution)/shard_map/ppermute | solution.py:37
  10.2 6.6 %collective-permute-start.1 = (bf16[256,128]{1,0:T(8,128)(2,1)S(1)}, bf16[256,128]{1,0:T(8,128)(2,1)S(1)}, u32[]{:S(2)}, u32[]{:S(2)}) collective-permute-start(bf16[256,128]{1,0:T(8,128)(2,1)S(1)} %get-tuple-element.7), channel_id=1, source_target_pairs={{8,0},{9,1},{10,2},{11,3},{12,4},{13,5},{14,6},{15,7},{0,8},{1,9},... | collective-permute-start | bytes 196616 | tf_op jit(solution)/shard_map/ppermute | solution.py:37
  11.9 8.4 %collective-permute-start.2 = (bf16[256,128]{1,0:T(8,128)(2,1)S(1)}, bf16[256,128]{1,0:T(8,128)(2,1)S(1)}, u32[]{:S(2)}, u32[]{:S(2)}) collective-permute-start(bf16[256,128]{1,0:T(8,128)(2,1)S(1)} %get-tuple-element.13), channel_id=1, source_target_pairs={{16,0},{17,1},{18,2},{19,3},{20,4},{21,5},{22,6},{23,7},{24,8},{25... | collective-permute-start | bytes 196616 | tf_op jit(solution)/shard_map/ppermute | solution.py:37
  14.4 8.2 %collective-permute-start.3 = (bf16[256,128]{1,0:T(8,128)(2,1)S(1)}, bf16[256,128]{1,0:T(8,128)(2,1)S(1)}, u32[]{:S(2)}, u32[]{:S(2)}) collective-permute-start(bf16[256,128]{1,0:T(8,128)(2,1)S(1)} %get-tuple-element.12), channel_id=1, source_target_pairs={{24,0},{25,1},{26,2},{27,3},{28,4},{29,5},{30,6},{31,7},{16,8},{17... | collective-permute-start | bytes 196616 | tf_op jit(solution)/shard_map/ppermute | solution.py:37
  14.7 7.9 %collective-permute-start.4 = (bf16[256,128]{1,0:T(8,128)(2,1)S(1)}, bf16[256,128]{1,0:T(8,128)(2,1)S(1)}, u32[]{:S(2)}, u32[]{:S(2)}) collective-permute-start(bf16[256,128]{1,0:T(8,128)(2,1)S(1)} %get-tuple-element.11), channel_id=1, source_target_pairs={{4,0},{5,1},{6,2},{7,3},{0,4},{1,5},{2,6},{3,7},{12,8},{13,9},{14,... | collective-permute-start | bytes 196616 | tf_op jit(solution)/shard_map/ppermute | solution.py:37
  15.0 7.6 %collective-permute-start.5 = (bf16[256,128]{1,0:T(8,128)(2,1)S(1)}, bf16[256,128]{1,0:T(8,128)(2,1)S(1)}, u32[]{:S(2)}, u32[]{:S(2)}) collective-permute-start(bf16[256,128]{1,0:T(8,128)(2,1)S(1)} %get-tuple-element.10), channel_id=1, source_target_pairs={{12,0},{13,1},{14,2},{15,3},{8,4},{9,5},{10,6},{11,7},{4,8},{5,9},... | collective-permute-start | bytes 196616 | tf_op jit(solution)/shard_map/ppermute | solution.py:37
  16.8 8.2 %collective-permute-start.6 = (bf16[256,128]{1,0:T(8,128)(2,1)S(1)}, bf16[256,128]{1,0:T(8,128)(2,1)S(1)}, u32[]{:S(2)}, u32[]{:S(2)}) collective-permute-start(bf16[256,128]{1,0:T(8,128)(2,1)S(1)} %get-tuple-element.9), channel_id=1, source_target_pairs={{20,0},{21,1},{22,2},{23,3},{16,4},{17,5},{18,6},{19,7},{28,8},{29... | collective-permute-start | bytes 196616 | tf_op jit(solution)/shard_map/ppermute | solution.py:37
  20.2 7.0 %collective-permute-start.7 = (bf16[256,128]{1,0:T(8,128)(2,1)S(1)}, bf16[256,128]{1,0:T(8,128)(2,1)S(1)}, u32[]{:S(2)}, u32[]{:S(2)}) collective-permute-start(bf16[256,128]{1,0:T(8,128)(2,1)S(1)} %get-tuple-element.8), channel_id=1, source_target_pairs={{28,0},{29,1},{30,2},{31,3},{24,4},{25,5},{26,6},{27,7},{20,8},{21... | collective-permute-start | bytes 196616 | tf_op jit(solution)/shard_map/ppermute | solution.py:37
  27.3 9.4 %collective-permute-start.10 = (bf16[256,128]{1,0:T(8,128)(2,1)S(1)}, bf16[256,128]{1,0:T(8,128)(2,1)S(1)}, u32[]{:S(2)}, u32[]{:S(2)}) collective-permute-start(bf16[256,128]{1,0:T(8,128)(2,1)S(1)} %add_convert_fusion.1.refs_0_), channel_id=1, source_target_pairs={{24,0},{25,1},{26,2},{27,3},{28,4},{29,5},{30,6},{31,7},{16,8},{17... | collective-permute-start | bytes 196616 | tf_op jit(solution)/shard_map/ppermute | solution.py:37
  30.0 6.8 %collective-permute-start.11 = (bf16[256,128]{1,0:T(8,128)(2,1)S(1)}, bf16[256,128]{1,0:T(8,128)(2,1)S(1)}, u32[]{:S(2)}, u32[]{:S(2)}) collective-permute-start(bf16[256,128]{1,0:T(8,128)(2,1)S(1)} %add_convert_fusion.1.refs_0_), channel_id=1, source_target_pairs={{1,0},{0,1},{3,2},{2,3},{5,4},{4,5},{7,6},{6,7},{9,8},{8,9},{11,10... | collective-permute-start | bytes 196616 | tf_op jit(solution)/shard_map/ppermute | solution.py:37
  31.5 7.1 %collective-permute-start.12 = (bf16[256,128]{1,0:T(8,128)(2,1)S(1)}, bf16[256,128]{1,0:T(8,128)(2,1)S(1)}, u32[]{:S(2)}, u32[]{:S(2)}) collective-permute-start(bf16[256,128]{1,0:T(8,128)(2,1)S(1)} %add_convert_fusion.1.refs_0_), channel_id=1, source_target_pairs={{9,0},{8,1},{11,2},{10,3},{13,4},{12,5},{15,6},{14,7},{1,8},{0,9},... | collective-permute-start | bytes 196616 | tf_op jit(solution)/shard_map/ppermute | solution.py:37
  31.5 7.7 %collective-permute-start.13 = (bf16[256,128]{1,0:T(8,128)(2,1)S(1)}, bf16[256,128]{1,0:T(8,128)(2,1)S(1)}, u32[]{:S(2)}, u32[]{:S(2)}) collective-permute-start(bf16[256,128]{1,0:T(8,128)(2,1)S(1)} %add_convert_fusion.1.refs_0_), channel_id=1, source_target_pairs={{17,0},{16,1},{19,2},{18,3},{21,4},{20,5},{23,6},{22,7},{25,8},{24... | collective-permute-start | bytes 196616 | tf_op jit(solution)/shard_map/ppermute | solution.py:37
  34.1 7.0 %collective-permute-start.14 = (bf16[256,128]{1,0:T(8,128)(2,1)S(1)}, bf16[256,128]{1,0:T(8,128)(2,1)S(1)}, u32[]{:S(2)}, u32[]{:S(2)}) collective-permute-start(bf16[256,128]{1,0:T(8,128)(2,1)S(1)} %add_convert_fusion.1.refs_0_), channel_id=1, source_target_pairs={{25,0},{24,1},{27,2},{26,3},{29,4},{28,5},{31,6},{30,7},{17,8},{16... | collective-permute-start | bytes 196616 | tf_op jit(solution)/shard_map/ppermute | solution.py:37
  36.7 4.4 %collective-permute-start.8 = (bf16[256,128]{1,0:T(8,128)(2,1)S(1)}, bf16[256,128]{1,0:T(8,128)(2,1)S(1)}, u32[]{:S(2)}, u32[]{:S(2)}) collective-permute-start(bf16[256,128]{1,0:T(8,128)(2,1)S(1)} %add_convert_fusion.1.refs_0_), channel_id=1, source_target_pairs={{8,0},{9,1},{10,2},{11,3},{12,4},{13,5},{14,6},{15,7},{0,8},{1,9},... | collective-permute-start | bytes 196616 | tf_op jit(solution)/shard_map/ppermute | solution.py:37
  36.7 5.2 %collective-permute-start.9 = (bf16[256,128]{1,0:T(8,128)(2,1)S(1)}, bf16[256,128]{1,0:T(8,128)(2,1)S(1)}, u32[]{:S(2)}, u32[]{:S(2)}) collective-permute-start(bf16[256,128]{1,0:T(8,128)(2,1)S(1)} %add_convert_fusion.1.refs_0_), channel_id=1, source_target_pairs={{16,0},{17,1},{18,2},{19,3},{20,4},{21,5},{22,6},{23,7},{24,8},{25... | collective-permute-start | bytes 196616 | tf_op jit(solution)/shard_map/ppermute | solution.py:37
  43.4 2.3 %collective-permute-start.15 = (bf16[1024,256]{1,0:T(8,128)(2,1)}, bf16[1024,256]{1,0:T(8,128)(2,1)}, u32[]{:S(2)}, u32[]{:S(2)}) collective-permute-start(bf16[1024,256]{1,0:T(8,128)(2,1)} %shard_map.55.mine), channel_id=1, source_target_pairs={{2,0},{3,1},{0,2},{1,3},{6,4},{7,5},{4,6},{5,7},{10,8},{11,9},{8,1... | collective-permute-start | bytes 1572872 | tf_op jit(solution)/shard_map/ppermute | solution.py:37
  49.2 15.8 %collective-permute-start.17 = (bf16[256,512]{1,0:T(8,128)(2,1)}, bf16[256,512]{1,0:T(8,128)(2,1)S(1)}, u32[]{:S(2)}, u32[]{:S(2)}) collective-permute-start(bf16[256,512]{1,0:T(8,128)(2,1)} %shard_map.56), channel_id=1, source_target_pairs={{4,0},{5,1},{12,2},{13,3},{20,4},{21,5},{28,6},{29,7},{6,8},{7,9},... | collective-permute-start | bytes 786440 | tf_op jit(solution)/shard_map/ppermute | solution.py:41
  50.1 18.0 %collective-permute-start.16 = (bf16[256,512]{1,0:T(8,128)(2,1)}, bf16[256,512]{1,0:T(8,128)(2,1)}, u32[]{:S(2)}, u32[]{:S(2)}) collective-permute-start(bf16[256,512]{1,0:T(8,128)(2,1)} %shard_map.56), channel_id=1, source_target_pairs={{0,0},{1,1},{8,2},{9,3},{16,4},{17,5},{24,6},{25,7},{2,8},{3,9},{1... | collective-permute-start | bytes 786440 | tf_op jit(solution)/shard_map/ppermute | solution.py:41
  57.9 12.4 %collective-permute-start.22 = (bf16[256,512]{1,0:T(8,128)(2,1)}, bf16[256,512]{1,0:T(8,128)(2,1)}, u32[]{:S(2)}, u32[]{:S(2)}) collective-permute-start(bf16[256,512]{1,0:T(8,128)(2,1)} %shard_map.57), channel_id=1, source_target_pairs={{1,0},{0,1},{3,2},{2,3},{5,4},{4,5},{7,6},{6,7},{9,8},{8,9},{11,10... | collective-permute-start | bytes 786440 | tf_op jit(solution)/shard_map/ppermute | solution.py:37
  62.9 1.0 copy-start.1
  64.7 38.9 %copy-start.2 = (bf16[512,512]{1,0:T(8,128)(2,1)S(1)}, bf16[512,512]{1,0:T(8,128)(2,1)}, u32[]{:S(2)}) copy-start(bf16[512,512]{1,0:T(8,128)(2,1)} %copy-done.1) | copy-start | bytes 1572868
  65.1 0.7 copy-start.13
  65.8 25.6 %collective-permute-start.20 = (bf16[512,512]{1,0:T(8,128)(2,1)}, bf16[512,512]{1,0:T(8,128)(2,1)S(1)}, u32[]{:S(2)}, u32[]{:S(2)}) collective-permute-start(bf16[512,512]{1,0:T(8,128)(2,1)} %shard_map.61), channel_id=1, source_target_pairs={{4,0},{5,1},{12,2},{13,3},{20,4},{21,5},{28,6},{29,7},{6,8},{7,9},... | collective-permute-start | bytes 1572872 | tf_op jit(solution)/shard_map/ppermute | solution.py:41
  68.0 27.4 %collective-permute-start.19 = (bf16[512,512]{1,0:T(8,128)(2,1)}, bf16[512,512]{1,0:T(8,128)(2,1)S(1)}, u32[]{:S(2)}, u32[]{:S(2)}) collective-permute-start(bf16[512,512]{1,0:T(8,128)(2,1)} %shard_map.60), channel_id=1, source_target_pairs={{0,0},{1,1},{8,2},{9,3},{16,4},{17,5},{24,6},{25,7},{2,8},{3,9},{1... | collective-permute-start | bytes 1572872 | tf_op jit(solution)/shard_map/ppermute | solution.py:41
  72.8 25.6 %collective-permute-start.18 = (bf16[512,512]{1,0:T(8,128)(2,1)}, bf16[512,512]{1,0:T(8,128)(2,1)S(1)}, u32[]{:S(2)}, u32[]{:S(2)}) collective-permute-start(bf16[512,512]{1,0:T(8,128)(2,1)} %shard_map.59), channel_id=1, source_target_pairs={{4,0},{5,1},{6,2},{7,3},{0,4},{1,5},{2,6},{3,7},{12,8},{13,9},{14,... | collective-permute-start | bytes 1572872 | tf_op jit(solution)/shard_map/ppermute | solution.py:37
  72.8 9.4 %collective-permute-start.23 = (bf16[256,512]{1,0:T(8,128)(2,1)}, bf16[256,512]{1,0:T(8,128)(2,1)S(1)}, u32[]{:S(2)}, u32[]{:S(2)}) collective-permute-start(bf16[256,512]{1,0:T(8,128)(2,1)} %collective-permute-done.16.refs_1_.refs_0_), channel_id=1, source_target_pairs={{1,0},{0,1},{3,2},{2,3},{5,4},{4,5},{7,6},{6,7},{9,8},{8,9},{11,10... | collective-permute-start | bytes 786440 | tf_op jit(solution)/shard_map/ppermute | solution.py:37
  74.0 13.6 %collective-permute-start.24 = (bf16[256,512]{1,0:T(8,128)(2,1)}, bf16[256,512]{1,0:T(8,128)(2,1)S(1)}, u32[]{:S(2)}, u32[]{:S(2)}) collective-permute-start(bf16[256,512]{1,0:T(8,128)(2,1)} %copy-done.13), channel_id=1, source_target_pairs={{1,0},{0,1},{3,2},{2,3},{5,4},{4,5},{7,6},{6,7},{9,8},{8,9},{11,10... | collective-permute-start | bytes 786440 | tf_op jit(solution)/shard_map/ppermute | solution.py:37
  82.2 16.2 %copy-start.9 = (bf16[256,512]{1,0:T(8,128)(2,1)}, bf16[256,512]{1,0:T(8,128)(2,1)S(1)}, u32[]{:S(2)}) copy-start(bf16[256,512]{1,0:T(8,128)(2,1)S(1)} %collective-permute-done.23.refs_2_.refs_1_.refs_0_) | copy-start | bytes 786436
  87.6 10.8 %copy-start.11 = (bf16[256,512]{1,0:T(8,128)(2,1)}, bf16[256,512]{1,0:T(8,128)(2,1)S(1)}, u32[]{:S(2)}) copy-start(bf16[256,512]{1,0:T(8,128)(2,1)S(1)} %collective-permute-done.24.refs_3_.refs_1_) | copy-start | bytes 786436
  91.4 7.0 %copy-start.3 = (bf16[512,512]{1,0:T(8,128)(2,1)}, bf16[512,512]{1,0:T(8,128)(2,1)S(1)}, u32[]{:S(2)}) copy-start(bf16[512,512]{1,0:T(8,128)(2,1)S(1)} %collective-permute-done.20.refs_2_.refs_5_.refs_0_) | copy-start | bytes 1572868
  95.4 3.0 %copy-start.5 = (bf16[512,512]{1,0:T(8,128)(2,1)}, bf16[512,512]{1,0:T(8,128)(2,1)S(1)}, u32[]{:S(2)}) copy-start(bf16[512,512]{1,0:T(8,128)(2,1)S(1)} %collective-permute-done.19.refs_1_.refs_4_.refs_0_) | copy-start | bytes 1572868
  98.4 0.8 copy-start.7
  99.2 7.7 %copy-start.14 = (bf16[256,512]{1,0:T(8,128)(2,1)S(1)}, bf16[256,512]{1,0:T(8,128)(2,1)}, u32[]{:S(2)}) copy-start(bf16[256,512]{1,0:T(8,128)(2,1)} %copy-done.13) | copy-start | bytes 786436
  99.2 4.4 %collective-permute-start.21 = (bf16[512,512]{1,0:T(8,128)(2,1)}, bf16[512,512]{1,0:T(8,128)(2,1)}, u32[]{:S(2)}, u32[]{:S(2)}) collective-permute-start(bf16[512,512]{1,0:T(8,128)(2,1)} %shard_map.62.refs_2_), channel_id=1, source_target_pairs={{2,0},{3,1},{0,2},{1,3},{6,4},{7,5},{4,6},{5,7},{10,8},{11,9},{8,1... | collective-permute-start | bytes 1572872 | tf_op jit(solution)/shard_map/ppermute | solution.py:37
  99.2 10.5 %copy-start.4 = (bf16[512,512]{1,0:T(8,128)(2,1)S(1)}, bf16[512,512]{1,0:T(8,128)(2,1)}, u32[]{:S(2)}) copy-start(bf16[512,512]{1,0:T(8,128)(2,1)} %shard_map.66.refs_1_) | copy-start | bytes 1572868
  99.2 15.2 %collective-permute-start.28 = (bf16[512,512]{1,0:T(8,128)(2,1)}, bf16[512,512]{1,0:T(8,128)(2,1)}, u32[]{:S(2)}, u32[]{:S(2)}) collective-permute-start(bf16[512,512]{1,0:T(8,128)(2,1)} %shard_map.66.refs_1_), channel_id=1, source_target_pairs={{1,0},{0,1},{3,2},{2,3},{5,4},{4,5},{7,6},{6,7},{9,8},{8,9},{11,10... | collective-permute-start | bytes 1572872 | tf_op jit(solution)/shard_map/ppermute | solution.py:37
  100.0 9.8 %copy-start.6 = (bf16[512,512]{1,0:T(8,128)(2,1)S(1)}, bf16[512,512]{1,0:T(8,128)(2,1)}, u32[]{:S(2)}) copy-start(bf16[512,512]{1,0:T(8,128)(2,1)} %shard_map.65.refs_0_) | copy-start | bytes 1572868
  100.0 25.2 %collective-permute-start.27 = (bf16[512,512]{1,0:T(8,128)(2,1)}, bf16[512,512]{1,0:T(8,128)(2,1)}, u32[]{:S(2)}, u32[]{:S(2)}) collective-permute-start(bf16[512,512]{1,0:T(8,128)(2,1)} %shard_map.65.refs_0_), channel_id=1, source_target_pairs={{1,0},{0,1},{3,2},{2,3},{5,4},{4,5},{7,6},{6,7},{9,8},{8,9},{11,10... | collective-permute-start | bytes 1572872 | tf_op jit(solution)/shard_map/ppermute | solution.py:37
  101.3 28.0 %collective-permute-start.25 = (bf16[512,512]{1,0:T(8,128)(2,1)}, bf16[512,512]{1,0:T(8,128)(2,1)S(1)}, u32[]{:S(2)}, u32[]{:S(2)}) collective-permute-start(bf16[512,512]{1,0:T(8,128)(2,1)} %shard_map.64), channel_id=1, source_target_pairs={{0,0},{1,1},{8,2},{9,3},{16,4},{17,5},{24,6},{25,7},{2,8},{3,9},{1... | collective-permute-start | bytes 1572872 | tf_op jit(solution)/shard_map/ppermute | solution.py:41
  103.3 26.0 %collective-permute-start.26 = (bf16[512,512]{1,0:T(8,128)(2,1)}, bf16[512,512]{1,0:T(8,128)(2,1)}, u32[]{:S(2)}, u32[]{:S(2)}) collective-permute-start(bf16[512,512]{1,0:T(8,128)(2,1)} %shard_map.64), channel_id=1, source_target_pairs={{4,0},{5,1},{12,2},{13,3},{20,4},{21,5},{28,6},{29,7},{6,8},{7,9},... | collective-permute-start | bytes 1572872 | tf_op jit(solution)/shard_map/ppermute | solution.py:41
  103.6 1.0 copy-start.8
  104.7 1.0 copy-start.15
  109.7 3.0 %copy-start.10 = (bf16[256,512]{1,0:T(8,128)(2,1)S(1)}, bf16[256,512]{1,0:T(8,128)(2,1)}, u32[]{:S(2)}) copy-start(bf16[256,512]{1,0:T(8,128)(2,1)} %copy-done.9) | copy-start | bytes 786436
  109.7 3.0 %copy-start.12 = (bf16[256,512]{1,0:T(8,128)(2,1)S(1)}, bf16[256,512]{1,0:T(8,128)(2,1)}, u32[]{:S(2)}) copy-start(bf16[256,512]{1,0:T(8,128)(2,1)} %copy-done.11) | copy-start | bytes 786436

commit v5 on v4

--- a/solution.py
+++ b/solution.py
@@ -198,24 +198,30 @@
     part = factor_cols.shape[1] // n_high
     block = modes // CORES // n_rows
     half = block * n_rows
-    away = lax.dynamic_slice_in_dim(modal_at_loads, (1 - core) * half, half, 0)
-    here = lax.dynamic_slice_in_dim(modal_at_loads, core * half, half, 0)
-    sent = jnp.dot(away, factor_cols, preferred_element_type=jnp.float32).astype(jnp.bfloat16)
-    came = swap(sent, sizes, 0, 1, 0)
-    total = jnp.dot(here, factor_cols, preferred_element_type=jnp.float32) + came.astype(jnp.float32)
-    total = total.astype(jnp.bfloat16)
+    near = n_rows // 2
+    size = half // 2
+
+    def partial(which, side):
+        rows = lax.dynamic_slice_in_dim(modal_at_loads, which * half + side * size, size, 0)
+        return jnp.dot(rows, factor_cols, preferred_element_type=jnp.float32)
+
     own = None
-    for dh in range(n_high):
-        for dr in range(n_rows):
-            piece = lax.dynamic_slice(total, ((row ^ dr) * block, (high ^ dh) * part), (block, part))
-            if dh or dr:
-                piece = swap(piece, sizes, dr, dh * CORES, 0)
-            piece = piece.astype(jnp.float32)
-            own = piece if own is None else own + piece
+    for part_of, side in ((1, (row // near) ^ 1), (0, row // near)):
+        came = swap(partial(1 - core, side).astype(jnp.bfloat16), sizes, 0, 1, 0)
+        total = (partial(core, side) + came.astype(jnp.float32)).astype(jnp.bfloat16)
+        for dh in reversed(range(n_high)):
+            for dr in reversed(range(near)):
+                first = ((row ^ dr) % near) * block
+                piece = lax.dynamic_slice(total, (first, (high ^ dh) * part), (block, part))
+                if dh or dr or part_of:
+                    piece = swap(piece, sizes, dr + part_of * near, dh * CORES, 0)
+                piece = piece.astype(jnp.float32)
+                own = piece if own is None else own + piece
     own = own.astype(jnp.bfloat16)
-    blocks = [
-        swap(own, sizes, dr, 0, dk) if dr or dk else own for dk in range(n_groups) for dr in range(n_rows)
-    ]
+    line = [swap(own, sizes, dr, 0, 0) if dr else own for dr in range(n_rows)]
+    blocks = list(line)
+    for dk in range(1, n_groups):
+        blocks += [swap(piece, sizes, 0, 0, dk) for piece in line]
     mine = gather_loads(blocks, row, group, n_rows)
     theirs = swap(mine, sizes, 0, 1, 0)
 

time: 135 us -> 133 us (0.985)
  starting transfers between devices: 40 us -> 35.8 us
  matrix products: 6.87 us -> 9.19 us
    ppermute x23 -> x24, starting transfers between devices: 29.3 us -> 24.8 us  [swap(): lax.ppermute(array, AXES, moves(sizes, lambda i, j, k: (i ^ di, j ^ dj, k...]
    dot_general x2 -> x4, matrix products: 6.87 us -> 9.19 us  [partial(): return jnp.dot(rows, factor_cols, preferred_element_type=jnp.float32)]
    ppermute x23 -> x24, waiting for transfers between devices: 37.8 us -> 36.6 us  [swap(): lax.ppermute(array, AXES, moves(sizes, lambda i, j, k: (i ^ di, j ^ dj, k...]
  transfers between devices with their start and end apart: 29 -> 30, of which waited for: 15 -> 16; matrix products, arithmetic and copies ran while one was open for 4% -> 9% of each run, Pallas kernels for 15% -> 15%
where the time goes in v5:
time: 133 us; the launch traced here: 131 us
  waiting for transfers between devices  46.7 us (35%)
  starting transfers between devices  35.8 us (27%)
  Pallas kernels  29.3 us (22%)
  matrix products  9.19 us (7%)
  local copies, waits for them, and re-layouts  7.33 us (6%)
  other arithmetic  2.94 us (2%)
    ppermute x24, waiting for transfers between devices, swap(): lax.ppermute(array, AXES, moves(sizes, lambda i, j, k: (i ^ di, j ^ dj, k...  36.6 us
    ppermute x24, starting transfers between devices, swap(): lax.ppermute(array, AXES, moves(sizes, lambda i, j, k: (i ^ di, j ^ dj, k...  24.8 us
    pallas_call x5, Pallas kernels, place_panel(): pl.pallas_call(functools.partial(panel_kernel, chunk, len(pieces)), grid_...  15.7 us
    ppermute x6, starting transfers between devices, across(): lax.ppermute(array, AXES, moves(sizes, lambda i, j, k: (j, i ^ flip, k)))  11 us
    pallas_call x3, Pallas kernels, project(): pl.pallas_call(project_kernel, grid_spec=pltpu.PrefetchScalarGridSpec(num...  10.7 us
    ppermute x6, waiting for transfers between devices, across(): lax.ppermute(array, AXES, moves(sizes, lambda i, j, k: (j, i ^ flip, k)))  10.1 us
    dot_general x4, matrix products, partial(): return jnp.dot(rows, factor_cols, preferred_element_type=jnp.float32)  9.19 us
    unnamed x38, local copies, waits for them, and re-layouts  6.59 us
  transfers between devices with their start and end apart: 30, of which 16 were waited for; matrix products, arithmetic and copies ran while one was open for 9% of the time, Pallas kernels for 15%

profile of v5, /device:TPU:4, one launch (start us, length us, event | category | flops | bytes accessed | tf_op | source)
XLA Modules:
  0.0 131.5 jit_solution(160247872595899057)
XLA Ops:
  0.0 1.2 copy-done
  1.2 2.3 %fusion.8 = bf16[512,256]{1,0:T(8,128)(2,1)S(1)} fusion(bf16[2048,256]{1,0:T(8,128)(2,1)S(1)} %copy-done, bf16[2048,2048]{1,0:T(8,128)(2,1)} %param.6, s32[]{:T(128)S(6)} %select_n.84), kind=kOutput, calls=%fused_computation.8 | convolution fusion | flops 537001984 | bytes 3407876 | tf_op jit(solution)/shard_map/dot_general | solution.py:206
  3.6 2.3 %fusion.11 = bf16[512,256]{1,0:T(8,128)(2,1)S(1)} fusion(bf16[2048,256]{1,0:T(8,128)(2,1)S(1)} %copy-done, bf16[2048,2048]{1,0:T(8,128)(2,1)} %param.6, s32[]{:T(128)S(6)} %select_n.92), kind=kOutput, calls=%fused_computation.9 | convolution fusion | flops 537001984 | bytes 3407876 | tf_op jit(solution)/shard_map/dot_general | solution.py:206
  5.9 0.5 collective-permute-start.5
  6.5 2.3 %add_convert_fusion.1 = bf16[512,256]{1,0:T(8,128)(2,1)S(1)} fusion(bf16[512,256]{1,0:T(8,128)(2,1)S(1)} %collective-permute-done, bf16[2048,256]{1,0:T(8,128)(2,1)S(1)} %copy-done, bf16[2048,2048]{1,0:T(8,128)(2,1)} %param.6, s32[]{:T(128)S(6)} %select_n.83), kind=kOutput, calls=%fused_computation.13 | convolution fusion | flops 537264128 | bytes 3670020 | tf_op jit(solution)/shard_map/dot_general | solution.py:206
  8.9 3.6 %collective-permute-start.1 = (bf16[256,128]{1,0:T(8,128)(2,1)S(1)}, bf16[256,128]{1,0:T(8,128)(2,1)S(1)}, u32[]{:S(2)}, u32[]{:S(2)}) collective-permute-start(bf16[256,128]{1,0:T(8,128)(2,1)S(1)} %get-tuple-element.8), channel_id=1, source_target_pairs={{28,0},{29,1},{30,2},{31,3},{24,4},{25,5},{26,6},{27,7},{20,8},{21... | collective-permute-start | bytes 196616 | tf_op jit(solution)/shard_map/ppermute | solution.py:37
  12.5 0.4 collective-permute-start.2
  12.9 2.5 %collective-permute-start.3 = (bf16[256,128]{1,0:T(8,128)(2,1)S(1)}, bf16[256,128]{1,0:T(8,128)(2,1)S(1)}, u32[]{:S(2)}, u32[]{:S(2)}) collective-permute-start(bf16[256,128]{1,0:T(8,128)(2,1)S(1)} %get-tuple-element.10), channel_id=1, source_target_pairs={{24,0},{25,1},{26,2},{27,3},{28,4},{29,5},{30,6},{31,7},{16,8},{17... | collective-permute-start | bytes 196616 | tf_op jit(solution)/shard_map/ppermute | solution.py:37
  15.4 1.0 collective-permute-start.4
  16.4 2.3 %add_convert_fusion = bf16[512,256]{1,0:T(8,128)(2,1)S(1)} fusion(bf16[512,256]{1,0:T(8,128)(2,1)S(1)} %collective-permute-done.5, bf16[2048,256]{1,0:T(8,128)(2,1)S(1)} %copy-done, bf16[2048,2048]{1,0:T(8,128)(2,1)} %param.6, s32[]{:T(128)S(6)} %select_n.91), kind=kOutput, calls=%fused_computation.12 | convolution fusion | flops 537264128 | bytes 3670020 | tf_op jit(solution)/shard_map/dot_general | solution.py:206
  18.7 1.5 %collective-permute-start.6 = (bf16[256,128]{1,0:T(8,128)(2,1)S(1)}, bf16[256,128]{1,0:T(8,128)(2,1)S(1)}, u32[]{:S(2)}, u32[]{:S(2)}) collective-permute-start(bf16[256,128]{1,0:T(8,128)(2,1)S(1)} %get-tuple-element.12), channel_id=1, source_target_pairs={{12,0},{13,1},{14,2},{15,3},{8,4},{9,5},{10,6},{11,7},{4,8},{5,9},... | collective-permute-start | bytes 196616 | tf_op jit(solution)/shard_map/ppermute | solution.py:37
  20.3 0.9 collective-permute-start.7
  21.2 1.4 %collective-permute-done.2 = bf16[256,128]{1,0:T(8,128)(2,1)S(1)} collective-permute-done((bf16[256,128]{1,0:T(8,128)(2,1)S(1)}, bf16[256,128]{1,0:T(8,128)(2,1)S(1)}, u32[]{:S(2)}, u32[]{:S(2)}) %collective-permute-start.2) | collective-permute-done | bytes 65568 | tf_op jit(solution)/shard_map/ppermute | solution.py:37
  22.6 1.9 %collective-permute-done.4 = bf16[256,128]{1,0:T(8,128)(2,1)S(1)} collective-permute-done((bf16[256,128]{1,0:T(8,128)(2,1)S(1)}, bf16[256,128]{1,0:T(8,128)(2,1)S(1)}, u32[]{:S(2)}, u32[]{:S(2)}) %collective-permute-start.4) | collective-permute-done | bytes 65568 | tf_op jit(solution)/shard_map/ppermute | solution.py:37
  24.5 1.0 collective-permute-done.6
  25.5 1.3 %collective-permute-done.8 = bf16[256,128]{1,0:T(8,128)(2,1)S(1)} collective-permute-done((bf16[256,128]{1,0:T(8,128)(2,1)S(1)}, bf16[256,128]{1,0:T(8,128)(2,1)S(1)}, u32[]{:S(2)}, u32[]{:S(2)}) %collective-permute-start.8) | collective-permute-done | bytes 65568 | tf_op jit(solution)/shard_map/ppermute | solution.py:37
  27.0 3.1 %collective-permute-start.10 = (bf16[256,128]{1,0:T(8,128)(2,1)S(1)}, bf16[256,128]{1,0:T(8,128)(2,1)S(1)}, u32[]{:S(2)}, u32[]{:S(2)}) collective-permute-start(bf16[256,128]{1,0:T(8,128)(2,1)S(1)} %add_convert_fusion.2.refs_0_), channel_id=1, source_target_pairs={{16,0},{17,1},{18,2},{19,3},{20,4},{21,5},{22,6},{23,7},{24,8},{25... | collective-permute-start | bytes 196616 | tf_op jit(solution)/shard_map/ppermute | solution.py:37
  30.1 1.3 collective-permute-start.11
  31.4 1.5 %collective-permute-start.12 = (bf16[256,128]{1,0:T(8,128)(2,1)S(1)}, bf16[256,128]{1,0:T(8,128)(2,1)S(1)}, u32[]{:S(2)}, u32[]{:S(2)}) collective-permute-start(bf16[256,128]{1,0:T(8,128)(2,1)S(1)} %add_convert_fusion.2.refs_0_), channel_id=1, source_target_pairs={{1,0},{0,1},{3,2},{2,3},{5,4},{4,5},{7,6},{6,7},{9,8},{8,9},{11,10... | collective-permute-start | bytes 196616 | tf_op jit(solution)/shard_map/ppermute | solution.py:37
  32.9 0.5 collective-permute-start.13
  33.4 1.5 %collective-permute-start.14 = (bf16[256,128]{1,0:T(8,128)(2,1)S(1)}, bf16[256,128]{1,0:T(8,128)(2,1)S(1)}, u32[]{:S(2)}, u32[]{:S(2)}) collective-permute-start(bf16[256,128]{1,0:T(8,128)(2,1)S(1)} %collective-permute-done.10.refs_2_), channel_id=1, source_target_pairs={{1,0},{0,1},{3,2},{2,3},{5,4},{4,5},{7,6},{6,7},{9,8},{8,9},{11,10... | collective-permute-start | bytes 196616 | tf_op jit(solution)/shard_map/ppermute | solution.py:37
  34.9 1.3 collective-permute-done.11.refs_3_
  36.2 1.5 %collective-permute-start.15 = (bf16[256,128]{1,0:T(8,128)(2,1)S(1)}, bf16[256,128]{1,0:T(8,128)(2,1)S(1)}, u32[]{:S(2)}, u32[]{:S(2)}) collective-permute-start(bf16[256,128]{1,0:T(8,128)(2,1)S(1)} %collective-permute-done.11.refs_3_), channel_id=1, source_target_pairs={{1,0},{0,1},{3,2},{2,3},{5,4},{4,5},{7,6},{6,7},{9,8},{8,9},{11,10... | collective-permute-start | bytes 196616 | tf_op jit(solution)/shard_map/ppermute | solution.py:37
  37.8 0.7 collective-permute-done.14.refs_6_
  38.5 2.0 %collective-permute-done.15.refs_7_ = bf16[256,128]{1,0:T(8,128)(2,1)S(1)} collective-permute-done((bf16[256,128]{1,0:T(8,128)(2,1)S(1)}, bf16[256,128]{1,0:T(8,128)(2,1)S(1)}, u32[]{:S(2)}, u32[]{:S(2)}) %collective-permute-start.15) | collective-permute-done | bytes 65568 | tf_op jit(solution)/shard_map/ppermute | solution.py:37
  40.4 1.4 %shard_map.55.mine = bf16[1024,256]{1,0:T(8,128)(2,1)} custom-call(s32[2]{0:T(128)S(1)} %pad_add_fusion.2.spots, bf16[256,128]{1,0:T(8,128)(2,1)S(1)} %add_convert_fusion.2.refs_0_, bf16[256,128]{1,0:T(8,128)(2,1)S(1)} %collective-permute-done.9.refs_1_, bf16[256,128]{1,0:T(8,128)(2,1)S(1)} %collective-permute-done.10.refs_2_, ...), custom_call_target="tpu_custom_call" | custom-call | flops 1 | bytes 1 | tf_op jit(solution)/shard_map/pallas_call | solution.py:80
  41.9 0.6 copy.17.scale
  42.6 1.6 %collective-permute-done.16.theirs = bf16[1024,256]{1,0:T(8,128)(2,1)} collective-permute-done((bf16[1024,256]{1,0:T(8,128)(2,1)}, bf16[1024,256]{1,0:T(8,128)(2,1)}, u32[]{:S(2)}, u32[]{:S(2)}) %collective-permute-start.16) | collective-permute-done | bytes 524320 | tf_op jit(solution)/shard_map/ppermute | solution.py:37
  44.1 3.6 %shard_map.56 = bf16[256,512]{1,0:T(8,128)(2,1)} custom-call(s32[1]{0:T(128)} %bitcast.2.spots, bf16[1024,256]{1,0:T(8,128)(2,1)} %shard_map.55.mine, bf16[1024,256]{1,0:T(8,128)(2,1)} %collective-permute-done.16.theirs, f32[2,2048,1]{2,1,0:T(8,128)S(1)} %copy.17.scale, bf16[1024,2048]{1,0:T(8,128)(2,1)} %shapes.5), custom_call_target="tpu_custom_call" | custom-call | flops 1 | bytes 1 | tf_op jit(solution)/shard_map/pallas_call | solution.py:114
  47.7 0.5 collective-permute-start.18
  48.2 3.5 %collective-permute-start.17 = (bf16[256,512]{1,0:T(8,128)(2,1)}, bf16[256,512]{1,0:T(8,128)(2,1)}, u32[]{:S(2)}, u32[]{:S(2)}) collective-permute-start(bf16[256,512]{1,0:T(8,128)(2,1)} %shard_map.56), channel_id=1, source_target_pairs={{0,0},{1,1},{8,2},{9,3},{16,4},{17,5},{24,6},{25,7},{2,8},{3,9},{1... | collective-permute-start | bytes 786440 | tf_op jit(solution)/shard_map/ppermute | solution.py:41
  51.8 3.6 %shard_map.57 = bf16[256,512]{1,0:T(8,128)(2,1)} custom-call(s32[1]{0:T(128)} %bitcast.2.spots, bf16[1024,256]{1,0:T(8,128)(2,1)} %shard_map.55.mine, bf16[1024,256]{1,0:T(8,128)(2,1)} %collective-permute-done.16.theirs, f32[2,2048,1]{2,1,0:T(8,128)S(1)} %copy.17.scale, bf16[1024,2048]{1,0:T(8,128)(2,1)} %shapes.5), custom_call_target="tpu_custom_call" | custom-call | flops 1 | bytes 1 | tf_op jit(solution)/shard_map/pallas_call | solution.py:114
  55.3 0.7 collective-permute-start.23
  56.0 3.6 %shard_map.58.refs_1_ = bf16[512,512]{1,0:T(8,128)(2,1)S(1)} custom-call(s32[1]{0:T(128)} %bitcast.2.spots, bf16[1024,256]{1,0:T(8,128)(2,1)} %shard_map.55.mine, bf16[1024,256]{1,0:T(8,128)(2,1)} %collective-permute-done.16.theirs, f32[2,2048,1]{2,1,0:T(8,128)S(1)} %copy.17.scale, bf16[1024,2048]{1,0:T(8,128)(2,1)} %shapes.5), custom_call_target="tpu_custom_call" | custom-call | flops 1 | bytes 1 | tf_op jit(solution)/shard_map/pallas_call | solution.py:114
  59.6 0.9 copy.22.refs_0_
  60.5 0.1 copy-done.1
  60.6 0.8 copy.21.refs_0_
  61.4 0.3 collective-permute-done.18.refs_2_.refs_1_
  61.6 0.7 copy-done.13
  62.3 1.7 %collective-permute-start.21 = (bf16[512,512]{1,0:T(8,128)(2,1)}, bf16[512,512]{1,0:T(8,128)(2,1)S(1)}, u32[]{:S(2)}, u32[]{:S(2)}) collective-permute-start(bf16[512,512]{1,0:T(8,128)(2,1)} %shard_map.61), channel_id=1, source_target_pairs={{4,0},{5,1},{12,2},{13,3},{20,4},{21,5},{28,6},{29,7},{6,8},{7,9},... | collective-permute-start | bytes 1572872 | tf_op jit(solution)/shard_map/ppermute | solution.py:41
  64.1 1.8 %collective-permute-done.17.refs_1_.refs_0_ = bf16[256,512]{1,0:T(8,128)(2,1)} collective-permute-done((bf16[256,512]{1,0:T(8,128)(2,1)}, bf16[256,512]{1,0:T(8,128)(2,1)}, u32[]{:S(2)}, u32[]{:S(2)}) %collective-permute-start.17) | collective-permute-done | bytes 262176 | tf_op jit(solution)/shard_map/ppermute | solution.py:41
  65.9 2.9 %collective-permute-start.20 = (bf16[512,512]{1,0:T(8,128)(2,1)}, bf16[512,512]{1,0:T(8,128)(2,1)S(1)}, u32[]{:S(2)}, u32[]{:S(2)}) collective-permute-start(bf16[512,512]{1,0:T(8,128)(2,1)} %shard_map.60), channel_id=1, source_target_pairs={{0,0},{1,1},{8,2},{9,3},{16,4},{17,5},{24,6},{25,7},{2,8},{3,9},{1... | collective-permute-start | bytes 1572872 | tf_op jit(solution)/shard_map/ppermute | solution.py:41
  68.7 2.5 %broadcast_select_fusion = (bf16[512,512]{1,0:T(8,128)(2,1)}, bf16[512,512]{1,0:T(8,128)(2,1)}, bf16[512,512]{1,0:T(8,128)(2,1)}) fusion(bf16[512,512]{1,0:T(8,128)(2,1)} %copy-done.1, pred[]{:T(512)S(6)} %eq.13, bf16[256,512]{1,0:T(8,128)(2,1)} %shard_map.57, bf16[256,512]{1,0:T(8,128)(2,1)} %shard_map.56, bf16[256,512]{1,0:T(8,128)(2,1)} %collective-permute-done.23), kind=kLoop, calls=%fused_computation.14 | loop fusion | flops 2359296 | bytes 2883585 | tf_op jit(solution)/shard_map/jit(_where)/select_n | solution.py:263
  71.3 0.5 collective-permute-start.24
  71.8 1.5 %collective-permute-start.25 = (bf16[256,512]{1,0:T(8,128)(2,1)}, bf16[256,512]{1,0:T(8,128)(2,1)S(1)}, u32[]{:S(2)}, u32[]{:S(2)}) collective-permute-start(bf16[256,512]{1,0:T(8,128)(2,1)} %copy-done.13), channel_id=1, source_target_pairs={{1,0},{0,1},{3,2},{2,3},{5,4},{4,5},{7,6},{6,7},{9,8},{8,9},{11,10... | collective-permute-start | bytes 786440 | tf_op jit(solution)/shard_map/ppermute | solution.py:37
  73.3 7.3 %collective-permute-done.24.refs_2_.refs_1_.refs_0_ = bf16[256,512]{1,0:T(8,128)(2,1)S(1)} collective-permute-done((bf16[256,512]{1,0:T(8,128)(2,1)}, bf16[256,512]{1,0:T(8,128)(2,1)S(1)}, u32[]{:S(2)}, u32[]{:S(2)}) %collective-permute-start.24) | collective-permute-done | bytes 262176 | tf_op jit(solution)/shard_map/ppermute | solution.py:37
  80.6 4.8 %collective-permute-done.25.refs_3_.refs_1_ = bf16[256,512]{1,0:T(8,128)(2,1)S(1)} collective-permute-done((bf16[256,512]{1,0:T(8,128)(2,1)}, bf16[256,512]{1,0:T(8,128)(2,1)S(1)}, u32[]{:S(2)}, u32[]{:S(2)}) %collective-permute-start.25) | collective-permute-done | bytes 262176 | tf_op jit(solution)/shard_map/ppermute | solution.py:37
  85.4 3.5 %collective-permute-done.21.refs_2_.refs_5_.refs_0_ = bf16[512,512]{1,0:T(8,128)(2,1)S(1)} collective-permute-done((bf16[512,512]{1,0:T(8,128)(2,1)}, bf16[512,512]{1,0:T(8,128)(2,1)S(1)}, u32[]{:S(2)}, u32[]{:S(2)}) %collective-permute-start.21) | collective-permute-done | bytes 524320 | tf_op jit(solution)/shard_map/ppermute | solution.py:41
  88.9 4.6 %collective-permute-done.20.refs_1_.refs_4_.refs_0_ = bf16[512,512]{1,0:T(8,128)(2,1)S(1)} collective-permute-done((bf16[512,512]{1,0:T(8,128)(2,1)}, bf16[512,512]{1,0:T(8,128)(2,1)S(1)}, u32[]{:S(2)}, u32[]{:S(2)}) %collective-permute-start.20) | collective-permute-done | bytes 524320 | tf_op jit(solution)/shard_map/ppermute | solution.py:41
  93.4 3.0 %collective-permute-done.19.refs_0_.refs_1_ = bf16[512,512]{1,0:T(8,128)(2,1)S(1)} collective-permute-done((bf16[512,512]{1,0:T(8,128)(2,1)}, bf16[512,512]{1,0:T(8,128)(2,1)S(1)}, u32[]{:S(2)}, u32[]{:S(2)}) %collective-permute-start.19) | collective-permute-done | bytes 524320 | tf_op jit(solution)/shard_map/ppermute | solution.py:37
  96.5 0.8 copy-done.7
  97.3 0.8 collective-permute-start.29
  98.1 1.3 %collective-permute-start.28 = (bf16[512,512]{1,0:T(8,128)(2,1)}, bf16[512,512]{1,0:T(8,128)(2,1)}, u32[]{:S(2)}, u32[]{:S(2)}) collective-permute-start(bf16[512,512]{1,0:T(8,128)(2,1)} %shard_map.65.refs_0_), channel_id=1, source_target_pairs={{1,0},{0,1},{3,2},{2,3},{5,4},{4,5},{7,6},{6,7},{9,8},{8,9},{11,10... | collective-permute-start | bytes 1572872 | tf_op jit(solution)/shard_map/ppermute | solution.py:37
  99.4 2.3 %collective-permute-start.26 = (bf16[512,512]{1,0:T(8,128)(2,1)}, bf16[512,512]{1,0:T(8,128)(2,1)S(1)}, u32[]{:S(2)}, u32[]{:S(2)}) collective-permute-start(bf16[512,512]{1,0:T(8,128)(2,1)} %shard_map.64), channel_id=1, source_target_pairs={{0,0},{1,1},{8,2},{9,3},{16,4},{17,5},{24,6},{25,7},{2,8},{3,9},{1... | collective-permute-start | bytes 1572872 | tf_op jit(solution)/shard_map/ppermute | solution.py:41
  101.7 0.1 pad_add_fusion.4.spots
  101.9 1.0 copy-done.8
  102.9 1.0 copy-done.15
  104.0 1.4 %shard_map.63.left = bf16[1024,1024]{1,0:T(8,128)(2,1)S(1)} custom-call(s32[2]{0:T(128)S(1)} %get-tuple-element.18.spots, bf16[512,512]{1,0:T(8,128)(2,1)S(1)} %copy-done.15, bf16[512,512]{1,0:T(8,128)(2,1)S(1)} %copy-done.2, bf16[512,512]{1,0:T(8,128)(2,1)S(1)} %copy-done.8, bf16[512,512]{1,0:T(8,128)(2,1)} %collective-permute-done.22.refs_3_), custom_call_target="tpu_custom_call" | custom-call | flops 1 | bytes 1 | tf_op jit(solution)/shard_map/pallas_call | solution.py:155
  105.4 2.7 %shard_map.67.refs_2_ = f32[1024,2048]{1,0:T(8,128)} custom-call(s32[1]{0:T(128)} %bitcast.14.spots, bf16[1024,1024]{1,0:T(8,128)(2,1)S(1)} %shard_map.63.left, bf16[256,512]{1,0:T(8,128)(2,1)} %collective-permute-done.17.refs_1_.refs_0_, bf16[256,512]{1,0:T(8,128)(2,1)S(1)} %copy-done.14), custom_call_target="tpu_custom_call" | custom-call | flops 1 | bytes 1 | tf_op jit(solution)/shard_map/pallas_call | solution.py:175
  108.2 3.0 %shard_map.68.refs_2_ = f32[1024,2048]{1,0:T(8,128)} custom-call(s32[2]{0:T(128)S(1)} %pad_add_fusion.4.spots, bf16[1024,1024]{1,0:T(8,128)(2,1)S(1)} %shard_map.63.left, bf16[512,512]{1,0:T(8,128)(2,1)S(1)} %copy-done.6, bf16[512,512]{1,0:T(8,128)(2,1)S(1)} %copy-done.4, f32[1024,2048]{1,0:T(8,128)} %shard_map.67.refs_2_), custom_call_target="tpu_custom_call", output_to_operand_aliasing={{}: (4, {})} | custom-call | flops 1 | bytes 1 | tf_op jit(solution)/shard_map/pallas_call | solution.py:175
  111.2 1.7 %shard_map.69.refs_2_ = f32[1024,2048]{1,0:T(8,128)} custom-call(s32[1]{0:T(128)} %bitcast.11.spots, bf16[1024,1024]{1,0:T(8,128)(2,1)S(1)} %shard_map.63.left, bf16[256,512]{1,0:T(8,128)(2,1)S(1)} %copy-done.10, bf16[256,512]{1,0:T(8,128)(2,1)S(1)} %copy-done.12, f32[1024,2048]{1,0:T(8,128)} %shard_map.68.refs_2_), custom_call_target="tpu_custom_call", output_to_operand_aliasing={{}: (4, {})} | custom-call | flops 1 | bytes 1 | tf_op jit(solution)/shard_map/pallas_call | solution.py:175
  112.9 10.3 %collective-permute-done.28.refs_0_ = bf16[512,512]{1,0:T(8,128)(2,1)} collective-permute-done((bf16[512,512]{1,0:T(8,128)(2,1)}, bf16[512,512]{1,0:T(8,128)(2,1)}, u32[]{:S(2)}, u32[]{:S(2)}) %collective-permute-start.28) | collective-permute-done | bytes 524320 | tf_op jit(solution)/shard_map/ppermute | solution.py:37
  123.2 4.2 %shard_map.70.refs_2_ = f32[1024,2048]{1,0:T(8,128)} custom-call(s32[2]{0:T(128)S(1)} %pad_add_fusion.3.spots, bf16[1024,1024]{1,0:T(8,128)(2,1)S(1)} %shard_map.63.left, bf16[512,512]{1,0:T(8,128)(2,1)} %collective-permute-done.28.refs_0_, bf16[512,512]{1,0:T(8,128)(2,1)} %collective-permute-done.29.refs_1_, ...), custom_call_target="tpu_custom_call", output_to_operand_aliasing={{}: (4, {})} | custom-call | flops 1 | bytes 1 | tf_op jit(solution)/shard_map/pallas_call | solution.py:175
  127.4 4.1 %shard_map.71 = f32[1024,2048]{1,0:T(8,128)} custom-call(s32[2]{0:T(128)S(1)} %get-tuple-element.17.spots, bf16[1024,1024]{1,0:T(8,128)(2,1)S(1)} %shard_map.63.left, bf16[512,512]{1,0:T(8,128)(2,1)S(1)} %collective-permute-done.26.refs_0_, bf16[512,512]{1,0:T(8,128)(2,1)} %collective-permute-done.27.refs_1_, ...), custom_call_target="tpu_custom_call", output_to_operand_aliasing={{}: (4, {})} | custom-call | flops 1 | bytes 1 | tf_op jit(solution)/shard_map/pallas_call | solution.py:175
  (66 shorter events, 0.8 us)
Async XLA Ops:
  0.0 1.2 copy-start
  3.5 3.0 %collective-permute-start = (bf16[512,256]{1,0:T(8,128)(2,1)S(1)}, bf16[512,256]{1,0:T(8,128)(2,1)S(1)}, u32[]{:S(2)}, u32[]{:S(2)}) collective-permute-start(bf16[512,256]{1,0:T(8,128)(2,1)S(1)} %fusion.8), channel_id=1, source_target_pairs={{2,0},{3,1},{0,2},{1,3},{6,4},{7,5},{4,6},{5,7},{10,8},{11,9},{8,1... | collective-permute-start | bytes 786440 | tf_op jit(solution)/shard_map/ppermute | solution.py:37
  5.9 36.0 %copy-start.16 = (f32[2048]{0:T(1024)S(1)}, f32[2048]{0:T(1024)}, u32[]{:S(2)}) copy-start(f32[2048]{0:T(1024)} %param.8) | copy-start | bytes 24580
  5.9 35.9 %copy-start.17 = (f32[2048]{0:T(1024)S(1)}, f32[2048]{0:T(1024)}, u32[]{:S(2)}) copy-start(f32[2048]{0:T(1024)} %param.9) | copy-start | bytes 24580
  5.9 10.4 %collective-permute-start.5 = (bf16[512,256]{1,0:T(8,128)(2,1)S(1)}, bf16[512,256]{1,0:T(8,128)(2,1)S(1)}, u32[]{:S(2)}, u32[]{:S(2)}) collective-permute-start(bf16[512,256]{1,0:T(8,128)(2,1)S(1)} %fusion.11), channel_id=1, source_target_pairs={{2,0},{3,1},{0,2},{1,3},{6,4},{7,5},{4,6},{5,7},{10,8},{11,9},{8,1... | collective-permute-start | bytes 786440 | tf_op jit(solution)/shard_map/ppermute | solution.py:37
  8.9 11.4 %collective-permute-start.1 = (bf16[256,128]{1,0:T(8,128)(2,1)S(1)}, bf16[256,128]{1,0:T(8,128)(2,1)S(1)}, u32[]{:S(2)}, u32[]{:S(2)}) collective-permute-start(bf16[256,128]{1,0:T(8,128)(2,1)S(1)} %get-tuple-element.8), channel_id=1, source_target_pairs={{28,0},{29,1},{30,2},{31,3},{24,4},{25,5},{26,6},{27,7},{20,8},{21... | collective-permute-start | bytes 196616 | tf_op jit(solution)/shard_map/ppermute | solution.py:37
  12.5 10.1 %collective-permute-start.2 = (bf16[256,128]{1,0:T(8,128)(2,1)S(1)}, bf16[256,128]{1,0:T(8,128)(2,1)S(1)}, u32[]{:S(2)}, u32[]{:S(2)}) collective-permute-start(bf16[256,128]{1,0:T(8,128)(2,1)S(1)} %get-tuple-element.11), channel_id=1, source_target_pairs={{20,0},{21,1},{22,2},{23,3},{16,4},{17,5},{18,6},{19,7},{28,8},{29... | collective-permute-start | bytes 196616 | tf_op jit(solution)/shard_map/ppermute | solution.py:37
  12.9 9.7 %collective-permute-start.3 = (bf16[256,128]{1,0:T(8,128)(2,1)S(1)}, bf16[256,128]{1,0:T(8,128)(2,1)S(1)}, u32[]{:S(2)}, u32[]{:S(2)}) collective-permute-start(bf16[256,128]{1,0:T(8,128)(2,1)S(1)} %get-tuple-element.10), channel_id=1, source_target_pairs={{24,0},{25,1},{26,2},{27,3},{28,4},{29,5},{30,6},{31,7},{16,8},{17... | collective-permute-start | bytes 196616 | tf_op jit(solution)/shard_map/ppermute | solution.py:37
  15.4 9.1 %collective-permute-start.4 = (bf16[256,128]{1,0:T(8,128)(2,1)S(1)}, bf16[256,128]{1,0:T(8,128)(2,1)S(1)}, u32[]{:S(2)}, u32[]{:S(2)}) collective-permute-start(bf16[256,128]{1,0:T(8,128)(2,1)S(1)} %get-tuple-element.9), channel_id=1, source_target_pairs={{16,0},{17,1},{18,2},{19,3},{20,4},{21,5},{22,6},{23,7},{24,8},{25... | collective-permute-start | bytes 196616 | tf_op jit(solution)/shard_map/ppermute | solution.py:37
  18.7 6.8 %collective-permute-start.6 = (bf16[256,128]{1,0:T(8,128)(2,1)S(1)}, bf16[256,128]{1,0:T(8,128)(2,1)S(1)}, u32[]{:S(2)}, u32[]{:S(2)}) collective-permute-start(bf16[256,128]{1,0:T(8,128)(2,1)S(1)} %get-tuple-element.12), channel_id=1, source_target_pairs={{12,0},{13,1},{14,2},{15,3},{8,4},{9,5},{10,6},{11,7},{4,8},{5,9},... | collective-permute-start | bytes 196616 | tf_op jit(solution)/shard_map/ppermute | solution.py:37
  20.3 5.2 %collective-permute-start.7 = (bf16[256,128]{1,0:T(8,128)(2,1)S(1)}, bf16[256,128]{1,0:T(8,128)(2,1)S(1)}, u32[]{:S(2)}, u32[]{:S(2)}) collective-permute-start(bf16[256,128]{1,0:T(8,128)(2,1)S(1)} %get-tuple-element.14), channel_id=1, source_target_pairs={{4,0},{5,1},{6,2},{7,3},{0,4},{1,5},{2,6},{3,7},{12,8},{13,9},{14,... | collective-permute-start | bytes 196616 | tf_op jit(solution)/shard_map/ppermute | solution.py:37
  22.6 4.3 %collective-permute-start.8 = (bf16[256,128]{1,0:T(8,128)(2,1)S(1)}, bf16[256,128]{1,0:T(8,128)(2,1)S(1)}, u32[]{:S(2)}, u32[]{:S(2)}) collective-permute-start(bf16[256,128]{1,0:T(8,128)(2,1)S(1)} %get-tuple-element.13), channel_id=1, source_target_pairs={{8,0},{9,1},{10,2},{11,3},{12,4},{13,5},{14,6},{15,7},{0,8},{1,9},... | collective-permute-start | bytes 196616 | tf_op jit(solution)/shard_map/ppermute | solution.py:37
  26.9 6.0 %collective-permute-start.9 = (bf16[256,128]{1,0:T(8,128)(2,1)S(1)}, bf16[256,128]{1,0:T(8,128)(2,1)S(1)}, u32[]{:S(2)}, u32[]{:S(2)}) collective-permute-start(bf16[256,128]{1,0:T(8,128)(2,1)S(1)} %add_convert_fusion.2.refs_0_), channel_id=1, source_target_pairs={{8,0},{9,1},{10,2},{11,3},{12,4},{13,5},{14,6},{15,7},{0,8},{1,9},... | collective-permute-start | bytes 196616 | tf_op jit(solution)/shard_map/ppermute | solution.py:37
  27.0 6.4 %collective-permute-start.10 = (bf16[256,128]{1,0:T(8,128)(2,1)S(1)}, bf16[256,128]{1,0:T(8,128)(2,1)S(1)}, u32[]{:S(2)}, u32[]{:S(2)}) collective-permute-start(bf16[256,128]{1,0:T(8,128)(2,1)S(1)} %add_convert_fusion.2.refs_0_), channel_id=1, source_target_pairs={{16,0},{17,1},{18,2},{19,3},{20,4},{21,5},{22,6},{23,7},{24,8},{25... | collective-permute-start | bytes 196616 | tf_op jit(solution)/shard_map/ppermute | solution.py:37
  30.1 6.1 %collective-permute-start.11 = (bf16[256,128]{1,0:T(8,128)(2,1)S(1)}, bf16[256,128]{1,0:T(8,128)(2,1)S(1)}, u32[]{:S(2)}, u32[]{:S(2)}) collective-permute-start(bf16[256,128]{1,0:T(8,128)(2,1)S(1)} %add_convert_fusion.2.refs_0_), channel_id=1, source_target_pairs={{24,0},{25,1},{26,2},{27,3},{28,4},{29,5},{30,6},{31,7},{16,8},{17... | collective-permute-start | bytes 196616 | tf_op jit(solution)/shard_map/ppermute | solution.py:37
  31.4 6.4 %collective-permute-start.12 = (bf16[256,128]{1,0:T(8,128)(2,1)S(1)}, bf16[256,128]{1,0:T(8,128)(2,1)S(1)}, u32[]{:S(2)}, u32[]{:S(2)}) collective-permute-start(bf16[256,128]{1,0:T(8,128)(2,1)S(1)} %add_convert_fusion.2.refs_0_), channel_id=1, source_target_pairs={{1,0},{0,1},{3,2},{2,3},{5,4},{4,5},{7,6},{6,7},{9,8},{8,9},{11,10... | collective-permute-start | bytes 196616 | tf_op jit(solution)/shard_map/ppermute | solution.py:37
  32.9 4.9 %collective-permute-start.13 = (bf16[256,128]{1,0:T(8,128)(2,1)S(1)}, bf16[256,128]{1,0:T(8,128)(2,1)S(1)}, u32[]{:S(2)}, u32[]{:S(2)}) collective-permute-start(bf16[256,128]{1,0:T(8,128)(2,1)S(1)} %collective-permute-done.9.refs_1_), channel_id=1, source_target_pairs={{1,0},{0,1},{3,2},{2,3},{5,4},{4,5},{7,6},{6,7},{9,8},{8,9},{11,10... | collective-permute-start | bytes 196616 | tf_op jit(solution)/shard_map/ppermute | solution.py:37
  33.4 5.1 %collective-permute-start.14 = (bf16[256,128]{1,0:T(8,128)(2,1)S(1)}, bf16[256,128]{1,0:T(8,128)(2,1)S(1)}, u32[]{:S(2)}, u32[]{:S(2)}) collective-permute-start(bf16[256,128]{1,0:T(8,128)(2,1)S(1)} %collective-permute-done.10.refs_2_), channel_id=1, source_target_pairs={{1,0},{0,1},{3,2},{2,3},{5,4},{4,5},{7,6},{6,7},{9,8},{8,9},{11,10... | collective-permute-start | bytes 196616 | tf_op jit(solution)/shard_map/ppermute | solution.py:37
  36.2 4.3 %collective-permute-start.15 = (bf16[256,128]{1,0:T(8,128)(2,1)S(1)}, bf16[256,128]{1,0:T(8,128)(2,1)S(1)}, u32[]{:S(2)}, u32[]{:S(2)}) collective-permute-start(bf16[256,128]{1,0:T(8,128)(2,1)S(1)} %collective-permute-done.11.refs_3_), channel_id=1, source_target_pairs={{1,0},{0,1},{3,2},{2,3},{5,4},{4,5},{7,6},{6,7},{9,8},{8,9},{11,10... | collective-permute-start | bytes 196616 | tf_op jit(solution)/shard_map/ppermute | solution.py:37
  41.9 2.3 %collective-permute-start.16 = (bf16[1024,256]{1,0:T(8,128)(2,1)}, bf16[1024,256]{1,0:T(8,128)(2,1)}, u32[]{:S(2)}, u32[]{:S(2)}) collective-permute-start(bf16[1024,256]{1,0:T(8,128)(2,1)} %shard_map.55.mine), channel_id=1, source_target_pairs={{2,0},{3,1},{0,2},{1,3},{6,4},{7,5},{4,6},{5,7},{10,8},{11,9},{8,1... | collective-permute-start | bytes 1572872 | tf_op jit(solution)/shard_map/ppermute | solution.py:37
  47.7 13.9 %collective-permute-start.18 = (bf16[256,512]{1,0:T(8,128)(2,1)}, bf16[256,512]{1,0:T(8,128)(2,1)S(1)}, u32[]{:S(2)}, u32[]{:S(2)}) collective-permute-start(bf16[256,512]{1,0:T(8,128)(2,1)} %shard_map.56), channel_id=1, source_target_pairs={{4,0},{5,1},{12,2},{13,3},{20,4},{21,5},{28,6},{29,7},{6,8},{7,9},... | collective-permute-start | bytes 786440 | tf_op jit(solution)/shard_map/ppermute | solution.py:41
  48.2 17.6 %collective-permute-start.17 = (bf16[256,512]{1,0:T(8,128)(2,1)}, bf16[256,512]{1,0:T(8,128)(2,1)}, u32[]{:S(2)}, u32[]{:S(2)}) collective-permute-start(bf16[256,512]{1,0:T(8,128)(2,1)} %shard_map.56), channel_id=1, source_target_pairs={{0,0},{1,1},{8,2},{9,3},{16,4},{17,5},{24,6},{25,7},{2,8},{3,9},{1... | collective-permute-start | bytes 786440 | tf_op jit(solution)/shard_map/ppermute | solution.py:41
  55.3 13.4 %collective-permute-start.23 = (bf16[256,512]{1,0:T(8,128)(2,1)}, bf16[256,512]{1,0:T(8,128)(2,1)}, u32[]{:S(2)}, u32[]{:S(2)}) collective-permute-start(bf16[256,512]{1,0:T(8,128)(2,1)} %shard_map.57), channel_id=1, source_target_pairs={{1,0},{0,1},{3,2},{2,3},{5,4},{4,5},{7,6},{6,7},{9,8},{8,9},{11,10... | collective-permute-start | bytes 786440 | tf_op jit(solution)/shard_map/ppermute | solution.py:37
  59.6 1.0 copy-start.1
  61.4 40.5 %copy-start.2 = (bf16[512,512]{1,0:T(8,128)(2,1)S(1)}, bf16[512,512]{1,0:T(8,128)(2,1)}, u32[]{:S(2)}) copy-start(bf16[512,512]{1,0:T(8,128)(2,1)} %copy-done.1) | copy-start | bytes 1572868
  61.6 0.7 copy-start.13
  62.3 26.5 %collective-permute-start.21 = (bf16[512,512]{1,0:T(8,128)(2,1)}, bf16[512,512]{1,0:T(8,128)(2,1)S(1)}, u32[]{:S(2)}, u32[]{:S(2)}) collective-permute-start(bf16[512,512]{1,0:T(8,128)(2,1)} %shard_map.61), channel_id=1, source_target_pairs={{4,0},{5,1},{12,2},{13,3},{20,4},{21,5},{28,6},{29,7},{6,8},{7,9},... | collective-permute-start | bytes 1572872 | tf_op jit(solution)/shard_map/ppermute | solution.py:41
  65.9 27.6 %collective-permute-start.20 = (bf16[512,512]{1,0:T(8,128)(2,1)}, bf16[512,512]{1,0:T(8,128)(2,1)S(1)}, u32[]{:S(2)}, u32[]{:S(2)}) collective-permute-start(bf16[512,512]{1,0:T(8,128)(2,1)} %shard_map.60), channel_id=1, source_target_pairs={{0,0},{1,1},{8,2},{9,3},{16,4},{17,5},{24,6},{25,7},{2,8},{3,9},{1... | collective-permute-start | bytes 1572872 | tf_op jit(solution)/shard_map/ppermute | solution.py:41
  71.3 25.2 %collective-permute-start.19 = (bf16[512,512]{1,0:T(8,128)(2,1)}, bf16[512,512]{1,0:T(8,128)(2,1)S(1)}, u32[]{:S(2)}, u32[]{:S(2)}) collective-permute-start(bf16[512,512]{1,0:T(8,128)(2,1)} %shard_map.59), channel_id=1, source_target_pairs={{4,0},{5,1},{6,2},{7,3},{0,4},{1,5},{2,6},{3,7},{12,8},{13,9},{14,... | collective-permute-start | bytes 1572872 | tf_op jit(solution)/shard_map/ppermute | solution.py:37
  71.3 9.4 %collective-permute-start.24 = (bf16[256,512]{1,0:T(8,128)(2,1)}, bf16[256,512]{1,0:T(8,128)(2,1)S(1)}, u32[]{:S(2)}, u32[]{:S(2)}) collective-permute-start(bf16[256,512]{1,0:T(8,128)(2,1)} %collective-permute-done.17.refs_1_.refs_0_), channel_id=1, source_target_pairs={{1,0},{0,1},{3,2},{2,3},{5,4},{4,5},{7,6},{6,7},{9,8},{8,9},{11,10... | collective-permute-start | bytes 786440 | tf_op jit(solution)/shard_map/ppermute | solution.py:37
  71.8 13.6 %collective-permute-start.25 = (bf16[256,512]{1,0:T(8,128)(2,1)}, bf16[256,512]{1,0:T(8,128)(2,1)S(1)}, u32[]{:S(2)}, u32[]{:S(2)}) collective-permute-start(bf16[256,512]{1,0:T(8,128)(2,1)} %copy-done.13), channel_id=1, source_target_pairs={{1,0},{0,1},{3,2},{2,3},{5,4},{4,5},{7,6},{6,7},{9,8},{8,9},{11,10... | collective-permute-start | bytes 786440 | tf_op jit(solution)/shard_map/ppermute | solution.py:37
  80.6 15.8 %copy-start.9 = (bf16[256,512]{1,0:T(8,128)(2,1)}, bf16[256,512]{1,0:T(8,128)(2,1)S(1)}, u32[]{:S(2)}) copy-start(bf16[256,512]{1,0:T(8,128)(2,1)S(1)} %collective-permute-done.24.refs_2_.refs_1_.refs_0_) | copy-start | bytes 786436
  85.4 11.1 %copy-start.11 = (bf16[256,512]{1,0:T(8,128)(2,1)}, bf16[256,512]{1,0:T(8,128)(2,1)S(1)}, u32[]{:S(2)}) copy-start(bf16[256,512]{1,0:T(8,128)(2,1)S(1)} %collective-permute-done.25.refs_3_.refs_1_) | copy-start | bytes 786436
  88.9 7.6 %copy-start.3 = (bf16[512,512]{1,0:T(8,128)(2,1)}, bf16[512,512]{1,0:T(8,128)(2,1)S(1)}, u32[]{:S(2)}) copy-start(bf16[512,512]{1,0:T(8,128)(2,1)S(1)} %collective-permute-done.21.refs_2_.refs_5_.refs_0_) | copy-start | bytes 1572868
  93.4 3.0 %copy-start.5 = (bf16[512,512]{1,0:T(8,128)(2,1)}, bf16[512,512]{1,0:T(8,128)(2,1)S(1)}, u32[]{:S(2)}) copy-start(bf16[512,512]{1,0:T(8,128)(2,1)S(1)} %collective-permute-done.20.refs_1_.refs_4_.refs_0_) | copy-start | bytes 1572868
  96.5 0.8 copy-start.7
  97.3 8.1 %copy-start.14 = (bf16[256,512]{1,0:T(8,128)(2,1)S(1)}, bf16[256,512]{1,0:T(8,128)(2,1)}, u32[]{:S(2)}) copy-start(bf16[256,512]{1,0:T(8,128)(2,1)} %copy-done.13) | copy-start | bytes 786436
  97.3 4.6 %collective-permute-start.22 = (bf16[512,512]{1,0:T(8,128)(2,1)}, bf16[512,512]{1,0:T(8,128)(2,1)}, u32[]{:S(2)}, u32[]{:S(2)}) collective-permute-start(bf16[512,512]{1,0:T(8,128)(2,1)} %shard_map.62.refs_2_), channel_id=1, source_target_pairs={{2,0},{3,1},{0,2},{1,3},{6,4},{7,5},{4,6},{5,7},{10,8},{11,9},{8,1... | collective-permute-start | bytes 1572872 | tf_op jit(solution)/shard_map/ppermute | solution.py:37
  97.3 10.9 %copy-start.4 = (bf16[512,512]{1,0:T(8,128)(2,1)S(1)}, bf16[512,512]{1,0:T(8,128)(2,1)}, u32[]{:S(2)}) copy-start(bf16[512,512]{1,0:T(8,128)(2,1)} %shard_map.66.refs_1_) | copy-start | bytes 1572868
  97.3 15.6 %collective-permute-start.29 = (bf16[512,512]{1,0:T(8,128)(2,1)}, bf16[512,512]{1,0:T(8,128)(2,1)}, u32[]{:S(2)}, u32[]{:S(2)}) collective-permute-start(bf16[512,512]{1,0:T(8,128)(2,1)} %shard_map.66.refs_1_), channel_id=1, source_target_pairs={{1,0},{0,1},{3,2},{2,3},{5,4},{4,5},{7,6},{6,7},{9,8},{8,9},{11,10... | collective-permute-start | bytes 1572872 | tf_op jit(solution)/shard_map/ppermute | solution.py:37
  98.1 10.1 %copy-start.6 = (bf16[512,512]{1,0:T(8,128)(2,1)S(1)}, bf16[512,512]{1,0:T(8,128)(2,1)}, u32[]{:S(2)}) copy-start(bf16[512,512]{1,0:T(8,128)(2,1)} %shard_map.65.refs_0_) | copy-start | bytes 1572868
  98.1 25.1 %collective-permute-start.28 = (bf16[512,512]{1,0:T(8,128)(2,1)}, bf16[512,512]{1,0:T(8,128)(2,1)}, u32[]{:S(2)}, u32[]{:S(2)}) collective-permute-start(bf16[512,512]{1,0:T(8,128)(2,1)} %shard_map.65.refs_0_), channel_id=1, source_target_pairs={{1,0},{0,1},{3,2},{2,3},{5,4},{4,5},{7,6},{6,7},{9,8},{8,9},{11,10... | collective-permute-start | bytes 1572872 | tf_op jit(solution)/shard_map/ppermute | solution.py:37
  99.4 28.0 %collective-permute-start.26 = (bf16[512,512]{1,0:T(8,128)(2,1)}, bf16[512,512]{1,0:T(8,128)(2,1)S(1)}, u32[]{:S(2)}, u32[]{:S(2)}) collective-permute-start(bf16[512,512]{1,0:T(8,128)(2,1)} %shard_map.64), channel_id=1, source_target_pairs={{0,0},{1,1},{8,2},{9,3},{16,4},{17,5},{24,6},{25,7},{2,8},{3,9},{1... | collective-permute-start | bytes 1572872 | tf_op jit(solution)/shard_map/ppermute | solution.py:41
  101.7 25.7 %collective-permute-start.27 = (bf16[512,512]{1,0:T(8,128)(2,1)}, bf16[512,512]{1,0:T(8,128)(2,1)}, u32[]{:S(2)}, u32[]{:S(2)}) collective-permute-start(bf16[512,512]{1,0:T(8,128)(2,1)} %shard_map.64), channel_id=1, source_target_pairs={{4,0},{5,1},{12,2},{13,3},{20,4},{21,5},{28,6},{29,7},{6,8},{7,9},... | collective-permute-start | bytes 1572872 | tf_op jit(solution)/shard_map/ppermute | solution.py:41
  101.9 1.0 copy-start.8
  102.9 1.0 copy-start.15
  108.1 3.0 %copy-start.10 = (bf16[256,512]{1,0:T(8,128)(2,1)S(1)}, bf16[256,512]{1,0:T(8,128)(2,1)}, u32[]{:S(2)}) copy-start(bf16[256,512]{1,0:T(8,128)(2,1)} %copy-done.9) | copy-start | bytes 786436
  108.2 3.0 %copy-start.12 = (bf16[256,512]{1,0:T(8,128)(2,1)S(1)}, bf16[256,512]{1,0:T(8,128)(2,1)}, u32[]{:S(2)}) copy-start(bf16[256,512]{1,0:T(8,128)(2,1)} %copy-done.11) | copy-start | bytes 786436

commit v6 on v5

--- a/solution.py
+++ b/solution.py
@@ -10,6 +10,7 @@
 AXES = ("prow", "pcol", "pl")
 CORES = 2
 UNITS = 4
+LANES = 128
 LAST = 1
 PROJECT = 48
 MIB = 1024 * 1024
@@ -82,7 +83,7 @@
         in_specs=[pl.BlockSpec(memory_space=pltpu.SMEM)] + [whole] * len(blocks),
         out_specs=whole,
         out_shape=jax.ShapeDtypeStruct(shape, jnp.bfloat16),
-        compiler_params=pltpu.CompilerParams(vmem_limit_bytes=12 * MIB),
+        compiler_params=pltpu.CompilerParams(vmem_limit_bytes=8 * MIB),
         cost_estimate=cheap(),
     )(jnp.stack([row, group]).astype(jnp.int32), *blocks)
 
@@ -92,7 +93,7 @@
 
     @pl.when(pl.program_id(0) == 0)
     def _():
-        strip = min(wide, 256)
+        strip = min(wide, LANES)
         for block, core in ((mine, spots[0]), (theirs, 1 - spots[0])):
             first = pl.multiple_of(core * half, half)
 
@@ -108,22 +109,23 @@
     out[...] = jnp.dot(shapes[...], loads[...], preferred_element_type=jnp.float32).astype(out.dtype)
 
 
-def project(mode_shapes, mine, theirs, scale, core, first, last, tile):
-    modes, wide = mode_shapes.shape[1], 2 * mine.shape[1]
+def project(shapes, mine, theirs, scale, core, span, tile, limit):
+    modes, wide = shapes.shape[1], 2 * mine.shape[1]
+    first, rows = span[0], (span[1] - span[0]) * tile
     whole = pl.BlockSpec(memory_space=pltpu.VMEM)
     return pl.pallas_call(
         project_kernel,
         grid_spec=pltpu.PrefetchScalarGridSpec(
             num_scalar_prefetch=1,
-            grid=(last - first,),
+            grid=(rows // tile,),
             in_specs=[whole] * 3 + [pl.BlockSpec((tile, modes), lambda g, spots: (first + g, 0))],
             out_specs=pl.BlockSpec((tile, wide), lambda g, spots: (g, 0)),
             scratch_shapes=[pltpu.VMEM((modes, wide), jnp.bfloat16)],
         ),
-        out_shape=jax.ShapeDtypeStruct((tile * (last - first), wide), jnp.bfloat16),
-        compiler_params=pltpu.CompilerParams(vmem_limit_bytes=PROJECT * MIB),
-        cost_estimate=cheap(),
-    )(jnp.reshape(core, (1,)).astype(jnp.int32), mine, theirs, scale, mode_shapes)
+        out_shape=jax.ShapeDtypeStruct((rows, wide), jnp.bfloat16),
+        compiler_params=pltpu.CompilerParams(vmem_limit_bytes=(limit if wide <= modes else PROJECT) * MIB),
+        cost_estimate=cheap(),
+    )(jnp.reshape(core, (1,)).astype(jnp.int32), mine, theirs, scale, shapes)
 
 
 def widen_kernel(sets, spots, *refs):
@@ -157,7 +159,7 @@
         in_specs=[pl.BlockSpec(memory_space=pltpu.SMEM)] + [whole] * (len(own) + len(others)),
         out_specs=whole,
         out_shape=jax.ShapeDtypeStruct((rows, wide), jnp.bfloat16),
-        compiler_params=pltpu.CompilerParams(vmem_limit_bytes=12 * MIB),
+        compiler_params=pltpu.CompilerParams(vmem_limit_bytes=8 * MIB),
         cost_estimate=cheap(),
     )(jnp.stack([core, turn]).astype(jnp.int32), *own, *others)
 
@@ -182,7 +184,7 @@
         ),
         out_shape=jax.ShapeDtypeStruct((rows, columns), jnp.float32),
         input_output_aliases={2 + len(pieces): 0} if given else {},
-        compiler_params=pltpu.CompilerParams(vmem_limit_bytes=12 * MIB),
+        compiler_params=pltpu.CompilerParams(vmem_limit_bytes=8 * MIB),
         cost_estimate=cheap(),
     )(jnp.stack(places).astype(jnp.int32), left, *pieces, *given)
 
@@ -193,6 +195,7 @@
     row, col, group = (lax.axis_index(axis) for axis in AXES)
     high, core = col // CORES, col % CORES
     scale = jnp.stack(transfer_pair(natural_freq, damping))[:, :, None]
+    scale = jnp.broadcast_to(scale, scale.shape[:2] + (LANES,))
     own_rows, modes = mode_shapes.shape
 
     part = factor_cols.shape[1] // n_high
@@ -209,8 +212,8 @@
     for part_of, side in ((1, (row // near) ^ 1), (0, row // near)):
         came = swap(partial(1 - core, side).astype(jnp.bfloat16), sizes, 0, 1, 0)
         total = (partial(core, side) + came.astype(jnp.float32)).astype(jnp.bfloat16)
-        for dh in reversed(range(n_high)):
-            for dr in reversed(range(near)):
+        for dh in range(n_high):
+            for dr in range(near):
                 first = ((row ^ dr) % near) * block
                 piece = lax.dynamic_slice(total, (first, (high ^ dh) * part), (block, part))
                 if dh or dr or part_of:
@@ -228,10 +231,9 @@
     unit = max(own_rows // UNITS, min(own_rows, 128))
     units = own_rows // unit
     bounds = (0, 1, units - 1, units) if units > 2 else tuple(range(units + 1))
-    lots = [
-        project(mode_shapes, mine, theirs, scale, core, first, last, unit)
-        for first, last in zip(bounds[:-1], bounds[1:])
-    ]
+    lots = [project(mode_shapes[: bounds[1] * unit], mine, theirs, scale, core, (0, bounds[1]), unit, 14)]
+    for first, last in zip(bounds[1:-1], bounds[2:]):
+        lots.append(project(mode_shapes, mine, theirs, scale, core, (first, last), unit, 14))
     size = own_rows // CORES
     if units == 4:
         sets = (((0, unit), (3 * unit, unit)), ((unit, 2 * unit),))

time: 133 us -> 131 us (0.985)
  Pallas kernels: 29.3 us -> 23.2 us
  local copies, waits for them, and re-layouts: 7.33 us -> 13 us
  waiting for transfers between devices: 46.7 us -> 42.4 us
  starting transfers between devices: 35.8 us -> 38.7 us
    pallas_call x3, Pallas kernels: 10.7 us -> 5.64 us  [project(): pl.pallas_call(project_kernel, grid_spec=pltpu.PrefetchScalarGridSpec(num...]
    unnamed x38 -> x50, local copies, waits for them, and re-layouts: 6.59 us -> 10.9 us
    ppermute x24, waiting for transfers between devices: 36.6 us -> 32.8 us  [swap(): lax.ppermute(array, AXES, moves(sizes, lambda i, j, k: (i ^ di, j ^ dj, k...]
    ppermute x24, starting transfers between devices: 24.8 us -> 27.4 us  [swap(): lax.ppermute(array, AXES, moves(sizes, lambda i, j, k: (i ^ di, j ^ dj, k...]
    slice x0 -> x1, local copies, waits for them, and re-layouts: none -> 1.41 us  [body(): mode_shapes[:bounds[1] * unit]]
  transfers between devices with their start and end apart: 30 -> 30, of which waited for: 16 -> 16; matrix products, arithmetic and copies ran while one was open for 9% -> 10% of each run, Pallas kernels for 15% -> 13%
where the time goes in v6:
time: 131 us; the launch traced here: 130 us
  waiting for transfers between devices  42.4 us (32%)
  starting transfers between devices  38.7 us (30%)
  Pallas kernels  23.2 us (18%)
  local copies, waits for them, and re-layouts  13 us (10%)
  matrix products  9.19 us (7%)
  other arithmetic  2.92 us (2%)
    ppermute x24, waiting for transfers between devices, swap(): lax.ppermute(array, AXES, moves(sizes, lambda i, j, k: (i ^ di, j ^ dj, k...  32.8 us
    ppermute x24, starting transfers between devices, swap(): lax.ppermute(array, AXES, moves(sizes, lambda i, j, k: (i ^ di, j ^ dj, k...  27.4 us
    pallas_call x5, Pallas kernels, place_panel(): pl.pallas_call(functools.partial(panel_kernel, chunk, len(pieces)), grid_...  15.7 us
    ppermute x6, starting transfers between devices, across(): lax.ppermute(array, AXES, moves(sizes, lambda i, j, k: (j, i ^ flip, k)))  11.3 us
    unnamed x50, local copies, waits for them, and re-layouts  10.9 us
    ppermute x6, waiting for transfers between devices, across(): lax.ppermute(array, AXES, moves(sizes, lambda i, j, k: (j, i ^ flip, k)))  9.59 us
    dot_general x4, matrix products, partial(): return jnp.dot(rows, factor_cols, preferred_element_type=jnp.float32)  9.19 us
    pallas_call x3, Pallas kernels, project(): pl.pallas_call(project_kernel, grid_spec=pltpu.PrefetchScalarGridSpec(num...  5.64 us
  transfers between devices with their start and end apart: 30, of which 16 were waited for; matrix products, arithmetic and copies ran while one was open for 10% of the time, Pallas kernels for 13%

profile of v6, /device:TPU:4, one launch (start us, length us, event | category | flops | bytes accessed | tf_op | source)
XLA Modules:
  0.0 129.7 jit_solution(15454935767003370730)
XLA Ops:
  0.0 1.2 copy-done
  1.2 2.3 %fusion.8 = bf16[512,256]{1,0:T(8,128)(2,1)S(1)} fusion(bf16[2048,256]{1,0:T(8,128)(2,1)S(1)} %copy-done, bf16[2048,2048]{1,0:T(8,128)(2,1)} %param.6, s32[]{:T(128)S(6)} %select_n.84), kind=kOutput, calls=%fused_computation.8 | convolution fusion | flops 537001984 | bytes 3407876 | tf_op jit(solution)/shard_map/dot_general | solution.py:209
  3.6 2.3 %fusion.11 = bf16[512,256]{1,0:T(8,128)(2,1)S(1)} fusion(bf16[2048,256]{1,0:T(8,128)(2,1)S(1)} %copy-done, bf16[2048,2048]{1,0:T(8,128)(2,1)} %param.6, s32[]{:T(128)S(6)} %select_n.92), kind=kOutput, calls=%fused_computation.9 | convolution fusion | flops 537001984 | bytes 3407876 | tf_op jit(solution)/shard_map/dot_general | solution.py:209
  5.9 0.5 collective-permute-start.5
  6.5 2.3 %add_convert_fusion.1 = bf16[512,256]{1,0:T(8,128)(2,1)S(1)} fusion(bf16[512,256]{1,0:T(8,128)(2,1)S(1)} %collective-permute-done, bf16[2048,256]{1,0:T(8,128)(2,1)S(1)} %copy-done, bf16[2048,2048]{1,0:T(8,128)(2,1)} %param.6, s32[]{:T(128)S(6)} %select_n.83), kind=kOutput, calls=%fused_computation.13 | convolution fusion | flops 537264128 | bytes 3670020 | tf_op jit(solution)/shard_map/dot_general | solution.py:209
  8.9 2.7 %collective-permute-start.1 = (bf16[256,128]{1,0:T(8,128)(2,1)S(1)}, bf16[256,128]{1,0:T(8,128)(2,1)S(1)}, u32[]{:S(2)}, u32[]{:S(2)}) collective-permute-start(bf16[256,128]{1,0:T(8,128)(2,1)S(1)} %get-tuple-element.8), channel_id=1, source_target_pairs={{16,0},{17,1},{18,2},{19,3},{20,4},{21,5},{22,6},{23,7},{24,8},{25... | collective-permute-start | bytes 196616 | tf_op jit(solution)/shard_map/ppermute | solution.py:38
  11.5 1.3 %collective-permute-start.2 = (bf16[256,128]{1,0:T(8,128)(2,1)S(1)}, bf16[256,128]{1,0:T(8,128)(2,1)S(1)}, u32[]{:S(2)}, u32[]{:S(2)}) collective-permute-start(bf16[256,128]{1,0:T(8,128)(2,1)S(1)} %get-tuple-element.11), channel_id=1, source_target_pairs={{24,0},{25,1},{26,2},{27,3},{28,4},{29,5},{30,6},{31,7},{16,8},{17... | collective-permute-start | bytes 196616 | tf_op jit(solution)/shard_map/ppermute | solution.py:38
  12.9 1.6 %collective-permute-start.3 = (bf16[256,128]{1,0:T(8,128)(2,1)S(1)}, bf16[256,128]{1,0:T(8,128)(2,1)S(1)}, u32[]{:S(2)}, u32[]{:S(2)}) collective-permute-start(bf16[256,128]{1,0:T(8,128)(2,1)S(1)} %get-tuple-element.10), channel_id=1, source_target_pairs={{20,0},{21,1},{22,2},{23,3},{16,4},{17,5},{18,6},{19,7},{28,8},{29... | collective-permute-start | bytes 196616 | tf_op jit(solution)/shard_map/ppermute | solution.py:38
  14.5 1.9 %collective-permute-start.4 = (bf16[256,128]{1,0:T(8,128)(2,1)S(1)}, bf16[256,128]{1,0:T(8,128)(2,1)S(1)}, u32[]{:S(2)}, u32[]{:S(2)}) collective-permute-start(bf16[256,128]{1,0:T(8,128)(2,1)S(1)} %get-tuple-element.9), channel_id=1, source_target_pairs={{28,0},{29,1},{30,2},{31,3},{24,4},{25,5},{26,6},{27,7},{20,8},{21... | collective-permute-start | bytes 196616 | tf_op jit(solution)/shard_map/ppermute | solution.py:38
  16.4 2.3 %add_convert_fusion = bf16[512,256]{1,0:T(8,128)(2,1)S(1)} fusion(bf16[512,256]{1,0:T(8,128)(2,1)S(1)} %collective-permute-done.5, bf16[2048,256]{1,0:T(8,128)(2,1)S(1)} %copy-done, bf16[2048,2048]{1,0:T(8,128)(2,1)} %param.6, s32[]{:T(128)S(6)} %select_n.91), kind=kOutput, calls=%fused_computation.12 | convolution fusion | flops 537264128 | bytes 3670020 | tf_op jit(solution)/shard_map/dot_general | solution.py:209
  18.7 1.0 collective-permute-start.6
  20.2 2.1 %collective-permute-start.8 = (bf16[256,128]{1,0:T(8,128)(2,1)S(1)}, bf16[256,128]{1,0:T(8,128)(2,1)S(1)}, u32[]{:S(2)}, u32[]{:S(2)}) collective-permute-start(bf16[256,128]{1,0:T(8,128)(2,1)S(1)} %get-tuple-element.13), channel_id=1, source_target_pairs={{12,0},{13,1},{14,2},{15,3},{8,4},{9,5},{10,6},{11,7},{4,8},{5,9},... | collective-permute-start | bytes 196616 | tf_op jit(solution)/shard_map/ppermute | solution.py:38
  22.3 0.6 collective-permute-done.3
  22.9 1.2 collective-permute-done.6
  24.1 0.6 collective-permute-done.7
  24.6 0.8 collective-permute-done.8
  25.5 1.6 %collective-permute-start.9 = (bf16[256,128]{1,0:T(8,128)(2,1)S(1)}, bf16[256,128]{1,0:T(8,128)(2,1)S(1)}, u32[]{:S(2)}, u32[]{:S(2)}) collective-permute-start(bf16[256,128]{1,0:T(8,128)(2,1)S(1)} %add_convert_fusion.2.refs_0_), channel_id=1, source_target_pairs={{8,0},{9,1},{10,2},{11,3},{12,4},{13,5},{14,6},{15,7},{0,8},{1,9},... | collective-permute-start | bytes 196616 | tf_op jit(solution)/shard_map/ppermute | solution.py:38
  27.1 2.5 %collective-permute-start.10 = (bf16[256,128]{1,0:T(8,128)(2,1)S(1)}, bf16[256,128]{1,0:T(8,128)(2,1)S(1)}, u32[]{:S(2)}, u32[]{:S(2)}) collective-permute-start(bf16[256,128]{1,0:T(8,128)(2,1)S(1)} %add_convert_fusion.2.refs_0_), channel_id=1, source_target_pairs={{16,0},{17,1},{18,2},{19,3},{20,4},{21,5},{22,6},{23,7},{24,8},{25... | collective-permute-start | bytes 196616 | tf_op jit(solution)/shard_map/ppermute | solution.py:38
  29.6 0.9 collective-permute-start.11
  30.5 1.5 %collective-permute-start.12 = (bf16[256,128]{1,0:T(8,128)(2,1)S(1)}, bf16[256,128]{1,0:T(8,128)(2,1)S(1)}, u32[]{:S(2)}, u32[]{:S(2)}) collective-permute-start(bf16[256,128]{1,0:T(8,128)(2,1)S(1)} %add_convert_fusion.2.refs_0_), channel_id=1, source_target_pairs={{1,0},{0,1},{3,2},{2,3},{5,4},{4,5},{7,6},{6,7},{9,8},{8,9},{11,10... | collective-permute-start | bytes 196616 | tf_op jit(solution)/shard_map/ppermute | solution.py:38
  32.5 1.5 %collective-permute-done.10.refs_2_ = bf16[256,128]{1,0:T(8,128)(2,1)S(1)} collective-permute-done((bf16[256,128]{1,0:T(8,128)(2,1)S(1)}, bf16[256,128]{1,0:T(8,128)(2,1)S(1)}, u32[]{:S(2)}, u32[]{:S(2)}) %collective-permute-start.10) | collective-permute-done | bytes 65568 | tf_op jit(solution)/shard_map/ppermute | solution.py:38
  34.0 1.5 %collective-permute-start.14 = (bf16[256,128]{1,0:T(8,128)(2,1)S(1)}, bf16[256,128]{1,0:T(8,128)(2,1)S(1)}, u32[]{:S(2)}, u32[]{:S(2)}) collective-permute-start(bf16[256,128]{1,0:T(8,128)(2,1)S(1)} %collective-permute-done.10.refs_2_), channel_id=1, source_target_pairs={{1,0},{0,1},{3,2},{2,3},{5,4},{4,5},{7,6},{6,7},{9,8},{8,9},{11,10... | collective-permute-start | bytes 196616 | tf_op jit(solution)/shard_map/ppermute | solution.py:38
  35.7 1.5 %collective-permute-start.15 = (bf16[256,128]{1,0:T(8,128)(2,1)S(1)}, bf16[256,128]{1,0:T(8,128)(2,1)S(1)}, u32[]{:S(2)}, u32[]{:S(2)}) collective-permute-start(bf16[256,128]{1,0:T(8,128)(2,1)S(1)} %collective-permute-done.11.refs_3_), channel_id=1, source_target_pairs={{1,0},{0,1},{3,2},{2,3},{5,4},{4,5},{7,6},{6,7},{9,8},{8,9},{11,10... | collective-permute-start | bytes 196616 | tf_op jit(solution)/shard_map/ppermute | solution.py:38
  37.2 1.0 collective-permute-done.14.refs_6_
  38.3 1.7 %collective-permute-done.15.refs_7_ = bf16[256,128]{1,0:T(8,128)(2,1)S(1)} collective-permute-done((bf16[256,128]{1,0:T(8,128)(2,1)S(1)}, bf16[256,128]{1,0:T(8,128)(2,1)S(1)}, u32[]{:S(2)}, u32[]{:S(2)}) %collective-permute-start.15) | collective-permute-done | bytes 65568 | tf_op jit(solution)/shard_map/ppermute | solution.py:38
  39.9 0.6 shard_map.55.mine
  40.7 1.4 %slice.3.shapes = bf16[256,2048]{1,0:T(8,128)(2,1)S(1)} slice(bf16[1024,2048]{1,0:T(8,128)(2,1)} %shapes.3), slice={[0:256], [0:2048]} | slice | bytes 2097152 | tf_op jit(solution)/shard_map/slice | solution.py:234
  42.6 0.6 broadcast_in_dim.2.scale
  43.2 1.9 %shard_map.56 = bf16[256,512]{1,0:T(8,128)(2,1)} custom-call(s32[1]{0:T(128)} %bitcast.2.spots, bf16[1024,256]{1,0:T(8,128)(2,1)S(1)} %shard_map.55.mine, bf16[1024,256]{1,0:T(8,128)(2,1)S(1)} %collective-permute-done.16.theirs, f32[2,2048,128]{2,1,0:T(8,128)S(1)} %broadcast_in_dim.2.scale, bf16[256,2048]{1,0:T(8,128)(2,1)S(1)} %slice.3.shapes), custom_call_target="tpu_custom_call" | custom-call | flops 1 | bytes 1 | tf_op jit(solution)/shard_map/pallas_call | solution.py:116
  45.0 1.5 %collective-permute-start.18 = (bf16[256,512]{1,0:T(8,128)(2,1)}, bf16[256,512]{1,0:T(8,128)(2,1)S(1)}, u32[]{:S(2)}, u32[]{:S(2)}) collective-permute-start(bf16[256,512]{1,0:T(8,128)(2,1)} %shard_map.56), channel_id=1, source_target_pairs={{4,0},{5,1},{12,2},{13,3},{20,4},{21,5},{28,6},{29,7},{6,8},{7,9},... | collective-permute-start | bytes 786440 | tf_op jit(solution)/shard_map/ppermute | solution.py:42
  46.6 3.1 %collective-permute-start.17 = (bf16[256,512]{1,0:T(8,128)(2,1)}, bf16[256,512]{1,0:T(8,128)(2,1)}, u32[]{:S(2)}, u32[]{:S(2)}) collective-permute-start(bf16[256,512]{1,0:T(8,128)(2,1)} %shard_map.56), channel_id=1, source_target_pairs={{0,0},{1,1},{8,2},{9,3},{16,4},{17,5},{24,6},{25,7},{2,8},{3,9},{1... | collective-permute-start | bytes 786440 | tf_op jit(solution)/shard_map/ppermute | solution.py:42
  49.6 1.9 %shard_map.57 = bf16[256,512]{1,0:T(8,128)(2,1)} custom-call(s32[1]{0:T(128)} %bitcast.2.spots, bf16[1024,256]{1,0:T(8,128)(2,1)S(1)} %shard_map.55.mine, bf16[1024,256]{1,0:T(8,128)(2,1)S(1)} %collective-permute-done.16.theirs, f32[2,2048,128]{2,1,0:T(8,128)S(1)} %broadcast_in_dim.2.scale, bf16[1024,2048]{1,0:T(8,128)(2,1)S(1)} %copy-done.1), custom_call_target="tpu_custom_call" | custom-call | flops 1 | bytes 1 | tf_op jit(solution)/shard_map/pallas_call | solution.py:116
  51.5 1.5 %collective-permute-start.23 = (bf16[256,512]{1,0:T(8,128)(2,1)}, bf16[256,512]{1,0:T(8,128)(2,1)}, u32[]{:S(2)}, u32[]{:S(2)}) collective-permute-start(bf16[256,512]{1,0:T(8,128)(2,1)} %shard_map.57), channel_id=1, source_target_pairs={{1,0},{0,1},{3,2},{2,3},{5,4},{4,5},{7,6},{6,7},{9,8},{8,9},{11,10... | collective-permute-start | bytes 786440 | tf_op jit(solution)/shard_map/ppermute | solution.py:38
  53.0 2.2 %copy-done.2 = bf16[1024,2048]{1,0:T(8,128)(2,1)S(1)} copy-done((bf16[1024,2048]{1,0:T(8,128)(2,1)S(1)}, bf16[1024,2048]{1,0:T(8,128)(2,1)}, u32[]{:S(2)}) %copy-start.2) | copy-done | bytes 4194328
  55.2 1.0 copy-done.10
  56.2 1.0 copy-done.14
  57.3 1.9 %shard_map.58.refs_1_ = bf16[512,512]{1,0:T(8,128)(2,1)S(1)} custom-call(s32[1]{0:T(128)} %bitcast.2.spots, bf16[1024,256]{1,0:T(8,128)(2,1)S(1)} %copy-done.10, bf16[1024,256]{1,0:T(8,128)(2,1)S(1)} %copy-done.14, f32[2,2048,128]{2,1,0:T(8,128)S(1)} %broadcast_in_dim.2.scale, bf16[1024,2048]{1,0:T(8,128)(2,1)S(1)} %copy-done.2), custom_call_target="tpu_custom_call" | custom-call | flops 1 | bytes 1 | tf_op jit(solution)/shard_map/pallas_call | solution.py:116
  59.2 0.8 copy.19.refs_0_
  60.1 0.8 copy.18.refs_0_
  60.9 0.7 copy-done.19
  61.6 1.4 %collective-permute-start.21 = (bf16[512,512]{1,0:T(8,128)(2,1)}, bf16[512,512]{1,0:T(8,128)(2,1)S(1)}, u32[]{:S(2)}, u32[]{:S(2)}) collective-permute-start(bf16[512,512]{1,0:T(8,128)(2,1)} %shard_map.61), channel_id=1, source_target_pairs={{4,0},{5,1},{12,2},{13,3},{20,4},{21,5},{28,6},{29,7},{6,8},{7,9},... | collective-permute-start | bytes 1572872 | tf_op jit(solution)/shard_map/ppermute | solution.py:42
  63.0 1.1 collective-permute-done.17.refs_1_.refs_0_
  64.1 2.9 %collective-permute-start.20 = (bf16[512,512]{1,0:T(8,128)(2,1)}, bf16[512,512]{1,0:T(8,128)(2,1)S(1)}, u32[]{:S(2)}, u32[]{:S(2)}) collective-permute-start(bf16[512,512]{1,0:T(8,128)(2,1)} %shard_map.60), channel_id=1, source_target_pairs={{0,0},{1,1},{8,2},{9,3},{16,4},{17,5},{24,6},{25,7},{2,8},{3,9},{1... | collective-permute-start | bytes 1572872 | tf_op jit(solution)/shard_map/ppermute | solution.py:42
  67.0 2.5 %broadcast_select_fusion = (bf16[512,512]{1,0:T(8,128)(2,1)}, bf16[512,512]{1,0:T(8,128)(2,1)}, bf16[512,512]{1,0:T(8,128)(2,1)}) fusion(bf16[512,512]{1,0:T(8,128)(2,1)} %copy-done.3, pred[]{:T(512)S(6)} %eq.13, bf16[256,512]{1,0:T(8,128)(2,1)} %shard_map.57, bf16[256,512]{1,0:T(8,128)(2,1)} %shard_map.56, bf16[256,512]{1,0:T(8,128)(2,1)} %collective-permute-done.23), kind=kLoop, calls=%fused_computation.14 | loop fusion | flops 2359296 | bytes 2883585 | tf_op jit(solution)/shard_map/jit(_where)/select_n | solution.py:265
  69.5 0.5 collective-permute-start.24
  70.0 1.5 %collective-permute-start.25 = (bf16[256,512]{1,0:T(8,128)(2,1)}, bf16[256,512]{1,0:T(8,128)(2,1)S(1)}, u32[]{:S(2)}, u32[]{:S(2)}) collective-permute-start(bf16[256,512]{1,0:T(8,128)(2,1)} %copy-done.19), channel_id=1, source_target_pairs={{1,0},{0,1},{3,2},{2,3},{5,4},{4,5},{7,6},{6,7},{9,8},{8,9},{11,10... | collective-permute-start | bytes 786440 | tf_op jit(solution)/shard_map/ppermute | solution.py:38
  71.5 7.3 %collective-permute-done.24.refs_2_.refs_1_.refs_0_ = bf16[256,512]{1,0:T(8,128)(2,1)S(1)} collective-permute-done((bf16[256,512]{1,0:T(8,128)(2,1)}, bf16[256,512]{1,0:T(8,128)(2,1)S(1)}, u32[]{:S(2)}, u32[]{:S(2)}) %collective-permute-start.24) | collective-permute-done | bytes 262176 | tf_op jit(solution)/shard_map/ppermute | solution.py:38
  78.9 4.8 %collective-permute-done.25.refs_3_.refs_1_ = bf16[256,512]{1,0:T(8,128)(2,1)S(1)} collective-permute-done((bf16[256,512]{1,0:T(8,128)(2,1)}, bf16[256,512]{1,0:T(8,128)(2,1)S(1)}, u32[]{:S(2)}, u32[]{:S(2)}) %collective-permute-start.25) | collective-permute-done | bytes 262176 | tf_op jit(solution)/shard_map/ppermute | solution.py:38
  83.6 4.3 %collective-permute-done.21.refs_2_.refs_5_.refs_0_ = bf16[512,512]{1,0:T(8,128)(2,1)S(1)} collective-permute-done((bf16[512,512]{1,0:T(8,128)(2,1)}, bf16[512,512]{1,0:T(8,128)(2,1)S(1)}, u32[]{:S(2)}, u32[]{:S(2)}) %collective-permute-start.21) | collective-permute-done | bytes 524320 | tf_op jit(solution)/shard_map/ppermute | solution.py:42
  87.9 4.2 %collective-permute-done.20.refs_1_.refs_4_.refs_0_ = bf16[512,512]{1,0:T(8,128)(2,1)S(1)} collective-permute-done((bf16[512,512]{1,0:T(8,128)(2,1)}, bf16[512,512]{1,0:T(8,128)(2,1)S(1)}, u32[]{:S(2)}, u32[]{:S(2)}) %collective-permute-start.20) | collective-permute-done | bytes 524320 | tf_op jit(solution)/shard_map/ppermute | solution.py:42
  92.2 2.5 %collective-permute-done.19.refs_0_.refs_1_ = bf16[512,512]{1,0:T(8,128)(2,1)S(1)} collective-permute-done((bf16[512,512]{1,0:T(8,128)(2,1)}, bf16[512,512]{1,0:T(8,128)(2,1)S(1)}, u32[]{:S(2)}, u32[]{:S(2)}) %collective-permute-start.19) | collective-permute-done | bytes 524320 | tf_op jit(solution)/shard_map/ppermute | solution.py:38
  94.7 0.8 copy-done.11
  95.5 0.8 collective-permute-start.29
  96.3 1.3 %collective-permute-start.28 = (bf16[512,512]{1,0:T(8,128)(2,1)}, bf16[512,512]{1,0:T(8,128)(2,1)}, u32[]{:S(2)}, u32[]{:S(2)}) collective-permute-start(bf16[512,512]{1,0:T(8,128)(2,1)} %shard_map.65.refs_0_), channel_id=1, source_target_pairs={{1,0},{0,1},{3,2},{2,3},{5,4},{4,5},{7,6},{6,7},{9,8},{8,9},{11,10... | collective-permute-start | bytes 1572872 | tf_op jit(solution)/shard_map/ppermute | solution.py:38
  97.6 2.4 %collective-permute-start.26 = (bf16[512,512]{1,0:T(8,128)(2,1)}, bf16[512,512]{1,0:T(8,128)(2,1)S(1)}, u32[]{:S(2)}, u32[]{:S(2)}) collective-permute-start(bf16[512,512]{1,0:T(8,128)(2,1)} %shard_map.64), channel_id=1, source_target_pairs={{0,0},{1,1},{8,2},{9,3},{16,4},{17,5},{24,6},{25,7},{2,8},{3,9},{1... | collective-permute-start | bytes 1572872 | tf_op jit(solution)/shard_map/ppermute | solution.py:42
  100.3 1.0 copy-done.12
  101.3 1.0 copy-done.21
  102.4 1.2 shard_map.63.left
  103.6 2.7 %shard_map.67.refs_2_ = f32[1024,2048]{1,0:T(8,128)} custom-call(s32[1]{0:T(128)} %bitcast.13.spots, bf16[1024,1024]{1,0:T(8,128)(2,1)S(1)} %shard_map.63.left, bf16[256,512]{1,0:T(8,128)(2,1)} %collective-permute-done.17.refs_1_.refs_0_, bf16[256,512]{1,0:T(8,128)(2,1)S(1)} %copy-done.20), custom_call_target="tpu_custom_call" | custom-call | flops 1 | bytes 1 | tf_op jit(solution)/shard_map/pallas_call | solution.py:177
  106.4 3.0 %shard_map.68.refs_2_ = f32[1024,2048]{1,0:T(8,128)} custom-call(s32[2]{0:T(128)S(1)} %pad_add_fusion.4.spots, bf16[1024,1024]{1,0:T(8,128)(2,1)S(1)} %shard_map.63.left, bf16[512,512]{1,0:T(8,128)(2,1)S(1)} %copy-done.8, bf16[512,512]{1,0:T(8,128)(2,1)S(1)} %copy-done.6, f32[1024,2048]{1,0:T(8,128)} %shard_map.67.refs_2_), custom_call_target="tpu_custom_call", output_to_operand_aliasing={{}: (4, {})} | custom-call | flops 1 | bytes 1 | tf_op jit(solution)/shard_map/pallas_call | solution.py:177
  109.4 1.7 %shard_map.69.refs_2_ = f32[1024,2048]{1,0:T(8,128)} custom-call(s32[1]{0:T(128)} %bitcast.10.spots, bf16[1024,1024]{1,0:T(8,128)(2,1)S(1)} %shard_map.63.left, bf16[256,512]{1,0:T(8,128)(2,1)S(1)} %copy-done.16, bf16[256,512]{1,0:T(8,128)(2,1)S(1)} %copy-done.18, f32[1024,2048]{1,0:T(8,128)} %shard_map.68.refs_2_), custom_call_target="tpu_custom_call", output_to_operand_aliasing={{}: (4, {})} | custom-call | flops 1 | bytes 1 | tf_op jit(solution)/shard_map/pallas_call | solution.py:177
  111.1 10.3 %collective-permute-done.28.refs_0_ = bf16[512,512]{1,0:T(8,128)(2,1)} collective-permute-done((bf16[512,512]{1,0:T(8,128)(2,1)}, bf16[512,512]{1,0:T(8,128)(2,1)}, u32[]{:S(2)}, u32[]{:S(2)}) %collective-permute-start.28) | collective-permute-done | bytes 524320 | tf_op jit(solution)/shard_map/ppermute | solution.py:38
  121.4 4.2 %shard_map.70.refs_2_ = f32[1024,2048]{1,0:T(8,128)} custom-call(s32[2]{0:T(128)S(1)} %pad_add_fusion.3.spots, bf16[1024,1024]{1,0:T(8,128)(2,1)S(1)} %shard_map.63.left, bf16[512,512]{1,0:T(8,128)(2,1)} %collective-permute-done.28.refs_0_, bf16[512,512]{1,0:T(8,128)(2,1)} %collective-permute-done.29.refs_1_, ...), custom_call_target="tpu_custom_call", output_to_operand_aliasing={{}: (4, {})} | custom-call | flops 1 | bytes 1 | tf_op jit(solution)/shard_map/pallas_call | solution.py:177
  125.6 4.1 %shard_map.71 = f32[1024,2048]{1,0:T(8,128)} custom-call(s32[2]{0:T(128)S(1)} %get-tuple-element.17.spots, bf16[1024,1024]{1,0:T(8,128)(2,1)S(1)} %shard_map.63.left, bf16[512,512]{1,0:T(8,128)(2,1)S(1)} %collective-permute-done.26.refs_0_, bf16[512,512]{1,0:T(8,128)(2,1)} %collective-permute-done.27.refs_1_, ...), custom_call_target="tpu_custom_call", output_to_operand_aliasing={{}: (4, {})} | custom-call | flops 1 | bytes 1 | tf_op jit(solution)/shard_map/pallas_call | solution.py:177
  (79 shorter events, 2.6 us)
Async XLA Ops:
  0.0 1.2 copy-start
  3.5 3.0 %collective-permute-start = (bf16[512,256]{1,0:T(8,128)(2,1)S(1)}, bf16[512,256]{1,0:T(8,128)(2,1)S(1)}, u32[]{:S(2)}, u32[]{:S(2)}) collective-permute-start(bf16[512,256]{1,0:T(8,128)(2,1)S(1)} %fusion.8), channel_id=1, source_target_pairs={{2,0},{3,1},{0,2},{1,3},{6,4},{7,5},{4,6},{5,7},{10,8},{11,9},{8,1... | collective-permute-start | bytes 786440 | tf_op jit(solution)/shard_map/ppermute | solution.py:38
  5.9 36.1 %copy-start.22 = (f32[2048]{0:T(1024)S(1)}, f32[2048]{0:T(1024)}, u32[]{:S(2)}) copy-start(f32[2048]{0:T(1024)} %param.8) | copy-start | bytes 24580
  5.9 36.1 %copy-start.23 = (f32[2048]{0:T(1024)S(1)}, f32[2048]{0:T(1024)}, u32[]{:S(2)}) copy-start(f32[2048]{0:T(1024)} %param.9) | copy-start | bytes 24580
  5.9 10.4 %collective-permute-start.5 = (bf16[512,256]{1,0:T(8,128)(2,1)S(1)}, bf16[512,256]{1,0:T(8,128)(2,1)S(1)}, u32[]{:S(2)}, u32[]{:S(2)}) collective-permute-start(bf16[512,256]{1,0:T(8,128)(2,1)S(1)} %fusion.11), channel_id=1, source_target_pairs={{2,0},{3,1},{0,2},{1,3},{6,4},{7,5},{4,6},{5,7},{10,8},{11,9},{8,1... | collective-permute-start | bytes 786440 | tf_op jit(solution)/shard_map/ppermute | solution.py:38
  8.9 10.8 %collective-permute-start.1 = (bf16[256,128]{1,0:T(8,128)(2,1)S(1)}, bf16[256,128]{1,0:T(8,128)(2,1)S(1)}, u32[]{:S(2)}, u32[]{:S(2)}) collective-permute-start(bf16[256,128]{1,0:T(8,128)(2,1)S(1)} %get-tuple-element.8), channel_id=1, source_target_pairs={{16,0},{17,1},{18,2},{19,3},{20,4},{21,5},{22,6},{23,7},{24,8},{25... | collective-permute-start | bytes 196616 | tf_op jit(solution)/shard_map/ppermute | solution.py:38
  11.5 8.7 %collective-permute-start.2 = (bf16[256,128]{1,0:T(8,128)(2,1)S(1)}, bf16[256,128]{1,0:T(8,128)(2,1)S(1)}, u32[]{:S(2)}, u32[]{:S(2)}) collective-permute-start(bf16[256,128]{1,0:T(8,128)(2,1)S(1)} %get-tuple-element.11), channel_id=1, source_target_pairs={{24,0},{25,1},{26,2},{27,3},{28,4},{29,5},{30,6},{31,7},{16,8},{17... | collective-permute-start | bytes 196616 | tf_op jit(solution)/shard_map/ppermute | solution.py:38
  12.9 10.0 %collective-permute-start.3 = (bf16[256,128]{1,0:T(8,128)(2,1)S(1)}, bf16[256,128]{1,0:T(8,128)(2,1)S(1)}, u32[]{:S(2)}, u32[]{:S(2)}) collective-permute-start(bf16[256,128]{1,0:T(8,128)(2,1)S(1)} %get-tuple-element.10), channel_id=1, source_target_pairs={{20,0},{21,1},{22,2},{23,3},{16,4},{17,5},{18,6},{19,7},{28,8},{29... | collective-permute-start | bytes 196616 | tf_op jit(solution)/shard_map/ppermute | solution.py:38
  14.5 8.4 %collective-permute-start.4 = (bf16[256,128]{1,0:T(8,128)(2,1)S(1)}, bf16[256,128]{1,0:T(8,128)(2,1)S(1)}, u32[]{:S(2)}, u32[]{:S(2)}) collective-permute-start(bf16[256,128]{1,0:T(8,128)(2,1)S(1)} %get-tuple-element.9), channel_id=1, source_target_pairs={{28,0},{29,1},{30,2},{31,3},{24,4},{25,5},{26,6},{27,7},{20,8},{21... | collective-permute-start | bytes 196616 | tf_op jit(solution)/shard_map/ppermute | solution.py:38
  18.7 5.3 %collective-permute-start.6 = (bf16[256,128]{1,0:T(8,128)(2,1)S(1)}, bf16[256,128]{1,0:T(8,128)(2,1)S(1)}, u32[]{:S(2)}, u32[]{:S(2)}) collective-permute-start(bf16[256,128]{1,0:T(8,128)(2,1)S(1)} %get-tuple-element.12), channel_id=1, source_target_pairs={{8,0},{9,1},{10,2},{11,3},{12,4},{13,5},{14,6},{15,7},{0,8},{1,9},... | collective-permute-start | bytes 196616 | tf_op jit(solution)/shard_map/ppermute | solution.py:38
  19.7 4.9 %collective-permute-start.7 = (bf16[256,128]{1,0:T(8,128)(2,1)S(1)}, bf16[256,128]{1,0:T(8,128)(2,1)S(1)}, u32[]{:S(2)}, u32[]{:S(2)}) collective-permute-start(bf16[256,128]{1,0:T(8,128)(2,1)S(1)} %get-tuple-element.14), channel_id=1, source_target_pairs={{4,0},{5,1},{6,2},{7,3},{0,4},{1,5},{2,6},{3,7},{12,8},{13,9},{14,... | collective-permute-start | bytes 196616 | tf_op jit(solution)/shard_map/ppermute | solution.py:38
  20.2 5.2 %collective-permute-start.8 = (bf16[256,128]{1,0:T(8,128)(2,1)S(1)}, bf16[256,128]{1,0:T(8,128)(2,1)S(1)}, u32[]{:S(2)}, u32[]{:S(2)}) collective-permute-start(bf16[256,128]{1,0:T(8,128)(2,1)S(1)} %get-tuple-element.13), channel_id=1, source_target_pairs={{12,0},{13,1},{14,2},{15,3},{8,4},{9,5},{10,6},{11,7},{4,8},{5,9},... | collective-permute-start | bytes 196616 | tf_op jit(solution)/shard_map/ppermute | solution.py:38
  25.5 6.5 %collective-permute-start.9 = (bf16[256,128]{1,0:T(8,128)(2,1)S(1)}, bf16[256,128]{1,0:T(8,128)(2,1)S(1)}, u32[]{:S(2)}, u32[]{:S(2)}) collective-permute-start(bf16[256,128]{1,0:T(8,128)(2,1)S(1)} %add_convert_fusion.2.refs_0_), channel_id=1, source_target_pairs={{8,0},{9,1},{10,2},{11,3},{12,4},{13,5},{14,6},{15,7},{0,8},{1,9},... | collective-permute-start | bytes 196616 | tf_op jit(solution)/shard_map/ppermute | solution.py:38
  27.1 6.9 %collective-permute-start.10 = (bf16[256,128]{1,0:T(8,128)(2,1)S(1)}, bf16[256,128]{1,0:T(8,128)(2,1)S(1)}, u32[]{:S(2)}, u32[]{:S(2)}) collective-permute-start(bf16[256,128]{1,0:T(8,128)(2,1)S(1)} %add_convert_fusion.2.refs_0_), channel_id=1, source_target_pairs={{16,0},{17,1},{18,2},{19,3},{20,4},{21,5},{22,6},{23,7},{24,8},{25... | collective-permute-start | bytes 196616 | tf_op jit(solution)/shard_map/ppermute | solution.py:38
  29.6 6.1 %collective-permute-start.11 = (bf16[256,128]{1,0:T(8,128)(2,1)S(1)}, bf16[256,128]{1,0:T(8,128)(2,1)S(1)}, u32[]{:S(2)}, u32[]{:S(2)}) collective-permute-start(bf16[256,128]{1,0:T(8,128)(2,1)S(1)} %add_convert_fusion.2.refs_0_), channel_id=1, source_target_pairs={{24,0},{25,1},{26,2},{27,3},{28,4},{29,5},{30,6},{31,7},{16,8},{17... | collective-permute-start | bytes 196616 | tf_op jit(solution)/shard_map/ppermute | solution.py:38
  30.5 19.1 %copy-start.1 = (bf16[1024,2048]{1,0:T(8,128)(2,1)S(1)}, bf16[1024,2048]{1,0:T(8,128)(2,1)}, u32[]{:S(2)}) copy-start(bf16[1024,2048]{1,0:T(8,128)(2,1)} %shapes.3) | copy-start | bytes 12582916
  30.5 6.7 %collective-permute-start.12 = (bf16[256,128]{1,0:T(8,128)(2,1)S(1)}, bf16[256,128]{1,0:T(8,128)(2,1)S(1)}, u32[]{:S(2)}, u32[]{:S(2)}) collective-permute-start(bf16[256,128]{1,0:T(8,128)(2,1)S(1)} %add_convert_fusion.2.refs_0_), channel_id=1, source_target_pairs={{1,0},{0,1},{3,2},{2,3},{5,4},{4,5},{7,6},{6,7},{9,8},{8,9},{11,10... | collective-permute-start | bytes 196616 | tf_op jit(solution)/shard_map/ppermute | solution.py:38
  32.0 5.2 %collective-permute-start.13 = (bf16[256,128]{1,0:T(8,128)(2,1)S(1)}, bf16[256,128]{1,0:T(8,128)(2,1)S(1)}, u32[]{:S(2)}, u32[]{:S(2)}) collective-permute-start(bf16[256,128]{1,0:T(8,128)(2,1)S(1)} %collective-permute-done.9.refs_1_), channel_id=1, source_target_pairs={{1,0},{0,1},{3,2},{2,3},{5,4},{4,5},{7,6},{6,7},{9,8},{8,9},{11,10... | collective-permute-start | bytes 196616 | tf_op jit(solution)/shard_map/ppermute | solution.py:38
  34.0 4.3 %collective-permute-start.14 = (bf16[256,128]{1,0:T(8,128)(2,1)S(1)}, bf16[256,128]{1,0:T(8,128)(2,1)S(1)}, u32[]{:S(2)}, u32[]{:S(2)}) collective-permute-start(bf16[256,128]{1,0:T(8,128)(2,1)S(1)} %collective-permute-done.10.refs_2_), channel_id=1, source_target_pairs={{1,0},{0,1},{3,2},{2,3},{5,4},{4,5},{7,6},{6,7},{9,8},{8,9},{11,10... | collective-permute-start | bytes 196616 | tf_op jit(solution)/shard_map/ppermute | solution.py:38
  35.7 4.3 %collective-permute-start.15 = (bf16[256,128]{1,0:T(8,128)(2,1)S(1)}, bf16[256,128]{1,0:T(8,128)(2,1)S(1)}, u32[]{:S(2)}, u32[]{:S(2)}) collective-permute-start(bf16[256,128]{1,0:T(8,128)(2,1)S(1)} %collective-permute-done.11.refs_3_), channel_id=1, source_target_pairs={{1,0},{0,1},{3,2},{2,3},{5,4},{4,5},{7,6},{6,7},{9,8},{8,9},{11,10... | collective-permute-start | bytes 196616 | tf_op jit(solution)/shard_map/ppermute | solution.py:38
  40.6 10.9 %copy-start.9 = (bf16[1024,256]{1,0:T(8,128)(2,1)}, bf16[1024,256]{1,0:T(8,128)(2,1)S(1)}, u32[]{:S(2)}) copy-start(bf16[1024,256]{1,0:T(8,128)(2,1)S(1)} %shard_map.55.mine) | copy-start | bytes 1572868
  40.6 2.0 %collective-permute-start.16 = (bf16[1024,256]{1,0:T(8,128)(2,1)S(1)}, bf16[1024,256]{1,0:T(8,128)(2,1)S(1)}, u32[]{:S(2)}, u32[]{:S(2)}) collective-permute-start(bf16[1024,256]{1,0:T(8,128)(2,1)S(1)} %shard_map.55.mine), channel_id=1, source_target_pairs={{2,0},{3,1},{0,2},{1,3},{6,4},{7,5},{4,6},{5,7},{10,8},{11,9},{8,1... | collective-permute-start | bytes 1572872 | tf_op jit(solution)/shard_map/ppermute | solution.py:38
  42.6 8.9 %copy-start.13 = (bf16[1024,256]{1,0:T(8,128)(2,1)}, bf16[1024,256]{1,0:T(8,128)(2,1)S(1)}, u32[]{:S(2)}) copy-start(bf16[1024,256]{1,0:T(8,128)(2,1)S(1)} %collective-permute-done.16.theirs) | copy-start | bytes 1572868
  45.0 15.9 %collective-permute-start.18 = (bf16[256,512]{1,0:T(8,128)(2,1)}, bf16[256,512]{1,0:T(8,128)(2,1)S(1)}, u32[]{:S(2)}, u32[]{:S(2)}) collective-permute-start(bf16[256,512]{1,0:T(8,128)(2,1)} %shard_map.56), channel_id=1, source_target_pairs={{4,0},{5,1},{12,2},{13,3},{20,4},{21,5},{28,6},{29,7},{6,8},{7,9},... | collective-permute-start | bytes 786440 | tf_op jit(solution)/shard_map/ppermute | solution.py:42
  46.6 17.5 %collective-permute-start.17 = (bf16[256,512]{1,0:T(8,128)(2,1)}, bf16[256,512]{1,0:T(8,128)(2,1)}, u32[]{:S(2)}, u32[]{:S(2)}) collective-permute-start(bf16[256,512]{1,0:T(8,128)(2,1)} %shard_map.56), channel_id=1, source_target_pairs={{0,0},{1,1},{8,2},{9,3},{16,4},{17,5},{24,6},{25,7},{2,8},{3,9},{1... | collective-permute-start | bytes 786440 | tf_op jit(solution)/shard_map/ppermute | solution.py:42
  51.5 15.4 %collective-permute-start.23 = (bf16[256,512]{1,0:T(8,128)(2,1)}, bf16[256,512]{1,0:T(8,128)(2,1)}, u32[]{:S(2)}, u32[]{:S(2)}) collective-permute-start(bf16[256,512]{1,0:T(8,128)(2,1)} %shard_map.57), channel_id=1, source_target_pairs={{1,0},{0,1},{3,2},{2,3},{5,4},{4,5},{7,6},{6,7},{9,8},{8,9},{11,10... | collective-permute-start | bytes 786440 | tf_op jit(solution)/shard_map/ppermute | solution.py:38
  53.0 2.2 %copy-start.2 = (bf16[1024,2048]{1,0:T(8,128)(2,1)S(1)}, bf16[1024,2048]{1,0:T(8,128)(2,1)}, u32[]{:S(2)}) copy-start(bf16[1024,2048]{1,0:T(8,128)(2,1)} %shapes.3) | copy-start | bytes 12582916
  55.2 1.0 copy-start.10
  56.2 1.0 copy-start.14
  59.2 1.0 copy-start.3
  60.9 39.4 %copy-start.4 = (bf16[512,512]{1,0:T(8,128)(2,1)S(1)}, bf16[512,512]{1,0:T(8,128)(2,1)}, u32[]{:S(2)}) copy-start(bf16[512,512]{1,0:T(8,128)(2,1)} %copy-done.3) | copy-start | bytes 1572868
  60.9 0.7 copy-start.19
  61.6 26.3 %collective-permute-start.21 = (bf16[512,512]{1,0:T(8,128)(2,1)}, bf16[512,512]{1,0:T(8,128)(2,1)S(1)}, u32[]{:S(2)}, u32[]{:S(2)}) collective-permute-start(bf16[512,512]{1,0:T(8,128)(2,1)} %shard_map.61), channel_id=1, source_target_pairs={{4,0},{5,1},{12,2},{13,3},{20,4},{21,5},{28,6},{29,7},{6,8},{7,9},... | collective-permute-start | bytes 1572872 | tf_op jit(solution)/shard_map/ppermute | solution.py:42
  64.1 28.1 %collective-permute-start.20 = (bf16[512,512]{1,0:T(8,128)(2,1)}, bf16[512,512]{1,0:T(8,128)(2,1)S(1)}, u32[]{:S(2)}, u32[]{:S(2)}) collective-permute-start(bf16[512,512]{1,0:T(8,128)(2,1)} %shard_map.60), channel_id=1, source_target_pairs={{0,0},{1,1},{8,2},{9,3},{16,4},{17,5},{24,6},{25,7},{2,8},{3,9},{1... | collective-permute-start | bytes 1572872 | tf_op jit(solution)/shard_map/ppermute | solution.py:42
  69.5 25.2 %collective-permute-start.19 = (bf16[512,512]{1,0:T(8,128)(2,1)}, bf16[512,512]{1,0:T(8,128)(2,1)S(1)}, u32[]{:S(2)}, u32[]{:S(2)}) collective-permute-start(bf16[512,512]{1,0:T(8,128)(2,1)} %shard_map.59), channel_id=1, source_target_pairs={{4,0},{5,1},{6,2},{7,3},{0,4},{1,5},{2,6},{3,7},{12,8},{13,9},{14,... | collective-permute-start | bytes 1572872 | tf_op jit(solution)/shard_map/ppermute | solution.py:38
  69.5 9.4 %collective-permute-start.24 = (bf16[256,512]{1,0:T(8,128)(2,1)}, bf16[256,512]{1,0:T(8,128)(2,1)S(1)}, u32[]{:S(2)}, u32[]{:S(2)}) collective-permute-start(bf16[256,512]{1,0:T(8,128)(2,1)} %collective-permute-done.17.refs_1_.refs_0_), channel_id=1, source_target_pairs={{1,0},{0,1},{3,2},{2,3},{5,4},{4,5},{7,6},{6,7},{9,8},{8,9},{11,10... | collective-permute-start | bytes 786440 | tf_op jit(solution)/shard_map/ppermute | solution.py:38
  70.0 13.6 %collective-permute-start.25 = (bf16[256,512]{1,0:T(8,128)(2,1)}, bf16[256,512]{1,0:T(8,128)(2,1)S(1)}, u32[]{:S(2)}, u32[]{:S(2)}) collective-permute-start(bf16[256,512]{1,0:T(8,128)(2,1)} %copy-done.19), channel_id=1, source_target_pairs={{1,0},{0,1},{3,2},{2,3},{5,4},{4,5},{7,6},{6,7},{9,8},{8,9},{11,10... | collective-permute-start | bytes 786440 | tf_op jit(solution)/shard_map/ppermute | solution.py:38
  78.9 15.8 %copy-start.15 = (bf16[256,512]{1,0:T(8,128)(2,1)}, bf16[256,512]{1,0:T(8,128)(2,1)S(1)}, u32[]{:S(2)}) copy-start(bf16[256,512]{1,0:T(8,128)(2,1)S(1)} %collective-permute-done.24.refs_2_.refs_1_.refs_0_) | copy-start | bytes 786436
  83.6 11.0 %copy-start.17 = (bf16[256,512]{1,0:T(8,128)(2,1)}, bf16[256,512]{1,0:T(8,128)(2,1)S(1)}, u32[]{:S(2)}) copy-start(bf16[256,512]{1,0:T(8,128)(2,1)S(1)} %collective-permute-done.25.refs_3_.refs_1_) | copy-start | bytes 786436
  87.9 6.8 %copy-start.5 = (bf16[512,512]{1,0:T(8,128)(2,1)}, bf16[512,512]{1,0:T(8,128)(2,1)S(1)}, u32[]{:S(2)}) copy-start(bf16[512,512]{1,0:T(8,128)(2,1)S(1)} %collective-permute-done.21.refs_2_.refs_5_.refs_0_) | copy-start | bytes 1572868
  92.1 2.5 %copy-start.7 = (bf16[512,512]{1,0:T(8,128)(2,1)}, bf16[512,512]{1,0:T(8,128)(2,1)S(1)}, u32[]{:S(2)}) copy-start(bf16[512,512]{1,0:T(8,128)(2,1)S(1)} %collective-permute-done.20.refs_1_.refs_4_.refs_0_) | copy-start | bytes 1572868
  94.7 0.8 copy-start.11
  95.5 8.1 %copy-start.20 = (bf16[256,512]{1,0:T(8,128)(2,1)S(1)}, bf16[256,512]{1,0:T(8,128)(2,1)}, u32[]{:S(2)}) copy-start(bf16[256,512]{1,0:T(8,128)(2,1)} %copy-done.19) | copy-start | bytes 786436
  95.5 4.8 %collective-permute-start.22 = (bf16[512,512]{1,0:T(8,128)(2,1)}, bf16[512,512]{1,0:T(8,128)(2,1)}, u32[]{:S(2)}, u32[]{:S(2)}) collective-permute-start(bf16[512,512]{1,0:T(8,128)(2,1)} %shard_map.62.refs_2_), channel_id=1, source_target_pairs={{2,0},{3,1},{0,2},{1,3},{6,4},{7,5},{4,6},{5,7},{10,8},{11,9},{8,1... | collective-permute-start | bytes 1572872 | tf_op jit(solution)/shard_map/ppermute | solution.py:38
  95.5 10.8 %copy-start.6 = (bf16[512,512]{1,0:T(8,128)(2,1)S(1)}, bf16[512,512]{1,0:T(8,128)(2,1)}, u32[]{:S(2)}) copy-start(bf16[512,512]{1,0:T(8,128)(2,1)} %shard_map.66.refs_1_) | copy-start | bytes 1572868
  95.5 15.6 %collective-permute-start.29 = (bf16[512,512]{1,0:T(8,128)(2,1)}, bf16[512,512]{1,0:T(8,128)(2,1)}, u32[]{:S(2)}, u32[]{:S(2)}) collective-permute-start(bf16[512,512]{1,0:T(8,128)(2,1)} %shard_map.66.refs_1_), channel_id=1, source_target_pairs={{1,0},{0,1},{3,2},{2,3},{5,4},{4,5},{7,6},{6,7},{9,8},{8,9},{11,10... | collective-permute-start | bytes 1572872 | tf_op jit(solution)/shard_map/ppermute | solution.py:38
  96.3 10.1 %copy-start.8 = (bf16[512,512]{1,0:T(8,128)(2,1)S(1)}, bf16[512,512]{1,0:T(8,128)(2,1)}, u32[]{:S(2)}) copy-start(bf16[512,512]{1,0:T(8,128)(2,1)} %shard_map.65.refs_0_) | copy-start | bytes 1572868
  96.3 25.1 %collective-permute-start.28 = (bf16[512,512]{1,0:T(8,128)(2,1)}, bf16[512,512]{1,0:T(8,128)(2,1)}, u32[]{:S(2)}, u32[]{:S(2)}) collective-permute-start(bf16[512,512]{1,0:T(8,128)(2,1)} %shard_map.65.refs_0_), channel_id=1, source_target_pairs={{1,0},{0,1},{3,2},{2,3},{5,4},{4,5},{7,6},{6,7},{9,8},{8,9},{11,10... | collective-permute-start | bytes 1572872 | tf_op jit(solution)/shard_map/ppermute | solution.py:38
  97.6 28.0 %collective-permute-start.26 = (bf16[512,512]{1,0:T(8,128)(2,1)}, bf16[512,512]{1,0:T(8,128)(2,1)S(1)}, u32[]{:S(2)}, u32[]{:S(2)}) collective-permute-start(bf16[512,512]{1,0:T(8,128)(2,1)} %shard_map.64), channel_id=1, source_target_pairs={{0,0},{1,1},{8,2},{9,3},{16,4},{17,5},{24,6},{25,7},{2,8},{3,9},{1... | collective-permute-start | bytes 1572872 | tf_op jit(solution)/shard_map/ppermute | solution.py:42
  100.0 25.6 %collective-permute-start.27 = (bf16[512,512]{1,0:T(8,128)(2,1)}, bf16[512,512]{1,0:T(8,128)(2,1)}, u32[]{:S(2)}, u32[]{:S(2)}) collective-permute-start(bf16[512,512]{1,0:T(8,128)(2,1)} %shard_map.64), channel_id=1, source_target_pairs={{4,0},{5,1},{12,2},{13,3},{20,4},{21,5},{28,6},{29,7},{6,8},{7,9},... | collective-permute-start | bytes 1572872 | tf_op jit(solution)/shard_map/ppermute | solution.py:42
  100.3 1.0 copy-start.12
  101.3 1.0 copy-start.21
  106.4 3.0 %copy-start.16 = (bf16[256,512]{1,0:T(8,128)(2,1)S(1)}, bf16[256,512]{1,0:T(8,128)(2,1)}, u32[]{:S(2)}) copy-start(bf16[256,512]{1,0:T(8,128)(2,1)} %copy-done.15) | copy-start | bytes 786436
  106.4 3.0 %copy-start.18 = (bf16[256,512]{1,0:T(8,128)(2,1)S(1)}, bf16[256,512]{1,0:T(8,128)(2,1)}, u32[]{:S(2)}) copy-start(bf16[256,512]{1,0:T(8,128)(2,1)} %copy-done.17) | copy-start | bytes 786436

commit v7 on v6

--- a/solution.py
+++ b/solution.py
@@ -164,9 +164,8 @@
     )(jnp.stack([core, turn]).astype(jnp.int32), *own, *others)
 
 
-def panel_kernel(chunk, count, spots, left, *refs):
-    first = pl.multiple_of(pl.program_id(0) * chunk, chunk)
-    right = jnp.concatenate([piece[pl.ds(first, chunk), :] for piece in refs[:count]], axis=1)
+def panel_kernel(count, spots, left, *refs):
+    right = jnp.concatenate([piece[...] for piece in refs[:count]], axis=1)
     refs[-1][...] = outer_rows(left[...], right)
 
 
@@ -175,11 +174,13 @@
     given = [] if panel is None else [panel]
     whole = pl.BlockSpec(memory_space=pltpu.VMEM)
     return pl.pallas_call(
-        functools.partial(panel_kernel, chunk, len(pieces)),
+        functools.partial(panel_kernel, len(pieces)),
         grid_spec=pltpu.PrefetchScalarGridSpec(
             num_scalar_prefetch=1,
             grid=(len(places),),
-            in_specs=[whole] * (1 + len(pieces)) + [pl.BlockSpec(memory_space=pl.ANY) for _ in given],
+            in_specs=[whole]
+            + [pl.BlockSpec((chunk, piece.shape[1]), lambda g, spots: (g, 0)) for piece in pieces]
+            + [pl.BlockSpec(memory_space=pl.ANY) for _ in given],
             out_specs=pl.BlockSpec((rows, chunk), lambda g, spots: (0, spots[g])),
         ),
         out_shape=jax.ShapeDtypeStruct((rows, columns), jnp.float32),

time: 131 us -> 131 us (level)
  no operation moved by 1% of the time
where the time goes in v7:
time: 131 us; the launch traced here: 129 us
  waiting for transfers between devices  42.4 us (32%)
  starting transfers between devices  38.7 us (30%)
  Pallas kernels  23 us (18%)
  local copies, waits for them, and re-layouts  13 us (10%)
  matrix products  9.19 us (7%)
  other arithmetic  2.92 us (2%)
    ppermute x24, waiting for transfers between devices, swap(): lax.ppermute(array, AXES, moves(sizes, lambda i, j, k: (i ^ di, j ^ dj, k...  32.8 us
    ppermute x24, starting transfers between devices, swap(): lax.ppermute(array, AXES, moves(sizes, lambda i, j, k: (i ^ di, j ^ dj, k...  27.4 us
    pallas_call x5, Pallas kernels, place_panel(): pl.pallas_call(functools.partial(panel_kernel, len(pieces)), grid_spec=pl...  15.5 us
    ppermute x6, starting transfers between devices, across(): lax.ppermute(array, AXES, moves(sizes, lambda i, j, k: (j, i ^ flip, k)))  11.3 us
    unnamed x50, local copies, waits for them, and re-layouts  10.9 us
    ppermute x6, waiting for transfers between devices, across(): lax.ppermute(array, AXES, moves(sizes, lambda i, j, k: (j, i ^ flip, k)))  9.59 us
    dot_general x4, matrix products, partial(): return jnp.dot(rows, factor_cols, preferred_element_type=jnp.float32)  9.19 us
    pallas_call x3, Pallas kernels, project(): pl.pallas_call(project_kernel, grid_spec=pltpu.PrefetchScalarGridSpec(num...  5.64 us
  transfers between devices with their start and end apart: 30, of which 16 were waited for; matrix products, arithmetic and copies ran while one was open for 10% of the time, Pallas kernels for 13%

profile of v7, /device:TPU:4, one launch (start us, length us, event | category | flops | bytes accessed | tf_op | source)
XLA Modules:
  0.0 129.5 jit_solution(12607689273403949701)
XLA Ops:
  0.0 1.2 copy-done
  1.2 2.3 %fusion.8 = bf16[512,256]{1,0:T(8,128)(2,1)S(1)} fusion(bf16[2048,256]{1,0:T(8,128)(2,1)S(1)} %copy-done, bf16[2048,2048]{1,0:T(8,128)(2,1)} %param.6, s32[]{:T(128)S(6)} %select_n.84), kind=kOutput, calls=%fused_computation.8 | convolution fusion | flops 537001984 | bytes 3407876 | tf_op jit(solution)/shard_map/dot_general | solution.py:210
  3.6 2.3 %fusion.11 = bf16[512,256]{1,0:T(8,128)(2,1)S(1)} fusion(bf16[2048,256]{1,0:T(8,128)(2,1)S(1)} %copy-done, bf16[2048,2048]{1,0:T(8,128)(2,1)} %param.6, s32[]{:T(128)S(6)} %select_n.92), kind=kOutput, calls=%fused_computation.9 | convolution fusion | flops 537001984 | bytes 3407876 | tf_op jit(solution)/shard_map/dot_general | solution.py:210
  5.9 0.5 collective-permute-start.5
  6.5 2.3 %add_convert_fusion.1 = bf16[512,256]{1,0:T(8,128)(2,1)S(1)} fusion(bf16[512,256]{1,0:T(8,128)(2,1)S(1)} %collective-permute-done, bf16[2048,256]{1,0:T(8,128)(2,1)S(1)} %copy-done, bf16[2048,2048]{1,0:T(8,128)(2,1)} %param.6, s32[]{:T(128)S(6)} %select_n.83), kind=kOutput, calls=%fused_computation.13 | convolution fusion | flops 537264128 | bytes 3670020 | tf_op jit(solution)/shard_map/dot_general | solution.py:210
  8.9 2.7 %collective-permute-start.1 = (bf16[256,128]{1,0:T(8,128)(2,1)S(1)}, bf16[256,128]{1,0:T(8,128)(2,1)S(1)}, u32[]{:S(2)}, u32[]{:S(2)}) collective-permute-start(bf16[256,128]{1,0:T(8,128)(2,1)S(1)} %get-tuple-element.8), channel_id=1, source_target_pairs={{16,0},{17,1},{18,2},{19,3},{20,4},{21,5},{22,6},{23,7},{24,8},{25... | collective-permute-start | bytes 196616 | tf_op jit(solution)/shard_map/ppermute | solution.py:38
  11.5 1.3 %collective-permute-start.2 = (bf16[256,128]{1,0:T(8,128)(2,1)S(1)}, bf16[256,128]{1,0:T(8,128)(2,1)S(1)}, u32[]{:S(2)}, u32[]{:S(2)}) collective-permute-start(bf16[256,128]{1,0:T(8,128)(2,1)S(1)} %get-tuple-element.11), channel_id=1, source_target_pairs={{24,0},{25,1},{26,2},{27,3},{28,4},{29,5},{30,6},{31,7},{16,8},{17... | collective-permute-start | bytes 196616 | tf_op jit(solution)/shard_map/ppermute | solution.py:38
  12.9 1.6 %collective-permute-start.3 = (bf16[256,128]{1,0:T(8,128)(2,1)S(1)}, bf16[256,128]{1,0:T(8,128)(2,1)S(1)}, u32[]{:S(2)}, u32[]{:S(2)}) collective-permute-start(bf16[256,128]{1,0:T(8,128)(2,1)S(1)} %get-tuple-element.10), channel_id=1, source_target_pairs={{20,0},{21,1},{22,2},{23,3},{16,4},{17,5},{18,6},{19,7},{28,8},{29... | collective-permute-start | bytes 196616 | tf_op jit(solution)/shard_map/ppermute | solution.py:38
  14.5 1.9 %collective-permute-start.4 = (bf16[256,128]{1,0:T(8,128)(2,1)S(1)}, bf16[256,128]{1,0:T(8,128)(2,1)S(1)}, u32[]{:S(2)}, u32[]{:S(2)}) collective-permute-start(bf16[256,128]{1,0:T(8,128)(2,1)S(1)} %get-tuple-element.9), channel_id=1, source_target_pairs={{28,0},{29,1},{30,2},{31,3},{24,4},{25,5},{26,6},{27,7},{20,8},{21... | collective-permute-start | bytes 196616 | tf_op jit(solution)/shard_map/ppermute | solution.py:38
  16.4 2.3 %add_convert_fusion = bf16[512,256]{1,0:T(8,128)(2,1)S(1)} fusion(bf16[512,256]{1,0:T(8,128)(2,1)S(1)} %collective-permute-done.5, bf16[2048,256]{1,0:T(8,128)(2,1)S(1)} %copy-done, bf16[2048,2048]{1,0:T(8,128)(2,1)} %param.6, s32[]{:T(128)S(6)} %select_n.91), kind=kOutput, calls=%fused_computation.12 | convolution fusion | flops 537264128 | bytes 3670020 | tf_op jit(solution)/shard_map/dot_general | solution.py:210
  18.7 1.0 collective-permute-start.6
  20.2 2.1 %collective-permute-start.8 = (bf16[256,128]{1,0:T(8,128)(2,1)S(1)}, bf16[256,128]{1,0:T(8,128)(2,1)S(1)}, u32[]{:S(2)}, u32[]{:S(2)}) collective-permute-start(bf16[256,128]{1,0:T(8,128)(2,1)S(1)} %get-tuple-element.13), channel_id=1, source_target_pairs={{12,0},{13,1},{14,2},{15,3},{8,4},{9,5},{10,6},{11,7},{4,8},{5,9},... | collective-permute-start | bytes 196616 | tf_op jit(solution)/shard_map/ppermute | solution.py:38
  22.3 0.6 collective-permute-done.3
  22.9 1.2 collective-permute-done.6
  24.1 0.6 collective-permute-done.7
  24.6 0.8 collective-permute-done.8
  25.5 1.6 %collective-permute-start.9 = (bf16[256,128]{1,0:T(8,128)(2,1)S(1)}, bf16[256,128]{1,0:T(8,128)(2,1)S(1)}, u32[]{:S(2)}, u32[]{:S(2)}) collective-permute-start(bf16[256,128]{1,0:T(8,128)(2,1)S(1)} %add_convert_fusion.2.refs_0_), channel_id=1, source_target_pairs={{8,0},{9,1},{10,2},{11,3},{12,4},{13,5},{14,6},{15,7},{0,8},{1,9},... | collective-permute-start | bytes 196616 | tf_op jit(solution)/shard_map/ppermute | solution.py:38
  27.1 2.5 %collective-permute-start.10 = (bf16[256,128]{1,0:T(8,128)(2,1)S(1)}, bf16[256,128]{1,0:T(8,128)(2,1)S(1)}, u32[]{:S(2)}, u32[]{:S(2)}) collective-permute-start(bf16[256,128]{1,0:T(8,128)(2,1)S(1)} %add_convert_fusion.2.refs_0_), channel_id=1, source_target_pairs={{16,0},{17,1},{18,2},{19,3},{20,4},{21,5},{22,6},{23,7},{24,8},{25... | collective-permute-start | bytes 196616 | tf_op jit(solution)/shard_map/ppermute | solution.py:38
  29.6 0.9 collective-permute-start.11
  30.5 1.5 %collective-permute-start.12 = (bf16[256,128]{1,0:T(8,128)(2,1)S(1)}, bf16[256,128]{1,0:T(8,128)(2,1)S(1)}, u32[]{:S(2)}, u32[]{:S(2)}) collective-permute-start(bf16[256,128]{1,0:T(8,128)(2,1)S(1)} %add_convert_fusion.2.refs_0_), channel_id=1, source_target_pairs={{1,0},{0,1},{3,2},{2,3},{5,4},{4,5},{7,6},{6,7},{9,8},{8,9},{11,10... | collective-permute-start | bytes 196616 | tf_op jit(solution)/shard_map/ppermute | solution.py:38
  32.5 1.5 %collective-permute-done.10.refs_2_ = bf16[256,128]{1,0:T(8,128)(2,1)S(1)} collective-permute-done((bf16[256,128]{1,0:T(8,128)(2,1)S(1)}, bf16[256,128]{1,0:T(8,128)(2,1)S(1)}, u32[]{:S(2)}, u32[]{:S(2)}) %collective-permute-start.10) | collective-permute-done | bytes 65568 | tf_op jit(solution)/shard_map/ppermute | solution.py:38
  34.0 1.5 %collective-permute-start.14 = (bf16[256,128]{1,0:T(8,128)(2,1)S(1)}, bf16[256,128]{1,0:T(8,128)(2,1)S(1)}, u32[]{:S(2)}, u32[]{:S(2)}) collective-permute-start(bf16[256,128]{1,0:T(8,128)(2,1)S(1)} %collective-permute-done.10.refs_2_), channel_id=1, source_target_pairs={{1,0},{0,1},{3,2},{2,3},{5,4},{4,5},{7,6},{6,7},{9,8},{8,9},{11,10... | collective-permute-start | bytes 196616 | tf_op jit(solution)/shard_map/ppermute | solution.py:38
  35.7 1.5 %collective-permute-start.15 = (bf16[256,128]{1,0:T(8,128)(2,1)S(1)}, bf16[256,128]{1,0:T(8,128)(2,1)S(1)}, u32[]{:S(2)}, u32[]{:S(2)}) collective-permute-start(bf16[256,128]{1,0:T(8,128)(2,1)S(1)} %collective-permute-done.11.refs_3_), channel_id=1, source_target_pairs={{1,0},{0,1},{3,2},{2,3},{5,4},{4,5},{7,6},{6,7},{9,8},{8,9},{11,10... | collective-permute-start | bytes 196616 | tf_op jit(solution)/shard_map/ppermute | solution.py:38
  37.2 1.0 collective-permute-done.14.refs_6_
  38.3 1.7 %collective-permute-done.15.refs_7_ = bf16[256,128]{1,0:T(8,128)(2,1)S(1)} collective-permute-done((bf16[256,128]{1,0:T(8,128)(2,1)S(1)}, bf16[256,128]{1,0:T(8,128)(2,1)S(1)}, u32[]{:S(2)}, u32[]{:S(2)}) %collective-permute-start.15) | collective-permute-done | bytes 65568 | tf_op jit(solution)/shard_map/ppermute | solution.py:38
  39.9 0.6 shard_map.55.mine
  40.7 1.4 %slice.3.shapes = bf16[256,2048]{1,0:T(8,128)(2,1)S(1)} slice(bf16[1024,2048]{1,0:T(8,128)(2,1)} %shapes.3), slice={[0:256], [0:2048]} | slice | bytes 2097152 | tf_op jit(solution)/shard_map/slice | solution.py:235
  42.6 0.6 broadcast_in_dim.2.scale
  43.2 1.9 %shard_map.56 = bf16[256,512]{1,0:T(8,128)(2,1)} custom-call(s32[1]{0:T(128)} %bitcast.2.spots, bf16[1024,256]{1,0:T(8,128)(2,1)S(1)} %shard_map.55.mine, bf16[1024,256]{1,0:T(8,128)(2,1)S(1)} %collective-permute-done.16.theirs, f32[2,2048,128]{2,1,0:T(8,128)S(1)} %broadcast_in_dim.2.scale, bf16[256,2048]{1,0:T(8,128)(2,1)S(1)} %slice.3.shapes), custom_call_target="tpu_custom_call" | custom-call | flops 1 | bytes 1 | tf_op jit(solution)/shard_map/pallas_call | solution.py:116
  45.0 1.5 %collective-permute-start.18 = (bf16[256,512]{1,0:T(8,128)(2,1)}, bf16[256,512]{1,0:T(8,128)(2,1)S(1)}, u32[]{:S(2)}, u32[]{:S(2)}) collective-permute-start(bf16[256,512]{1,0:T(8,128)(2,1)} %shard_map.56), channel_id=1, source_target_pairs={{4,0},{5,1},{12,2},{13,3},{20,4},{21,5},{28,6},{29,7},{6,8},{7,9},... | collective-permute-start | bytes 786440 | tf_op jit(solution)/shard_map/ppermute | solution.py:42
  46.6 3.1 %collective-permute-start.17 = (bf16[256,512]{1,0:T(8,128)(2,1)}, bf16[256,512]{1,0:T(8,128)(2,1)}, u32[]{:S(2)}, u32[]{:S(2)}) collective-permute-start(bf16[256,512]{1,0:T(8,128)(2,1)} %shard_map.56), channel_id=1, source_target_pairs={{0,0},{1,1},{8,2},{9,3},{16,4},{17,5},{24,6},{25,7},{2,8},{3,9},{1... | collective-permute-start | bytes 786440 | tf_op jit(solution)/shard_map/ppermute | solution.py:42
  49.6 1.9 %shard_map.57 = bf16[256,512]{1,0:T(8,128)(2,1)} custom-call(s32[1]{0:T(128)} %bitcast.2.spots, bf16[1024,256]{1,0:T(8,128)(2,1)S(1)} %shard_map.55.mine, bf16[1024,256]{1,0:T(8,128)(2,1)S(1)} %collective-permute-done.16.theirs, f32[2,2048,128]{2,1,0:T(8,128)S(1)} %broadcast_in_dim.2.scale, bf16[1024,2048]{1,0:T(8,128)(2,1)S(1)} %copy-done.1), custom_call_target="tpu_custom_call" | custom-call | flops 1 | bytes 1 | tf_op jit(solution)/shard_map/pallas_call | solution.py:116
  51.5 1.5 %collective-permute-start.23 = (bf16[256,512]{1,0:T(8,128)(2,1)}, bf16[256,512]{1,0:T(8,128)(2,1)}, u32[]{:S(2)}, u32[]{:S(2)}) collective-permute-start(bf16[256,512]{1,0:T(8,128)(2,1)} %shard_map.57), channel_id=1, source_target_pairs={{1,0},{0,1},{3,2},{2,3},{5,4},{4,5},{7,6},{6,7},{9,8},{8,9},{11,10... | collective-permute-start | bytes 786440 | tf_op jit(solution)/shard_map/ppermute | solution.py:38
  53.0 2.2 %copy-done.2 = bf16[1024,2048]{1,0:T(8,128)(2,1)S(1)} copy-done((bf16[1024,2048]{1,0:T(8,128)(2,1)S(1)}, bf16[1024,2048]{1,0:T(8,128)(2,1)}, u32[]{:S(2)}) %copy-start.2) | copy-done | bytes 4194328
  55.2 1.0 copy-done.10
  56.2 1.0 copy-done.14
  57.3 1.9 %shard_map.58.refs_1_ = bf16[512,512]{1,0:T(8,128)(2,1)S(1)} custom-call(s32[1]{0:T(128)} %bitcast.2.spots, bf16[1024,256]{1,0:T(8,128)(2,1)S(1)} %copy-done.10, bf16[1024,256]{1,0:T(8,128)(2,1)S(1)} %copy-done.14, f32[2,2048,128]{2,1,0:T(8,128)S(1)} %broadcast_in_dim.2.scale, bf16[1024,2048]{1,0:T(8,128)(2,1)S(1)} %copy-done.2), custom_call_target="tpu_custom_call" | custom-call | flops 1 | bytes 1 | tf_op jit(solution)/shard_map/pallas_call | solution.py:116
  59.2 0.8 copy.19.refs_0_
  60.1 0.8 copy.18.refs_0_
  60.9 0.7 copy-done.19
  61.6 1.4 %collective-permute-start.21 = (bf16[512,512]{1,0:T(8,128)(2,1)}, bf16[512,512]{1,0:T(8,128)(2,1)S(1)}, u32[]{:S(2)}, u32[]{:S(2)}) collective-permute-start(bf16[512,512]{1,0:T(8,128)(2,1)} %shard_map.61), channel_id=1, source_target_pairs={{4,0},{5,1},{12,2},{13,3},{20,4},{21,5},{28,6},{29,7},{6,8},{7,9},... | collective-permute-start | bytes 1572872 | tf_op jit(solution)/shard_map/ppermute | solution.py:42
  63.0 1.1 collective-permute-done.17.refs_1_.refs_0_
  64.1 2.9 %collective-permute-start.20 = (bf16[512,512]{1,0:T(8,128)(2,1)}, bf16[512,512]{1,0:T(8,128)(2,1)S(1)}, u32[]{:S(2)}, u32[]{:S(2)}) collective-permute-start(bf16[512,512]{1,0:T(8,128)(2,1)} %shard_map.60), channel_id=1, source_target_pairs={{0,0},{1,1},{8,2},{9,3},{16,4},{17,5},{24,6},{25,7},{2,8},{3,9},{1... | collective-permute-start | bytes 1572872 | tf_op jit(solution)/shard_map/ppermute | solution.py:42
  67.0 2.5 %broadcast_select_fusion = (bf16[512,512]{1,0:T(8,128)(2,1)}, bf16[512,512]{1,0:T(8,128)(2,1)}, bf16[512,512]{1,0:T(8,128)(2,1)}) fusion(bf16[512,512]{1,0:T(8,128)(2,1)} %copy-done.3, pred[]{:T(512)S(6)} %eq.13, bf16[256,512]{1,0:T(8,128)(2,1)} %shard_map.57, bf16[256,512]{1,0:T(8,128)(2,1)} %shard_map.56, bf16[256,512]{1,0:T(8,128)(2,1)} %collective-permute-done.23), kind=kLoop, calls=%fused_computation.14 | loop fusion | flops 2359296 | bytes 2883585 | tf_op jit(solution)/shard_map/jit(_where)/select_n | solution.py:266
  69.5 0.5 collective-permute-start.24
  70.0 1.5 %collective-permute-start.25 = (bf16[256,512]{1,0:T(8,128)(2,1)}, bf16[256,512]{1,0:T(8,128)(2,1)S(1)}, u32[]{:S(2)}, u32[]{:S(2)}) collective-permute-start(bf16[256,512]{1,0:T(8,128)(2,1)} %copy-done.19), channel_id=1, source_target_pairs={{1,0},{0,1},{3,2},{2,3},{5,4},{4,5},{7,6},{6,7},{9,8},{8,9},{11,10... | collective-permute-start | bytes 786440 | tf_op jit(solution)/shard_map/ppermute | solution.py:38
  71.5 7.3 %collective-permute-done.24.refs_2_.refs_1_.refs_0_ = bf16[256,512]{1,0:T(8,128)(2,1)S(1)} collective-permute-done((bf16[256,512]{1,0:T(8,128)(2,1)}, bf16[256,512]{1,0:T(8,128)(2,1)S(1)}, u32[]{:S(2)}, u32[]{:S(2)}) %collective-permute-start.24) | collective-permute-done | bytes 262176 | tf_op jit(solution)/shard_map/ppermute | solution.py:38
  78.9 4.8 %collective-permute-done.25.refs_3_.refs_1_ = bf16[256,512]{1,0:T(8,128)(2,1)S(1)} collective-permute-done((bf16[256,512]{1,0:T(8,128)(2,1)}, bf16[256,512]{1,0:T(8,128)(2,1)S(1)}, u32[]{:S(2)}, u32[]{:S(2)}) %collective-permute-start.25) | collective-permute-done | bytes 262176 | tf_op jit(solution)/shard_map/ppermute | solution.py:38
  83.6 4.3 %collective-permute-done.21.refs_2_.refs_5_.refs_0_ = bf16[512,512]{1,0:T(8,128)(2,1)S(1)} collective-permute-done((bf16[512,512]{1,0:T(8,128)(2,1)}, bf16[512,512]{1,0:T(8,128)(2,1)S(1)}, u32[]{:S(2)}, u32[]{:S(2)}) %collective-permute-start.21) | collective-permute-done | bytes 524320 | tf_op jit(solution)/shard_map/ppermute | solution.py:42
  87.9 4.2 %collective-permute-done.20.refs_1_.refs_4_.refs_0_ = bf16[512,512]{1,0:T(8,128)(2,1)S(1)} collective-permute-done((bf16[512,512]{1,0:T(8,128)(2,1)}, bf16[512,512]{1,0:T(8,128)(2,1)S(1)}, u32[]{:S(2)}, u32[]{:S(2)}) %collective-permute-start.20) | collective-permute-done | bytes 524320 | tf_op jit(solution)/shard_map/ppermute | solution.py:42
  92.2 2.5 %collective-permute-done.19.refs_0_.refs_1_ = bf16[512,512]{1,0:T(8,128)(2,1)S(1)} collective-permute-done((bf16[512,512]{1,0:T(8,128)(2,1)}, bf16[512,512]{1,0:T(8,128)(2,1)S(1)}, u32[]{:S(2)}, u32[]{:S(2)}) %collective-permute-start.19) | collective-permute-done | bytes 524320 | tf_op jit(solution)/shard_map/ppermute | solution.py:38
  94.7 0.8 copy-done.11
  95.5 0.8 collective-permute-start.29
  96.3 1.3 %collective-permute-start.28 = (bf16[512,512]{1,0:T(8,128)(2,1)}, bf16[512,512]{1,0:T(8,128)(2,1)}, u32[]{:S(2)}, u32[]{:S(2)}) collective-permute-start(bf16[512,512]{1,0:T(8,128)(2,1)} %shard_map.65.refs_0_), channel_id=1, source_target_pairs={{1,0},{0,1},{3,2},{2,3},{5,4},{4,5},{7,6},{6,7},{9,8},{8,9},{11,10... | collective-permute-start | bytes 1572872 | tf_op jit(solution)/shard_map/ppermute | solution.py:38
  97.6 2.4 %collective-permute-start.26 = (bf16[512,512]{1,0:T(8,128)(2,1)}, bf16[512,512]{1,0:T(8,128)(2,1)S(1)}, u32[]{:S(2)}, u32[]{:S(2)}) collective-permute-start(bf16[512,512]{1,0:T(8,128)(2,1)} %shard_map.64), channel_id=1, source_target_pairs={{0,0},{1,1},{8,2},{9,3},{16,4},{17,5},{24,6},{25,7},{2,8},{3,9},{1... | collective-permute-start | bytes 1572872 | tf_op jit(solution)/shard_map/ppermute | solution.py:42
  100.3 1.0 copy-done.12
  101.3 1.0 copy-done.21
  102.4 1.2 shard_map.63.left
  103.6 2.7 %shard_map.67.refs_2_ = f32[1024,2048]{1,0:T(8,128)} custom-call(s32[1]{0:T(128)} %bitcast.13.spots, bf16[1024,1024]{1,0:T(8,128)(2,1)S(1)} %shard_map.63.left, bf16[256,512]{1,0:T(8,128)(2,1)} %collective-permute-done.17.refs_1_.refs_0_, bf16[256,512]{1,0:T(8,128)(2,1)S(1)} %copy-done.20), custom_call_target="tpu_custom_call" | custom-call | flops 1 | bytes 1 | tf_op jit(solution)/shard_map/pallas_call | solution.py:176
  106.4 3.0 %shard_map.68.refs_2_ = f32[1024,2048]{1,0:T(8,128)} custom-call(s32[2]{0:T(128)S(1)} %pad_add_fusion.4.spots, bf16[1024,1024]{1,0:T(8,128)(2,1)S(1)} %shard_map.63.left, bf16[512,512]{1,0:T(8,128)(2,1)S(1)} %copy-done.8, bf16[512,512]{1,0:T(8,128)(2,1)S(1)} %copy-done.6, f32[1024,2048]{1,0:T(8,128)} %shard_map.67.refs_2_), custom_call_target="tpu_custom_call", output_to_operand_aliasing={{}: (4, {})} | custom-call | flops 1 | bytes 1 | tf_op jit(solution)/shard_map/pallas_call | solution.py:176
  109.4 1.7 %shard_map.69.refs_2_ = f32[1024,2048]{1,0:T(8,128)} custom-call(s32[1]{0:T(128)} %bitcast.10.spots, bf16[1024,1024]{1,0:T(8,128)(2,1)S(1)} %shard_map.63.left, bf16[256,512]{1,0:T(8,128)(2,1)S(1)} %copy-done.16, bf16[256,512]{1,0:T(8,128)(2,1)S(1)} %copy-done.18, f32[1024,2048]{1,0:T(8,128)} %shard_map.68.refs_2_), custom_call_target="tpu_custom_call", output_to_operand_aliasing={{}: (4, {})} | custom-call | flops 1 | bytes 1 | tf_op jit(solution)/shard_map/pallas_call | solution.py:176
  111.1 10.3 %collective-permute-done.28.refs_0_ = bf16[512,512]{1,0:T(8,128)(2,1)} collective-permute-done((bf16[512,512]{1,0:T(8,128)(2,1)}, bf16[512,512]{1,0:T(8,128)(2,1)}, u32[]{:S(2)}, u32[]{:S(2)}) %collective-permute-start.28) | collective-permute-done | bytes 524320 | tf_op jit(solution)/shard_map/ppermute | solution.py:38
  121.4 4.1 %shard_map.70.refs_2_ = f32[1024,2048]{1,0:T(8,128)} custom-call(s32[2]{0:T(128)S(1)} %pad_add_fusion.3.spots, bf16[1024,1024]{1,0:T(8,128)(2,1)S(1)} %shard_map.63.left, bf16[512,512]{1,0:T(8,128)(2,1)} %collective-permute-done.28.refs_0_, bf16[512,512]{1,0:T(8,128)(2,1)} %collective-permute-done.29.refs_1_, ...), custom_call_target="tpu_custom_call", output_to_operand_aliasing={{}: (4, {})} | custom-call | flops 1 | bytes 1 | tf_op jit(solution)/shard_map/pallas_call | solution.py:176
  125.5 4.0 %shard_map.71 = f32[1024,2048]{1,0:T(8,128)} custom-call(s32[2]{0:T(128)S(1)} %get-tuple-element.17.spots, bf16[1024,1024]{1,0:T(8,128)(2,1)S(1)} %shard_map.63.left, bf16[512,512]{1,0:T(8,128)(2,1)S(1)} %collective-permute-done.26.refs_0_, bf16[512,512]{1,0:T(8,128)(2,1)} %collective-permute-done.27.refs_1_, ...), custom_call_target="tpu_custom_call", output_to_operand_aliasing={{}: (4, {})} | custom-call | flops 1 | bytes 1 | tf_op jit(solution)/shard_map/pallas_call | solution.py:176
  (79 shorter events, 2.6 us)
Async XLA Ops:
  0.0 1.2 copy-start
  3.5 3.0 %collective-permute-start = (bf16[512,256]{1,0:T(8,128)(2,1)S(1)}, bf16[512,256]{1,0:T(8,128)(2,1)S(1)}, u32[]{:S(2)}, u32[]{:S(2)}) collective-permute-start(bf16[512,256]{1,0:T(8,128)(2,1)S(1)} %fusion.8), channel_id=1, source_target_pairs={{2,0},{3,1},{0,2},{1,3},{6,4},{7,5},{4,6},{5,7},{10,8},{11,9},{8,1... | collective-permute-start | bytes 786440 | tf_op jit(solution)/shard_map/ppermute | solution.py:38
  5.9 36.1 %copy-start.22 = (f32[2048]{0:T(1024)S(1)}, f32[2048]{0:T(1024)}, u32[]{:S(2)}) copy-start(f32[2048]{0:T(1024)} %param.8) | copy-start | bytes 24580
  5.9 36.1 %copy-start.23 = (f32[2048]{0:T(1024)S(1)}, f32[2048]{0:T(1024)}, u32[]{:S(2)}) copy-start(f32[2048]{0:T(1024)} %param.9) | copy-start | bytes 24580
  5.9 10.4 %collective-permute-start.5 = (bf16[512,256]{1,0:T(8,128)(2,1)S(1)}, bf16[512,256]{1,0:T(8,128)(2,1)S(1)}, u32[]{:S(2)}, u32[]{:S(2)}) collective-permute-start(bf16[512,256]{1,0:T(8,128)(2,1)S(1)} %fusion.11), channel_id=1, source_target_pairs={{2,0},{3,1},{0,2},{1,3},{6,4},{7,5},{4,6},{5,7},{10,8},{11,9},{8,1... | collective-permute-start | bytes 786440 | tf_op jit(solution)/shard_map/ppermute | solution.py:38
  8.9 10.8 %collective-permute-start.1 = (bf16[256,128]{1,0:T(8,128)(2,1)S(1)}, bf16[256,128]{1,0:T(8,128)(2,1)S(1)}, u32[]{:S(2)}, u32[]{:S(2)}) collective-permute-start(bf16[256,128]{1,0:T(8,128)(2,1)S(1)} %get-tuple-element.8), channel_id=1, source_target_pairs={{16,0},{17,1},{18,2},{19,3},{20,4},{21,5},{22,6},{23,7},{24,8},{25... | collective-permute-start | bytes 196616 | tf_op jit(solution)/shard_map/ppermute | solution.py:38
  11.5 8.7 %collective-permute-start.2 = (bf16[256,128]{1,0:T(8,128)(2,1)S(1)}, bf16[256,128]{1,0:T(8,128)(2,1)S(1)}, u32[]{:S(2)}, u32[]{:S(2)}) collective-permute-start(bf16[256,128]{1,0:T(8,128)(2,1)S(1)} %get-tuple-element.11), channel_id=1, source_target_pairs={{24,0},{25,1},{26,2},{27,3},{28,4},{29,5},{30,6},{31,7},{16,8},{17... | collective-permute-start | bytes 196616 | tf_op jit(solution)/shard_map/ppermute | solution.py:38
  12.9 10.0 %collective-permute-start.3 = (bf16[256,128]{1,0:T(8,128)(2,1)S(1)}, bf16[256,128]{1,0:T(8,128)(2,1)S(1)}, u32[]{:S(2)}, u32[]{:S(2)}) collective-permute-start(bf16[256,128]{1,0:T(8,128)(2,1)S(1)} %get-tuple-element.10), channel_id=1, source_target_pairs={{20,0},{21,1},{22,2},{23,3},{16,4},{17,5},{18,6},{19,7},{28,8},{29... | collective-permute-start | bytes 196616 | tf_op jit(solution)/shard_map/ppermute | solution.py:38
  14.5 8.4 %collective-permute-start.4 = (bf16[256,128]{1,0:T(8,128)(2,1)S(1)}, bf16[256,128]{1,0:T(8,128)(2,1)S(1)}, u32[]{:S(2)}, u32[]{:S(2)}) collective-permute-start(bf16[256,128]{1,0:T(8,128)(2,1)S(1)} %get-tuple-element.9), channel_id=1, source_target_pairs={{28,0},{29,1},{30,2},{31,3},{24,4},{25,5},{26,6},{27,7},{20,8},{21... | collective-permute-start | bytes 196616 | tf_op jit(solution)/shard_map/ppermute | solution.py:38
  18.7 5.3 %collective-permute-start.6 = (bf16[256,128]{1,0:T(8,128)(2,1)S(1)}, bf16[256,128]{1,0:T(8,128)(2,1)S(1)}, u32[]{:S(2)}, u32[]{:S(2)}) collective-permute-start(bf16[256,128]{1,0:T(8,128)(2,1)S(1)} %get-tuple-element.12), channel_id=1, source_target_pairs={{8,0},{9,1},{10,2},{11,3},{12,4},{13,5},{14,6},{15,7},{0,8},{1,9},... | collective-permute-start | bytes 196616 | tf_op jit(solution)/shard_map/ppermute | solution.py:38
  19.7 4.9 %collective-permute-start.7 = (bf16[256,128]{1,0:T(8,128)(2,1)S(1)}, bf16[256,128]{1,0:T(8,128)(2,1)S(1)}, u32[]{:S(2)}, u32[]{:S(2)}) collective-permute-start(bf16[256,128]{1,0:T(8,128)(2,1)S(1)} %get-tuple-element.14), channel_id=1, source_target_pairs={{4,0},{5,1},{6,2},{7,3},{0,4},{1,5},{2,6},{3,7},{12,8},{13,9},{14,... | collective-permute-start | bytes 196616 | tf_op jit(solution)/shard_map/ppermute | solution.py:38
  20.2 5.2 %collective-permute-start.8 = (bf16[256,128]{1,0:T(8,128)(2,1)S(1)}, bf16[256,128]{1,0:T(8,128)(2,1)S(1)}, u32[]{:S(2)}, u32[]{:S(2)}) collective-permute-start(bf16[256,128]{1,0:T(8,128)(2,1)S(1)} %get-tuple-element.13), channel_id=1, source_target_pairs={{12,0},{13,1},{14,2},{15,3},{8,4},{9,5},{10,6},{11,7},{4,8},{5,9},... | collective-permute-start | bytes 196616 | tf_op jit(solution)/shard_map/ppermute | solution.py:38
  25.5 6.5 %collective-permute-start.9 = (bf16[256,128]{1,0:T(8,128)(2,1)S(1)}, bf16[256,128]{1,0:T(8,128)(2,1)S(1)}, u32[]{:S(2)}, u32[]{:S(2)}) collective-permute-start(bf16[256,128]{1,0:T(8,128)(2,1)S(1)} %add_convert_fusion.2.refs_0_), channel_id=1, source_target_pairs={{8,0},{9,1},{10,2},{11,3},{12,4},{13,5},{14,6},{15,7},{0,8},{1,9},... | collective-permute-start | bytes 196616 | tf_op jit(solution)/shard_map/ppermute | solution.py:38
  27.1 6.9 %collective-permute-start.10 = (bf16[256,128]{1,0:T(8,128)(2,1)S(1)}, bf16[256,128]{1,0:T(8,128)(2,1)S(1)}, u32[]{:S(2)}, u32[]{:S(2)}) collective-permute-start(bf16[256,128]{1,0:T(8,128)(2,1)S(1)} %add_convert_fusion.2.refs_0_), channel_id=1, source_target_pairs={{16,0},{17,1},{18,2},{19,3},{20,4},{21,5},{22,6},{23,7},{24,8},{25... | collective-permute-start | bytes 196616 | tf_op jit(solution)/shard_map/ppermute | solution.py:38
  29.6 6.1 %collective-permute-start.11 = (bf16[256,128]{1,0:T(8,128)(2,1)S(1)}, bf16[256,128]{1,0:T(8,128)(2,1)S(1)}, u32[]{:S(2)}, u32[]{:S(2)}) collective-permute-start(bf16[256,128]{1,0:T(8,128)(2,1)S(1)} %add_convert_fusion.2.refs_0_), channel_id=1, source_target_pairs={{24,0},{25,1},{26,2},{27,3},{28,4},{29,5},{30,6},{31,7},{16,8},{17... | collective-permute-start | bytes 196616 | tf_op jit(solution)/shard_map/ppermute | solution.py:38
  30.5 19.1 %copy-start.1 = (bf16[1024,2048]{1,0:T(8,128)(2,1)S(1)}, bf16[1024,2048]{1,0:T(8,128)(2,1)}, u32[]{:S(2)}) copy-start(bf16[1024,2048]{1,0:T(8,128)(2,1)} %shapes.3) | copy-start | bytes 12582916
  30.5 6.7 %collective-permute-start.12 = (bf16[256,128]{1,0:T(8,128)(2,1)S(1)}, bf16[256,128]{1,0:T(8,128)(2,1)S(1)}, u32[]{:S(2)}, u32[]{:S(2)}) collective-permute-start(bf16[256,128]{1,0:T(8,128)(2,1)S(1)} %add_convert_fusion.2.refs_0_), channel_id=1, source_target_pairs={{1,0},{0,1},{3,2},{2,3},{5,4},{4,5},{7,6},{6,7},{9,8},{8,9},{11,10... | collective-permute-start | bytes 196616 | tf_op jit(solution)/shard_map/ppermute | solution.py:38
  32.0 5.2 %collective-permute-start.13 = (bf16[256,128]{1,0:T(8,128)(2,1)S(1)}, bf16[256,128]{1,0:T(8,128)(2,1)S(1)}, u32[]{:S(2)}, u32[]{:S(2)}) collective-permute-start(bf16[256,128]{1,0:T(8,128)(2,1)S(1)} %collective-permute-done.9.refs_1_), channel_id=1, source_target_pairs={{1,0},{0,1},{3,2},{2,3},{5,4},{4,5},{7,6},{6,7},{9,8},{8,9},{11,10... | collective-permute-start | bytes 196616 | tf_op jit(solution)/shard_map/ppermute | solution.py:38
  34.0 4.3 %collective-permute-start.14 = (bf16[256,128]{1,0:T(8,128)(2,1)S(1)}, bf16[256,128]{1,0:T(8,128)(2,1)S(1)}, u32[]{:S(2)}, u32[]{:S(2)}) collective-permute-start(bf16[256,128]{1,0:T(8,128)(2,1)S(1)} %collective-permute-done.10.refs_2_), channel_id=1, source_target_pairs={{1,0},{0,1},{3,2},{2,3},{5,4},{4,5},{7,6},{6,7},{9,8},{8,9},{11,10... | collective-permute-start | bytes 196616 | tf_op jit(solution)/shard_map/ppermute | solution.py:38
  35.7 4.3 %collective-permute-start.15 = (bf16[256,128]{1,0:T(8,128)(2,1)S(1)}, bf16[256,128]{1,0:T(8,128)(2,1)S(1)}, u32[]{:S(2)}, u32[]{:S(2)}) collective-permute-start(bf16[256,128]{1,0:T(8,128)(2,1)S(1)} %collective-permute-done.11.refs_3_), channel_id=1, source_target_pairs={{1,0},{0,1},{3,2},{2,3},{5,4},{4,5},{7,6},{6,7},{9,8},{8,9},{11,10... | collective-permute-start | bytes 196616 | tf_op jit(solution)/shard_map/ppermute | solution.py:38
  40.6 10.9 %copy-start.9 = (bf16[1024,256]{1,0:T(8,128)(2,1)}, bf16[1024,256]{1,0:T(8,128)(2,1)S(1)}, u32[]{:S(2)}) copy-start(bf16[1024,256]{1,0:T(8,128)(2,1)S(1)} %shard_map.55.mine) | copy-start | bytes 1572868
  40.6 2.0 %collective-permute-start.16 = (bf16[1024,256]{1,0:T(8,128)(2,1)S(1)}, bf16[1024,256]{1,0:T(8,128)(2,1)S(1)}, u32[]{:S(2)}, u32[]{:S(2)}) collective-permute-start(bf16[1024,256]{1,0:T(8,128)(2,1)S(1)} %shard_map.55.mine), channel_id=1, source_target_pairs={{2,0},{3,1},{0,2},{1,3},{6,4},{7,5},{4,6},{5,7},{10,8},{11,9},{8,1... | collective-permute-start | bytes 1572872 | tf_op jit(solution)/shard_map/ppermute | solution.py:38
  42.6 8.9 %copy-start.13 = (bf16[1024,256]{1,0:T(8,128)(2,1)}, bf16[1024,256]{1,0:T(8,128)(2,1)S(1)}, u32[]{:S(2)}) copy-start(bf16[1024,256]{1,0:T(8,128)(2,1)S(1)} %collective-permute-done.16.theirs) | copy-start | bytes 1572868
  45.0 15.9 %collective-permute-start.18 = (bf16[256,512]{1,0:T(8,128)(2,1)}, bf16[256,512]{1,0:T(8,128)(2,1)S(1)}, u32[]{:S(2)}, u32[]{:S(2)}) collective-permute-start(bf16[256,512]{1,0:T(8,128)(2,1)} %shard_map.56), channel_id=1, source_target_pairs={{4,0},{5,1},{12,2},{13,3},{20,4},{21,5},{28,6},{29,7},{6,8},{7,9},... | collective-permute-start | bytes 786440 | tf_op jit(solution)/shard_map/ppermute | solution.py:42
  46.6 17.5 %collective-permute-start.17 = (bf16[256,512]{1,0:T(8,128)(2,1)}, bf16[256,512]{1,0:T(8,128)(2,1)}, u32[]{:S(2)}, u32[]{:S(2)}) collective-permute-start(bf16[256,512]{1,0:T(8,128)(2,1)} %shard_map.56), channel_id=1, source_target_pairs={{0,0},{1,1},{8,2},{9,3},{16,4},{17,5},{24,6},{25,7},{2,8},{3,9},{1... | collective-permute-start | bytes 786440 | tf_op jit(solution)/shard_map/ppermute | solution.py:42
  51.5 15.4 %collective-permute-start.23 = (bf16[256,512]{1,0:T(8,128)(2,1)}, bf16[256,512]{1,0:T(8,128)(2,1)}, u32[]{:S(2)}, u32[]{:S(2)}) collective-permute-start(bf16[256,512]{1,0:T(8,128)(2,1)} %shard_map.57), channel_id=1, source_target_pairs={{1,0},{0,1},{3,2},{2,3},{5,4},{4,5},{7,6},{6,7},{9,8},{8,9},{11,10... | collective-permute-start | bytes 786440 | tf_op jit(solution)/shard_map/ppermute | solution.py:38
  53.0 2.2 %copy-start.2 = (bf16[1024,2048]{1,0:T(8,128)(2,1)S(1)}, bf16[1024,2048]{1,0:T(8,128)(2,1)}, u32[]{:S(2)}) copy-start(bf16[1024,2048]{1,0:T(8,128)(2,1)} %shapes.3) | copy-start | bytes 12582916
  55.2 1.0 copy-start.10
  56.2 1.0 copy-start.14
  59.2 1.0 copy-start.3
  60.9 39.4 %copy-start.4 = (bf16[512,512]{1,0:T(8,128)(2,1)S(1)}, bf16[512,512]{1,0:T(8,128)(2,1)}, u32[]{:S(2)}) copy-start(bf16[512,512]{1,0:T(8,128)(2,1)} %copy-done.3) | copy-start | bytes 1572868
  60.9 0.7 copy-start.19
  61.6 26.3 %collective-permute-start.21 = (bf16[512,512]{1,0:T(8,128)(2,1)}, bf16[512,512]{1,0:T(8,128)(2,1)S(1)}, u32[]{:S(2)}, u32[]{:S(2)}) collective-permute-start(bf16[512,512]{1,0:T(8,128)(2,1)} %shard_map.61), channel_id=1, source_target_pairs={{4,0},{5,1},{12,2},{13,3},{20,4},{21,5},{28,6},{29,7},{6,8},{7,9},... | collective-permute-start | bytes 1572872 | tf_op jit(solution)/shard_map/ppermute | solution.py:42
  64.1 28.1 %collective-permute-start.20 = (bf16[512,512]{1,0:T(8,128)(2,1)}, bf16[512,512]{1,0:T(8,128)(2,1)S(1)}, u32[]{:S(2)}, u32[]{:S(2)}) collective-permute-start(bf16[512,512]{1,0:T(8,128)(2,1)} %shard_map.60), channel_id=1, source_target_pairs={{0,0},{1,1},{8,2},{9,3},{16,4},{17,5},{24,6},{25,7},{2,8},{3,9},{1... | collective-permute-start | bytes 1572872 | tf_op jit(solution)/shard_map/ppermute | solution.py:42
  69.5 25.2 %collective-permute-start.19 = (bf16[512,512]{1,0:T(8,128)(2,1)}, bf16[512,512]{1,0:T(8,128)(2,1)S(1)}, u32[]{:S(2)}, u32[]{:S(2)}) collective-permute-start(bf16[512,512]{1,0:T(8,128)(2,1)} %shard_map.59), channel_id=1, source_target_pairs={{4,0},{5,1},{6,2},{7,3},{0,4},{1,5},{2,6},{3,7},{12,8},{13,9},{14,... | collective-permute-start | bytes 1572872 | tf_op jit(solution)/shard_map/ppermute | solution.py:38
  69.5 9.4 %collective-permute-start.24 = (bf16[256,512]{1,0:T(8,128)(2,1)}, bf16[256,512]{1,0:T(8,128)(2,1)S(1)}, u32[]{:S(2)}, u32[]{:S(2)}) collective-permute-start(bf16[256,512]{1,0:T(8,128)(2,1)} %collective-permute-done.17.refs_1_.refs_0_), channel_id=1, source_target_pairs={{1,0},{0,1},{3,2},{2,3},{5,4},{4,5},{7,6},{6,7},{9,8},{8,9},{11,10... | collective-permute-start | bytes 786440 | tf_op jit(solution)/shard_map/ppermute | solution.py:38
  70.0 13.6 %collective-permute-start.25 = (bf16[256,512]{1,0:T(8,128)(2,1)}, bf16[256,512]{1,0:T(8,128)(2,1)S(1)}, u32[]{:S(2)}, u32[]{:S(2)}) collective-permute-start(bf16[256,512]{1,0:T(8,128)(2,1)} %copy-done.19), channel_id=1, source_target_pairs={{1,0},{0,1},{3,2},{2,3},{5,4},{4,5},{7,6},{6,7},{9,8},{8,9},{11,10... | collective-permute-start | bytes 786440 | tf_op jit(solution)/shard_map/ppermute | solution.py:38
  78.9 15.8 %copy-start.15 = (bf16[256,512]{1,0:T(8,128)(2,1)}, bf16[256,512]{1,0:T(8,128)(2,1)S(1)}, u32[]{:S(2)}) copy-start(bf16[256,512]{1,0:T(8,128)(2,1)S(1)} %collective-permute-done.24.refs_2_.refs_1_.refs_0_) | copy-start | bytes 786436
  83.6 11.0 %copy-start.17 = (bf16[256,512]{1,0:T(8,128)(2,1)}, bf16[256,512]{1,0:T(8,128)(2,1)S(1)}, u32[]{:S(2)}) copy-start(bf16[256,512]{1,0:T(8,128)(2,1)S(1)} %collective-permute-done.25.refs_3_.refs_1_) | copy-start | bytes 786436
  87.9 6.8 %copy-start.5 = (bf16[512,512]{1,0:T(8,128)(2,1)}, bf16[512,512]{1,0:T(8,128)(2,1)S(1)}, u32[]{:S(2)}) copy-start(bf16[512,512]{1,0:T(8,128)(2,1)S(1)} %collective-permute-done.21.refs_2_.refs_5_.refs_0_) | copy-start | bytes 1572868
  92.1 2.5 %copy-start.7 = (bf16[512,512]{1,0:T(8,128)(2,1)}, bf16[512,512]{1,0:T(8,128)(2,1)S(1)}, u32[]{:S(2)}) copy-start(bf16[512,512]{1,0:T(8,128)(2,1)S(1)} %collective-permute-done.20.refs_1_.refs_4_.refs_0_) | copy-start | bytes 1572868
  94.7 0.8 copy-start.11
  95.5 8.1 %copy-start.20 = (bf16[256,512]{1,0:T(8,128)(2,1)S(1)}, bf16[256,512]{1,0:T(8,128)(2,1)}, u32[]{:S(2)}) copy-start(bf16[256,512]{1,0:T(8,128)(2,1)} %copy-done.19) | copy-start | bytes 786436
  95.5 4.8 %collective-permute-start.22 = (bf16[512,512]{1,0:T(8,128)(2,1)}, bf16[512,512]{1,0:T(8,128)(2,1)}, u32[]{:S(2)}, u32[]{:S(2)}) collective-permute-start(bf16[512,512]{1,0:T(8,128)(2,1)} %shard_map.62.refs_2_), channel_id=1, source_target_pairs={{2,0},{3,1},{0,2},{1,3},{6,4},{7,5},{4,6},{5,7},{10,8},{11,9},{8,1... | collective-permute-start | bytes 1572872 | tf_op jit(solution)/shard_map/ppermute | solution.py:38
  95.5 10.8 %copy-start.6 = (bf16[512,512]{1,0:T(8,128)(2,1)S(1)}, bf16[512,512]{1,0:T(8,128)(2,1)}, u32[]{:S(2)}) copy-start(bf16[512,512]{1,0:T(8,128)(2,1)} %shard_map.66.refs_1_) | copy-start | bytes 1572868
  95.5 15.6 %collective-permute-start.29 = (bf16[512,512]{1,0:T(8,128)(2,1)}, bf16[512,512]{1,0:T(8,128)(2,1)}, u32[]{:S(2)}, u32[]{:S(2)}) collective-permute-start(bf16[512,512]{1,0:T(8,128)(2,1)} %shard_map.66.refs_1_), channel_id=1, source_target_pairs={{1,0},{0,1},{3,2},{2,3},{5,4},{4,5},{7,6},{6,7},{9,8},{8,9},{11,10... | collective-permute-start | bytes 1572872 | tf_op jit(solution)/shard_map/ppermute | solution.py:38
  96.3 10.1 %copy-start.8 = (bf16[512,512]{1,0:T(8,128)(2,1)S(1)}, bf16[512,512]{1,0:T(8,128)(2,1)}, u32[]{:S(2)}) copy-start(bf16[512,512]{1,0:T(8,128)(2,1)} %shard_map.65.refs_0_) | copy-start | bytes 1572868
  96.3 25.1 %collective-permute-start.28 = (bf16[512,512]{1,0:T(8,128)(2,1)}, bf16[512,512]{1,0:T(8,128)(2,1)}, u32[]{:S(2)}, u32[]{:S(2)}) collective-permute-start(bf16[512,512]{1,0:T(8,128)(2,1)} %shard_map.65.refs_0_), channel_id=1, source_target_pairs={{1,0},{0,1},{3,2},{2,3},{5,4},{4,5},{7,6},{6,7},{9,8},{8,9},{11,10... | collective-permute-start | bytes 1572872 | tf_op jit(solution)/shard_map/ppermute | solution.py:38
  97.6 27.9 %collective-permute-start.26 = (bf16[512,512]{1,0:T(8,128)(2,1)}, bf16[512,512]{1,0:T(8,128)(2,1)S(1)}, u32[]{:S(2)}, u32[]{:S(2)}) collective-permute-start(bf16[512,512]{1,0:T(8,128)(2,1)} %shard_map.64), channel_id=1, source_target_pairs={{0,0},{1,1},{8,2},{9,3},{16,4},{17,5},{24,6},{25,7},{2,8},{3,9},{1... | collective-permute-start | bytes 1572872 | tf_op jit(solution)/shard_map/ppermute | solution.py:42
  100.0 25.4 %collective-permute-start.27 = (bf16[512,512]{1,0:T(8,128)(2,1)}, bf16[512,512]{1,0:T(8,128)(2,1)}, u32[]{:S(2)}, u32[]{:S(2)}) collective-permute-start(bf16[512,512]{1,0:T(8,128)(2,1)} %shard_map.64), channel_id=1, source_target_pairs={{4,0},{5,1},{12,2},{13,3},{20,4},{21,5},{28,6},{29,7},{6,8},{7,9},... | collective-permute-start | bytes 1572872 | tf_op jit(solution)/shard_map/ppermute | solution.py:42
  100.3 1.0 copy-start.12
  101.3 1.0 copy-start.21
  106.4 3.1 %copy-start.16 = (bf16[256,512]{1,0:T(8,128)(2,1)S(1)}, bf16[256,512]{1,0:T(8,128)(2,1)}, u32[]{:S(2)}) copy-start(bf16[256,512]{1,0:T(8,128)(2,1)} %copy-done.15) | copy-start | bytes 786436
  106.4 3.1 %copy-start.18 = (bf16[256,512]{1,0:T(8,128)(2,1)S(1)}, bf16[256,512]{1,0:T(8,128)(2,1)}, u32[]{:S(2)}) copy-start(bf16[256,512]{1,0:T(8,128)(2,1)} %copy-done.17) | copy-start | bytes 786436

commit v8 on v7

--- a/solution.py
+++ b/solution.py
@@ -259,7 +259,8 @@
     landed = cross(lots[0], [])
     both = []
     if units > 2:
-        both = [lots[2]] + [swap(lots[2], sizes, 0, 0, dk) for dk in range(1, n_groups)]
+        held = after(lots[2], landed[0])
+        both = [held] + [swap(held, sizes, 0, 0, dk) for dk in range(1, n_groups)]
     landed, others = relay(landed, [])
     pieces = [(landed, others, 0)]
 

time: 131 us -> 130 us (level)
  local copies, waits for them, and re-layouts: 13 us -> 10.1 us
  waiting for transfers between devices: 42.4 us -> 45.3 us
  Pallas kernels: 23 us -> 21.4 us
  other arithmetic: 2.92 us -> 4.44 us
    ppermute x6, waiting for transfers between devices: 9.59 us -> 18.2 us  [across(): lax.ppermute(array, AXES, moves(sizes, lambda i, j, k: (j, i ^ flip, k)))]
    ppermute x24, waiting for transfers between devices: 32.8 us -> 27.1 us  [swap(): lax.ppermute(array, AXES, moves(sizes, lambda i, j, k: (i ^ di, j ^ dj, k...]
    unnamed x50 -> x42, local copies, waits for them, and re-layouts: 10.9 us -> 7.97 us
    concatenate x0 -> x1, other arithmetic: none -> 1.86 us  [body(): landed = cross(jnp.concatenate(both, axis=0), [done] * n_high)]
  transfers between devices with their start and end apart: 30 -> 30, of which waited for: 16 -> 19; matrix products, arithmetic and copies ran while one was open for 10% -> 11% of each run, Pallas kernels for 13% -> 11%
where the time goes in v8:
time: 130 us
  waiting for transfers between devices  45.3 us (35%)
  starting transfers between devices  38.7 us (30%)
  Pallas kernels  21.4 us (16%)
  local copies, waits for them, and re-layouts  10.1 us (8%)
  matrix products  9.19 us (7%)
  other arithmetic  4.44 us (3%)
    ppermute x24, starting transfers between devices, swap(): lax.ppermute(array, AXES, moves(sizes, lambda i, j, k: (i ^ di, j ^ dj, k...  28 us
    ppermute x24, waiting for transfers between devices, swap(): lax.ppermute(array, AXES, moves(sizes, lambda i, j, k: (i ^ di, j ^ dj, k...  27.1 us
    ppermute x6, waiting for transfers between devices, across(): lax.ppermute(array, AXES, moves(sizes, lambda i, j, k: (j, i ^ flip, k)))  18.2 us
    pallas_call x5, Pallas kernels, place_panel(): pl.pallas_call(functools.partial(panel_kernel, len(pieces)), grid_spec=pl...  14.6 us
    ppermute x6, starting transfers between devices, across(): lax.ppermute(array, AXES, moves(sizes, lambda i, j, k: (j, i ^ flip, k)))  10.7 us
    dot_general x4, matrix products, partial(): return jnp.dot(rows, factor_cols, preferred_element_type=jnp.float32)  9.19 us
    unnamed x42, local copies, waits for them, and re-layouts  7.97 us
    pallas_call x3, Pallas kernels, project(): pl.pallas_call(project_kernel, grid_spec=pltpu.PrefetchScalarGridSpec(num...  4.96 us
  transfers between devices with their start and end apart: 30, of which 19 were waited for; matrix products, arithmetic and copies ran while one was open for 11% of the time, Pallas kernels for 11%

profile of v8, /device:TPU:4, one launch (start us, length us, event | category | flops | bytes accessed | tf_op | source)
XLA Modules:
  0.0 129.6 jit_solution(6464629283099539523)
XLA Ops:
  0.0 1.2 copy-done
  1.2 2.3 %fusion.8 = bf16[512,256]{1,0:T(8,128)(2,1)S(1)} fusion(bf16[2048,256]{1,0:T(8,128)(2,1)S(1)} %copy-done, bf16[2048,2048]{1,0:T(8,128)(2,1)} %param.6, s32[]{:T(128)S(6)} %select_n.84), kind=kOutput, calls=%fused_computation.8 | convolution fusion | flops 537001984 | bytes 3407876 | tf_op jit(solution)/shard_map/dot_general | solution.py:210
  3.6 2.3 %fusion.11 = bf16[512,256]{1,0:T(8,128)(2,1)S(1)} fusion(bf16[2048,256]{1,0:T(8,128)(2,1)S(1)} %copy-done, bf16[2048,2048]{1,0:T(8,128)(2,1)} %param.6, s32[]{:T(128)S(6)} %select_n.92), kind=kOutput, calls=%fused_computation.9 | convolution fusion | flops 537001984 | bytes 3407876 | tf_op jit(solution)/shard_map/dot_general | solution.py:210
  6.5 2.3 %add_convert_fusion.1 = bf16[512,256]{1,0:T(8,128)(2,1)S(1)} fusion(bf16[512,256]{1,0:T(8,128)(2,1)S(1)} %collective-permute-done, bf16[2048,256]{1,0:T(8,128)(2,1)S(1)} %copy-done, bf16[2048,2048]{1,0:T(8,128)(2,1)} %param.6, s32[]{:T(128)S(6)} %select_n.83), kind=kOutput, calls=%fused_computation.13 | convolution fusion | flops 537264128 | bytes 3670020 | tf_op jit(solution)/shard_map/dot_general | solution.py:210
  8.9 2.7 %collective-permute-start.1 = (bf16[256,128]{1,0:T(8,128)(2,1)S(1)}, bf16[256,128]{1,0:T(8,128)(2,1)S(1)}, u32[]{:S(2)}, u32[]{:S(2)}) collective-permute-start(bf16[256,128]{1,0:T(8,128)(2,1)S(1)} %get-tuple-element.7), channel_id=1, source_target_pairs={{16,0},{17,1},{18,2},{19,3},{20,4},{21,5},{22,6},{23,7},{24,8},{25... | collective-permute-start | bytes 196616 | tf_op jit(solution)/shard_map/ppermute | solution.py:38
  11.5 1.3 %collective-permute-start.2 = (bf16[256,128]{1,0:T(8,128)(2,1)S(1)}, bf16[256,128]{1,0:T(8,128)(2,1)S(1)}, u32[]{:S(2)}, u32[]{:S(2)}) collective-permute-start(bf16[256,128]{1,0:T(8,128)(2,1)S(1)} %get-tuple-element.10), channel_id=1, source_target_pairs={{24,0},{25,1},{26,2},{27,3},{28,4},{29,5},{30,6},{31,7},{16,8},{17... | collective-permute-start | bytes 196616 | tf_op jit(solution)/shard_map/ppermute | solution.py:38
  12.9 1.6 %collective-permute-start.3 = (bf16[256,128]{1,0:T(8,128)(2,1)S(1)}, bf16[256,128]{1,0:T(8,128)(2,1)S(1)}, u32[]{:S(2)}, u32[]{:S(2)}) collective-permute-start(bf16[256,128]{1,0:T(8,128)(2,1)S(1)} %get-tuple-element.9), channel_id=1, source_target_pairs={{20,0},{21,1},{22,2},{23,3},{16,4},{17,5},{18,6},{19,7},{28,8},{29... | collective-permute-start | bytes 196616 | tf_op jit(solution)/shard_map/ppermute | solution.py:38
  14.5 1.9 %collective-permute-start.4 = (bf16[256,128]{1,0:T(8,128)(2,1)S(1)}, bf16[256,128]{1,0:T(8,128)(2,1)S(1)}, u32[]{:S(2)}, u32[]{:S(2)}) collective-permute-start(bf16[256,128]{1,0:T(8,128)(2,1)S(1)} %get-tuple-element.8), channel_id=1, source_target_pairs={{28,0},{29,1},{30,2},{31,3},{24,4},{25,5},{26,6},{27,7},{20,8},{21... | collective-permute-start | bytes 196616 | tf_op jit(solution)/shard_map/ppermute | solution.py:38
  16.4 2.3 %add_convert_fusion = bf16[512,256]{1,0:T(8,128)(2,1)S(1)} fusion(bf16[512,256]{1,0:T(8,128)(2,1)S(1)} %collective-permute-done.5, bf16[2048,256]{1,0:T(8,128)(2,1)S(1)} %copy-done, bf16[2048,2048]{1,0:T(8,128)(2,1)} %param.6, s32[]{:T(128)S(6)} %select_n.91), kind=kOutput, calls=%fused_computation.12 | convolution fusion | flops 537264128 | bytes 3670020 | tf_op jit(solution)/shard_map/dot_general | solution.py:210
  18.7 1.0 collective-permute-start.6
  20.2 2.1 %collective-permute-start.8 = (bf16[256,128]{1,0:T(8,128)(2,1)S(1)}, bf16[256,128]{1,0:T(8,128)(2,1)S(1)}, u32[]{:S(2)}, u32[]{:S(2)}) collective-permute-start(bf16[256,128]{1,0:T(8,128)(2,1)S(1)} %get-tuple-element.12), channel_id=1, source_target_pairs={{12,0},{13,1},{14,2},{15,3},{8,4},{9,5},{10,6},{11,7},{4,8},{5,9},... | collective-permute-start | bytes 196616 | tf_op jit(solution)/shard_map/ppermute | solution.py:38
  22.3 0.6 collective-permute-done.3
  22.9 1.2 collective-permute-done.6
  24.1 0.6 collective-permute-done.7
  24.6 0.8 collective-permute-done.8
  25.5 1.6 %collective-permute-start.9 = (bf16[256,128]{1,0:T(8,128)(2,1)S(1)}, bf16[256,128]{1,0:T(8,128)(2,1)S(1)}, u32[]{:S(2)}, u32[]{:S(2)}) collective-permute-start(bf16[256,128]{1,0:T(8,128)(2,1)S(1)} %add_convert_fusion.2.refs_0_), channel_id=1, source_target_pairs={{8,0},{9,1},{10,2},{11,3},{12,4},{13,5},{14,6},{15,7},{0,8},{1,9},... | collective-permute-start | bytes 196616 | tf_op jit(solution)/shard_map/ppermute | solution.py:38
  27.1 2.5 %collective-permute-start.10 = (bf16[256,128]{1,0:T(8,128)(2,1)S(1)}, bf16[256,128]{1,0:T(8,128)(2,1)S(1)}, u32[]{:S(2)}, u32[]{:S(2)}) collective-permute-start(bf16[256,128]{1,0:T(8,128)(2,1)S(1)} %add_convert_fusion.2.refs_0_), channel_id=1, source_target_pairs={{16,0},{17,1},{18,2},{19,3},{20,4},{21,5},{22,6},{23,7},{24,8},{25... | collective-permute-start | bytes 196616 | tf_op jit(solution)/shard_map/ppermute | solution.py:38
  29.6 0.9 collective-permute-start.11
  30.5 1.5 %collective-permute-start.12 = (bf16[256,128]{1,0:T(8,128)(2,1)S(1)}, bf16[256,128]{1,0:T(8,128)(2,1)S(1)}, u32[]{:S(2)}, u32[]{:S(2)}) collective-permute-start(bf16[256,128]{1,0:T(8,128)(2,1)S(1)} %add_convert_fusion.2.refs_0_), channel_id=1, source_target_pairs={{1,0},{0,1},{3,2},{2,3},{5,4},{4,5},{7,6},{6,7},{9,8},{8,9},{11,10... | collective-permute-start | bytes 196616 | tf_op jit(solution)/shard_map/ppermute | solution.py:38
  32.5 1.5 %collective-permute-done.10.refs_2_ = bf16[256,128]{1,0:T(8,128)(2,1)S(1)} collective-permute-done((bf16[256,128]{1,0:T(8,128)(2,1)S(1)}, bf16[256,128]{1,0:T(8,128)(2,1)S(1)}, u32[]{:S(2)}, u32[]{:S(2)}) %collective-permute-start.10) | collective-permute-done | bytes 65568 | tf_op jit(solution)/shard_map/ppermute | solution.py:38
  34.0 1.5 %collective-permute-start.14 = (bf16[256,128]{1,0:T(8,128)(2,1)S(1)}, bf16[256,128]{1,0:T(8,128)(2,1)S(1)}, u32[]{:S(2)}, u32[]{:S(2)}) collective-permute-start(bf16[256,128]{1,0:T(8,128)(2,1)S(1)} %collective-permute-done.10.refs_2_), channel_id=1, source_target_pairs={{1,0},{0,1},{3,2},{2,3},{5,4},{4,5},{7,6},{6,7},{9,8},{8,9},{11,10... | collective-permute-start | bytes 196616 | tf_op jit(solution)/shard_map/ppermute | solution.py:38
  35.7 1.5 %collective-permute-start.15 = (bf16[256,128]{1,0:T(8,128)(2,1)S(1)}, bf16[256,128]{1,0:T(8,128)(2,1)S(1)}, u32[]{:S(2)}, u32[]{:S(2)}) collective-permute-start(bf16[256,128]{1,0:T(8,128)(2,1)S(1)} %collective-permute-done.11.refs_3_), channel_id=1, source_target_pairs={{1,0},{0,1},{3,2},{2,3},{5,4},{4,5},{7,6},{6,7},{9,8},{8,9},{11,10... | collective-permute-start | bytes 196616 | tf_op jit(solution)/shard_map/ppermute | solution.py:38
  37.2 1.0 collective-permute-done.14.refs_6_
  38.3 1.7 %collective-permute-done.15.refs_7_ = bf16[256,128]{1,0:T(8,128)(2,1)S(1)} collective-permute-done((bf16[256,128]{1,0:T(8,128)(2,1)S(1)}, bf16[256,128]{1,0:T(8,128)(2,1)S(1)}, u32[]{:S(2)}, u32[]{:S(2)}) %collective-permute-start.15) | collective-permute-done | bytes 65568 | tf_op jit(solution)/shard_map/ppermute | solution.py:38
  39.9 0.6 shard_map.55.mine
  40.7 1.4 %slice.3.shapes = bf16[256,2048]{1,0:T(8,128)(2,1)S(1)} slice(bf16[1024,2048]{1,0:T(8,128)(2,1)} %shapes.3), slice={[0:256], [0:2048]} | slice | bytes 2097152 | tf_op jit(solution)/shard_map/slice | solution.py:235
  42.5 0.6 broadcast_in_dim.2.scale
  43.1 1.9 %shard_map.56 = bf16[256,512]{1,0:T(8,128)(2,1)} custom-call(s32[1]{0:T(128)} %bitcast.2.spots, bf16[1024,256]{1,0:T(8,128)(2,1)S(1)} %shard_map.55.mine, bf16[1024,256]{1,0:T(8,128)(2,1)S(1)} %collective-permute-done.16.theirs, f32[2,2048,128]{2,1,0:T(8,128)S(1)} %broadcast_in_dim.2.scale, bf16[256,2048]{1,0:T(8,128)(2,1)S(1)} %slice.3.shapes), custom_call_target="tpu_custom_call" | custom-call | flops 1 | bytes 1 | tf_op jit(solution)/shard_map/pallas_call | solution.py:116
  45.0 1.5 %collective-permute-start.18 = (bf16[256,512]{1,0:T(8,128)(2,1)}, bf16[256,512]{1,0:T(8,128)(2,1)S(1)}, u32[]{:S(2)}, u32[]{:S(2)}) collective-permute-start(bf16[256,512]{1,0:T(8,128)(2,1)} %shard_map.56), channel_id=1, source_target_pairs={{4,0},{5,1},{12,2},{13,3},{20,4},{21,5},{28,6},{29,7},{6,8},{7,9},... | collective-permute-start | bytes 786440 | tf_op jit(solution)/shard_map/ppermute | solution.py:42
  46.5 3.1 %collective-permute-start.17 = (bf16[256,512]{1,0:T(8,128)(2,1)}, bf16[256,512]{1,0:T(8,128)(2,1)S(1)}, u32[]{:S(2)}, u32[]{:S(2)}) collective-permute-start(bf16[256,512]{1,0:T(8,128)(2,1)} %shard_map.56), channel_id=1, source_target_pairs={{0,0},{1,1},{8,2},{9,3},{16,4},{17,5},{24,6},{25,7},{2,8},{3,9},{1... | collective-permute-start | bytes 786440 | tf_op jit(solution)/shard_map/ppermute | solution.py:42
  49.6 1.9 %shard_map.58.refs_1_ = bf16[512,512]{1,0:T(8,128)(2,1)S(1)} custom-call(s32[1]{0:T(128)} %bitcast.2.spots, bf16[1024,256]{1,0:T(8,128)(2,1)S(1)} %shard_map.55.mine, bf16[1024,256]{1,0:T(8,128)(2,1)S(1)} %collective-permute-done.16.theirs, f32[2,2048,128]{2,1,0:T(8,128)S(1)} %broadcast_in_dim.2.scale, bf16[1024,2048]{1,0:T(8,128)(2,1)S(1)} %copy-done.1), custom_call_target="tpu_custom_call" | custom-call | flops 1 | bytes 1 | tf_op jit(solution)/shard_map/pallas_call | solution.py:116
  51.5 0.8 copy.20.refs_0_
  52.4 0.8 copy.19.refs_0_
  53.2 1.2 shard_map.57.refs_0_
  54.3 2.2 %broadcast_select_fusion = (bf16[512,512]{1,0:T(8,128)(2,1)}, bf16[512,512]{1,0:T(8,128)(2,1)}) fusion(bf16[512,512]{1,0:T(8,128)(2,1)S(1)} %shard_map.58.refs_1_, pred[]{:T(512)S(6)} %eq.13, bf16[256,512]{1,0:T(8,128)(2,1)S(1)} %shard_map.57.refs_0_, bf16[256,512]{1,0:T(8,128)(2,1)} %shard_map.56), kind=kLoop, calls=%fused_computation.14 | loop fusion | flops 1310720 | bytes 2097153 | tf_op jit(solution)/shard_map/jit(_where)/select_n | solution.py:267
  56.5 2.8 %collective-permute-done.18.refs_2_.refs_1_ = bf16[256,512]{1,0:T(8,128)(2,1)S(1)} collective-permute-done((bf16[256,512]{1,0:T(8,128)(2,1)}, bf16[256,512]{1,0:T(8,128)(2,1)S(1)}, u32[]{:S(2)}, u32[]{:S(2)}) %collective-permute-start.18) | collective-permute-done | bytes 262176 | tf_op jit(solution)/shard_map/ppermute | solution.py:42
  59.3 0.7 copy-done.15
  60.0 4.0 %collective-permute-done.17.refs_1_.refs_0_ = bf16[256,512]{1,0:T(8,128)(2,1)S(1)} collective-permute-done((bf16[256,512]{1,0:T(8,128)(2,1)}, bf16[256,512]{1,0:T(8,128)(2,1)S(1)}, u32[]{:S(2)}, u32[]{:S(2)}) %collective-permute-start.17) | collective-permute-done | bytes 262176 | tf_op jit(solution)/shard_map/ppermute | solution.py:42
  64.0 0.7 copy-done.8
  64.7 1.1 collective-permute-start.23
  65.8 1.9 %collective-permute-start.20 = (bf16[512,512]{1,0:T(8,128)(2,1)}, bf16[512,512]{1,0:T(8,128)(2,1)S(1)}, u32[]{:S(2)}, u32[]{:S(2)}) collective-permute-start(bf16[512,512]{1,0:T(8,128)(2,1)} %shard_map.60), channel_id=1, source_target_pairs={{0,0},{1,1},{8,2},{9,3},{16,4},{17,5},{24,6},{25,7},{2,8},{3,9},{1... | collective-permute-start | bytes 1572872 | tf_op jit(solution)/shard_map/ppermute | solution.py:42
  67.8 1.0 collective-permute-start.24
  68.8 4.5 %collective-permute-done.23 = bf16[256,512]{1,0:T(8,128)(2,1)} collective-permute-done((bf16[256,512]{1,0:T(8,128)(2,1)}, bf16[256,512]{1,0:T(8,128)(2,1)}, u32[]{:S(2)}, u32[]{:S(2)}) %collective-permute-start.23) | collective-permute-done | bytes 262176 | tf_op jit(solution)/shard_map/ppermute | solution.py:38
  73.3 2.0 %collective-permute-start.25 = (bf16[256,512]{1,0:T(8,128)(2,1)}, bf16[256,512]{1,0:T(8,128)(2,1)S(1)}, u32[]{:S(2)}, u32[]{:S(2)}) collective-permute-start(bf16[256,512]{1,0:T(8,128)(2,1)} %copy-done.15), channel_id=1, source_target_pairs={{1,0},{0,1},{3,2},{2,3},{5,4},{4,5},{7,6},{6,7},{9,8},{8,9},{11,10... | collective-permute-start | bytes 786440 | tf_op jit(solution)/shard_map/ppermute | solution.py:38
  75.2 1.9 %pad_maximum_fusion.1.refs_0_ = bf16[512,512]{1,0:T(8,128)(2,1)} fusion(bf16[256,512]{1,0:T(8,128)(2,1)} %collective-permute-done.23, bf16[256,512]{1,0:T(8,128)(2,1)} %shard_map.64), kind=kLoop, calls=%fused_computation.11 | loop fusion | flops 1048576 | bytes 1048576 | tf_op jit(solution)/shard_map/concatenate | solution.py:278
  77.1 1.7 %collective-permute-done.24.refs_2_.refs_1_.refs_0_ = bf16[256,512]{1,0:T(8,128)(2,1)S(1)} collective-permute-done((bf16[256,512]{1,0:T(8,128)(2,1)}, bf16[256,512]{1,0:T(8,128)(2,1)S(1)}, u32[]{:S(2)}, u32[]{:S(2)}) %collective-permute-start.24) | collective-permute-done | bytes 262176 | tf_op jit(solution)/shard_map/ppermute | solution.py:38
  78.8 3.7 %collective-permute-done.25.refs_3_.refs_1_ = bf16[256,512]{1,0:T(8,128)(2,1)S(1)} collective-permute-done((bf16[256,512]{1,0:T(8,128)(2,1)}, bf16[256,512]{1,0:T(8,128)(2,1)S(1)}, u32[]{:S(2)}, u32[]{:S(2)}) %collective-permute-start.25) | collective-permute-done | bytes 262176 | tf_op jit(solution)/shard_map/ppermute | solution.py:38
  82.5 1.9 %collective-permute-done.21.refs_2_.refs_5_.refs_0_ = bf16[512,512]{1,0:T(8,128)(2,1)S(1)} collective-permute-done((bf16[512,512]{1,0:T(8,128)(2,1)}, bf16[512,512]{1,0:T(8,128)(2,1)S(1)}, u32[]{:S(2)}, u32[]{:S(2)}) %collective-permute-start.21) | collective-permute-done | bytes 524320 | tf_op jit(solution)/shard_map/ppermute | solution.py:42
  84.4 8.2 %collective-permute-done.20.refs_1_.refs_4_.refs_0_ = bf16[512,512]{1,0:T(8,128)(2,1)S(1)} collective-permute-done((bf16[512,512]{1,0:T(8,128)(2,1)}, bf16[512,512]{1,0:T(8,128)(2,1)S(1)}, u32[]{:S(2)}, u32[]{:S(2)}) %collective-permute-start.20) | collective-permute-done | bytes 524320 | tf_op jit(solution)/shard_map/ppermute | solution.py:42
  92.6 0.8 copy-done.4
  93.4 0.8 copy-done.6
  94.2 0.6 collective-permute-start.29
  94.8 1.5 %collective-permute-start.28 = (bf16[512,512]{1,0:T(8,128)(2,1)}, bf16[512,512]{1,0:T(8,128)(2,1)}, u32[]{:S(2)}, u32[]{:S(2)}) collective-permute-start(bf16[512,512]{1,0:T(8,128)(2,1)} %shard_map.66.refs_0_), channel_id=1, source_target_pairs={{1,0},{0,1},{3,2},{2,3},{5,4},{4,5},{7,6},{6,7},{9,8},{8,9},{11,10... | collective-permute-start | bytes 1572872 | tf_op jit(solution)/shard_map/ppermute | solution.py:38
  96.3 4.2 %collective-permute-start.26 = (bf16[512,512]{1,0:T(8,128)(2,1)}, bf16[512,512]{1,0:T(8,128)(2,1)}, u32[]{:S(2)}, u32[]{:S(2)}) collective-permute-start(bf16[512,512]{1,0:T(8,128)(2,1)} %shard_map.65), channel_id=1, source_target_pairs={{0,0},{1,1},{8,2},{9,3},{16,4},{17,5},{24,6},{25,7},{2,8},{3,9},{1... | collective-permute-start | bytes 1572872 | tf_op jit(solution)/shard_map/ppermute | solution.py:42
  100.7 1.0 copy-done.7
  101.8 1.0 copy-done.17
  102.8 1.2 shard_map.63.left
  104.1 1.7 %shard_map.68.refs_2_ = f32[1024,2048]{1,0:T(8,128)} custom-call(s32[1]{0:T(128)} %bitcast.13.spots, bf16[1024,1024]{1,0:T(8,128)(2,1)S(1)} %shard_map.63.left, bf16[256,512]{1,0:T(8,128)(2,1)S(1)} %copy-done.9, bf16[256,512]{1,0:T(8,128)(2,1)S(1)} %copy-done.16), custom_call_target="tpu_custom_call" | custom-call | flops 1 | bytes 1 | tf_op jit(solution)/shard_map/pallas_call | solution.py:176
  105.9 3.0 %shard_map.69.refs_2_ = f32[1024,2048]{1,0:T(8,128)} custom-call(s32[2]{0:T(128)S(1)} %pad_add_fusion.4.spots, bf16[1024,1024]{1,0:T(8,128)(2,1)S(1)} %shard_map.63.left, bf16[512,512]{1,0:T(8,128)(2,1)S(1)} %copy-done.5, bf16[512,512]{1,0:T(8,128)(2,1)S(1)} %copy-done.3, f32[1024,2048]{1,0:T(8,128)} %shard_map.68.refs_2_), custom_call_target="tpu_custom_call", output_to_operand_aliasing={{}: (4, {})} | custom-call | flops 1 | bytes 1 | tf_op jit(solution)/shard_map/pallas_call | solution.py:176
  108.9 1.7 %shard_map.70.refs_2_ = f32[1024,2048]{1,0:T(8,128)} custom-call(s32[1]{0:T(128)} %bitcast.10.spots, bf16[1024,1024]{1,0:T(8,128)(2,1)S(1)} %shard_map.63.left, bf16[256,512]{1,0:T(8,128)(2,1)S(1)} %copy-done.12, bf16[256,512]{1,0:T(8,128)(2,1)S(1)} %copy-done.14, f32[1024,2048]{1,0:T(8,128)} %shard_map.69.refs_2_), custom_call_target="tpu_custom_call", output_to_operand_aliasing={{}: (4, {})} | custom-call | flops 1 | bytes 1 | tf_op jit(solution)/shard_map/pallas_call | solution.py:176
  110.7 9.4 %collective-permute-done.28.refs_0_ = bf16[512,512]{1,0:T(8,128)(2,1)} collective-permute-done((bf16[512,512]{1,0:T(8,128)(2,1)}, bf16[512,512]{1,0:T(8,128)(2,1)}, u32[]{:S(2)}, u32[]{:S(2)}) %collective-permute-start.28) | collective-permute-done | bytes 524320 | tf_op jit(solution)/shard_map/ppermute | solution.py:38
  120.1 4.1 %shard_map.71.refs_2_ = f32[1024,2048]{1,0:T(8,128)} custom-call(s32[2]{0:T(128)S(1)} %pad_add_fusion.3.spots, bf16[1024,1024]{1,0:T(8,128)(2,1)S(1)} %shard_map.63.left, bf16[512,512]{1,0:T(8,128)(2,1)} %collective-permute-done.28.refs_0_, bf16[512,512]{1,0:T(8,128)(2,1)} %collective-permute-done.29.refs_1_, ...), custom_call_target="tpu_custom_call", output_to_operand_aliasing={{}: (4, {})} | custom-call | flops 1 | bytes 1 | tf_op jit(solution)/shard_map/pallas_call | solution.py:176
  124.2 1.0 collective-permute-done.26.refs_0_
  125.5 4.1 %shard_map.72 = f32[1024,2048]{1,0:T(8,128)} custom-call(s32[2]{0:T(128)S(1)} %get-tuple-element.16.spots, bf16[1024,1024]{1,0:T(8,128)(2,1)S(1)} %shard_map.63.left, bf16[512,512]{1,0:T(8,128)(2,1)} %collective-permute-done.26.refs_0_, bf16[512,512]{1,0:T(8,128)(2,1)} %collective-permute-done.27.refs_1_, ...), custom_call_target="tpu_custom_call", output_to_operand_aliasing={{}: (4, {})} | custom-call | flops 1 | bytes 1 | tf_op jit(solution)/shard_map/pallas_call | solution.py:176
  (73 shorter events, 3.4 us)
Async XLA Ops:
  0.0 1.2 copy-start
  3.5 3.0 %collective-permute-start = (bf16[512,256]{1,0:T(8,128)(2,1)S(1)}, bf16[512,256]{1,0:T(8,128)(2,1)S(1)}, u32[]{:S(2)}, u32[]{:S(2)}) collective-permute-start(bf16[512,256]{1,0:T(8,128)(2,1)S(1)} %fusion.8), channel_id=1, source_target_pairs={{2,0},{3,1},{0,2},{1,3},{6,4},{7,5},{4,6},{5,7},{10,8},{11,9},{8,1... | collective-permute-start | bytes 786440 | tf_op jit(solution)/shard_map/ppermute | solution.py:38
  5.9 36.2 %copy-start.18 = (f32[2048]{0:T(1024)S(1)}, f32[2048]{0:T(1024)}, u32[]{:S(2)}) copy-start(f32[2048]{0:T(1024)} %param.8) | copy-start | bytes 24580
  5.9 36.2 %copy-start.19 = (f32[2048]{0:T(1024)S(1)}, f32[2048]{0:T(1024)}, u32[]{:S(2)}) copy-start(f32[2048]{0:T(1024)} %param.9) | copy-start | bytes 24580
  5.9 10.4 %collective-permute-start.5 = (bf16[512,256]{1,0:T(8,128)(2,1)S(1)}, bf16[512,256]{1,0:T(8,128)(2,1)S(1)}, u32[]{:S(2)}, u32[]{:S(2)}) collective-permute-start(bf16[512,256]{1,0:T(8,128)(2,1)S(1)} %fusion.11), channel_id=1, source_target_pairs={{2,0},{3,1},{0,2},{1,3},{6,4},{7,5},{4,6},{5,7},{10,8},{11,9},{8,1... | collective-permute-start | bytes 786440 | tf_op jit(solution)/shard_map/ppermute | solution.py:38
  8.9 10.8 %collective-permute-start.1 = (bf16[256,128]{1,0:T(8,128)(2,1)S(1)}, bf16[256,128]{1,0:T(8,128)(2,1)S(1)}, u32[]{:S(2)}, u32[]{:S(2)}) collective-permute-start(bf16[256,128]{1,0:T(8,128)(2,1)S(1)} %get-tuple-element.7), channel_id=1, source_target_pairs={{16,0},{17,1},{18,2},{19,3},{20,4},{21,5},{22,6},{23,7},{24,8},{25... | collective-permute-start | bytes 196616 | tf_op jit(solution)/shard_map/ppermute | solution.py:38
  11.5 8.7 %collective-permute-start.2 = (bf16[256,128]{1,0:T(8,128)(2,1)S(1)}, bf16[256,128]{1,0:T(8,128)(2,1)S(1)}, u32[]{:S(2)}, u32[]{:S(2)}) collective-permute-start(bf16[256,128]{1,0:T(8,128)(2,1)S(1)} %get-tuple-element.10), channel_id=1, source_target_pairs={{24,0},{25,1},{26,2},{27,3},{28,4},{29,5},{30,6},{31,7},{16,8},{17... | collective-permute-start | bytes 196616 | tf_op jit(solution)/shard_map/ppermute | solution.py:38
  12.9 10.0 %collective-permute-start.3 = (bf16[256,128]{1,0:T(8,128)(2,1)S(1)}, bf16[256,128]{1,0:T(8,128)(2,1)S(1)}, u32[]{:S(2)}, u32[]{:S(2)}) collective-permute-start(bf16[256,128]{1,0:T(8,128)(2,1)S(1)} %get-tuple-element.9), channel_id=1, source_target_pairs={{20,0},{21,1},{22,2},{23,3},{16,4},{17,5},{18,6},{19,7},{28,8},{29... | collective-permute-start | bytes 196616 | tf_op jit(solution)/shard_map/ppermute | solution.py:38
  14.5 8.4 %collective-permute-start.4 = (bf16[256,128]{1,0:T(8,128)(2,1)S(1)}, bf16[256,128]{1,0:T(8,128)(2,1)S(1)}, u32[]{:S(2)}, u32[]{:S(2)}) collective-permute-start(bf16[256,128]{1,0:T(8,128)(2,1)S(1)} %get-tuple-element.8), channel_id=1, source_target_pairs={{28,0},{29,1},{30,2},{31,3},{24,4},{25,5},{26,6},{27,7},{20,8},{21... | collective-permute-start | bytes 196616 | tf_op jit(solution)/shard_map/ppermute | solution.py:38
  18.7 5.3 %collective-permute-start.6 = (bf16[256,128]{1,0:T(8,128)(2,1)S(1)}, bf16[256,128]{1,0:T(8,128)(2,1)S(1)}, u32[]{:S(2)}, u32[]{:S(2)}) collective-permute-start(bf16[256,128]{1,0:T(8,128)(2,1)S(1)} %get-tuple-element.11), channel_id=1, source_target_pairs={{8,0},{9,1},{10,2},{11,3},{12,4},{13,5},{14,6},{15,7},{0,8},{1,9},... | collective-permute-start | bytes 196616 | tf_op jit(solution)/shard_map/ppermute | solution.py:38
  19.7 4.9 %collective-permute-start.7 = (bf16[256,128]{1,0:T(8,128)(2,1)S(1)}, bf16[256,128]{1,0:T(8,128)(2,1)S(1)}, u32[]{:S(2)}, u32[]{:S(2)}) collective-permute-start(bf16[256,128]{1,0:T(8,128)(2,1)S(1)} %get-tuple-element.13), channel_id=1, source_target_pairs={{4,0},{5,1},{6,2},{7,3},{0,4},{1,5},{2,6},{3,7},{12,8},{13,9},{14,... | collective-permute-start | bytes 196616 | tf_op jit(solution)/shard_map/ppermute | solution.py:38
  20.2 5.2 %collective-permute-start.8 = (bf16[256,128]{1,0:T(8,128)(2,1)S(1)}, bf16[256,128]{1,0:T(8,128)(2,1)S(1)}, u32[]{:S(2)}, u32[]{:S(2)}) collective-permute-start(bf16[256,128]{1,0:T(8,128)(2,1)S(1)} %get-tuple-element.12), channel_id=1, source_target_pairs={{12,0},{13,1},{14,2},{15,3},{8,4},{9,5},{10,6},{11,7},{4,8},{5,9},... | collective-permute-start | bytes 196616 | tf_op jit(solution)/shard_map/ppermute | solution.py:38
  25.5 6.5 %collective-permute-start.9 = (bf16[256,128]{1,0:T(8,128)(2,1)S(1)}, bf16[256,128]{1,0:T(8,128)(2,1)S(1)}, u32[]{:S(2)}, u32[]{:S(2)}) collective-permute-start(bf16[256,128]{1,0:T(8,128)(2,1)S(1)} %add_convert_fusion.2.refs_0_), channel_id=1, source_target_pairs={{8,0},{9,1},{10,2},{11,3},{12,4},{13,5},{14,6},{15,7},{0,8},{1,9},... | collective-permute-start | bytes 196616 | tf_op jit(solution)/shard_map/ppermute | solution.py:38
  27.1 6.9 %collective-permute-start.10 = (bf16[256,128]{1,0:T(8,128)(2,1)S(1)}, bf16[256,128]{1,0:T(8,128)(2,1)S(1)}, u32[]{:S(2)}, u32[]{:S(2)}) collective-permute-start(bf16[256,128]{1,0:T(8,128)(2,1)S(1)} %add_convert_fusion.2.refs_0_), channel_id=1, source_target_pairs={{16,0},{17,1},{18,2},{19,3},{20,4},{21,5},{22,6},{23,7},{24,8},{25... | collective-permute-start | bytes 196616 | tf_op jit(solution)/shard_map/ppermute | solution.py:38
  29.6 6.1 %collective-permute-start.11 = (bf16[256,128]{1,0:T(8,128)(2,1)S(1)}, bf16[256,128]{1,0:T(8,128)(2,1)S(1)}, u32[]{:S(2)}, u32[]{:S(2)}) collective-permute-start(bf16[256,128]{1,0:T(8,128)(2,1)S(1)} %add_convert_fusion.2.refs_0_), channel_id=1, source_target_pairs={{24,0},{25,1},{26,2},{27,3},{28,4},{29,5},{30,6},{31,7},{16,8},{17... | collective-permute-start | bytes 196616 | tf_op jit(solution)/shard_map/ppermute | solution.py:38
  30.5 6.7 %collective-permute-start.12 = (bf16[256,128]{1,0:T(8,128)(2,1)S(1)}, bf16[256,128]{1,0:T(8,128)(2,1)S(1)}, u32[]{:S(2)}, u32[]{:S(2)}) collective-permute-start(bf16[256,128]{1,0:T(8,128)(2,1)S(1)} %add_convert_fusion.2.refs_0_), channel_id=1, source_target_pairs={{1,0},{0,1},{3,2},{2,3},{5,4},{4,5},{7,6},{6,7},{9,8},{8,9},{11,10... | collective-permute-start | bytes 196616 | tf_op jit(solution)/shard_map/ppermute | solution.py:38
  32.0 5.2 %collective-permute-start.13 = (bf16[256,128]{1,0:T(8,128)(2,1)S(1)}, bf16[256,128]{1,0:T(8,128)(2,1)S(1)}, u32[]{:S(2)}, u32[]{:S(2)}) collective-permute-start(bf16[256,128]{1,0:T(8,128)(2,1)S(1)} %collective-permute-done.9.refs_1_), channel_id=1, source_target_pairs={{1,0},{0,1},{3,2},{2,3},{5,4},{4,5},{7,6},{6,7},{9,8},{8,9},{11,10... | collective-permute-start | bytes 196616 | tf_op jit(solution)/shard_map/ppermute | solution.py:38
  34.0 4.3 %collective-permute-start.14 = (bf16[256,128]{1,0:T(8,128)(2,1)S(1)}, bf16[256,128]{1,0:T(8,128)(2,1)S(1)}, u32[]{:S(2)}, u32[]{:S(2)}) collective-permute-start(bf16[256,128]{1,0:T(8,128)(2,1)S(1)} %collective-permute-done.10.refs_2_), channel_id=1, source_target_pairs={{1,0},{0,1},{3,2},{2,3},{5,4},{4,5},{7,6},{6,7},{9,8},{8,9},{11,10... | collective-permute-start | bytes 196616 | tf_op jit(solution)/shard_map/ppermute | solution.py:38
  35.7 4.3 %collective-permute-start.15 = (bf16[256,128]{1,0:T(8,128)(2,1)S(1)}, bf16[256,128]{1,0:T(8,128)(2,1)S(1)}, u32[]{:S(2)}, u32[]{:S(2)}) collective-permute-start(bf16[256,128]{1,0:T(8,128)(2,1)S(1)} %collective-permute-done.11.refs_3_), channel_id=1, source_target_pairs={{1,0},{0,1},{3,2},{2,3},{5,4},{4,5},{7,6},{6,7},{9,8},{8,9},{11,10... | collective-permute-start | bytes 196616 | tf_op jit(solution)/shard_map/ppermute | solution.py:38
  40.6 2.0 %collective-permute-start.16 = (bf16[1024,256]{1,0:T(8,128)(2,1)S(1)}, bf16[1024,256]{1,0:T(8,128)(2,1)S(1)}, u32[]{:S(2)}, u32[]{:S(2)}) collective-permute-start(bf16[1024,256]{1,0:T(8,128)(2,1)S(1)} %shard_map.55.mine), channel_id=1, source_target_pairs={{2,0},{3,1},{0,2},{1,3},{6,4},{7,5},{4,6},{5,7},{10,8},{11,9},{8,1... | collective-permute-start | bytes 1572872 | tf_op jit(solution)/shard_map/ppermute | solution.py:38
  40.6 9.0 %copy-start.1 = (bf16[1024,2048]{1,0:T(8,128)(2,1)S(1)}, bf16[1024,2048]{1,0:T(8,128)(2,1)}, u32[]{:S(2)}) copy-start(bf16[1024,2048]{1,0:T(8,128)(2,1)} %shapes.3) | copy-start | bytes 12582916
  45.0 14.3 %collective-permute-start.18 = (bf16[256,512]{1,0:T(8,128)(2,1)}, bf16[256,512]{1,0:T(8,128)(2,1)S(1)}, u32[]{:S(2)}, u32[]{:S(2)}) collective-permute-start(bf16[256,512]{1,0:T(8,128)(2,1)} %shard_map.56), channel_id=1, source_target_pairs={{4,0},{5,1},{12,2},{13,3},{20,4},{21,5},{28,6},{29,7},{6,8},{7,9},... | collective-permute-start | bytes 786440 | tf_op jit(solution)/shard_map/ppermute | solution.py:42
  46.5 17.4 %collective-permute-start.17 = (bf16[256,512]{1,0:T(8,128)(2,1)}, bf16[256,512]{1,0:T(8,128)(2,1)S(1)}, u32[]{:S(2)}, u32[]{:S(2)}) collective-permute-start(bf16[256,512]{1,0:T(8,128)(2,1)} %shard_map.56), channel_id=1, source_target_pairs={{0,0},{1,1},{8,2},{9,3},{16,4},{17,5},{24,6},{25,7},{2,8},{3,9},{1... | collective-permute-start | bytes 786440 | tf_op jit(solution)/shard_map/ppermute | solution.py:42
  54.3 9.6 %copy-start.10 = (bf16[256,512]{1,0:T(8,128)(2,1)}, bf16[256,512]{1,0:T(8,128)(2,1)S(1)}, u32[]{:S(2)}) copy-start(bf16[256,512]{1,0:T(8,128)(2,1)S(1)} %shard_map.57.refs_0_) | copy-start | bytes 786436
  59.3 0.7 copy-start.15
  60.0 24.4 %collective-permute-start.21 = (bf16[512,512]{1,0:T(8,128)(2,1)}, bf16[512,512]{1,0:T(8,128)(2,1)S(1)}, u32[]{:S(2)}, u32[]{:S(2)}) collective-permute-start(bf16[512,512]{1,0:T(8,128)(2,1)} %shard_map.61), channel_id=1, source_target_pairs={{4,0},{5,1},{12,2},{13,3},{20,4},{21,5},{28,6},{29,7},{6,8},{7,9},... | collective-permute-start | bytes 1572872 | tf_op jit(solution)/shard_map/ppermute | solution.py:42
  64.0 0.7 copy-start.8
  64.7 39.4 %copy-start.9 = (bf16[256,512]{1,0:T(8,128)(2,1)S(1)}, bf16[256,512]{1,0:T(8,128)(2,1)}, u32[]{:S(2)}) copy-start(bf16[256,512]{1,0:T(8,128)(2,1)} %copy-done.8) | copy-start | bytes 786436
  64.7 8.6 %collective-permute-start.23 = (bf16[256,512]{1,0:T(8,128)(2,1)}, bf16[256,512]{1,0:T(8,128)(2,1)}, u32[]{:S(2)}, u32[]{:S(2)}) collective-permute-start(bf16[256,512]{1,0:T(8,128)(2,1)} %shard_map.64), channel_id=1, source_target_pairs={{1,0},{0,1},{3,2},{2,3},{5,4},{4,5},{7,6},{6,7},{9,8},{8,9},{11,10... | collective-permute-start | bytes 786440 | tf_op jit(solution)/shard_map/ppermute | solution.py:38
  65.8 26.8 %collective-permute-start.20 = (bf16[512,512]{1,0:T(8,128)(2,1)}, bf16[512,512]{1,0:T(8,128)(2,1)S(1)}, u32[]{:S(2)}, u32[]{:S(2)}) collective-permute-start(bf16[512,512]{1,0:T(8,128)(2,1)} %shard_map.60), channel_id=1, source_target_pairs={{0,0},{1,1},{8,2},{9,3},{16,4},{17,5},{24,6},{25,7},{2,8},{3,9},{1... | collective-permute-start | bytes 1572872 | tf_op jit(solution)/shard_map/ppermute | solution.py:42
  67.7 24.9 %collective-permute-start.19 = (bf16[512,512]{1,0:T(8,128)(2,1)}, bf16[512,512]{1,0:T(8,128)(2,1)S(1)}, u32[]{:S(2)}, u32[]{:S(2)}) collective-permute-start(bf16[512,512]{1,0:T(8,128)(2,1)} %shard_map.59), channel_id=1, source_target_pairs={{4,0},{5,1},{6,2},{7,3},{0,4},{1,5},{2,6},{3,7},{12,8},{13,9},{14,... | collective-permute-start | bytes 1572872 | tf_op jit(solution)/shard_map/ppermute | solution.py:38
  67.8 11.0 %collective-permute-start.24 = (bf16[256,512]{1,0:T(8,128)(2,1)}, bf16[256,512]{1,0:T(8,128)(2,1)S(1)}, u32[]{:S(2)}, u32[]{:S(2)}) collective-permute-start(bf16[256,512]{1,0:T(8,128)(2,1)} %copy-done.8), channel_id=1, source_target_pairs={{1,0},{0,1},{3,2},{2,3},{5,4},{4,5},{7,6},{6,7},{9,8},{8,9},{11,10... | collective-permute-start | bytes 786440 | tf_op jit(solution)/shard_map/ppermute | solution.py:38
  73.3 9.2 %collective-permute-start.25 = (bf16[256,512]{1,0:T(8,128)(2,1)}, bf16[256,512]{1,0:T(8,128)(2,1)S(1)}, u32[]{:S(2)}, u32[]{:S(2)}) collective-permute-start(bf16[256,512]{1,0:T(8,128)(2,1)} %copy-done.15), channel_id=1, source_target_pairs={{1,0},{0,1},{3,2},{2,3},{5,4},{4,5},{7,6},{6,7},{9,8},{8,9},{11,10... | collective-permute-start | bytes 786440 | tf_op jit(solution)/shard_map/ppermute | solution.py:38
  78.8 13.8 %copy-start.11 = (bf16[256,512]{1,0:T(8,128)(2,1)}, bf16[256,512]{1,0:T(8,128)(2,1)S(1)}, u32[]{:S(2)}) copy-start(bf16[256,512]{1,0:T(8,128)(2,1)S(1)} %collective-permute-done.24.refs_2_.refs_1_.refs_0_) | copy-start | bytes 786436
  82.5 10.1 %copy-start.13 = (bf16[256,512]{1,0:T(8,128)(2,1)}, bf16[256,512]{1,0:T(8,128)(2,1)S(1)}, u32[]{:S(2)}) copy-start(bf16[256,512]{1,0:T(8,128)(2,1)S(1)} %collective-permute-done.25.refs_3_.refs_1_) | copy-start | bytes 786436
  84.4 8.2 %copy-start.2 = (bf16[512,512]{1,0:T(8,128)(2,1)}, bf16[512,512]{1,0:T(8,128)(2,1)S(1)}, u32[]{:S(2)}) copy-start(bf16[512,512]{1,0:T(8,128)(2,1)S(1)} %collective-permute-done.21.refs_2_.refs_5_.refs_0_) | copy-start | bytes 1572868
  92.6 0.8 copy-start.4
  93.4 0.8 copy-start.6
  94.2 9.9 %copy-start.16 = (bf16[256,512]{1,0:T(8,128)(2,1)S(1)}, bf16[256,512]{1,0:T(8,128)(2,1)}, u32[]{:S(2)}) copy-start(bf16[256,512]{1,0:T(8,128)(2,1)} %copy-done.15) | copy-start | bytes 786436
  94.2 6.6 %collective-permute-start.22 = (bf16[512,512]{1,0:T(8,128)(2,1)}, bf16[512,512]{1,0:T(8,128)(2,1)}, u32[]{:S(2)}, u32[]{:S(2)}) collective-permute-start(bf16[512,512]{1,0:T(8,128)(2,1)} %shard_map.62.refs_2_), channel_id=1, source_target_pairs={{2,0},{3,1},{0,2},{1,3},{6,4},{7,5},{4,6},{5,7},{10,8},{11,9},{8,1... | collective-permute-start | bytes 1572872 | tf_op jit(solution)/shard_map/ppermute | solution.py:38
  94.2 11.7 %copy-start.3 = (bf16[512,512]{1,0:T(8,128)(2,1)S(1)}, bf16[512,512]{1,0:T(8,128)(2,1)}, u32[]{:S(2)}) copy-start(bf16[512,512]{1,0:T(8,128)(2,1)} %shard_map.67.refs_1_) | copy-start | bytes 1572868
  94.2 16.4 %collective-permute-start.29 = (bf16[512,512]{1,0:T(8,128)(2,1)}, bf16[512,512]{1,0:T(8,128)(2,1)}, u32[]{:S(2)}, u32[]{:S(2)}) collective-permute-start(bf16[512,512]{1,0:T(8,128)(2,1)} %shard_map.67.refs_1_), channel_id=1, source_target_pairs={{1,0},{0,1},{3,2},{2,3},{5,4},{4,5},{7,6},{6,7},{9,8},{8,9},{11,10... | collective-permute-start | bytes 1572872 | tf_op jit(solution)/shard_map/ppermute | solution.py:38
  94.8 11.1 %copy-start.5 = (bf16[512,512]{1,0:T(8,128)(2,1)S(1)}, bf16[512,512]{1,0:T(8,128)(2,1)}, u32[]{:S(2)}) copy-start(bf16[512,512]{1,0:T(8,128)(2,1)} %shard_map.66.refs_0_) | copy-start | bytes 1572868
  94.8 25.3 %collective-permute-start.28 = (bf16[512,512]{1,0:T(8,128)(2,1)}, bf16[512,512]{1,0:T(8,128)(2,1)}, u32[]{:S(2)}, u32[]{:S(2)}) collective-permute-start(bf16[512,512]{1,0:T(8,128)(2,1)} %shard_map.66.refs_0_), channel_id=1, source_target_pairs={{1,0},{0,1},{3,2},{2,3},{5,4},{4,5},{7,6},{6,7},{9,8},{8,9},{11,10... | collective-permute-start | bytes 1572872 | tf_op jit(solution)/shard_map/ppermute | solution.py:38
  96.3 28.8 %collective-permute-start.26 = (bf16[512,512]{1,0:T(8,128)(2,1)}, bf16[512,512]{1,0:T(8,128)(2,1)}, u32[]{:S(2)}, u32[]{:S(2)}) collective-permute-start(bf16[512,512]{1,0:T(8,128)(2,1)} %shard_map.65), channel_id=1, source_target_pairs={{0,0},{1,1},{8,2},{9,3},{16,4},{17,5},{24,6},{25,7},{2,8},{3,9},{1... | collective-permute-start | bytes 1572872 | tf_op jit(solution)/shard_map/ppermute | solution.py:42
  100.5 25.0 %collective-permute-start.27 = (bf16[512,512]{1,0:T(8,128)(2,1)}, bf16[512,512]{1,0:T(8,128)(2,1)}, u32[]{:S(2)}, u32[]{:S(2)}) collective-permute-start(bf16[512,512]{1,0:T(8,128)(2,1)} %shard_map.65), channel_id=1, source_target_pairs={{4,0},{5,1},{12,2},{13,3},{20,4},{21,5},{28,6},{29,7},{6,8},{7,9},... | collective-permute-start | bytes 1572872 | tf_op jit(solution)/shard_map/ppermute | solution.py:42
  100.7 1.0 copy-start.7
  101.8 1.0 copy-start.17
  105.9 3.1 %copy-start.12 = (bf16[256,512]{1,0:T(8,128)(2,1)S(1)}, bf16[256,512]{1,0:T(8,128)(2,1)}, u32[]{:S(2)}) copy-start(bf16[256,512]{1,0:T(8,128)(2,1)} %copy-done.11) | copy-start | bytes 786436
  105.9 3.1 %copy-start.14 = (bf16[256,512]{1,0:T(8,128)(2,1)S(1)}, bf16[256,512]{1,0:T(8,128)(2,1)}, u32[]{:S(2)}) copy-start(bf16[256,512]{1,0:T(8,128)(2,1)} %copy-done.13) | copy-start | bytes 786436
